TPU v7x, 32 devices: a whole 2x2x4 slice. The times are simulated.
32 devices in a mesh: member: 2 (over y), polar: 4 (over z), azimuth: 4 (over x, core).
Axes of the slice: x: 2, y: 2, z: 4, core: 2. Of those that a mesh axis runs over, the one named last changes fastest.
Arguments:
- conv_out: bfloat16 [32, 720, 640], P(('member', 'polar'), 'azimuth'), parts along dimension 0, may hold values from -6 to 6
- grad_out: bfloat16 [32, 720, 640], P(('member', 'polar'), 'azimuth'), parts along dimension 0, may hold values from -6 to 6
- w_in: bfloat16 [640, 1280], replicated, may hold values from -0.25 to 0.25
- b_in: float32 [1280], replicated, may hold values from -4 to 4
- w_out: bfloat16 [1280, 640], replicated, may hold values from -0.15625 to 0.15625
- basis_weight: float32 [9, 640], replicated, may hold values from -1 to 1
- filt: bfloat16 [9, 16, 640], replicated, may hold values from -2 to 2
- offsets: int32 [16, 9], replicated, may hold values from 0 to 15, as said below
Outputs:
- grad_in: bfloat16 [32, 720, 640], P(('member', 'polar'), 'azimuth'), parts along dimension 0
There are 2 independent parts, one for each index of `member`. A program takes and returns all parts, laid end to end along the dimension named above; an argument that names none is the same for every part. Nothing has to cross between parts.
Inputs may be any that keep to these rules, and one draw needn't show every extreme that they name: offsets[i, k] lies within 3 rows of i; column 0 is i, column 1 is min(i + 3, 15), column 2 is max(i - 3, 0).
All inputs are finite; a program needn't handle non-finite values.
Results may differ from a plain program's by a relative error of at most 0.006.
Values may be sent and summed in bfloat16 or wider, within the bound.
No kernel may reach another device: no remote copies, remote signals or barrier semaphores. Data moves between devices by JAX's collectives and lax.ppermute only.
A program may use at most 64 MiB of HBM per device.

v0:
```python
import functools
import math

import jax
import jax.numpy as jnp
import ml_dtypes
import numpy as np
from jax import lax
from jax.experimental import pallas as pl
from jax.experimental.pallas import tpu as pltpu
from jax.sharding import PartitionSpec as P

REACH = 3
LANES = 128
HALF = 64
TERMS = 3
NEAR = 1
VMEM = pltpu.MemorySpace.VMEM
NO_COST = pl.CostEstimate(flops=0, bytes_accessed=0, transcendentals=0)


def round_up(value, unit):
    return -(-value // unit) * unit


def partner(me, step, count, sign):
    if count & (count - 1) == 0:
        return me ^ step
    return lax.rem(me + sign * step + count, count)


def far_first(number, count):
    return sorted(range(number), key=lambda i: (i // count, i % count <= NEAR))


def exchange(block, step, count):
    if step == 0:
        return block
    pairs = [(a, int(partner_static(a, step, count))) for a in range(count)]
    return lax.ppermute(block, "azimuth", pairs)


def partner_static(a, step, count, sign=1):
    return a ^ step if count & (count - 1) == 0 else (a + sign * step) % count


def tables(count, part, modes):
    length = count * part
    whole = modes // LANES * LANES
    order = np.concatenate(
        [
            np.arange(whole),
            modes + np.arange(whole),
            np.arange(whole, modes),
            modes + np.arange(whole, modes),
        ]
    )
    positions = np.arange(length)
    waves = np.arange(modes)
    phase = (positions[:, None] * waves[None, :]) % length
    angle = (2.0 * math.pi / length) * phase
    scale = 1.0 / math.sqrt(length)
    factor = np.where(waves == 0, 1.0, 2.0)
    analysis = np.concatenate([np.cos(angle), -np.sin(angle)], axis=1) * scale
    synth = np.concatenate([np.cos(angle) * factor, -np.sin(angle) * factor], axis=1) * scale
    analysis = analysis.astype(np.float32).astype(ml_dtypes.bfloat16)[:, order]
    synth = synth.astype(np.float32).astype(ml_dtypes.bfloat16)[:, order]
    wide = round_up(part, HALF)
    window = round_up(HALF + wide, LANES)
    forth = np.zeros((count, HALF + window, 2 * modes), ml_dtypes.bfloat16)
    back = np.zeros((count * wide, 2 * modes), ml_dtypes.bfloat16)
    for s in range(count):
        forth[s, HALF : HALF + part] = analysis[s * part : (s + 1) * part]
        back[s * wide : s * wide + part] = synth[s * part : (s + 1) * part]
    return forth, back


def twice_gelu_slope(scaled):
    power = math.log2(2.0 / math.sqrt(math.pi)) - (1.0 / math.log(2.0)) * (scaled * scaled)
    return (1.0 + lax.erf(scaled)) + scaled * jnp.exp2(power)


def dot_nt(left, right):
    return lax.dot_general(left, right, (((1,), (1,)), ((), ())), preferred_element_type=jnp.float32)


def dot_nn(left, right):
    return jnp.dot(left, right, preferred_element_type=jnp.float32)


def mlp_kernel(count, half, sent, chunks, conv_ref, grad_ref, win_ref, bias_ref, wout_ref, *rest):
    outs, (tall_conv, tall_grad, pre_ref, back_ref, slope_ref, total_ref) = rest[-6 - len(sent) : -6], rest[-6:]
    part, channels = conv_ref.shape[1:]
    wide = round_up(part, HALF)
    rows = tall_conv.shape[0] // wide
    owned = channels // count
    block = pre_ref.shape[2]
    steps = win_ref.shape[1] // block
    me = lax.axis_index("azimuth")
    def stack(tall, source):
        for row in range(rows):
            whole = part // 16 * 16
            tall[row * wide + whole : (row + 1) * wide, :] = jnp.zeros((wide - whole, channels), jnp.bfloat16)
            tall[row * wide : row * wide + part, :] = source[half * rows + row]

    group = 48
    groups = rows * wide // group

    def span(step):
        return slice(step * block, (step + 1) * block)

    def project_pre(step):
        pre_ref[step % 2] = dot_nn(tall_conv[...], win_ref[:, span(step)])

    def project_back(step):
        back_ref[step % 2] = dot_nt(tall_grad[...], wout_ref[span(step), :])

    def slope(step, first, last):
        root = math.sqrt(0.5)
        bias = bias_ref[span(step)].reshape(1, block) * root
        for g in range(first, last):
            some = slice(g * group, (g + 1) * group)
            value = back_ref[step % 2, some, :] * twice_gelu_slope(pre_ref[step % 2, some, :] * root + bias)
            slope_ref[some, span(step)] = value.astype(jnp.bfloat16)

    def gather(first, last):
        at = slice(first * block, last * block)
        term = dot_nt(win_ref[:, at], slope_ref[:, at])
        total_ref[...] = term if first == 0 else total_ref[...] + term

    stack(tall_conv, conv_ref)
    project_pre(0)
    stack(tall_grad, grad_ref)
    project_back(0)
    gathered = 0
    thirds = [groups * n // 3 for n in range(4)]
    for step in range(steps):
        if step + 1 < steps:
            project_pre(step + 1)
        slope(step, thirds[0], thirds[1])
        if step - gathered == 2:
            gather(gathered, step)
            gathered = step
        slope(step, thirds[1], thirds[2])
        if step + 1 < steps:
            project_back(step + 1)
        slope(step, thirds[2], thirds[3])
    gather(gathered, steps)
    for out, (k, start, size) in zip(outs, sent):
        target = partner(me, k, count, 1)
        for begin, width in chunks:
            if start <= begin < start + size:
                first = pl.multiple_of(count * begin + target * width, 32)
                value = 0.5 * total_ref[pl.ds(first, width), :]
                out[begin - start : begin - start + width, :] = value.astype(jnp.bfloat16)


def mlp(conv_out, grad_out, w_in, b_in, w_out, count, half, halves, sent, chunks, after):
    rows, part, channels = conv_out.shape
    rows //= halves
    block = 256
    wide = round_up(part, HALF)
    vmem = pl.BlockSpec(memory_space=VMEM)
    out_shape = [jax.ShapeDtypeStruct((size, rows * wide), jnp.bfloat16) for _, _, size in sent]
    return pl.pallas_call(
        functools.partial(mlp_kernel, count, half, sent, chunks),
        in_specs=[vmem] * 5 + [pl.BlockSpec(memory_space=pl.ANY)] * len(after),
        out_specs=[vmem] * len(out_shape),
        out_shape=out_shape,
        scratch_shapes=[
            pltpu.VMEM((rows * wide, channels), jnp.bfloat16),
            pltpu.VMEM((rows * wide, channels), jnp.bfloat16),
            pltpu.VMEM((2, rows * wide, block), jnp.float32),
            pltpu.VMEM((2, rows * wide, block), jnp.float32),
            pltpu.VMEM((rows * wide, w_in.shape[1]), jnp.bfloat16),
            pltpu.VMEM((channels, rows * wide), jnp.float32),
        ],
        compiler_params=pltpu.CompilerParams(vmem_limit_bytes=16 * 2**20),
        cost_estimate=NO_COST,
        name="mlp",
    )(conv_out, grad_out, w_in, b_in, w_out, *after)


def analysis_kernel(count, rows, chunk, *refs):
    own_ref, first_ref, second_ref = refs[-3:]
    start, size = chunk
    halves = next(h for h in range(1, rows + 1) if refs[h * count].ndim == 3)
    table_ref = refs[halves * count]
    ranks = far_first(halves * count, count)
    pieces = [refs[ranks.index(i)] for i in range(halves * count)]
    rows_each = rows // halves
    wide = refs[0].shape[1] // rows_each
    window = table_ref.shape[1] - HALF
    even = lax.rem(lax.axis_index("polar"), 2) == 0

    def columns(row, k):
        half, row = divmod(row, rows_each)
        piece = pieces[half * count + k]
        base = 0 if half == halves - 1 and k > NEAR else start
        first = row * wide // LANES * LANES
        return piece[base : base + size, first : first + window]

    shifts = [row % rows_each * wide % LANES for row in range(rows)]
    for shift in sorted(set(shifts)):
        group = [row for row in range(rows) if shifts[row] == shift]
        total = None
        for k in range(count):
            left = jnp.concatenate([columns(row, k) for row in group], axis=0)
            term = dot_nn(left, table_ref[k, HALF - shift : HALF - shift + window, :])
            total = term if total is None else total + term
        for at, row in enumerate(group):
            mine = total[at * size : (at + 1) * size]
            own_ref[row] = mine

    def share(above, below):
        for h in range(REACH):
            above[h] = own_ref[rows - REACH + h].astype(jnp.bfloat16)
            below[h] = own_ref[h].astype(jnp.bfloat16)

    pl.when(even)(lambda: share(first_ref, second_ref))
    pl.when(jnp.logical_not(even))(lambda: share(second_ref, first_ref))


def analyze(pieces, table, rows, chunk, count, after):
    size = chunk[1]
    width = table.shape[2]
    halo = jax.ShapeDtypeStruct((REACH, size, width), jnp.bfloat16)
    return pl.pallas_call(
        functools.partial(analysis_kernel, count, rows, chunk),
        in_specs=[pl.BlockSpec(memory_space=VMEM)] * (len(pieces) + 1)
        + [pl.BlockSpec(memory_space=pl.ANY)] * len(after),
        out_specs=[pl.BlockSpec(memory_space=VMEM)] * 3,
        out_shape=[jax.ShapeDtypeStruct((rows, size, width), jnp.float32), halo, halo],
        compiler_params=pltpu.CompilerParams(vmem_limit_bytes=12 * 2**20),
        cost_estimate=NO_COST,
        name="analysis",
    )(*(pieces[i] for i in far_first(len(pieces), count)), table, *after)


def add_row(accs, spectrum, weight, target_row, filter_row, targets):
    size = spectrum.shape[0]
    masked = jnp.concatenate([jnp.where(target_row == t, weight, 0.0) for t in targets], axis=0)
    gains = dot_nn(masked.astype(jnp.bfloat16), filter_row)
    whole = (gains.shape[1] // 2) // LANES * LANES - LANES
    spec_re = spectrum[:, :whole]
    spec_im = spectrum[:, whole : 2 * whole]
    spec_x = spectrum[:, 2 * whole :]
    swapped = pltpu.roll(spec_x, HALF, 1)
    for at, target in enumerate(targets):
        gain = gains[at * size : (at + 1) * size]
        gain_re = gain[:, :whole]
        gain_rx = gain[:, whole : whole + LANES]
        gain_im = gain[:, whole + LANES : 2 * whole + LANES]
        gain_ix = gain[:, 2 * whole + LANES :]
        acc_re, acc_im, acc_x = accs[target]
        acc_re = acc_re + (gain_re * spec_re + gain_im * spec_im)
        acc_im = acc_im + (gain_re * spec_im - gain_im * spec_re)
        acc_x = acc_x + (gain_rx * spec_x + gain_ix * swapped)
        accs[target] = acc_re, acc_im, acc_x


def split_tiles(value):
    whole = (value.shape[1] - LANES) // 2
    return value[:, :whole], value[:, whole : 2 * whole], value[:, 2 * whole :]


def own_kernel(own_ref, weight_ref, target_ref, filter_ref, out_ref):
    rows, size, width = own_ref.shape
    accs = {t: split_tiles(jnp.zeros((size, width), jnp.float32)) for t in range(rows)}
    for row in range(rows):
        at = row + REACH
        targets = [t for t in range(rows) if abs(row - t) <= REACH]
        add_row(accs, own_ref[row], weight_ref[...], target_ref[at : at + 1, :], filter_ref[at], targets)
    for t in range(rows):
        out_ref[t] = jnp.concatenate(accs[t], axis=1)


def own_terms(own, weight, target, filters):
    return pl.pallas_call(
        own_kernel,
        in_specs=[pl.BlockSpec(memory_space=VMEM)] * 4,
        out_specs=pl.BlockSpec(memory_space=VMEM),
        out_shape=jax.ShapeDtypeStruct(own.shape, jnp.float32),
        compiler_params=pltpu.CompilerParams(vmem_limit_bytes=12 * 2**20),
        cost_estimate=NO_COST,
        name="own_terms",
    )(own, weight, target, filters)


def add_halo(accs, sides, rows, weight_ref, target_ref, filter_ref):
    for side, base in sides:
        for h in range(REACH):
            at = base + h + REACH
            targets = [t for t in range(rows) if abs(base + h - t) <= REACH]
            add_row(
                accs,
                side[h].astype(jnp.float32),
                weight_ref[...],
                target_ref[at : at + 1, :],
                filter_ref[at],
                targets,
            )


def side_kernel(part_ref, first_ref, weight_ref, target_ref, filter_ref, out_ref):
    rows = part_ref.shape[0]
    even = lax.rem(lax.axis_index("polar"), 2) == 0

    def combine(base):
        accs = {t: split_tiles(part_ref[t]) for t in range(rows)}
        add_halo(accs, [(first_ref, base)], rows, weight_ref, target_ref, filter_ref)
        for t in range(rows):
            out_ref[t] = jnp.concatenate(accs[t], axis=1)

    pl.when(even)(lambda: combine(rows))
    pl.when(jnp.logical_not(even))(lambda: combine(-REACH))


def side_terms(own, first, weight, target, filters):
    return pl.pallas_call(
        side_kernel,
        in_specs=[pl.BlockSpec(memory_space=VMEM)] * 5,
        out_specs=pl.BlockSpec(memory_space=VMEM),
        out_shape=jax.ShapeDtypeStruct(own.shape, jnp.float32),
        compiler_params=pltpu.CompilerParams(vmem_limit_bytes=12 * 2**20),
        cost_estimate=NO_COST,
        name="side_terms",
    )(own, first, weight, target, filters)


def finish_kernel(count, swaps, part_ref, *refs):
    halos, (weight_ref, target_ref, filter_ref, table_ref) = refs[:swaps], refs[swaps : swaps + 4]
    outs, stacked_ref = refs[-count - 1 : -1], refs[-1]
    rows, size, width = part_ref.shape
    part = outs[0].shape[0]
    even = lax.rem(lax.axis_index("polar"), 2) == 0

    def combine(bases):
        accs = {t: split_tiles(part_ref[t]) for t in range(rows)}
        sides = list(zip(halos, bases[-swaps:]))
        add_halo(accs, sides, rows, weight_ref, target_ref, filter_ref)
        for t in range(rows):
            stacked_ref[t * size : (t + 1) * size, :] = jnp.concatenate(accs[t], axis=1).astype(jnp.bfloat16)

    pl.when(even)(lambda: combine((rows, -REACH)))
    pl.when(jnp.logical_not(even))(lambda: combine((-REACH, rows)))
    grid = dot_nt(table_ref[...], stacked_ref[...])
    wide = grid.shape[0] // count
    for k in range(count):
        outs[k][...] = grid[k * wide : k * wide + part].astype(jnp.bfloat16)


def finish(own, halos, weight, target, filters, table, count, part, after):
    rows, size, width = own.shape
    return pl.pallas_call(
        functools.partial(finish_kernel, count, len(halos)),
        in_specs=[pl.BlockSpec(memory_space=VMEM)] * (5 + len(halos)) + [pl.BlockSpec(memory_space=pl.ANY)] * len(after),
        out_specs=[pl.BlockSpec(memory_space=VMEM)] * count,
        out_shape=[jax.ShapeDtypeStruct((part, rows * size), jnp.bfloat16)] * count,
        scratch_shapes=[pltpu.VMEM((rows * size, width), jnp.bfloat16)],
        compiler_params=pltpu.CompilerParams(vmem_limit_bytes=12 * 2**20),
        cost_estimate=NO_COST,
        name="finish",
    )(own, *halos, weight, target, filters, table, *after)


def add_kernel(count, chunk, grad_ref, *refs):
    out_ref, tall_ref, done_ref, sems = refs[-4:]
    ranks = far_first(count, count)
    pieces = [refs[ranks.index(k)] for k in range(count)]
    tiles, part, rows, _ = done_ref.shape
    start, size = chunk
    me = lax.axis_index("azimuth")

    def add(tile, mine):
        order = [[k for k in range(count) if partner_static(mine, k, count, -1) == s][0] for s in range(count)]
        lanes = range(tile * LANES, (tile + 1) * LANES)
        for row in range(rows):
            parts = []
            for s in range(lanes[0] // size, lanes[-1] // size + 1):
                low, high = max(lanes[0], s * size) - s * size, min(lanes[-1] + 1, (s + 1) * size) - s * size
                parts.append(pieces[order[s]][:, row * size + low : row * size + high])
            conv = jnp.concatenate(parts, axis=1).astype(jnp.float32)
            first = count * start + tile * LANES
            total = grad_ref[row, :, first : first + LANES].astype(jnp.float32) + conv
            tall_ref[tile, pl.ds(row, part, stride=rows), :] = total
        done_ref[tile] = tall_ref[tile].reshape(part, rows, LANES).astype(jnp.bfloat16)

    copies = []
    for tile in range(tiles):
        for mine in range(count):
            pl.when(me == mine)(functools.partial(add, tile, mine))
        lanes = pl.ds(count * start + tile * LANES, LANES)
        copies.append(pltpu.make_async_copy(done_ref.at[tile], out_ref.at[:, :, lanes], sems.at[tile]))
        copies[-1].start()
    for copy in copies:
        copy.wait()


def add_chunk(grad_out, pieces, chunk, count, before):
    rows, part, channels = grad_out.shape
    start, size = chunk
    tiles = count * size // LANES
    vmem = pl.BlockSpec(memory_space=VMEM)
    anywhere = pl.BlockSpec(memory_space=pl.ANY)
    return pl.pallas_call(
        functools.partial(add_kernel, count, chunk),
        in_specs=[vmem] * (1 + count) + [anywhere] * len(before),
        out_specs=anywhere,
        out_shape=jax.ShapeDtypeStruct((part, rows, channels), jnp.bfloat16),
        scratch_shapes=[
            pltpu.VMEM((tiles, rows * part, LANES), jnp.float32),
            pltpu.VMEM((tiles, part, rows, LANES), jnp.bfloat16),
            pltpu.SemaphoreType.DMA((tiles,)),
        ],
        input_output_aliases={1 + count: 0} if before else {},
        compiler_params=pltpu.CompilerParams(vmem_limit_bytes=12 * 2**20),
        cost_estimate=NO_COST,
        name="add_chunk",
    )(grad_out, *(pieces[i] for i in far_first(count, count)), *before)


def prepare_kernel(count, chunks, weight_ref, filt_ref, offset_ref, forth_ref, back_ref, *outs):
    filter_out, target_out, forth_out, back_out = outs[:4]
    me = lax.axis_index("azimuth")
    wide = back_ref.shape[0] // count
    for k in range(count):
        forth_out[k] = forth_ref[partner(me, k, count, -1)]
        first = pl.multiple_of(partner(me, k, count, 1) * wide, HALF)
        back_out[k * wide : (k + 1) * wide, :] = back_ref[pl.ds(first, wide), :]
    bases, channels = weight_ref.shape
    lats, width = filt_ref.shape[1:]
    ext, depth = target_out.shape
    rows = ext - 2 * REACH
    modes = width // 2
    whole = modes // LANES * LANES
    used = TERMS * bases
    for (start, size), out in zip(chunks, outs[4:]):
        first = count * start + lax.axis_index("azimuth") * size
        weight = pltpu.roll(weight_ref[...], lax.rem(channels - first, channels), 1)[:, :size]
        parts = []
        for _ in range(TERMS):
            rounded = weight.astype(jnp.bfloat16).astype(jnp.float32)
            parts.append(rounded)
            weight = weight - rounded
        parts.append(jnp.zeros((depth - used, size), jnp.float32))
        out[...] = jnp.concatenate(parts, axis=0).T
    start_lat = lax.axis_index("polar") * rows
    table = filt_ref[...].reshape(bases * lats, width)
    base = lax.broadcasted_iota(jnp.int32, (depth, bases * lats), 0)
    valid = base < used
    for _ in range(TERMS - 1):
        base = jnp.where(base >= bases, base - bases, base)
    column = lax.broadcasted_iota(jnp.int32, (depth, bases * lats), 1)
    for i in range(ext):
        lat = start_lat + (i - REACH)
        inside = (lat >= 0) & (lat < lats)
        lat = jnp.clip(lat, 0, lats - 1)
        pick = jnp.where(valid & (column == base * lats + lat), 1.0, 0.0).astype(jnp.bfloat16)
        row = dot_nn(pick, table)
        real, imag = row[:, :modes], row[:, modes:]
        rest_re, rest_im = real[:, whole:], imag[:, whole:]
        filter_out[i] = jnp.concatenate(
            [real[:, :whole], rest_re, rest_re, imag[:, :whole], rest_im, -rest_im], axis=1
        ).astype(jnp.bfloat16)
        local = jnp.where(inside, offset_ref[pl.ds(lat, 1), :] - start_lat, -1)
        spare = jnp.full((1, depth - used), -1, jnp.int32)
        target_out[i : i + 1, :] = jnp.concatenate([local] * TERMS + [spare], axis=1)


def prepare(basis_weight, filt, offsets, forth, back, rows, count, chunks):
    bases = filt.shape[0]
    width = filt.shape[2]
    ext = rows + 2 * REACH
    depth = round_up(TERMS * bases, 16)
    shapes = [
        jax.ShapeDtypeStruct((ext, depth, width + LANES), jnp.bfloat16),
        jax.ShapeDtypeStruct((ext, depth), jnp.int32),
        jax.ShapeDtypeStruct(forth.shape, forth.dtype),
        jax.ShapeDtypeStruct(back.shape, back.dtype),
    ] + [jax.ShapeDtypeStruct((size, depth), jnp.float32) for _, size in chunks]
    return pl.pallas_call(
        functools.partial(prepare_kernel, count, chunks),
        in_specs=[pl.BlockSpec(memory_space=VMEM)] * 5,
        out_specs=[pl.BlockSpec(memory_space=VMEM)] * len(shapes),
        out_shape=shapes,
        compiler_params=pltpu.CompilerParams(vmem_limit_bytes=16 * 2**20),
        cost_estimate=NO_COST,
        name="prepare",
    )(basis_weight, filt, offsets, forth, back)


def halo(first, second):
    bands, count = lax.axis_size("polar"), lax.axis_size("azimuth")
    blocks = []
    for odd, block in ((0, first), (1, second)):
        pairs = []
        for a in range(bands):
            other = ((a + odd) ^ 1) - odd
            for b in range(count):
                paired = 0 <= other < bands
                target = (other, b) if paired else (a, b ^ 1 if b ^ 1 < count else b)
                pairs.append((a * count + b, target[0] * count + target[1]))
        blocks.append(lax.ppermute(block, ("polar", "azimuth"), pairs))
    return blocks


def on_device(chunks, conv_out, grad_out, w_in, b_in, w_out, basis_weight, filt, offsets):
    rows, part, channels = conv_out.shape
    count = lax.axis_size("azimuth")
    forth, back = tables(count, part, filt.shape[2] // 2)
    forth, back = jnp.asarray(forth), jnp.asarray(back)
    owned = channels // count
    halves = 2 if rows % 2 == 0 else 1
    pieces = []
    for half in range(halves):
        final = half == halves - 1
        far = range(NEAR + 1, count)
        sent = [(k, 0, owned) for k in range(count)]
        if final:
            sent[NEAR + 1 :] = [(k,) + chunk for chunk in chunks for k in far]
        blocks = mlp(conv_out, grad_out, w_in, b_in, w_out, count, half, halves, sent, chunks, pieces[1:2])
        steps = [] if final else list(far)
        moved = {k: exchange(blocks[k], k, count) for k in steps + list(range(NEAR + 1))}
        pieces += [moved[k] for k in sorted(moved)]
    filters, target, forth, back, *weights = prepare(
        basis_weight, filt, offsets, forth, back, rows, count, chunks
    )
    spectra, terms, grids, returned = {}, {}, {}, []

    def open_chunk(q, after):
        tail = [exchange(blocks[NEAR + 1 + q * len(far) + i], k, count) for i, k in enumerate(far)]
        own, first, second = analyze(pieces + tail, forth, rows, chunks[q], count, after)
        spectra[q] = halo(first, second)
        terms[q] = own_terms(own, weights[q], target, filters)

    def close_chunk(q):
        after = [returned[(q - 1) * count + 1]] if q else []
        halos = spectra[q]
        if q == 0:
            terms[q] = side_terms(terms[q], halos[0], weights[q], target, filters)
            halos = halos[1:]
        grids[q] = finish(terms[q], halos, weights[q], target, filters, back, count, part, after)
        blocks = {k: exchange(grids[q][k], k, count) for k in [*far, *range(NEAR + 1)]}
        returned.extend(blocks[k] for k in range(count))

    last = len(chunks) - 1
    open_chunk(0, [])
    if last > 0:
        open_chunk(1, [terms[0]])
    for q in range(last + 1):
        close_chunk(q)
        if q + 2 <= last:
            open_chunk(q + 2, [grids[q][0]])
    total = []
    for q, chunk in enumerate(chunks):
        total = [add_chunk(grad_out, returned[q * count : (q + 1) * count], chunk, count, total)]
    return jnp.transpose(total[0], (1, 0, 2))


def solution(mesh):
    grid = P(("member", "polar"), "azimuth", None)

    def run(conv_out, grad_out, *others):
        owned = conv_out.shape[2] // mesh.shape["azimuth"]
        sizes = [owned]
        if owned % 32 == 0 and owned >= 96:
            big = owned * 3 // 5 // 32 * 32
            sizes = [big, owned - big]
        chunks = tuple((sum(sizes[:q]), size) for q, size in enumerate(sizes))
        return jax.shard_map(
            functools.partial(on_device, chunks),
            mesh=mesh,
            in_specs=(grid, grid) + (P(),) * 6,
            out_specs=grid,
            check_vma=False,
        )(conv_out, grad_out, *others)

    return run
```

profile of v0, /device:TPU:17, one launch (start us, length us, event | category | flops | bytes accessed | tf_op | source)
XLA Modules:
  0.0 46.6 jit_solution(4290408529263483955)
XLA Ops:
  0.0 0.0 copy-start.1
  0.0 0.0 copy-start.6
  0.0 0.0 copy-start
  0.0 1.4 %copy.17.grad_ref = bf16[4,180,640]{2,1,0:T(8,128)(2,1)S(1)} copy(bf16[4,180,640]{2,0,1:T(4,128)(2,1)} %param.11) | data formatting | bytes 1843200 | tf_op args[1]
  1.5 1.3 %copy.12.conv_ref = bf16[4,180,640]{2,1,0:T(8,128)(2,1)S(1)} copy(bf16[4,180,640]{2,0,1:T(4,128)(2,1)} %param.10) | data formatting | bytes 1843200 | tf_op args[0]
  2.8 0.0 copy-done.1
  2.8 0.0 copy-done.6
  2.8 0.0 copy-done
  2.8 2.8 %mlp.2 = (bf16[160,384]{1,0:T(8,128)(2,1)S(1)}, bf16[160,384]{1,0:T(8,128)(2,1)S(1)}, bf16[160,384]{1,0:T(8,128)(2,1)S(1)}, bf16[160,384]{1,0:T(8,128)(2,1)S(1)}) custom-call(bf16[4,180,640]{2,1,0:T(8,128)(2,1)S(1)} %copy.12.conv_ref, bf16[4,180,640]{2,1,0:T(8,128)(2,1)S(1)} %copy.17.grad_ref, bf16[640,1280]{1,0:T(8,128)(2,1)S(1)} %copy-done, ...), custom_call_target="tpu_custom_call" | custom-call | tf_op jit(solution)/shard_map/mlp/pallas_call | solution.py:165
  5.5 0.7 %collective-permute-start.2 = (bf16[160,384]{1,0:T(8,128)(2,1)S(1)}, bf16[160,384]{1,0:T(8,128)(2,1)S(1)}, u32[]{:S(2)}, u32[]{:S(2)}) collective-permute-start(bf16[160,384]{1,0:T(8,128)(2,1)S(1)} %get-tuple-element.38), channel_id=1, source_target_pairs={{0,1},{1,0},{2,3},{3,2},{4,5},{5,4},{6,7},{7,6},{8,9},{9,8},{10,11... | collective-permute-start | bytes 368648 | tf_op jit(solution)/shard_map/ppermute | solution.py:40
  6.3 1.2 %collective-permute-start = (bf16[160,384]{1,0:T(8,128)(2,1)S(1)}, bf16[160,384]{1,0:T(8,128)(2,1)S(1)}, u32[]{:S(2)}, u32[]{:S(2)}) collective-permute-start(bf16[160,384]{1,0:T(8,128)(2,1)S(1)} %get-tuple-element.35), channel_id=1, source_target_pairs={{0,2},{1,3},{2,0},{3,1},{4,6},{5,7},{6,4},{7,5},{8,10},{9,11},{10,... | collective-permute-start | bytes 368648 | tf_op jit(solution)/shard_map/ppermute | solution.py:40
  7.5 0.0 copy-start.2
  7.5 0.0 copy-start.3
  7.5 0.0 copy-start.7
  7.5 0.6 %collective-permute-start.1 = (bf16[160,384]{1,0:T(8,128)(2,1)S(1)}, bf16[160,384]{1,0:T(8,128)(2,1)S(1)}, u32[]{:S(2)}, u32[]{:S(2)}) collective-permute-start(bf16[160,384]{1,0:T(8,128)(2,1)S(1)} %get-tuple-element.36), channel_id=1, source_target_pairs={{0,3},{1,2},{2,1},{3,0},{4,7},{5,6},{6,5},{7,4},{8,11},{9,10},{10,... | collective-permute-start | bytes 368648 | tf_op jit(solution)/shard_map/ppermute | solution.py:40
  8.1 0.0 collective-permute-done.2.rest_0_.refs_3_
  8.1 2.7 %mlp.3 = (bf16[160,384]{1,0:T(8,128)(2,1)S(1)}, bf16[160,384]{1,0:T(8,128)(2,1)S(1)}, bf16[96,384]{1,0:T(8,128)(2,1)S(1)}, bf16[96,384]{1,0:T(8,128)(2,1)S(1)}, ...) custom-call(bf16[4,180,640]{2,1,0:T(8,128)(2,1)S(1)} %copy.12.conv_ref, bf16[4,180,640]{2,1,0:T(8,128)(2,1)S(1)} %copy.17.grad_ref, ...), custom_call_target="tpu_custom_call" | custom-call | tf_op jit(solution)/shard_map/mlp/pallas_call | solution.py:165
  10.8 0.2 collective-permute-start.5
  11.1 1.2 %collective-permute-start.6 = (bf16[96,384]{1,0:T(8,128)(2,1)S(1)}, bf16[96,384]{1,0:T(8,128)(2,1)S(1)}, u32[]{:S(2)}, u32[]{:S(2)}) collective-permute-start(bf16[96,384]{1,0:T(8,128)(2,1)S(1)} %get-tuple-element.44), channel_id=1, source_target_pairs={{0,2},{1,3},{2,0},{3,1},{4,6},{5,7},{6,4},{7,5},{8,10},{9,11},{10,... | collective-permute-start | bytes 221192 | tf_op jit(solution)/shard_map/ppermute | solution.py:40
  12.3 0.8 %collective-permute-start.7 = (bf16[96,384]{1,0:T(8,128)(2,1)S(1)}, bf16[96,384]{1,0:T(8,128)(2,1)S(1)}, u32[]{:S(2)}, u32[]{:S(2)}) collective-permute-start(bf16[96,384]{1,0:T(8,128)(2,1)S(1)} %get-tuple-element.45), channel_id=1, source_target_pairs={{0,3},{1,2},{2,1},{3,0},{4,7},{5,6},{6,5},{7,4},{8,11},{9,10},{10,... | collective-permute-start | bytes 221192 | tf_op jit(solution)/shard_map/ppermute | solution.py:40
  13.0 0.0 copy-done.2
  13.1 0.0 copy-done.3
  13.1 0.0 copy-done.4
  13.1 0.0 copy-done.5
  13.1 0.0 copy-done.7
  13.1 0.7 %prepare.1 = (bf16[10,32,768]{2,1,0:T(8,128)(2,1)S(1)}, s32[10,32]{1,0:T(8,128)S(1)}, bf16[4,320,640]{2,1,0:T(8,128)(2,1)S(1)}, bf16[768,640]{1,0:T(8,128)(2,1)S...) custom-call(f32[9,640]{1,0:T(8,128)S(1)} %copy-done.5, bf16[9,16,640]{2,1,0:T(8,128)(2,1)S(1)} %copy-done.4, ...), custom_call_target="tpu_custom_call" | custom-call | tf_op jit(solution)/shard_map/prepare/pallas_call | solution.py:482
  13.8 0.0 collective-permute-done.refs_0_
  13.8 0.6 %collective-permute-done.1.refs_1_ = bf16[160,384]{1,0:T(8,128)(2,1)S(1)} collective-permute-done((bf16[160,384]{1,0:T(8,128)(2,1)S(1)}, bf16[160,384]{1,0:T(8,128)(2,1)S(1)}, u32[]{:S(2)}, u32[]{:S(2)}) %collective-permute-start.1) | collective-permute-done | bytes 122912 | tf_op jit(solution)/shard_map/ppermute | solution.py:40
  14.4 1.0 %collective-permute-done.6.refs_4_ = bf16[96,384]{1,0:T(8,128)(2,1)S(1)} collective-permute-done((bf16[96,384]{1,0:T(8,128)(2,1)S(1)}, bf16[96,384]{1,0:T(8,128)(2,1)S(1)}, u32[]{:S(2)}, u32[]{:S(2)}) %collective-permute-start.6) | collective-permute-done | bytes 73760 | tf_op jit(solution)/shard_map/ppermute | solution.py:40
  15.4 1.8 %collective-permute-done.7.refs_5_ = bf16[96,384]{1,0:T(8,128)(2,1)S(1)} collective-permute-done((bf16[96,384]{1,0:T(8,128)(2,1)S(1)}, bf16[96,384]{1,0:T(8,128)(2,1)S(1)}, u32[]{:S(2)}, u32[]{:S(2)}) %collective-permute-start.7) | collective-permute-done | bytes 73760 | tf_op jit(solution)/shard_map/ppermute | solution.py:40
  17.2 0.0 collective-permute-done.5.refs_7_
  17.2 0.8 %analysis.2 = (f32[4,96,640]{2,1,0:T(8,128)S(1)}, bf16[3,96,640]{2,1,0:T(8,128)(2,1)S(1)}, bf16[3,96,640]{2,1,0:T(8,128)(2,1)S(1)}) custom-call(bf16[160,384]{1,0:T(8,128)(2,1)S(1)} %collective-permute-done.refs_0_, bf16[160,384]{1,0:T(8,128)(2,1)S(1)} %collective-permute-done.1.refs_1_, bf16[160,384]{1,0:T(8,128)(2,1)S(1)} %get-tuple-element.37.refs_2_, ...), custom_call_target="tpu_custom_call" | custom-call | tf_op jit(solution)/shard_map/analysis/pallas_call | solution.py:228
  18.0 1.4 %collective-permute-start.10 = (bf16[3,96,640]{2,1,0:T(8,128)(2,1)S(1)}, bf16[3,96,640]{2,1,0:T(8,128)(2,1)S(1)}, u32[]{:S(2)}, u32[]{:S(2)}) collective-permute-start(bf16[3,96,640]{2,1,0:T(8,128)(2,1)S(1)} %get-tuple-element.55), channel_id=1, source_target_pairs={{0,4},{1,5},{2,6},{3,7},{4,0},{5,1},{6,2},{7,3},{8,12},{9,13},{10,... | collective-permute-start | bytes 1105928 | tf_op jit(solution)/shard_map/ppermute | solution.py:504
  19.4 0.0 collective-permute-start.11
  19.4 1.2 %collective-permute-start.3 = (bf16[64,384]{1,0:T(8,128)(2,1)S(1)}, bf16[64,384]{1,0:T(8,128)(2,1)S(1)}, u32[]{:S(2)}, u32[]{:S(2)}) collective-permute-start(bf16[64,384]{1,0:T(8,128)(2,1)S(1)} %get-tuple-element.39), channel_id=1, source_target_pairs={{0,2},{1,3},{2,0},{3,1},{4,6},{5,7},{6,4},{7,5},{8,10},{9,11},{10,... | collective-permute-start | bytes 147464 | tf_op jit(solution)/shard_map/ppermute | solution.py:40
  20.6 1.1 %collective-permute-start.4 = (bf16[64,384]{1,0:T(8,128)(2,1)S(1)}, bf16[64,384]{1,0:T(8,128)(2,1)S(1)}, u32[]{:S(2)}, u32[]{:S(2)}) collective-permute-start(bf16[64,384]{1,0:T(8,128)(2,1)S(1)} %get-tuple-element.40), channel_id=1, source_target_pairs={{0,3},{1,2},{2,1},{3,0},{4,7},{5,6},{6,5},{7,4},{8,11},{9,10},{10,... | collective-permute-start | bytes 147464 | tf_op jit(solution)/shard_map/ppermute | solution.py:40
  21.7 1.0 %own_terms.2.refs_9_.part_ref = f32[4,96,640]{2,1,0:T(8,128)S(1)} custom-call(f32[4,96,640]{2,1,0:T(8,128)S(1)} %get-tuple-element.46.own_ref, f32[96,32]{1,0:T(8,128)S(1)} %get-tuple-element.47.weight_ref.refs_1_, s32[10,32]{1,0:T(8,128)S(1)} %get-tuple-element.48.target_ref.refs_2_.refs_3_, ...), custom_call_target="tpu_custom_call" | custom-call | tf_op jit(solution)/shard_map/own_terms/pallas_call | solution.py:279
  22.7 0.0 collective-permute-done.3.refs_4_
  22.7 2.1 %collective-permute-done.4.refs_5_ = bf16[64,384]{1,0:T(8,128)(2,1)S(1)} collective-permute-done((bf16[64,384]{1,0:T(8,128)(2,1)S(1)}, bf16[64,384]{1,0:T(8,128)(2,1)S(1)}, u32[]{:S(2)}, u32[]{:S(2)}) %collective-permute-start.4) | collective-permute-done | bytes 49184 | tf_op jit(solution)/shard_map/ppermute | solution.py:40
  24.8 0.6 %analysis.3 = (f32[4,64,640]{2,1,0:T(8,128)S(1)}, bf16[3,64,640]{2,1,0:T(8,128)(2,1)S(1)}, bf16[3,64,640]{2,1,0:T(8,128)(2,1)S(1)}) custom-call(bf16[160,384]{1,0:T(8,128)(2,1)S(1)} %collective-permute-done.refs_0_, bf16[160,384]{1,0:T(8,128)(2,1)S(1)} %collective-permute-done.1.refs_1_, bf16[160,384]{1,0:T(8,128)(2,1)S(1)} %get-tuple-element.37.refs_2_, ...), custom_call_target="tpu_custom_call" | custom-call | tf_op jit(solution)/shard_map/analysis/pallas_call | solution.py:228
  25.4 0.4 collective-permute-start.8
  25.9 1.3 %collective-permute-start.9 = (bf16[3,64,640]{2,1,0:T(8,128)(2,1)S(1)}, bf16[3,64,640]{2,1,0:T(8,128)(2,1)S(1)}, u32[]{:S(2)}, u32[]{:S(2)}) collective-permute-start(bf16[3,64,640]{2,1,0:T(8,128)(2,1)S(1)} %get-tuple-element.53), channel_id=1, source_target_pairs={{0,1},{1,0},{2,3},{3,2},{4,8},{5,9},{6,10},{7,11},{8,4},{9,5},{10,... | collective-permute-start | bytes 737288 | tf_op jit(solution)/shard_map/ppermute | solution.py:504
  27.2 0.7 %collective-permute-done.10.first_ref = bf16[3,96,640]{2,1,0:T(8,128)(2,1)S(1)} collective-permute-done((bf16[3,96,640]{2,1,0:T(8,128)(2,1)S(1)}, bf16[3,96,640]{2,1,0:T(8,128)(2,1)S(1)}, u32[]{:S(2)}, u32[]{:S(2)}) %collective-permute-start.10) | collective-permute-done | bytes 368672 | tf_op jit(solution)/shard_map/ppermute | solution.py:504
  27.9 0.5 %side_terms.1.part_ref = f32[4,96,640]{2,1,0:T(8,128)S(1)} custom-call(f32[4,96,640]{2,1,0:T(8,128)S(1)} %own_terms.2.refs_9_.part_ref, bf16[3,96,640]{2,1,0:T(8,128)(2,1)S(1)} %collective-permute-done.10.first_ref, f32[96,32]{1,0:T(8,128)S(1)} %get-tuple-element.47.weight_ref.refs_1_, s32[10,32]{1,0:T(8,128)S(1)} %get-tuple-element.48.target_ref.refs_2_.refs_3_, ...), custom_call_target="tpu_custom_call" | custom-call | tf_op jit(solution)/shard_map/side_terms/pallas_call | solution.py:320
  28.3 0.5 %collective-permute-done.11.refs_0_ = bf16[3,96,640]{2,1,0:T(8,128)(2,1)S(1)} collective-permute-done((bf16[3,96,640]{2,1,0:T(8,128)(2,1)S(1)}, bf16[3,96,640]{2,1,0:T(8,128)(2,1)S(1)}, u32[]{:S(2)}, u32[]{:S(2)}) %collective-permute-start.11) | collective-permute-done | bytes 368672 | tf_op jit(solution)/shard_map/ppermute | solution.py:504
  28.9 1.2 %finish.2 = (bf16[180,384]{1,0:T(8,128)(2,1)S(1)}, bf16[180,384]{1,0:T(8,128)(2,1)S(1)}, bf16[180,384]{1,0:T(8,128)(2,1)S(1)}, bf16[180,384]{1,0:T(8,128)(2,1)S(1)}) custom-call(f32[4,96,640]{2,1,0:T(8,128)S(1)} %side_terms.1.part_ref, bf16[3,96,640]{2,1,0:T(8,128)(2,1)S(1)} %collective-permute-done.11.refs_0_, ...), custom_call_target="tpu_custom_call" | custom-call | tf_op jit(solution)/shard_map/finish/pallas_call | solution.py:355
  30.1 2.8 %collective-permute-start.12 = (bf16[180,384]{1,0:T(8,128)(2,1)S(1)}, bf16[180,384]{1,0:T(8,128)(2,1)S(1)}, u32[]{:S(2)}, u32[]{:S(2)}) collective-permute-start(bf16[180,384]{1,0:T(8,128)(2,1)S(1)} %get-tuple-element.57), channel_id=1, source_target_pairs={{0,1},{1,0},{2,3},{3,2},{4,5},{5,4},{6,7},{7,6},{8,9},{9,8},{10,11... | collective-permute-start | bytes 414728 | tf_op jit(solution)/shard_map/ppermute | solution.py:40
  32.8 1.0 %collective-permute-start.16 = (bf16[180,384]{1,0:T(8,128)(2,1)S(1)}, bf16[180,384]{1,0:T(8,128)(2,1)S(1)}, u32[]{:S(2)}, u32[]{:S(2)}) collective-permute-start(bf16[180,384]{1,0:T(8,128)(2,1)S(1)} %get-tuple-element.62), channel_id=1, source_target_pairs={{0,2},{1,3},{2,0},{3,1},{4,6},{5,7},{6,4},{7,5},{8,10},{9,11},{10,... | collective-permute-start | bytes 414728 | tf_op jit(solution)/shard_map/ppermute | solution.py:40
  33.8 0.7 %collective-permute-start.17 = (bf16[180,384]{1,0:T(8,128)(2,1)S(1)}, bf16[180,384]{1,0:T(8,128)(2,1)S(1)}, u32[]{:S(2)}, u32[]{:S(2)}) collective-permute-start(bf16[180,384]{1,0:T(8,128)(2,1)S(1)} %get-tuple-element.63), channel_id=1, source_target_pairs={{0,3},{1,2},{2,1},{3,0},{4,7},{5,6},{6,5},{7,4},{8,11},{9,10},{10,... | collective-permute-start | bytes 414728 | tf_op jit(solution)/shard_map/ppermute | solution.py:40
  34.5 0.7 %own_terms.3.part_ref = f32[4,64,640]{2,1,0:T(8,128)S(1)} custom-call(f32[4,64,640]{2,1,0:T(8,128)S(1)} %get-tuple-element.50.own_ref, f32[64,32]{1,0:T(8,128)S(1)} %get-tuple-element.51.weight_ref.refs_2_, s32[10,32]{1,0:T(8,128)S(1)} %get-tuple-element.48.target_ref.refs_2_.refs_3_, bf16[10,32,768]{2,1,0:T(8,128)(2,1)S(1)} %get-tuple-element.49.filter_ref.refs_3_.refs_4_), custom_call_target="tpu_custom_call" | custom-call | tf_op jit(solution)/shard_map/own_terms/pallas_call | solution.py:279
  35.2 0.0 collective-permute-done.8.refs_0_
  35.2 0.0 collective-permute-done.9.refs_1_
  35.2 0.0 collective-permute-done.12.refs_6_.refs_3_
  35.3 1.3 %finish.3 = (bf16[180,256]{1,0:T(8,128)(2,1)S(1)}, bf16[180,256]{1,0:T(8,128)(2,1)S(1)}, bf16[180,256]{1,0:T(8,128)(2,1)S(1)}, bf16[180,256]{1,0:T(8,128)(2,1)S(1)}) custom-call(f32[4,64,640]{2,1,0:T(8,128)S(1)} %own_terms.3.part_ref, bf16[3,64,640]{2,1,0:T(8,128)(2,1)S(1)} %collective-permute-done.8.refs_0_, ...), custom_call_target="tpu_custom_call" | custom-call | tf_op jit(solution)/shard_map/finish/pallas_call | solution.py:355
  36.6 1.1 %collective-permute-start.13 = (bf16[180,256]{1,0:T(8,128)(2,1)S(1)}, bf16[180,256]{1,0:T(8,128)(2,1)S(1)}, u32[]{:S(2)}, u32[]{:S(2)}) collective-permute-start(bf16[180,256]{1,0:T(8,128)(2,1)S(1)} %get-tuple-element.58), channel_id=1, source_target_pairs={{0,2},{1,3},{2,0},{3,1},{4,6},{5,7},{6,4},{7,5},{8,10},{9,11},{10,... | collective-permute-start | bytes 276488 | tf_op jit(solution)/shard_map/ppermute | solution.py:40
  37.6 0.9 %collective-permute-start.14 = (bf16[180,256]{1,0:T(8,128)(2,1)S(1)}, bf16[180,256]{1,0:T(8,128)(2,1)S(1)}, u32[]{:S(2)}, u32[]{:S(2)}) collective-permute-start(bf16[180,256]{1,0:T(8,128)(2,1)S(1)} %get-tuple-element.59), channel_id=1, source_target_pairs={{0,3},{1,2},{2,1},{3,0},{4,7},{5,6},{6,5},{7,4},{8,11},{9,10},{10,... | collective-permute-start | bytes 276488 | tf_op jit(solution)/shard_map/ppermute | solution.py:40
  38.5 0.0 collective-permute-start.15
  38.5 0.0 collective-permute-done.16.refs_0_
  38.5 3.2 %collective-permute-done.17.refs_1_ = bf16[180,384]{1,0:T(8,128)(2,1)S(1)} collective-permute-done((bf16[180,384]{1,0:T(8,128)(2,1)S(1)}, bf16[180,384]{1,0:T(8,128)(2,1)S(1)}, u32[]{:S(2)}, u32[]{:S(2)}) %collective-permute-start.17) | collective-permute-done | bytes 138272 | tf_op jit(solution)/shard_map/ppermute | solution.py:40
  41.8 1.4 %add_chunk.2.refs_4_ = bf16[180,4,640]{2,1,0:T(4,128)(2,1)} custom-call(bf16[4,180,640]{2,1,0:T(8,128)(2,1)S(1)} %copy.17.grad_ref, bf16[180,384]{1,0:T(8,128)(2,1)S(1)} %collective-permute-done.16.refs_0_, bf16[180,384]{1,0:T(8,128)(2,1)S(1)} %collective-permute-done.17.refs_1_, bf16[180,384]{1,0:T(8,128)(2,1)S(1)} %get-tuple-element.64.refs_2_, ...), custom_call_target="tpu_custom_call" | custom-call | tf_op jit(solution)/shard_map/add_chunk/pallas_call | solution.py:406
  43.2 0.0 collective-permute-done.13.refs_0_
  43.2 2.2 %collective-permute-done.14.refs_1_ = bf16[180,256]{1,0:T(8,128)(2,1)S(1)} collective-permute-done((bf16[180,256]{1,0:T(8,128)(2,1)S(1)}, bf16[180,256]{1,0:T(8,128)(2,1)S(1)}, u32[]{:S(2)}, u32[]{:S(2)}) %collective-permute-start.14) | collective-permute-done | bytes 92192 | tf_op jit(solution)/shard_map/ppermute | solution.py:40
  45.3 0.0 collective-permute-done.15.refs_3_
  45.4 1.1 %add_chunk.3 = bf16[180,4,640]{2,1,0:T(4,128)(2,1)} custom-call(bf16[4,180,640]{2,1,0:T(8,128)(2,1)S(1)} %copy.17.grad_ref, bf16[180,256]{1,0:T(8,128)(2,1)S(1)} %collective-permute-done.13.refs_0_, bf16[180,256]{1,0:T(8,128)(2,1)S(1)} %collective-permute-done.14.refs_1_, ...), custom_call_target="tpu_custom_call", output_to_operand_aliasing={{}: (5, {})} | custom-call | tf_op jit(solution)/shard_map/add_chunk/pallas_call | solution.py:406
  (2 shorter events, 0.0 us)
Async XLA Ops:
  0.0 2.8 %copy-start.1 = (bf16[1280,640]{1,0:T(8,128)(2,1)S(1)}, bf16[1280,640]{1,0:T(8,128)(2,1)}, u32[]{:S(2)}) copy-start(bf16[1280,640]{1,0:T(8,128)(2,1)} %wout_ref.3) | copy-start | bytes 4915204
  0.0 2.8 %copy-start.6 = (f32[1280]{0:T(1024)S(1)}, f32[1280]{0:T(1024)}, u32[]{:S(2)}) copy-start(f32[1280]{0:T(1024)} %bias_ref.3) | copy-start | bytes 15364
  0.0 2.8 %copy-start = (bf16[640,1280]{1,0:T(8,128)(2,1)S(1)}, bf16[640,1280]{1,0:T(8,128)(2,1)}, u32[]{:S(2)}) copy-start(bf16[640,1280]{1,0:T(8,128)(2,1)} %win_ref.3) | copy-start | bytes 4915204
  5.5 2.5 %collective-permute-start.2 = (bf16[160,384]{1,0:T(8,128)(2,1)S(1)}, bf16[160,384]{1,0:T(8,128)(2,1)S(1)}, u32[]{:S(2)}, u32[]{:S(2)}) collective-permute-start(bf16[160,384]{1,0:T(8,128)(2,1)S(1)} %get-tuple-element.38), channel_id=1, source_target_pairs={{0,1},{1,0},{2,3},{3,2},{4,5},{5,4},{6,7},{7,6},{8,9},{9,8},{10,11... | collective-permute-start | bytes 368648 | tf_op jit(solution)/shard_map/ppermute | solution.py:40
  6.3 7.5 %collective-permute-start = (bf16[160,384]{1,0:T(8,128)(2,1)S(1)}, bf16[160,384]{1,0:T(8,128)(2,1)S(1)}, u32[]{:S(2)}, u32[]{:S(2)}) collective-permute-start(bf16[160,384]{1,0:T(8,128)(2,1)S(1)} %get-tuple-element.35), channel_id=1, source_target_pairs={{0,2},{1,3},{2,0},{3,1},{4,6},{5,7},{6,4},{7,5},{8,10},{9,11},{10,... | collective-permute-start | bytes 368648 | tf_op jit(solution)/shard_map/ppermute | solution.py:40
  7.5 5.5 %copy-start.2 = (bf16[4,320,640]{2,1,0:T(8,128)(2,1)S(1)}, bf16[4,320,640]{2,1,0:T(8,128)(2,1)}, u32[]{:S(2)}) copy-start(bf16[4,320,640]{2,1,0:T(8,128)(2,1)} %constant.4.clone.forth_ref) | copy-start | bytes 4915204
  7.5 5.5 %copy-start.3 = (bf16[768,640]{1,0:T(8,128)(2,1)S(1)}, bf16[768,640]{1,0:T(8,128)(2,1)}, u32[]{:S(2)}) copy-start(bf16[768,640]{1,0:T(8,128)(2,1)} %constant.5.clone.back_ref) | copy-start | bytes 2949124
  7.5 5.5 %copy-start.4 = (bf16[9,16,640]{2,1,0:T(8,128)(2,1)S(1)}, bf16[9,16,640]{2,1,0:T(8,128)(2,1)}, u32[]{:S(2)}) copy-start(bf16[9,16,640]{2,1,0:T(8,128)(2,1)} %filt_ref.1) | copy-start | bytes 552964
  7.5 5.5 %copy-start.5 = (f32[9,640]{1,0:T(8,128)S(1)}, f32[9,640]{1,0:T(8,128)}, u32[]{:S(2)}) copy-start(f32[9,640]{1,0:T(8,128)} %weight_ref.1) | copy-start | bytes 69124
  7.5 5.5 %copy-start.7 = (s32[16,9]{1,0:T(8,128)S(1)}, s32[16,9]{1,0:T(8,128)}, u32[]{:S(2)}) copy-start(s32[16,9]{1,0:T(8,128)} %offset_ref.1) | copy-start | bytes 1732
  7.5 6.9 %collective-permute-start.1 = (bf16[160,384]{1,0:T(8,128)(2,1)S(1)}, bf16[160,384]{1,0:T(8,128)(2,1)S(1)}, u32[]{:S(2)}, u32[]{:S(2)}) collective-permute-start(bf16[160,384]{1,0:T(8,128)(2,1)S(1)} %get-tuple-element.36), channel_id=1, source_target_pairs={{0,3},{1,2},{2,1},{3,0},{4,7},{5,6},{6,5},{7,4},{8,11},{9,10},{10,... | collective-permute-start | bytes 368648 | tf_op jit(solution)/shard_map/ppermute | solution.py:40
  10.8 6.3 %collective-permute-start.5 = (bf16[160,384]{1,0:T(8,128)(2,1)S(1)}, bf16[160,384]{1,0:T(8,128)(2,1)S(1)}, u32[]{:S(2)}, u32[]{:S(2)}) collective-permute-start(bf16[160,384]{1,0:T(8,128)(2,1)S(1)} %get-tuple-element.42), channel_id=1, source_target_pairs={{0,1},{1,0},{2,3},{3,2},{4,5},{5,4},{6,7},{7,6},{8,9},{9,8},{10,11... | collective-permute-start | bytes 368648 | tf_op jit(solution)/shard_map/ppermute | solution.py:40
  11.1 4.3 %collective-permute-start.6 = (bf16[96,384]{1,0:T(8,128)(2,1)S(1)}, bf16[96,384]{1,0:T(8,128)(2,1)S(1)}, u32[]{:S(2)}, u32[]{:S(2)}) collective-permute-start(bf16[96,384]{1,0:T(8,128)(2,1)S(1)} %get-tuple-element.44), channel_id=1, source_target_pairs={{0,2},{1,3},{2,0},{3,1},{4,6},{5,7},{6,4},{7,5},{8,10},{9,11},{10,... | collective-permute-start | bytes 221192 | tf_op jit(solution)/shard_map/ppermute | solution.py:40
  12.3 4.9 %collective-permute-start.7 = (bf16[96,384]{1,0:T(8,128)(2,1)S(1)}, bf16[96,384]{1,0:T(8,128)(2,1)S(1)}, u32[]{:S(2)}, u32[]{:S(2)}) collective-permute-start(bf16[96,384]{1,0:T(8,128)(2,1)S(1)} %get-tuple-element.45), channel_id=1, source_target_pairs={{0,3},{1,2},{2,1},{3,0},{4,7},{5,6},{6,5},{7,4},{8,11},{9,10},{10,... | collective-permute-start | bytes 221192 | tf_op jit(solution)/shard_map/ppermute | solution.py:40
  18.0 9.8 %collective-permute-start.10 = (bf16[3,96,640]{2,1,0:T(8,128)(2,1)S(1)}, bf16[3,96,640]{2,1,0:T(8,128)(2,1)S(1)}, u32[]{:S(2)}, u32[]{:S(2)}) collective-permute-start(bf16[3,96,640]{2,1,0:T(8,128)(2,1)S(1)} %get-tuple-element.55), channel_id=1, source_target_pairs={{0,4},{1,5},{2,6},{3,7},{4,0},{5,1},{6,2},{7,3},{8,12},{9,13},{10,... | collective-permute-start | bytes 1105928 | tf_op jit(solution)/shard_map/ppermute | solution.py:504
  19.4 9.5 %collective-permute-start.11 = (bf16[3,96,640]{2,1,0:T(8,128)(2,1)S(1)}, bf16[3,96,640]{2,1,0:T(8,128)(2,1)S(1)}, u32[]{:S(2)}, u32[]{:S(2)}) collective-permute-start(bf16[3,96,640]{2,1,0:T(8,128)(2,1)S(1)} %get-tuple-element.56), channel_id=1, source_target_pairs={{0,1},{1,0},{2,3},{3,2},{4,8},{5,9},{6,10},{7,11},{8,4},{9,5},{10,... | collective-permute-start | bytes 1105928 | tf_op jit(solution)/shard_map/ppermute | solution.py:504
  19.4 3.3 %collective-permute-start.3 = (bf16[64,384]{1,0:T(8,128)(2,1)S(1)}, bf16[64,384]{1,0:T(8,128)(2,1)S(1)}, u32[]{:S(2)}, u32[]{:S(2)}) collective-permute-start(bf16[64,384]{1,0:T(8,128)(2,1)S(1)} %get-tuple-element.39), channel_id=1, source_target_pairs={{0,2},{1,3},{2,0},{3,1},{4,6},{5,7},{6,4},{7,5},{8,10},{9,11},{10,... | collective-permute-start | bytes 147464 | tf_op jit(solution)/shard_map/ppermute | solution.py:40
  20.6 4.2 %collective-permute-start.4 = (bf16[64,384]{1,0:T(8,128)(2,1)S(1)}, bf16[64,384]{1,0:T(8,128)(2,1)S(1)}, u32[]{:S(2)}, u32[]{:S(2)}) collective-permute-start(bf16[64,384]{1,0:T(8,128)(2,1)S(1)} %get-tuple-element.40), channel_id=1, source_target_pairs={{0,3},{1,2},{2,1},{3,0},{4,7},{5,6},{6,5},{7,4},{8,11},{9,10},{10,... | collective-permute-start | bytes 147464 | tf_op jit(solution)/shard_map/ppermute | solution.py:40
  25.4 9.8 %collective-permute-start.8 = (bf16[3,64,640]{2,1,0:T(8,128)(2,1)S(1)}, bf16[3,64,640]{2,1,0:T(8,128)(2,1)S(1)}, u32[]{:S(2)}, u32[]{:S(2)}) collective-permute-start(bf16[3,64,640]{2,1,0:T(8,128)(2,1)S(1)} %get-tuple-element.52), channel_id=1, source_target_pairs={{0,4},{1,5},{2,6},{3,7},{4,0},{5,1},{6,2},{7,3},{8,12},{9,13},{10,... | collective-permute-start | bytes 737288 | tf_op jit(solution)/shard_map/ppermute | solution.py:504
  25.9 9.3 %collective-permute-start.9 = (bf16[3,64,640]{2,1,0:T(8,128)(2,1)S(1)}, bf16[3,64,640]{2,1,0:T(8,128)(2,1)S(1)}, u32[]{:S(2)}, u32[]{:S(2)}) collective-permute-start(bf16[3,64,640]{2,1,0:T(8,128)(2,1)S(1)} %get-tuple-element.53), channel_id=1, source_target_pairs={{0,1},{1,0},{2,3},{3,2},{4,8},{5,9},{6,10},{7,11},{8,4},{9,5},{10,... | collective-permute-start | bytes 737288 | tf_op jit(solution)/shard_map/ppermute | solution.py:504
  30.1 5.2 %collective-permute-start.12 = (bf16[180,384]{1,0:T(8,128)(2,1)S(1)}, bf16[180,384]{1,0:T(8,128)(2,1)S(1)}, u32[]{:S(2)}, u32[]{:S(2)}) collective-permute-start(bf16[180,384]{1,0:T(8,128)(2,1)S(1)} %get-tuple-element.57), channel_id=1, source_target_pairs={{0,1},{1,0},{2,3},{3,2},{4,5},{5,4},{6,7},{7,6},{8,9},{9,8},{10,11... | collective-permute-start | bytes 414728 | tf_op jit(solution)/shard_map/ppermute | solution.py:40
  32.8 5.7 %collective-permute-start.16 = (bf16[180,384]{1,0:T(8,128)(2,1)S(1)}, bf16[180,384]{1,0:T(8,128)(2,1)S(1)}, u32[]{:S(2)}, u32[]{:S(2)}) collective-permute-start(bf16[180,384]{1,0:T(8,128)(2,1)S(1)} %get-tuple-element.62), channel_id=1, source_target_pairs={{0,2},{1,3},{2,0},{3,1},{4,6},{5,7},{6,4},{7,5},{8,10},{9,11},{10,... | collective-permute-start | bytes 414728 | tf_op jit(solution)/shard_map/ppermute | solution.py:40
  33.8 7.9 %collective-permute-start.17 = (bf16[180,384]{1,0:T(8,128)(2,1)S(1)}, bf16[180,384]{1,0:T(8,128)(2,1)S(1)}, u32[]{:S(2)}, u32[]{:S(2)}) collective-permute-start(bf16[180,384]{1,0:T(8,128)(2,1)S(1)} %get-tuple-element.63), channel_id=1, source_target_pairs={{0,3},{1,2},{2,1},{3,0},{4,7},{5,6},{6,5},{7,4},{8,11},{9,10},{10,... | collective-permute-start | bytes 414728 | tf_op jit(solution)/shard_map/ppermute | solution.py:40
  36.6 6.6 %collective-permute-start.13 = (bf16[180,256]{1,0:T(8,128)(2,1)S(1)}, bf16[180,256]{1,0:T(8,128)(2,1)S(1)}, u32[]{:S(2)}, u32[]{:S(2)}) collective-permute-start(bf16[180,256]{1,0:T(8,128)(2,1)S(1)} %get-tuple-element.58), channel_id=1, source_target_pairs={{0,2},{1,3},{2,0},{3,1},{4,6},{5,7},{6,4},{7,5},{8,10},{9,11},{10,... | collective-permute-start | bytes 276488 | tf_op jit(solution)/shard_map/ppermute | solution.py:40
  37.6 7.7 %collective-permute-start.14 = (bf16[180,256]{1,0:T(8,128)(2,1)S(1)}, bf16[180,256]{1,0:T(8,128)(2,1)S(1)}, u32[]{:S(2)}, u32[]{:S(2)}) collective-permute-start(bf16[180,256]{1,0:T(8,128)(2,1)S(1)} %get-tuple-element.59), channel_id=1, source_target_pairs={{0,3},{1,2},{2,1},{3,0},{4,7},{5,6},{6,5},{7,4},{8,11},{9,10},{10,... | collective-permute-start | bytes 276488 | tf_op jit(solution)/shard_map/ppermute | solution.py:40
  38.5 6.9 %collective-permute-start.15 = (bf16[180,256]{1,0:T(8,128)(2,1)S(1)}, bf16[180,256]{1,0:T(8,128)(2,1)S(1)}, u32[]{:S(2)}, u32[]{:S(2)}) collective-permute-start(bf16[180,256]{1,0:T(8,128)(2,1)S(1)} %get-tuple-element.61), channel_id=1, source_target_pairs={{0,1},{1,0},{2,3},{3,2},{4,5},{5,4},{6,7},{7,6},{8,9},{9,8},{10,11... | collective-permute-start | bytes 276488 | tf_op jit(solution)/shard_map/ppermute | solution.py:40
where the time goes:
time: 46.7 us; the launch traced here: 46.6 us
  starting transfers between devices  16.5 us (35%)
  Pallas kernels  14.8 us (32%)
  waiting for transfers between devices  12.1 us (26%)
  local copies, waits for them, and re-layouts  2.77 us (6%)
    ppermute x14, starting transfers between devices, exchange(): return lax.ppermute(block, 'azimuth', pairs)  13.4 us
    ppermute x14, waiting for transfers between devices, exchange(): return lax.ppermute(block, 'azimuth', pairs)  10.9 us
    pallas_call x2, Pallas kernels, mlp(): pl.pallas_call(functools.partial(mlp_kernel, count, half, sent, chunks),...  5.5 us
    ppermute x4, starting transfers between devices, halo(): blocks.append(lax.ppermute(block, ('polar', 'azimuth'), pairs))  3.1 us
    unnamed x18, local copies, waits for them, and re-layouts  2.77 us
    pallas_call x2, Pallas kernels, finish(): pl.pallas_call(functools.partial(finish_kernel, count, len(halos)), in_sp...  2.52 us
    pallas_call x2, Pallas kernels, add_chunk(): pl.pallas_call(functools.partial(add_kernel, count, chunk), in_specs=[vme...  2.47 us
    pallas_call x2, Pallas kernels, own_terms(): pl.pallas_call(own_kernel, in_specs=[pl.BlockSpec(memory_space=VMEM)] * 4...  1.67 us
  transfers between devices with their start and end apart: 18, of which 8 were waited for; matrix products, arithmetic and copies ran while one was open for 0% of the time, Pallas kernels for 22%

commit v1 on v0

--- a/solution.py
+++ b/solution.py
@@ -15,6 +15,7 @@
 HALF = 64
 TERMS = 3
 NEAR = 1
+TOKEN = -1
 VMEM = pltpu.MemorySpace.VMEM
 NO_COST = pl.CostEstimate(flops=0, bytes_accessed=0, transcendentals=0)
 
@@ -328,11 +329,10 @@
     )(own, first, weight, target, filters)
 
 
-def finish_kernel(count, swaps, part_ref, *refs):
+def finish_kernel(count, swaps, steps, part_ref, *refs):
     halos, (weight_ref, target_ref, filter_ref, table_ref) = refs[:swaps], refs[swaps : swaps + 4]
-    outs, stacked_ref = refs[-count - 1 : -1], refs[-1]
+    outs, stacked_ref = refs[-len(steps) - 1 : -1], refs[-1]
     rows, size, width = part_ref.shape
-    part = outs[0].shape[0]
     even = lax.rem(lax.axis_index("polar"), 2) == 0
 
     def combine(bases):
@@ -346,28 +346,35 @@
     pl.when(jnp.logical_not(even))(lambda: combine((-REACH, rows)))
     grid = dot_nt(table_ref[...], stacked_ref[...])
     wide = grid.shape[0] // count
-    for k in range(count):
-        outs[k][...] = grid[k * wide : k * wide + part].astype(jnp.bfloat16)
-
-
-def finish(own, halos, weight, target, filters, table, count, part, after):
+    for k, out in zip(steps, outs):
+        out[...] = grid[k * wide : k * wide + out.shape[0]].astype(jnp.bfloat16)
+
+
+def finish(own, halos, weight, target, filters, table, count, part, cut, after):
     rows, size, width = own.shape
-    return pl.pallas_call(
-        functools.partial(finish_kernel, count, len(halos)),
+    wide = table.shape[0] // count
+    ends = {k: wide if cut and k == NEAR else part for k in range(count)}
+    if cut:
+        ends[TOKEN] = cut
+    steps = [NEAR if k == TOKEN else k for k in ends]
+    blocks = pl.pallas_call(
+        functools.partial(finish_kernel, count, len(halos), steps),
         in_specs=[pl.BlockSpec(memory_space=VMEM)] * (5 + len(halos)) + [pl.BlockSpec(memory_space=pl.ANY)] * len(after),
-        out_specs=[pl.BlockSpec(memory_space=VMEM)] * count,
-        out_shape=[jax.ShapeDtypeStruct((part, rows * size), jnp.bfloat16)] * count,
+        out_specs=[pl.BlockSpec(memory_space=VMEM)] * len(ends),
+        out_shape=[
+            jax.ShapeDtypeStruct((end, rows * size), jnp.bfloat16) for end in ends.values()
+        ],
         scratch_shapes=[pltpu.VMEM((rows * size, width), jnp.bfloat16)],
         compiler_params=pltpu.CompilerParams(vmem_limit_bytes=12 * 2**20),
         cost_estimate=NO_COST,
         name="finish",
     )(own, *halos, weight, target, filters, table, *after)
-
-
-def add_kernel(count, chunk, grad_ref, *refs):
+    return dict(zip(ends, blocks))
+
+
+def add_kernel(count, chunk, steps, grad_ref, *refs):
     out_ref, tall_ref, done_ref, sems = refs[-4:]
-    ranks = far_first(count, count)
-    pieces = [refs[ranks.index(k)] for k in range(count)]
+    pieces = dict(zip(steps, refs))
     tiles, part, rows, _ = done_ref.shape
     start, size = chunk
     me = lax.axis_index("azimuth")
@@ -379,7 +386,7 @@
             parts = []
             for s in range(lanes[0] // size, lanes[-1] // size + 1):
                 low, high = max(lanes[0], s * size) - s * size, min(lanes[-1] + 1, (s + 1) * size) - s * size
-                parts.append(pieces[order[s]][:, row * size + low : row * size + high])
+                parts.append(pieces[order[s]][:part, row * size + low : row * size + high])
             conv = jnp.concatenate(parts, axis=1).astype(jnp.float32)
             first = count * start + tile * LANES
             total = grad_ref[row, :, first : first + LANES].astype(jnp.float32) + conv
@@ -401,11 +408,12 @@
     rows, part, channels = grad_out.shape
     start, size = chunk
     tiles = count * size // LANES
+    pieces = sorted(pieces.items(), key=lambda item: item[0] <= NEAR)
     vmem = pl.BlockSpec(memory_space=VMEM)
     anywhere = pl.BlockSpec(memory_space=pl.ANY)
     return pl.pallas_call(
-        functools.partial(add_kernel, count, chunk),
-        in_specs=[vmem] * (1 + count) + [anywhere] * len(before),
+        functools.partial(add_kernel, count, chunk, [k for k, _ in pieces]),
+        in_specs=[vmem] * (1 + len(pieces)) + [anywhere] * len(before),
         out_specs=anywhere,
         out_shape=jax.ShapeDtypeStruct((part, rows, channels), jnp.bfloat16),
         scratch_shapes=[
@@ -413,11 +421,11 @@
             pltpu.VMEM((tiles, part, rows, LANES), jnp.bfloat16),
             pltpu.SemaphoreType.DMA((tiles,)),
         ],
-        input_output_aliases={1 + count: 0} if before else {},
+        input_output_aliases={1 + len(pieces): 0} if before else {},
         compiler_params=pltpu.CompilerParams(vmem_limit_bytes=12 * 2**20),
         cost_estimate=NO_COST,
         name="add_chunk",
-    )(grad_out, *(pieces[i] for i in far_first(count, count)), *before)
+    )(grad_out, *(block for _, block in pieces), *before)
 
 
 def prepare_kernel(count, chunks, weight_ref, filt_ref, offset_ref, forth_ref, back_ref, *outs):
@@ -526,7 +534,7 @@
     filters, target, forth, back, *weights = prepare(
         basis_weight, filt, offsets, forth, back, rows, count, chunks
     )
-    spectra, terms, grids, returned = {}, {}, {}, []
+    spectra, terms, grids, returned = {}, {}, {}, {}
 
     def open_chunk(q, after):
         tail = [exchange(blocks[NEAR + 1 + q * len(far) + i], k, count) for i, k in enumerate(far)]
@@ -535,14 +543,14 @@
         terms[q] = own_terms(own, weights[q], target, filters)
 
     def close_chunk(q):
-        after = [returned[(q - 1) * count + 1]] if q else []
+        after = [returned[q - 1].pop(TOKEN)] if q else []
+        cut = 0 if q == last else 16
         halos = spectra[q]
         if q == 0:
             terms[q] = side_terms(terms[q], halos[0], weights[q], target, filters)
             halos = halos[1:]
-        grids[q] = finish(terms[q], halos, weights[q], target, filters, back, count, part, after)
-        blocks = {k: exchange(grids[q][k], k, count) for k in [*far, *range(NEAR + 1)]}
-        returned.extend(blocks[k] for k in range(count))
+        grids[q] = finish(terms[q], halos, weights[q], target, filters, back, count, part, cut, after)
+        returned[q] = {k: exchange(block, NEAR if k == TOKEN else k, count) for k, block in grids[q].items()}
 
     last = len(chunks) - 1
     open_chunk(0, [])
@@ -554,7 +562,7 @@
             open_chunk(q + 2, [grids[q][0]])
     total = []
     for q, chunk in enumerate(chunks):
-        total = [add_chunk(grad_out, returned[q * count : (q + 1) * count], chunk, count, total)]
+        total = [add_chunk(grad_out, returned[q], chunk, count, total)]
     return jnp.transpose(total[0], (1, 0, 2))
 
 

time: 46.7 us -> 46.1 us (0.987)
  the two profiles are of different devices: /device:TPU:17 before, /device:TPU:1 now
where the time goes in v1:
time: 46.1 us; the launch traced here: 45.8 us
  starting transfers between devices  17.2 us (37%)
  Pallas kernels  14.7 us (32%)
  waiting for transfers between devices  10.7 us (23%)
  local copies, waits for them, and re-layouts  2.77 us (6%)
    ppermute x15, starting transfers between devices, exchange(): return lax.ppermute(block, 'azimuth', pairs)  11.7 us
    ppermute x15, waiting for transfers between devices, exchange(): return lax.ppermute(block, 'azimuth', pairs)  9.42 us
    pallas_call x2, Pallas kernels, mlp(): pl.pallas_call(functools.partial(mlp_kernel, count, half, sent, chunks),...  5.5 us
    ppermute x4, starting transfers between devices, halo(): blocks.append(lax.ppermute(block, ('polar', 'azimuth'), pairs))  5.46 us
    unnamed x18, local copies, waits for them, and re-layouts  2.77 us
    pallas_call x2, Pallas kernels, add_chunk(): pl.pallas_call(functools.partial(add_kernel, count, chunk, [k for k, _ in...  2.47 us
    pallas_call x2, Pallas kernels, finish(): pl.pallas_call(functools.partial(finish_kernel, count, len(halos), steps)...  2.44 us
    pallas_call x2, Pallas kernels, own_terms(): pl.pallas_call(own_kernel, in_specs=[pl.BlockSpec(memory_space=VMEM)] * 4...  1.69 us
  transfers between devices with their start and end apart: 19, of which 10 were waited for; matrix products, arithmetic and copies ran while one was open for 0% of the time, Pallas kernels for 22%

profile of v1, /device:TPU:1, one launch (start us, length us, event | category | flops | bytes accessed | tf_op | source)
XLA Modules:
  0.0 45.8 jit_solution(18370755067591178805)
XLA Ops:
  0.0 0.0 copy-start.1
  0.0 0.0 copy-start.6
  0.0 0.0 copy-start
  0.0 1.4 %copy.17.grad_ref = bf16[4,180,640]{2,1,0:T(8,128)(2,1)S(1)} copy(bf16[4,180,640]{2,0,1:T(4,128)(2,1)} %param.11) | data formatting | bytes 1843200 | tf_op args[1]
  1.5 1.3 %copy.12.conv_ref = bf16[4,180,640]{2,1,0:T(8,128)(2,1)S(1)} copy(bf16[4,180,640]{2,0,1:T(4,128)(2,1)} %param.10) | data formatting | bytes 1843200 | tf_op args[0]
  2.8 0.0 copy-done.1
  2.8 0.0 copy-done.6
  2.8 0.0 copy-done
  2.8 2.8 %mlp.2 = (bf16[160,384]{1,0:T(8,128)(2,1)S(1)}, bf16[160,384]{1,0:T(8,128)(2,1)S(1)}, bf16[160,384]{1,0:T(8,128)(2,1)S(1)}, bf16[160,384]{1,0:T(8,128)(2,1)S(1)}) custom-call(bf16[4,180,640]{2,1,0:T(8,128)(2,1)S(1)} %copy.12.conv_ref, bf16[4,180,640]{2,1,0:T(8,128)(2,1)S(1)} %copy.17.grad_ref, bf16[640,1280]{1,0:T(8,128)(2,1)S(1)} %copy-done, ...), custom_call_target="tpu_custom_call" | custom-call | tf_op jit(solution)/shard_map/mlp/pallas_call | solution.py:166
  5.5 0.1 collective-permute-start.2
  5.7 2.7 %collective-permute-start = (bf16[160,384]{1,0:T(8,128)(2,1)S(1)}, bf16[160,384]{1,0:T(8,128)(2,1)S(1)}, u32[]{:S(2)}, u32[]{:S(2)}) collective-permute-start(bf16[160,384]{1,0:T(8,128)(2,1)S(1)} %get-tuple-element.36), channel_id=1, source_target_pairs={{0,2},{1,3},{2,0},{3,1},{4,6},{5,7},{6,4},{7,5},{8,10},{9,11},{10,... | collective-permute-start | bytes 368648 | tf_op jit(solution)/shard_map/ppermute | solution.py:41
  8.3 0.0 copy-start.7
  8.4 0.1 collective-permute-start.1
  8.4 0.0 collective-permute-done.2.rest_0_.refs_3_
  8.5 2.7 %mlp.3 = (bf16[160,384]{1,0:T(8,128)(2,1)S(1)}, bf16[160,384]{1,0:T(8,128)(2,1)S(1)}, bf16[96,384]{1,0:T(8,128)(2,1)S(1)}, bf16[96,384]{1,0:T(8,128)(2,1)S(1)}, ...) custom-call(bf16[4,180,640]{2,1,0:T(8,128)(2,1)S(1)} %copy.12.conv_ref, bf16[4,180,640]{2,1,0:T(8,128)(2,1)S(1)} %copy.17.grad_ref, ...), custom_call_target="tpu_custom_call" | custom-call | tf_op jit(solution)/shard_map/mlp/pallas_call | solution.py:166
  11.2 0.5 %collective-permute-start.5 = (bf16[160,384]{1,0:T(8,128)(2,1)S(1)}, bf16[160,384]{1,0:T(8,128)(2,1)S(1)}, u32[]{:S(2)}, u32[]{:S(2)}) collective-permute-start(bf16[160,384]{1,0:T(8,128)(2,1)S(1)} %get-tuple-element.43), channel_id=1, source_target_pairs={{0,1},{1,0},{2,3},{3,2},{4,5},{5,4},{6,7},{7,6},{8,9},{9,8},{10,11... | collective-permute-start | bytes 368648 | tf_op jit(solution)/shard_map/ppermute | solution.py:41
  11.7 1.4 %collective-permute-start.6 = (bf16[96,384]{1,0:T(8,128)(2,1)S(1)}, bf16[96,384]{1,0:T(8,128)(2,1)S(1)}, u32[]{:S(2)}, u32[]{:S(2)}) collective-permute-start(bf16[96,384]{1,0:T(8,128)(2,1)S(1)} %get-tuple-element.45), channel_id=1, source_target_pairs={{0,2},{1,3},{2,0},{3,1},{4,6},{5,7},{6,4},{7,5},{8,10},{9,11},{10,... | collective-permute-start | bytes 221192 | tf_op jit(solution)/shard_map/ppermute | solution.py:41
  13.1 0.3 collective-permute-start.7
  13.4 0.0 copy-done.2
  13.4 0.0 copy-done.3
  13.4 0.0 copy-done.4
  13.4 0.0 copy-done.5
  13.4 0.0 copy-done.7
  13.4 0.7 %prepare.1 = (bf16[10,32,768]{2,1,0:T(8,128)(2,1)S(1)}, s32[10,32]{1,0:T(8,128)S(1)}, bf16[4,320,640]{2,1,0:T(8,128)(2,1)S(1)}, bf16[768,640]{1,0:T(8,128)(2,1)S...) custom-call(f32[9,640]{1,0:T(8,128)S(1)} %copy-done.5, bf16[9,16,640]{2,1,0:T(8,128)(2,1)S(1)} %copy-done.4, ...), custom_call_target="tpu_custom_call" | custom-call | tf_op jit(solution)/shard_map/prepare/pallas_call | solution.py:490
  14.2 0.0 collective-permute-done.refs_0_
  14.2 0.6 %collective-permute-done.1.refs_1_ = bf16[160,384]{1,0:T(8,128)(2,1)S(1)} collective-permute-done((bf16[160,384]{1,0:T(8,128)(2,1)S(1)}, bf16[160,384]{1,0:T(8,128)(2,1)S(1)}, u32[]{:S(2)}, u32[]{:S(2)}) %collective-permute-start.1) | collective-permute-done | bytes 122912 | tf_op jit(solution)/shard_map/ppermute | solution.py:41
  14.8 1.4 %collective-permute-done.6.refs_4_ = bf16[96,384]{1,0:T(8,128)(2,1)S(1)} collective-permute-done((bf16[96,384]{1,0:T(8,128)(2,1)S(1)}, bf16[96,384]{1,0:T(8,128)(2,1)S(1)}, u32[]{:S(2)}, u32[]{:S(2)}) %collective-permute-start.6) | collective-permute-done | bytes 73760 | tf_op jit(solution)/shard_map/ppermute | solution.py:41
  16.2 1.8 %collective-permute-done.7.refs_5_ = bf16[96,384]{1,0:T(8,128)(2,1)S(1)} collective-permute-done((bf16[96,384]{1,0:T(8,128)(2,1)S(1)}, bf16[96,384]{1,0:T(8,128)(2,1)S(1)}, u32[]{:S(2)}, u32[]{:S(2)}) %collective-permute-start.7) | collective-permute-done | bytes 73760 | tf_op jit(solution)/shard_map/ppermute | solution.py:41
  18.0 0.0 collective-permute-done.5.refs_7_
  18.0 0.8 %analysis.2 = (f32[4,96,640]{2,1,0:T(8,128)S(1)}, bf16[3,96,640]{2,1,0:T(8,128)(2,1)S(1)}, bf16[3,96,640]{2,1,0:T(8,128)(2,1)S(1)}) custom-call(bf16[160,384]{1,0:T(8,128)(2,1)S(1)} %collective-permute-done.refs_0_, bf16[160,384]{1,0:T(8,128)(2,1)S(1)} %collective-permute-done.1.refs_1_, bf16[160,384]{1,0:T(8,128)(2,1)S(1)} %get-tuple-element.38.refs_2_, ...), custom_call_target="tpu_custom_call" | custom-call | tf_op jit(solution)/shard_map/analysis/pallas_call | solution.py:229
  18.8 1.4 %collective-permute-start.10 = (bf16[3,96,640]{2,1,0:T(8,128)(2,1)S(1)}, bf16[3,96,640]{2,1,0:T(8,128)(2,1)S(1)}, u32[]{:S(2)}, u32[]{:S(2)}) collective-permute-start(bf16[3,96,640]{2,1,0:T(8,128)(2,1)S(1)} %get-tuple-element.56), channel_id=1, source_target_pairs={{0,4},{1,5},{2,6},{3,7},{4,0},{5,1},{6,2},{7,3},{8,12},{9,13},{10,... | collective-permute-start | bytes 1105928 | tf_op jit(solution)/shard_map/ppermute | solution.py:512
  20.2 0.7 %collective-permute-start.11 = (bf16[3,96,640]{2,1,0:T(8,128)(2,1)S(1)}, bf16[3,96,640]{2,1,0:T(8,128)(2,1)S(1)}, u32[]{:S(2)}, u32[]{:S(2)}) collective-permute-start(bf16[3,96,640]{2,1,0:T(8,128)(2,1)S(1)} %get-tuple-element.57), channel_id=1, source_target_pairs={{0,1},{1,0},{2,3},{3,2},{4,8},{5,9},{6,10},{7,11},{8,4},{9,5},{10,... | collective-permute-start | bytes 1105928 | tf_op jit(solution)/shard_map/ppermute | solution.py:512
  20.9 1.0 %collective-permute-start.3 = (bf16[64,384]{1,0:T(8,128)(2,1)S(1)}, bf16[64,384]{1,0:T(8,128)(2,1)S(1)}, u32[]{:S(2)}, u32[]{:S(2)}) collective-permute-start(bf16[64,384]{1,0:T(8,128)(2,1)S(1)} %get-tuple-element.40), channel_id=1, source_target_pairs={{0,2},{1,3},{2,0},{3,1},{4,6},{5,7},{6,4},{7,5},{8,10},{9,11},{10,... | collective-permute-start | bytes 147464 | tf_op jit(solution)/shard_map/ppermute | solution.py:41
  21.9 0.6 %collective-permute-start.4 = (bf16[64,384]{1,0:T(8,128)(2,1)S(1)}, bf16[64,384]{1,0:T(8,128)(2,1)S(1)}, u32[]{:S(2)}, u32[]{:S(2)}) collective-permute-start(bf16[64,384]{1,0:T(8,128)(2,1)S(1)} %get-tuple-element.41), channel_id=1, source_target_pairs={{0,3},{1,2},{2,1},{3,0},{4,7},{5,6},{6,5},{7,4},{8,11},{9,10},{10,... | collective-permute-start | bytes 147464 | tf_op jit(solution)/shard_map/ppermute | solution.py:41
  22.5 1.0 %own_terms.2.refs_9_.part_ref = f32[4,96,640]{2,1,0:T(8,128)S(1)} custom-call(f32[4,96,640]{2,1,0:T(8,128)S(1)} %get-tuple-element.47.own_ref, f32[96,32]{1,0:T(8,128)S(1)} %get-tuple-element.48.weight_ref.refs_1_, s32[10,32]{1,0:T(8,128)S(1)} %get-tuple-element.49.target_ref.refs_2_.refs_3_, ...), custom_call_target="tpu_custom_call" | custom-call | tf_op jit(solution)/shard_map/own_terms/pallas_call | solution.py:280
  23.5 0.7 %collective-permute-done.3.refs_4_ = bf16[64,384]{1,0:T(8,128)(2,1)S(1)} collective-permute-done((bf16[64,384]{1,0:T(8,128)(2,1)S(1)}, bf16[64,384]{1,0:T(8,128)(2,1)S(1)}, u32[]{:S(2)}, u32[]{:S(2)}) %collective-permute-start.3) | collective-permute-done | bytes 49184 | tf_op jit(solution)/shard_map/ppermute | solution.py:41
  24.3 1.6 %collective-permute-done.4.refs_5_ = bf16[64,384]{1,0:T(8,128)(2,1)S(1)} collective-permute-done((bf16[64,384]{1,0:T(8,128)(2,1)S(1)}, bf16[64,384]{1,0:T(8,128)(2,1)S(1)}, u32[]{:S(2)}, u32[]{:S(2)}) %collective-permute-start.4) | collective-permute-done | bytes 49184 | tf_op jit(solution)/shard_map/ppermute | solution.py:41
  25.8 0.6 %analysis.3 = (f32[4,64,640]{2,1,0:T(8,128)S(1)}, bf16[3,64,640]{2,1,0:T(8,128)(2,1)S(1)}, bf16[3,64,640]{2,1,0:T(8,128)(2,1)S(1)}) custom-call(bf16[160,384]{1,0:T(8,128)(2,1)S(1)} %collective-permute-done.refs_0_, bf16[160,384]{1,0:T(8,128)(2,1)S(1)} %collective-permute-done.1.refs_1_, bf16[160,384]{1,0:T(8,128)(2,1)S(1)} %get-tuple-element.38.refs_2_, ...), custom_call_target="tpu_custom_call" | custom-call | tf_op jit(solution)/shard_map/analysis/pallas_call | solution.py:229
  26.5 2.6 %collective-permute-start.8 = (bf16[3,64,640]{2,1,0:T(8,128)(2,1)S(1)}, bf16[3,64,640]{2,1,0:T(8,128)(2,1)S(1)}, u32[]{:S(2)}, u32[]{:S(2)}) collective-permute-start(bf16[3,64,640]{2,1,0:T(8,128)(2,1)S(1)} %get-tuple-element.53), channel_id=1, source_target_pairs={{0,4},{1,5},{2,6},{3,7},{4,0},{5,1},{6,2},{7,3},{8,12},{9,13},{10,... | collective-permute-start | bytes 737288 | tf_op jit(solution)/shard_map/ppermute | solution.py:512
  29.1 0.8 %collective-permute-start.9 = (bf16[3,64,640]{2,1,0:T(8,128)(2,1)S(1)}, bf16[3,64,640]{2,1,0:T(8,128)(2,1)S(1)}, u32[]{:S(2)}, u32[]{:S(2)}) collective-permute-start(bf16[3,64,640]{2,1,0:T(8,128)(2,1)S(1)} %get-tuple-element.54), channel_id=1, source_target_pairs={{0,1},{1,0},{2,3},{3,2},{4,8},{5,9},{6,10},{7,11},{8,4},{9,5},{10,... | collective-permute-start | bytes 737288 | tf_op jit(solution)/shard_map/ppermute | solution.py:512
  29.9 0.0 collective-permute-done.10.first_ref
  29.9 0.5 %side_terms.1.part_ref = f32[4,96,640]{2,1,0:T(8,128)S(1)} custom-call(f32[4,96,640]{2,1,0:T(8,128)S(1)} %own_terms.2.refs_9_.part_ref, bf16[3,96,640]{2,1,0:T(8,128)(2,1)S(1)} %collective-permute-done.10.first_ref, f32[96,32]{1,0:T(8,128)S(1)} %get-tuple-element.48.weight_ref.refs_1_, s32[10,32]{1,0:T(8,128)S(1)} %get-tuple-element.49.target_ref.refs_2_.refs_3_, ...), custom_call_target="tpu_custom_call" | custom-call | tf_op jit(solution)/shard_map/side_terms/pallas_call | solution.py:321
  30.4 0.0 collective-permute-done.11.refs_0_
  30.4 1.2 %finish.2 = (bf16[180,384]{1,0:T(8,128)(2,1)S(1)}, bf16[192,384]{1,0:T(8,128)(2,1)S(1)}, bf16[180,384]{1,0:T(8,128)(2,1)S(1)}, bf16[180,384]{1,0:T(8,128)(2,1)S(1)}, bf16[16,384]{1,0:T(8,128)(2,1)S(1)}) custom-call(f32[4,96,640]{2,1,0:T(8,128)S(1)} %side_terms.1.part_ref, bf16[3,96,640]{2,1,0:T(8,128)(2,1)S(1)} %collective-permute-done.11.refs_0_, ...), custom_call_target="tpu_custom_call" | custom-call | tf_op jit(solution)/shard_map/finish/pallas_call | solution.py:360
  31.6 0.7 %collective-permute-start.16 = (bf16[180,384]{1,0:T(8,128)(2,1)S(1)}, bf16[180,384]{1,0:T(8,128)(2,1)S(1)}, u32[]{:S(2)}, u32[]{:S(2)}) collective-permute-start(bf16[180,384]{1,0:T(8,128)(2,1)S(1)} %get-tuple-element.63), channel_id=1, source_target_pairs={{0,2},{1,3},{2,0},{3,1},{4,6},{5,7},{6,4},{7,5},{8,10},{9,11},{10,... | collective-permute-start | bytes 414728 | tf_op jit(solution)/shard_map/ppermute | solution.py:41
  32.3 0.8 %collective-permute-start.18 = (bf16[192,384]{1,0:T(8,128)(2,1)S(1)}, bf16[192,384]{1,0:T(8,128)(2,1)S(1)}, u32[]{:S(2)}, u32[]{:S(2)}) collective-permute-start(bf16[192,384]{1,0:T(8,128)(2,1)S(1)} %get-tuple-element.66), channel_id=1, source_target_pairs={{0,1},{1,0},{2,3},{3,2},{4,5},{5,4},{6,7},{7,6},{8,9},{9,8},{10,11... | collective-permute-start | bytes 442376 | tf_op jit(solution)/shard_map/ppermute | solution.py:41
  33.2 0.4 collective-permute-start.17
  33.6 1.3 %collective-permute-done.8.refs_0_ = bf16[3,64,640]{2,1,0:T(8,128)(2,1)S(1)} collective-permute-done((bf16[3,64,640]{2,1,0:T(8,128)(2,1)S(1)}, bf16[3,64,640]{2,1,0:T(8,128)(2,1)S(1)}, u32[]{:S(2)}, u32[]{:S(2)}) %collective-permute-start.8) | collective-permute-done | bytes 245792 | tf_op jit(solution)/shard_map/ppermute | solution.py:512
  34.9 1.1 %collective-permute-start.12 = (bf16[16,384]{1,0:T(8,128)(2,1)S(1)}, bf16[16,384]{1,0:T(8,128)(2,1)S(1)}, u32[]{:S(2)}, u32[]{:S(2)}) collective-permute-start(bf16[16,384]{1,0:T(8,128)(2,1)S(1)} %get-tuple-element.58), channel_id=1, source_target_pairs={{0,1},{1,0},{2,3},{3,2},{4,5},{5,4},{6,7},{7,6},{8,9},{9,8},{10,11... | collective-permute-start | bytes 36872 | tf_op jit(solution)/shard_map/ppermute | solution.py:41
  36.0 0.7 %own_terms.3.part_ref = f32[4,64,640]{2,1,0:T(8,128)S(1)} custom-call(f32[4,64,640]{2,1,0:T(8,128)S(1)} %get-tuple-element.51.own_ref, f32[64,32]{1,0:T(8,128)S(1)} %get-tuple-element.52.weight_ref.refs_2_, s32[10,32]{1,0:T(8,128)S(1)} %get-tuple-element.49.target_ref.refs_2_.refs_3_, bf16[10,32,768]{2,1,0:T(8,128)(2,1)S(1)} %get-tuple-element.50.filter_ref.refs_3_.refs_4_), custom_call_target="tpu_custom_call" | custom-call | tf_op jit(solution)/shard_map/own_terms/pallas_call | solution.py:280
  36.7 0.0 collective-permute-done.9.refs_1_
  36.7 0.1 collective-permute-done.12.refs_6_
  36.8 1.2 %finish.3 = (bf16[180,256]{1,0:T(8,128)(2,1)S(1)}, bf16[180,256]{1,0:T(8,128)(2,1)S(1)}, bf16[180,256]{1,0:T(8,128)(2,1)S(1)}, bf16[180,256]{1,0:T(8,128)(2,1)S(1)}) custom-call(f32[4,64,640]{2,1,0:T(8,128)S(1)} %own_terms.3.part_ref, bf16[3,64,640]{2,1,0:T(8,128)(2,1)S(1)} %collective-permute-done.8.refs_0_, ...), custom_call_target="tpu_custom_call" | custom-call | tf_op jit(solution)/shard_map/finish/pallas_call | solution.py:360
  38.0 1.3 %collective-permute-start.13 = (bf16[180,256]{1,0:T(8,128)(2,1)S(1)}, bf16[180,256]{1,0:T(8,128)(2,1)S(1)}, u32[]{:S(2)}, u32[]{:S(2)}) collective-permute-start(bf16[180,256]{1,0:T(8,128)(2,1)S(1)} %get-tuple-element.59), channel_id=1, source_target_pairs={{0,2},{1,3},{2,0},{3,1},{4,6},{5,7},{6,4},{7,5},{8,10},{9,11},{10,... | collective-permute-start | bytes 276488 | tf_op jit(solution)/shard_map/ppermute | solution.py:41
  39.3 0.7 %collective-permute-start.14 = (bf16[180,256]{1,0:T(8,128)(2,1)S(1)}, bf16[180,256]{1,0:T(8,128)(2,1)S(1)}, u32[]{:S(2)}, u32[]{:S(2)}) collective-permute-start(bf16[180,256]{1,0:T(8,128)(2,1)S(1)} %get-tuple-element.60), channel_id=1, source_target_pairs={{0,3},{1,2},{2,1},{3,0},{4,7},{5,6},{6,5},{7,4},{8,11},{9,10},{10,... | collective-permute-start | bytes 276488 | tf_op jit(solution)/shard_map/ppermute | solution.py:41
  40.0 0.0 collective-permute-done.16.refs_0_
  40.0 0.0 collective-permute-start.15
  40.0 0.2 collective-permute-done.17.refs_1_
  40.2 0.0 collective-permute-done.18.refs_3_
  40.2 1.4 %add_chunk.2.refs_4_ = bf16[180,4,640]{2,1,0:T(4,128)(2,1)} custom-call(bf16[4,180,640]{2,1,0:T(8,128)(2,1)S(1)} %copy.17.grad_ref, bf16[180,384]{1,0:T(8,128)(2,1)S(1)} %collective-permute-done.16.refs_0_, bf16[180,384]{1,0:T(8,128)(2,1)S(1)} %collective-permute-done.17.refs_1_, bf16[180,384]{1,0:T(8,128)(2,1)S(1)} %get-tuple-element.65.refs_2_, ...), custom_call_target="tpu_custom_call" | custom-call | tf_op jit(solution)/shard_map/add_chunk/pallas_call | solution.py:414
  41.6 0.5 %collective-permute-done.13.refs_0_ = bf16[180,256]{1,0:T(8,128)(2,1)S(1)} collective-permute-done((bf16[180,256]{1,0:T(8,128)(2,1)S(1)}, bf16[180,256]{1,0:T(8,128)(2,1)S(1)}, u32[]{:S(2)}, u32[]{:S(2)}) %collective-permute-start.13) | collective-permute-done | bytes 92192 | tf_op jit(solution)/shard_map/ppermute | solution.py:41
  42.1 2.4 %collective-permute-done.14.refs_1_ = bf16[180,256]{1,0:T(8,128)(2,1)S(1)} collective-permute-done((bf16[180,256]{1,0:T(8,128)(2,1)S(1)}, bf16[180,256]{1,0:T(8,128)(2,1)S(1)}, u32[]{:S(2)}, u32[]{:S(2)}) %collective-permute-start.14) | collective-permute-done | bytes 92192 | tf_op jit(solution)/shard_map/ppermute | solution.py:41
  44.5 0.0 collective-permute-done.15.refs_3_
  44.5 1.1 %add_chunk.3 = bf16[180,4,640]{2,1,0:T(4,128)(2,1)} custom-call(bf16[4,180,640]{2,1,0:T(8,128)(2,1)S(1)} %copy.17.grad_ref, bf16[180,256]{1,0:T(8,128)(2,1)S(1)} %collective-permute-done.13.refs_0_, bf16[180,256]{1,0:T(8,128)(2,1)S(1)} %collective-permute-done.14.refs_1_, ...), custom_call_target="tpu_custom_call", output_to_operand_aliasing={{}: (5, {})} | custom-call | tf_op jit(solution)/shard_map/add_chunk/pallas_call | solution.py:414
  (4 shorter events, 0.0 us)
Async XLA Ops:
  0.0 2.8 %copy-start.1 = (bf16[1280,640]{1,0:T(8,128)(2,1)S(1)}, bf16[1280,640]{1,0:T(8,128)(2,1)}, u32[]{:S(2)}) copy-start(bf16[1280,640]{1,0:T(8,128)(2,1)} %wout_ref.3) | copy-start | bytes 4915204
  0.0 2.8 %copy-start.6 = (f32[1280]{0:T(1024)S(1)}, f32[1280]{0:T(1024)}, u32[]{:S(2)}) copy-start(f32[1280]{0:T(1024)} %bias_ref.3) | copy-start | bytes 15364
  0.0 2.8 %copy-start = (bf16[640,1280]{1,0:T(8,128)(2,1)S(1)}, bf16[640,1280]{1,0:T(8,128)(2,1)}, u32[]{:S(2)}) copy-start(bf16[640,1280]{1,0:T(8,128)(2,1)} %win_ref.3) | copy-start | bytes 4915204
  5.5 2.9 %collective-permute-start.2 = (bf16[160,384]{1,0:T(8,128)(2,1)S(1)}, bf16[160,384]{1,0:T(8,128)(2,1)S(1)}, u32[]{:S(2)}, u32[]{:S(2)}) collective-permute-start(bf16[160,384]{1,0:T(8,128)(2,1)S(1)} %get-tuple-element.39), channel_id=1, source_target_pairs={{0,1},{1,0},{2,3},{3,2},{4,5},{5,4},{6,7},{7,6},{8,9},{9,8},{10,11... | collective-permute-start | bytes 368648 | tf_op jit(solution)/shard_map/ppermute | solution.py:41
  5.7 8.5 %collective-permute-start = (bf16[160,384]{1,0:T(8,128)(2,1)S(1)}, bf16[160,384]{1,0:T(8,128)(2,1)S(1)}, u32[]{:S(2)}, u32[]{:S(2)}) collective-permute-start(bf16[160,384]{1,0:T(8,128)(2,1)S(1)} %get-tuple-element.36), channel_id=1, source_target_pairs={{0,2},{1,3},{2,0},{3,1},{4,6},{5,7},{6,4},{7,5},{8,10},{9,11},{10,... | collective-permute-start | bytes 368648 | tf_op jit(solution)/shard_map/ppermute | solution.py:41
  8.3 5.1 %copy-start.2 = (bf16[4,320,640]{2,1,0:T(8,128)(2,1)S(1)}, bf16[4,320,640]{2,1,0:T(8,128)(2,1)}, u32[]{:S(2)}) copy-start(bf16[4,320,640]{2,1,0:T(8,128)(2,1)} %constant.4.clone.forth_ref) | copy-start | bytes 4915204
  8.3 5.1 %copy-start.3 = (bf16[768,640]{1,0:T(8,128)(2,1)S(1)}, bf16[768,640]{1,0:T(8,128)(2,1)}, u32[]{:S(2)}) copy-start(bf16[768,640]{1,0:T(8,128)(2,1)} %constant.5.clone.back_ref) | copy-start | bytes 2949124
  8.3 5.1 %copy-start.4 = (bf16[9,16,640]{2,1,0:T(8,128)(2,1)S(1)}, bf16[9,16,640]{2,1,0:T(8,128)(2,1)}, u32[]{:S(2)}) copy-start(bf16[9,16,640]{2,1,0:T(8,128)(2,1)} %filt_ref.1) | copy-start | bytes 552964
  8.3 5.1 %copy-start.5 = (f32[9,640]{1,0:T(8,128)S(1)}, f32[9,640]{1,0:T(8,128)}, u32[]{:S(2)}) copy-start(f32[9,640]{1,0:T(8,128)} %weight_ref.1) | copy-start | bytes 69124
  8.3 5.1 %copy-start.7 = (s32[16,9]{1,0:T(8,128)S(1)}, s32[16,9]{1,0:T(8,128)}, u32[]{:S(2)}) copy-start(s32[16,9]{1,0:T(8,128)} %offset_ref.1) | copy-start | bytes 1732
  8.4 6.4 %collective-permute-start.1 = (bf16[160,384]{1,0:T(8,128)(2,1)S(1)}, bf16[160,384]{1,0:T(8,128)(2,1)S(1)}, u32[]{:S(2)}, u32[]{:S(2)}) collective-permute-start(bf16[160,384]{1,0:T(8,128)(2,1)S(1)} %get-tuple-element.37), channel_id=1, source_target_pairs={{0,3},{1,2},{2,1},{3,0},{4,7},{5,6},{6,5},{7,4},{8,11},{9,10},{10,... | collective-permute-start | bytes 368648 | tf_op jit(solution)/shard_map/ppermute | solution.py:41
  11.2 6.8 %collective-permute-start.5 = (bf16[160,384]{1,0:T(8,128)(2,1)S(1)}, bf16[160,384]{1,0:T(8,128)(2,1)S(1)}, u32[]{:S(2)}, u32[]{:S(2)}) collective-permute-start(bf16[160,384]{1,0:T(8,128)(2,1)S(1)} %get-tuple-element.43), channel_id=1, source_target_pairs={{0,1},{1,0},{2,3},{3,2},{4,5},{5,4},{6,7},{7,6},{8,9},{9,8},{10,11... | collective-permute-start | bytes 368648 | tf_op jit(solution)/shard_map/ppermute | solution.py:41
  11.7 4.5 %collective-permute-start.6 = (bf16[96,384]{1,0:T(8,128)(2,1)S(1)}, bf16[96,384]{1,0:T(8,128)(2,1)S(1)}, u32[]{:S(2)}, u32[]{:S(2)}) collective-permute-start(bf16[96,384]{1,0:T(8,128)(2,1)S(1)} %get-tuple-element.45), channel_id=1, source_target_pairs={{0,2},{1,3},{2,0},{3,1},{4,6},{5,7},{6,4},{7,5},{8,10},{9,11},{10,... | collective-permute-start | bytes 221192 | tf_op jit(solution)/shard_map/ppermute | solution.py:41
  13.1 4.9 %collective-permute-start.7 = (bf16[96,384]{1,0:T(8,128)(2,1)S(1)}, bf16[96,384]{1,0:T(8,128)(2,1)S(1)}, u32[]{:S(2)}, u32[]{:S(2)}) collective-permute-start(bf16[96,384]{1,0:T(8,128)(2,1)S(1)} %get-tuple-element.46), channel_id=1, source_target_pairs={{0,3},{1,2},{2,1},{3,0},{4,7},{5,6},{6,5},{7,4},{8,11},{9,10},{10,... | collective-permute-start | bytes 221192 | tf_op jit(solution)/shard_map/ppermute | solution.py:41
  18.8 11.0 %collective-permute-start.10 = (bf16[3,96,640]{2,1,0:T(8,128)(2,1)S(1)}, bf16[3,96,640]{2,1,0:T(8,128)(2,1)S(1)}, u32[]{:S(2)}, u32[]{:S(2)}) collective-permute-start(bf16[3,96,640]{2,1,0:T(8,128)(2,1)S(1)} %get-tuple-element.56), channel_id=1, source_target_pairs={{0,4},{1,5},{2,6},{3,7},{4,0},{5,1},{6,2},{7,3},{8,12},{9,13},{10,... | collective-permute-start | bytes 1105928 | tf_op jit(solution)/shard_map/ppermute | solution.py:512
  20.2 10.2 %collective-permute-start.11 = (bf16[3,96,640]{2,1,0:T(8,128)(2,1)S(1)}, bf16[3,96,640]{2,1,0:T(8,128)(2,1)S(1)}, u32[]{:S(2)}, u32[]{:S(2)}) collective-permute-start(bf16[3,96,640]{2,1,0:T(8,128)(2,1)S(1)} %get-tuple-element.57), channel_id=1, source_target_pairs={{0,1},{1,0},{2,3},{3,2},{4,8},{5,9},{6,10},{7,11},{8,4},{9,5},{10,... | collective-permute-start | bytes 1105928 | tf_op jit(solution)/shard_map/ppermute | solution.py:512
  20.9 3.4 %collective-permute-start.3 = (bf16[64,384]{1,0:T(8,128)(2,1)S(1)}, bf16[64,384]{1,0:T(8,128)(2,1)S(1)}, u32[]{:S(2)}, u32[]{:S(2)}) collective-permute-start(bf16[64,384]{1,0:T(8,128)(2,1)S(1)} %get-tuple-element.40), channel_id=1, source_target_pairs={{0,2},{1,3},{2,0},{3,1},{4,6},{5,7},{6,4},{7,5},{8,10},{9,11},{10,... | collective-permute-start | bytes 147464 | tf_op jit(solution)/shard_map/ppermute | solution.py:41
  21.9 3.9 %collective-permute-start.4 = (bf16[64,384]{1,0:T(8,128)(2,1)S(1)}, bf16[64,384]{1,0:T(8,128)(2,1)S(1)}, u32[]{:S(2)}, u32[]{:S(2)}) collective-permute-start(bf16[64,384]{1,0:T(8,128)(2,1)S(1)} %get-tuple-element.41), channel_id=1, source_target_pairs={{0,3},{1,2},{2,1},{3,0},{4,7},{5,6},{6,5},{7,4},{8,11},{9,10},{10,... | collective-permute-start | bytes 147464 | tf_op jit(solution)/shard_map/ppermute | solution.py:41
  26.5 8.4 %collective-permute-start.8 = (bf16[3,64,640]{2,1,0:T(8,128)(2,1)S(1)}, bf16[3,64,640]{2,1,0:T(8,128)(2,1)S(1)}, u32[]{:S(2)}, u32[]{:S(2)}) collective-permute-start(bf16[3,64,640]{2,1,0:T(8,128)(2,1)S(1)} %get-tuple-element.53), channel_id=1, source_target_pairs={{0,4},{1,5},{2,6},{3,7},{4,0},{5,1},{6,2},{7,3},{8,12},{9,13},{10,... | collective-permute-start | bytes 737288 | tf_op jit(solution)/shard_map/ppermute | solution.py:512
  29.1 7.6 %collective-permute-start.9 = (bf16[3,64,640]{2,1,0:T(8,128)(2,1)S(1)}, bf16[3,64,640]{2,1,0:T(8,128)(2,1)S(1)}, u32[]{:S(2)}, u32[]{:S(2)}) collective-permute-start(bf16[3,64,640]{2,1,0:T(8,128)(2,1)S(1)} %get-tuple-element.54), channel_id=1, source_target_pairs={{0,1},{1,0},{2,3},{3,2},{4,8},{5,9},{6,10},{7,11},{8,4},{9,5},{10,... | collective-permute-start | bytes 737288 | tf_op jit(solution)/shard_map/ppermute | solution.py:512
  31.6 8.3 %collective-permute-start.16 = (bf16[180,384]{1,0:T(8,128)(2,1)S(1)}, bf16[180,384]{1,0:T(8,128)(2,1)S(1)}, u32[]{:S(2)}, u32[]{:S(2)}) collective-permute-start(bf16[180,384]{1,0:T(8,128)(2,1)S(1)} %get-tuple-element.63), channel_id=1, source_target_pairs={{0,2},{1,3},{2,0},{3,1},{4,6},{5,7},{6,4},{7,5},{8,10},{9,11},{10,... | collective-permute-start | bytes 414728 | tf_op jit(solution)/shard_map/ppermute | solution.py:41
  32.3 7.8 %collective-permute-start.18 = (bf16[192,384]{1,0:T(8,128)(2,1)S(1)}, bf16[192,384]{1,0:T(8,128)(2,1)S(1)}, u32[]{:S(2)}, u32[]{:S(2)}) collective-permute-start(bf16[192,384]{1,0:T(8,128)(2,1)S(1)} %get-tuple-element.66), channel_id=1, source_target_pairs={{0,1},{1,0},{2,3},{3,2},{4,5},{5,4},{6,7},{7,6},{8,9},{9,8},{10,11... | collective-permute-start | bytes 442376 | tf_op jit(solution)/shard_map/ppermute | solution.py:41
  33.2 7.0 %collective-permute-start.17 = (bf16[180,384]{1,0:T(8,128)(2,1)S(1)}, bf16[180,384]{1,0:T(8,128)(2,1)S(1)}, u32[]{:S(2)}, u32[]{:S(2)}) collective-permute-start(bf16[180,384]{1,0:T(8,128)(2,1)S(1)} %get-tuple-element.64), channel_id=1, source_target_pairs={{0,3},{1,2},{2,1},{3,0},{4,7},{5,6},{6,5},{7,4},{8,11},{9,10},{10,... | collective-permute-start | bytes 414728 | tf_op jit(solution)/shard_map/ppermute | solution.py:41
  34.9 1.9 %collective-permute-start.12 = (bf16[16,384]{1,0:T(8,128)(2,1)S(1)}, bf16[16,384]{1,0:T(8,128)(2,1)S(1)}, u32[]{:S(2)}, u32[]{:S(2)}) collective-permute-start(bf16[16,384]{1,0:T(8,128)(2,1)S(1)} %get-tuple-element.58), channel_id=1, source_target_pairs={{0,1},{1,0},{2,3},{3,2},{4,5},{5,4},{6,7},{7,6},{8,9},{9,8},{10,11... | collective-permute-start | bytes 36872 | tf_op jit(solution)/shard_map/ppermute | solution.py:41
  38.0 4.1 %collective-permute-start.13 = (bf16[180,256]{1,0:T(8,128)(2,1)S(1)}, bf16[180,256]{1,0:T(8,128)(2,1)S(1)}, u32[]{:S(2)}, u32[]{:S(2)}) collective-permute-start(bf16[180,256]{1,0:T(8,128)(2,1)S(1)} %get-tuple-element.59), channel_id=1, source_target_pairs={{0,2},{1,3},{2,0},{3,1},{4,6},{5,7},{6,4},{7,5},{8,10},{9,11},{10,... | collective-permute-start | bytes 276488 | tf_op jit(solution)/shard_map/ppermute | solution.py:41
  39.3 5.3 %collective-permute-start.14 = (bf16[180,256]{1,0:T(8,128)(2,1)S(1)}, bf16[180,256]{1,0:T(8,128)(2,1)S(1)}, u32[]{:S(2)}, u32[]{:S(2)}) collective-permute-start(bf16[180,256]{1,0:T(8,128)(2,1)S(1)} %get-tuple-element.60), channel_id=1, source_target_pairs={{0,3},{1,2},{2,1},{3,0},{4,7},{5,6},{6,5},{7,4},{8,11},{9,10},{10,... | collective-permute-start | bytes 276488 | tf_op jit(solution)/shard_map/ppermute | solution.py:41
  40.0 4.6 %collective-permute-start.15 = (bf16[180,256]{1,0:T(8,128)(2,1)S(1)}, bf16[180,256]{1,0:T(8,128)(2,1)S(1)}, u32[]{:S(2)}, u32[]{:S(2)}) collective-permute-start(bf16[180,256]{1,0:T(8,128)(2,1)S(1)} %get-tuple-element.62), channel_id=1, source_target_pairs={{0,1},{1,0},{2,3},{3,2},{4,5},{5,4},{6,7},{7,6},{8,9},{9,8},{10,11... | collective-permute-start | bytes 276488 | tf_op jit(solution)/shard_map/ppermute | solution.py:41

commit v2 on v1

--- a/solution.py
+++ b/solution.py
@@ -303,7 +303,8 @@
             )
 
 
-def side_kernel(part_ref, first_ref, weight_ref, target_ref, filter_ref, out_ref):
+def side_kernel(part_ref, first_ref, weight_ref, target_ref, filter_ref, *rest):
+    out_ref = rest[-1]
     rows = part_ref.shape[0]
     even = lax.rem(lax.axis_index("polar"), 2) == 0
 
@@ -317,16 +318,16 @@
     pl.when(jnp.logical_not(even))(lambda: combine(-REACH))
 
 
-def side_terms(own, first, weight, target, filters):
+def side_terms(own, first, weight, target, filters, after):
     return pl.pallas_call(
         side_kernel,
-        in_specs=[pl.BlockSpec(memory_space=VMEM)] * 5,
+        in_specs=[pl.BlockSpec(memory_space=VMEM)] * 5 + [pl.BlockSpec(memory_space=pl.ANY)] * len(after),
         out_specs=pl.BlockSpec(memory_space=VMEM),
         out_shape=jax.ShapeDtypeStruct(own.shape, jnp.float32),
         compiler_params=pltpu.CompilerParams(vmem_limit_bytes=12 * 2**20),
         cost_estimate=NO_COST,
         name="side_terms",
-    )(own, first, weight, target, filters)
+    )(own, first, weight, target, filters, *after)
 
 
 def finish_kernel(count, swaps, steps, part_ref, *refs):
@@ -543,11 +544,12 @@
         terms[q] = own_terms(own, weights[q], target, filters)
 
     def close_chunk(q):
-        after = [returned[q - 1].pop(TOKEN)] if q else []
-        cut = 0 if q == last else 16
+        after = []
+        cut = 0
         halos = spectra[q]
         if q == 0:
-            terms[q] = side_terms(terms[q], halos[0], weights[q], target, filters)
+            others = [terms[other] for other in terms if other > q]
+            terms[q] = side_terms(terms[q], halos[0], weights[q], target, filters, others)
             halos = halos[1:]
         grids[q] = finish(terms[q], halos, weights[q], target, filters, back, count, part, cut, after)
         returned[q] = {k: exchange(block, NEAR if k == TOKEN else k, count) for k, block in grids[q].items()}

time: 46.1 us -> 46.5 us (level)
  waiting for transfers between devices: 10.7 us -> 11.4 us
    ppermute x15 -> x14, waiting for transfers between devices: 9.42 us -> 10.7 us  [exchange(): return lax.ppermute(block, 'azimuth', pairs)]
    ppermute x4, waiting for transfers between devices: 1.31 us -> 0.65 us  [halo(): blocks.append(lax.ppermute(block, ('polar', 'azimuth'), pairs))]
    ppermute x15 -> x14, starting transfers between devices: 11.7 us -> 11.5 us  [exchange(): return lax.ppermute(block, 'azimuth', pairs)]
  transfers between devices with their start and end apart: 19 -> 18, of which waited for: 10 -> 9; matrix products, arithmetic and copies ran while one was open for 0% -> 0% of each run, Pallas kernels for 22% -> 22%
where the time goes in v2:
time: 46.5 us; the launch traced here: 46.1 us
  starting transfers between devices  17 us (37%)
  Pallas kernels  14.6 us (31%)
  waiting for transfers between devices  11.4 us (25%)
  local copies, waits for them, and re-layouts  2.77 us (6%)
    ppermute x14, starting transfers between devices, exchange(): return lax.ppermute(block, 'azimuth', pairs)  11.5 us
    ppermute x14, waiting for transfers between devices, exchange(): return lax.ppermute(block, 'azimuth', pairs)  10.7 us
    pallas_call x2, Pallas kernels, mlp(): pl.pallas_call(functools.partial(mlp_kernel, count, half, sent, chunks),...  5.5 us
    ppermute x4, starting transfers between devices, halo(): blocks.append(lax.ppermute(block, ('polar', 'azimuth'), pairs))  5.46 us
    unnamed x18, local copies, waits for them, and re-layouts  2.77 us
    pallas_call x2, Pallas kernels, add_chunk(): pl.pallas_call(functools.partial(add_kernel, count, chunk, [k for k, _ in...  2.47 us
    pallas_call x2, Pallas kernels, finish(): pl.pallas_call(functools.partial(finish_kernel, count, len(halos), steps)...  2.31 us
    pallas_call x2, Pallas kernels, own_terms(): pl.pallas_call(own_kernel, in_specs=[pl.BlockSpec(memory_space=VMEM)] * 4...  1.65 us
  transfers between devices with their start and end apart: 18, of which 9 were waited for; matrix products, arithmetic and copies ran while one was open for 0% of the time, Pallas kernels for 22%

profile of v2, /device:TPU:1, one launch (start us, length us, event | category | flops | bytes accessed | tf_op | source)
XLA Modules:
  0.0 46.1 jit_solution(5105630354781579564)
XLA Ops:
  0.0 0.0 copy-start.1
  0.0 0.0 copy-start.6
  0.0 0.0 copy-start
  0.0 1.4 %copy.17.grad_ref = bf16[4,180,640]{2,1,0:T(8,128)(2,1)S(1)} copy(bf16[4,180,640]{2,0,1:T(4,128)(2,1)} %param.11) | data formatting | bytes 1843200 | tf_op args[1]
  1.5 1.3 %copy.12.conv_ref = bf16[4,180,640]{2,1,0:T(8,128)(2,1)S(1)} copy(bf16[4,180,640]{2,0,1:T(4,128)(2,1)} %param.10) | data formatting | bytes 1843200 | tf_op args[0]
  2.8 0.0 copy-done.1
  2.8 0.0 copy-done.6
  2.8 0.0 copy-done
  2.8 2.8 %mlp.2 = (bf16[160,384]{1,0:T(8,128)(2,1)S(1)}, bf16[160,384]{1,0:T(8,128)(2,1)S(1)}, bf16[160,384]{1,0:T(8,128)(2,1)S(1)}, bf16[160,384]{1,0:T(8,128)(2,1)S(1)}) custom-call(bf16[4,180,640]{2,1,0:T(8,128)(2,1)S(1)} %copy.12.conv_ref, bf16[4,180,640]{2,1,0:T(8,128)(2,1)S(1)} %copy.17.grad_ref, bf16[640,1280]{1,0:T(8,128)(2,1)S(1)} %copy-done, ...), custom_call_target="tpu_custom_call" | custom-call | tf_op jit(solution)/shard_map/mlp/pallas_call | solution.py:166
  5.5 0.1 collective-permute-start.2
  5.7 2.7 %collective-permute-start = (bf16[160,384]{1,0:T(8,128)(2,1)S(1)}, bf16[160,384]{1,0:T(8,128)(2,1)S(1)}, u32[]{:S(2)}, u32[]{:S(2)}) collective-permute-start(bf16[160,384]{1,0:T(8,128)(2,1)S(1)} %get-tuple-element.35), channel_id=1, source_target_pairs={{0,2},{1,3},{2,0},{3,1},{4,6},{5,7},{6,4},{7,5},{8,10},{9,11},{10,... | collective-permute-start | bytes 368648 | tf_op jit(solution)/shard_map/ppermute | solution.py:41
  8.3 0.0 copy-start.2
  8.3 0.0 copy-start.3
  8.3 0.0 copy-start.7
  8.4 0.1 collective-permute-start.1
  8.4 0.0 collective-permute-done.2.rest_0_.refs_3_
  8.5 2.7 %mlp.3 = (bf16[160,384]{1,0:T(8,128)(2,1)S(1)}, bf16[160,384]{1,0:T(8,128)(2,1)S(1)}, bf16[96,384]{1,0:T(8,128)(2,1)S(1)}, bf16[96,384]{1,0:T(8,128)(2,1)S(1)}, ...) custom-call(bf16[4,180,640]{2,1,0:T(8,128)(2,1)S(1)} %copy.12.conv_ref, bf16[4,180,640]{2,1,0:T(8,128)(2,1)S(1)} %copy.17.grad_ref, ...), custom_call_target="tpu_custom_call" | custom-call | tf_op jit(solution)/shard_map/mlp/pallas_call | solution.py:166
  11.2 0.5 %collective-permute-start.5 = (bf16[160,384]{1,0:T(8,128)(2,1)S(1)}, bf16[160,384]{1,0:T(8,128)(2,1)S(1)}, u32[]{:S(2)}, u32[]{:S(2)}) collective-permute-start(bf16[160,384]{1,0:T(8,128)(2,1)S(1)} %get-tuple-element.42), channel_id=1, source_target_pairs={{0,1},{1,0},{2,3},{3,2},{4,5},{5,4},{6,7},{7,6},{8,9},{9,8},{10,11... | collective-permute-start | bytes 368648 | tf_op jit(solution)/shard_map/ppermute | solution.py:41
  11.7 1.4 %collective-permute-start.6 = (bf16[96,384]{1,0:T(8,128)(2,1)S(1)}, bf16[96,384]{1,0:T(8,128)(2,1)S(1)}, u32[]{:S(2)}, u32[]{:S(2)}) collective-permute-start(bf16[96,384]{1,0:T(8,128)(2,1)S(1)} %get-tuple-element.44), channel_id=1, source_target_pairs={{0,2},{1,3},{2,0},{3,1},{4,6},{5,7},{6,4},{7,5},{8,10},{9,11},{10,... | collective-permute-start | bytes 221192 | tf_op jit(solution)/shard_map/ppermute | solution.py:41
  13.1 0.3 collective-permute-start.7
  13.4 0.0 copy-done.2
  13.4 0.0 copy-done.3
  13.4 0.0 copy-done.4
  13.4 0.0 copy-done.5
  13.4 0.0 copy-done.7
  13.4 0.7 %prepare.1 = (bf16[10,32,768]{2,1,0:T(8,128)(2,1)S(1)}, s32[10,32]{1,0:T(8,128)S(1)}, bf16[4,320,640]{2,1,0:T(8,128)(2,1)S(1)}, bf16[768,640]{1,0:T(8,128)(2,1)S...) custom-call(f32[9,640]{1,0:T(8,128)S(1)} %copy-done.5, bf16[9,16,640]{2,1,0:T(8,128)(2,1)S(1)} %copy-done.4, ...), custom_call_target="tpu_custom_call" | custom-call | tf_op jit(solution)/shard_map/prepare/pallas_call | solution.py:491
  14.2 0.0 collective-permute-done.refs_0_
  14.2 0.6 %collective-permute-done.1.refs_1_ = bf16[160,384]{1,0:T(8,128)(2,1)S(1)} collective-permute-done((bf16[160,384]{1,0:T(8,128)(2,1)S(1)}, bf16[160,384]{1,0:T(8,128)(2,1)S(1)}, u32[]{:S(2)}, u32[]{:S(2)}) %collective-permute-start.1) | collective-permute-done | bytes 122912 | tf_op jit(solution)/shard_map/ppermute | solution.py:41
  14.8 1.4 %collective-permute-done.6.refs_4_ = bf16[96,384]{1,0:T(8,128)(2,1)S(1)} collective-permute-done((bf16[96,384]{1,0:T(8,128)(2,1)S(1)}, bf16[96,384]{1,0:T(8,128)(2,1)S(1)}, u32[]{:S(2)}, u32[]{:S(2)}) %collective-permute-start.6) | collective-permute-done | bytes 73760 | tf_op jit(solution)/shard_map/ppermute | solution.py:41
  16.2 1.8 %collective-permute-done.7.refs_5_ = bf16[96,384]{1,0:T(8,128)(2,1)S(1)} collective-permute-done((bf16[96,384]{1,0:T(8,128)(2,1)S(1)}, bf16[96,384]{1,0:T(8,128)(2,1)S(1)}, u32[]{:S(2)}, u32[]{:S(2)}) %collective-permute-start.7) | collective-permute-done | bytes 73760 | tf_op jit(solution)/shard_map/ppermute | solution.py:41
  18.0 0.0 collective-permute-done.5.refs_7_
  18.0 0.8 %analysis.2 = (f32[4,96,640]{2,1,0:T(8,128)S(1)}, bf16[3,96,640]{2,1,0:T(8,128)(2,1)S(1)}, bf16[3,96,640]{2,1,0:T(8,128)(2,1)S(1)}) custom-call(bf16[160,384]{1,0:T(8,128)(2,1)S(1)} %collective-permute-done.refs_0_, bf16[160,384]{1,0:T(8,128)(2,1)S(1)} %collective-permute-done.1.refs_1_, bf16[160,384]{1,0:T(8,128)(2,1)S(1)} %get-tuple-element.37.refs_2_, ...), custom_call_target="tpu_custom_call" | custom-call | tf_op jit(solution)/shard_map/analysis/pallas_call | solution.py:229
  18.8 1.4 %collective-permute-start.13 = (bf16[3,96,640]{2,1,0:T(8,128)(2,1)S(1)}, bf16[3,96,640]{2,1,0:T(8,128)(2,1)S(1)}, u32[]{:S(2)}, u32[]{:S(2)}) collective-permute-start(bf16[3,96,640]{2,1,0:T(8,128)(2,1)S(1)} %get-tuple-element.59), channel_id=1, source_target_pairs={{0,4},{1,5},{2,6},{3,7},{4,0},{5,1},{6,2},{7,3},{8,12},{9,13},{10,... | collective-permute-start | bytes 1105928 | tf_op jit(solution)/shard_map/ppermute | solution.py:513
  20.2 0.7 %collective-permute-start.14 = (bf16[3,96,640]{2,1,0:T(8,128)(2,1)S(1)}, bf16[3,96,640]{2,1,0:T(8,128)(2,1)S(1)}, u32[]{:S(2)}, u32[]{:S(2)}) collective-permute-start(bf16[3,96,640]{2,1,0:T(8,128)(2,1)S(1)} %get-tuple-element.60), channel_id=1, source_target_pairs={{0,1},{1,0},{2,3},{3,2},{4,8},{5,9},{6,10},{7,11},{8,4},{9,5},{10,... | collective-permute-start | bytes 1105928 | tf_op jit(solution)/shard_map/ppermute | solution.py:513
  20.9 1.0 %collective-permute-start.3 = (bf16[64,384]{1,0:T(8,128)(2,1)S(1)}, bf16[64,384]{1,0:T(8,128)(2,1)S(1)}, u32[]{:S(2)}, u32[]{:S(2)}) collective-permute-start(bf16[64,384]{1,0:T(8,128)(2,1)S(1)} %get-tuple-element.39), channel_id=1, source_target_pairs={{0,2},{1,3},{2,0},{3,1},{4,6},{5,7},{6,4},{7,5},{8,10},{9,11},{10,... | collective-permute-start | bytes 147464 | tf_op jit(solution)/shard_map/ppermute | solution.py:41
  21.9 0.6 %collective-permute-start.4 = (bf16[64,384]{1,0:T(8,128)(2,1)S(1)}, bf16[64,384]{1,0:T(8,128)(2,1)S(1)}, u32[]{:S(2)}, u32[]{:S(2)}) collective-permute-start(bf16[64,384]{1,0:T(8,128)(2,1)S(1)} %get-tuple-element.40), channel_id=1, source_target_pairs={{0,3},{1,2},{2,1},{3,0},{4,7},{5,6},{6,5},{7,4},{8,11},{9,10},{10,... | collective-permute-start | bytes 147464 | tf_op jit(solution)/shard_map/ppermute | solution.py:41
  22.5 1.0 %own_terms.2.refs_9_.part_ref = f32[4,96,640]{2,1,0:T(8,128)S(1)} custom-call(f32[4,96,640]{2,1,0:T(8,128)S(1)} %get-tuple-element.46.own_ref, f32[96,32]{1,0:T(8,128)S(1)} %get-tuple-element.47.weight_ref.refs_1_, s32[10,32]{1,0:T(8,128)S(1)} %get-tuple-element.48.target_ref.refs_3_.refs_2_, ...), custom_call_target="tpu_custom_call" | custom-call | tf_op jit(solution)/shard_map/own_terms/pallas_call | solution.py:280
  23.5 0.7 %collective-permute-done.3.refs_4_ = bf16[64,384]{1,0:T(8,128)(2,1)S(1)} collective-permute-done((bf16[64,384]{1,0:T(8,128)(2,1)S(1)}, bf16[64,384]{1,0:T(8,128)(2,1)S(1)}, u32[]{:S(2)}, u32[]{:S(2)}) %collective-permute-start.3) | collective-permute-done | bytes 49184 | tf_op jit(solution)/shard_map/ppermute | solution.py:41
  24.3 1.6 %collective-permute-done.4.refs_5_ = bf16[64,384]{1,0:T(8,128)(2,1)S(1)} collective-permute-done((bf16[64,384]{1,0:T(8,128)(2,1)S(1)}, bf16[64,384]{1,0:T(8,128)(2,1)S(1)}, u32[]{:S(2)}, u32[]{:S(2)}) %collective-permute-start.4) | collective-permute-done | bytes 49184 | tf_op jit(solution)/shard_map/ppermute | solution.py:41
  25.8 0.6 %analysis.3 = (f32[4,64,640]{2,1,0:T(8,128)S(1)}, bf16[3,64,640]{2,1,0:T(8,128)(2,1)S(1)}, bf16[3,64,640]{2,1,0:T(8,128)(2,1)S(1)}) custom-call(bf16[160,384]{1,0:T(8,128)(2,1)S(1)} %collective-permute-done.refs_0_, bf16[160,384]{1,0:T(8,128)(2,1)S(1)} %collective-permute-done.1.refs_1_, bf16[160,384]{1,0:T(8,128)(2,1)S(1)} %get-tuple-element.37.refs_2_, ...), custom_call_target="tpu_custom_call" | custom-call | tf_op jit(solution)/shard_map/analysis/pallas_call | solution.py:229
  26.5 2.6 %collective-permute-start.8 = (bf16[3,64,640]{2,1,0:T(8,128)(2,1)S(1)}, bf16[3,64,640]{2,1,0:T(8,128)(2,1)S(1)}, u32[]{:S(2)}, u32[]{:S(2)}) collective-permute-start(bf16[3,64,640]{2,1,0:T(8,128)(2,1)S(1)} %get-tuple-element.52), channel_id=1, source_target_pairs={{0,4},{1,5},{2,6},{3,7},{4,0},{5,1},{6,2},{7,3},{8,12},{9,13},{10,... | collective-permute-start | bytes 737288 | tf_op jit(solution)/shard_map/ppermute | solution.py:513
  29.1 0.8 %collective-permute-start.9 = (bf16[3,64,640]{2,1,0:T(8,128)(2,1)S(1)}, bf16[3,64,640]{2,1,0:T(8,128)(2,1)S(1)}, u32[]{:S(2)}, u32[]{:S(2)}) collective-permute-start(bf16[3,64,640]{2,1,0:T(8,128)(2,1)S(1)} %get-tuple-element.53), channel_id=1, source_target_pairs={{0,1},{1,0},{2,3},{3,2},{4,8},{5,9},{6,10},{7,11},{8,4},{9,5},{10,... | collective-permute-start | bytes 737288 | tf_op jit(solution)/shard_map/ppermute | solution.py:513
  29.9 0.6 %own_terms.3.part_ref.rest_0_ = f32[4,64,640]{2,1,0:T(8,128)S(1)} custom-call(f32[4,64,640]{2,1,0:T(8,128)S(1)} %get-tuple-element.50.own_ref, f32[64,32]{1,0:T(8,128)S(1)} %get-tuple-element.51.weight_ref.refs_2_, s32[10,32]{1,0:T(8,128)S(1)} %get-tuple-element.48.target_ref.refs_3_.refs_2_, ...), custom_call_target="tpu_custom_call" | custom-call | tf_op jit(solution)/shard_map/own_terms/pallas_call | solution.py:280
  30.5 0.0 collective-permute-done.13.first_ref
  30.6 0.5 %side_terms.1.part_ref = f32[4,96,640]{2,1,0:T(8,128)S(1)} custom-call(f32[4,96,640]{2,1,0:T(8,128)S(1)} %own_terms.2.refs_9_.part_ref, bf16[3,96,640]{2,1,0:T(8,128)(2,1)S(1)} %collective-permute-done.13.first_ref, f32[96,32]{1,0:T(8,128)S(1)} %get-tuple-element.47.weight_ref.refs_1_, s32[10,32]{1,0:T(8,128)S(1)} %get-tuple-element.48.target_ref.refs_3_.refs_2_, ...), custom_call_target="tpu_custom_call" | custom-call | tf_op jit(solution)/shard_map/side_terms/pallas_call | solution.py:322
  31.1 0.0 collective-permute-done.14.refs_0_
  31.1 1.2 %finish.3 = (bf16[180,384]{1,0:T(8,128)(2,1)S(1)}, bf16[180,384]{1,0:T(8,128)(2,1)S(1)}, bf16[180,384]{1,0:T(8,128)(2,1)S(1)}, bf16[180,384]{1,0:T(8,128)(2,1)S(1)}) custom-call(f32[4,96,640]{2,1,0:T(8,128)S(1)} %side_terms.1.part_ref, bf16[3,96,640]{2,1,0:T(8,128)(2,1)S(1)} %collective-permute-done.14.refs_0_, ...), custom_call_target="tpu_custom_call" | custom-call | tf_op jit(solution)/shard_map/finish/pallas_call | solution.py:361
  32.3 0.7 %collective-permute-start.15 = (bf16[180,384]{1,0:T(8,128)(2,1)S(1)}, bf16[180,384]{1,0:T(8,128)(2,1)S(1)}, u32[]{:S(2)}, u32[]{:S(2)}) collective-permute-start(bf16[180,384]{1,0:T(8,128)(2,1)S(1)} %get-tuple-element.61), channel_id=1, source_target_pairs={{0,2},{1,3},{2,0},{3,1},{4,6},{5,7},{6,4},{7,5},{8,10},{9,11},{10,... | collective-permute-start | bytes 414728 | tf_op jit(solution)/shard_map/ppermute | solution.py:41
  33.0 1.0 %collective-permute-start.16 = (bf16[180,384]{1,0:T(8,128)(2,1)S(1)}, bf16[180,384]{1,0:T(8,128)(2,1)S(1)}, u32[]{:S(2)}, u32[]{:S(2)}) collective-permute-start(bf16[180,384]{1,0:T(8,128)(2,1)S(1)} %get-tuple-element.62), channel_id=1, source_target_pairs={{0,3},{1,2},{2,1},{3,0},{4,7},{5,6},{6,5},{7,4},{8,11},{9,10},{10,... | collective-permute-start | bytes 414728 | tf_op jit(solution)/shard_map/ppermute | solution.py:41
  34.0 0.2 collective-permute-start.17
  34.2 0.6 %collective-permute-done.8.refs_0_ = bf16[3,64,640]{2,1,0:T(8,128)(2,1)S(1)} collective-permute-done((bf16[3,64,640]{2,1,0:T(8,128)(2,1)S(1)}, bf16[3,64,640]{2,1,0:T(8,128)(2,1)S(1)}, u32[]{:S(2)}, u32[]{:S(2)}) %collective-permute-start.8) | collective-permute-done | bytes 245792 | tf_op jit(solution)/shard_map/ppermute | solution.py:513
  34.9 0.0 collective-permute-done.9.refs_1_
  34.9 1.1 %finish.2 = (bf16[180,256]{1,0:T(8,128)(2,1)S(1)}, bf16[180,256]{1,0:T(8,128)(2,1)S(1)}, bf16[180,256]{1,0:T(8,128)(2,1)S(1)}, bf16[180,256]{1,0:T(8,128)(2,1)S(1)}) custom-call(f32[4,64,640]{2,1,0:T(8,128)S(1)} %own_terms.3.part_ref.rest_0_, bf16[3,64,640]{2,1,0:T(8,128)(2,1)S(1)} %collective-permute-done.8.refs_0_, ...), custom_call_target="tpu_custom_call" | custom-call | tf_op jit(solution)/shard_map/finish/pallas_call | solution.py:361
  36.0 1.8 %collective-permute-start.10 = (bf16[180,256]{1,0:T(8,128)(2,1)S(1)}, bf16[180,256]{1,0:T(8,128)(2,1)S(1)}, u32[]{:S(2)}, u32[]{:S(2)}) collective-permute-start(bf16[180,256]{1,0:T(8,128)(2,1)S(1)} %get-tuple-element.55), channel_id=1, source_target_pairs={{0,2},{1,3},{2,0},{3,1},{4,6},{5,7},{6,4},{7,5},{8,10},{9,11},{10,... | collective-permute-start | bytes 276488 | tf_op jit(solution)/shard_map/ppermute | solution.py:41
  37.8 1.0 %collective-permute-start.11 = (bf16[180,256]{1,0:T(8,128)(2,1)S(1)}, bf16[180,256]{1,0:T(8,128)(2,1)S(1)}, u32[]{:S(2)}, u32[]{:S(2)}) collective-permute-start(bf16[180,256]{1,0:T(8,128)(2,1)S(1)} %get-tuple-element.56), channel_id=1, source_target_pairs={{0,3},{1,2},{2,1},{3,0},{4,7},{5,6},{6,5},{7,4},{8,11},{9,10},{10,... | collective-permute-start | bytes 276488 | tf_op jit(solution)/shard_map/ppermute | solution.py:41
  38.8 0.0 collective-permute-done.15.refs_0_
  38.8 0.1 collective-permute-start.12
  38.9 2.3 %collective-permute-done.16.refs_1_ = bf16[180,384]{1,0:T(8,128)(2,1)S(1)} collective-permute-done((bf16[180,384]{1,0:T(8,128)(2,1)S(1)}, bf16[180,384]{1,0:T(8,128)(2,1)S(1)}, u32[]{:S(2)}, u32[]{:S(2)}) %collective-permute-start.16) | collective-permute-done | bytes 138272 | tf_op jit(solution)/shard_map/ppermute | solution.py:41
  41.2 0.0 collective-permute-done.17.refs_3_
  41.2 1.4 %add_chunk.2.refs_4_ = bf16[180,4,640]{2,1,0:T(4,128)(2,1)} custom-call(bf16[4,180,640]{2,1,0:T(8,128)(2,1)S(1)} %copy.17.grad_ref, bf16[180,384]{1,0:T(8,128)(2,1)S(1)} %collective-permute-done.15.refs_0_, bf16[180,384]{1,0:T(8,128)(2,1)S(1)} %collective-permute-done.16.refs_1_, bf16[180,384]{1,0:T(8,128)(2,1)S(1)} %get-tuple-element.63.refs_2_, ...), custom_call_target="tpu_custom_call" | custom-call | tf_op jit(solution)/shard_map/add_chunk/pallas_call | solution.py:415
  42.6 0.1 collective-permute-done.10.refs_0_
  42.8 2.1 %collective-permute-done.11.refs_1_ = bf16[180,256]{1,0:T(8,128)(2,1)S(1)} collective-permute-done((bf16[180,256]{1,0:T(8,128)(2,1)S(1)}, bf16[180,256]{1,0:T(8,128)(2,1)S(1)}, u32[]{:S(2)}, u32[]{:S(2)}) %collective-permute-start.11) | collective-permute-done | bytes 92192 | tf_op jit(solution)/shard_map/ppermute | solution.py:41
  44.9 0.0 collective-permute-done.12.refs_3_
  44.9 1.1 %add_chunk.3 = bf16[180,4,640]{2,1,0:T(4,128)(2,1)} custom-call(bf16[4,180,640]{2,1,0:T(8,128)(2,1)S(1)} %copy.17.grad_ref, bf16[180,256]{1,0:T(8,128)(2,1)S(1)} %collective-permute-done.10.refs_0_, bf16[180,256]{1,0:T(8,128)(2,1)S(1)} %collective-permute-done.11.refs_1_, ...), custom_call_target="tpu_custom_call", output_to_operand_aliasing={{}: (5, {})} | custom-call | tf_op jit(solution)/shard_map/add_chunk/pallas_call | solution.py:415
  (2 shorter events, 0.0 us)
Async XLA Ops:
  0.0 2.8 %copy-start.1 = (bf16[1280,640]{1,0:T(8,128)(2,1)S(1)}, bf16[1280,640]{1,0:T(8,128)(2,1)}, u32[]{:S(2)}) copy-start(bf16[1280,640]{1,0:T(8,128)(2,1)} %wout_ref.3) | copy-start | bytes 4915204
  0.0 2.8 %copy-start.6 = (f32[1280]{0:T(1024)S(1)}, f32[1280]{0:T(1024)}, u32[]{:S(2)}) copy-start(f32[1280]{0:T(1024)} %bias_ref.3) | copy-start | bytes 15364
  0.0 2.8 %copy-start = (bf16[640,1280]{1,0:T(8,128)(2,1)S(1)}, bf16[640,1280]{1,0:T(8,128)(2,1)}, u32[]{:S(2)}) copy-start(bf16[640,1280]{1,0:T(8,128)(2,1)} %win_ref.3) | copy-start | bytes 4915204
  5.5 2.9 %collective-permute-start.2 = (bf16[160,384]{1,0:T(8,128)(2,1)S(1)}, bf16[160,384]{1,0:T(8,128)(2,1)S(1)}, u32[]{:S(2)}, u32[]{:S(2)}) collective-permute-start(bf16[160,384]{1,0:T(8,128)(2,1)S(1)} %get-tuple-element.38), channel_id=1, source_target_pairs={{0,1},{1,0},{2,3},{3,2},{4,5},{5,4},{6,7},{7,6},{8,9},{9,8},{10,11... | collective-permute-start | bytes 368648 | tf_op jit(solution)/shard_map/ppermute | solution.py:41
  5.7 8.5 %collective-permute-start = (bf16[160,384]{1,0:T(8,128)(2,1)S(1)}, bf16[160,384]{1,0:T(8,128)(2,1)S(1)}, u32[]{:S(2)}, u32[]{:S(2)}) collective-permute-start(bf16[160,384]{1,0:T(8,128)(2,1)S(1)} %get-tuple-element.35), channel_id=1, source_target_pairs={{0,2},{1,3},{2,0},{3,1},{4,6},{5,7},{6,4},{7,5},{8,10},{9,11},{10,... | collective-permute-start | bytes 368648 | tf_op jit(solution)/shard_map/ppermute | solution.py:41
  8.3 5.1 %copy-start.2 = (bf16[4,320,640]{2,1,0:T(8,128)(2,1)S(1)}, bf16[4,320,640]{2,1,0:T(8,128)(2,1)}, u32[]{:S(2)}) copy-start(bf16[4,320,640]{2,1,0:T(8,128)(2,1)} %constant.4.clone.forth_ref) | copy-start | bytes 4915204
  8.3 5.1 %copy-start.3 = (bf16[768,640]{1,0:T(8,128)(2,1)S(1)}, bf16[768,640]{1,0:T(8,128)(2,1)}, u32[]{:S(2)}) copy-start(bf16[768,640]{1,0:T(8,128)(2,1)} %constant.5.clone.back_ref) | copy-start | bytes 2949124
  8.3 5.1 %copy-start.4 = (bf16[9,16,640]{2,1,0:T(8,128)(2,1)S(1)}, bf16[9,16,640]{2,1,0:T(8,128)(2,1)}, u32[]{:S(2)}) copy-start(bf16[9,16,640]{2,1,0:T(8,128)(2,1)} %filt_ref.1) | copy-start | bytes 552964
  8.3 5.1 %copy-start.5 = (f32[9,640]{1,0:T(8,128)S(1)}, f32[9,640]{1,0:T(8,128)}, u32[]{:S(2)}) copy-start(f32[9,640]{1,0:T(8,128)} %weight_ref.1) | copy-start | bytes 69124
  8.3 5.1 %copy-start.7 = (s32[16,9]{1,0:T(8,128)S(1)}, s32[16,9]{1,0:T(8,128)}, u32[]{:S(2)}) copy-start(s32[16,9]{1,0:T(8,128)} %offset_ref.1) | copy-start | bytes 1732
  8.4 6.4 %collective-permute-start.1 = (bf16[160,384]{1,0:T(8,128)(2,1)S(1)}, bf16[160,384]{1,0:T(8,128)(2,1)S(1)}, u32[]{:S(2)}, u32[]{:S(2)}) collective-permute-start(bf16[160,384]{1,0:T(8,128)(2,1)S(1)} %get-tuple-element.36), channel_id=1, source_target_pairs={{0,3},{1,2},{2,1},{3,0},{4,7},{5,6},{6,5},{7,4},{8,11},{9,10},{10,... | collective-permute-start | bytes 368648 | tf_op jit(solution)/shard_map/ppermute | solution.py:41
  11.2 6.8 %collective-permute-start.5 = (bf16[160,384]{1,0:T(8,128)(2,1)S(1)}, bf16[160,384]{1,0:T(8,128)(2,1)S(1)}, u32[]{:S(2)}, u32[]{:S(2)}) collective-permute-start(bf16[160,384]{1,0:T(8,128)(2,1)S(1)} %get-tuple-element.42), channel_id=1, source_target_pairs={{0,1},{1,0},{2,3},{3,2},{4,5},{5,4},{6,7},{7,6},{8,9},{9,8},{10,11... | collective-permute-start | bytes 368648 | tf_op jit(solution)/shard_map/ppermute | solution.py:41
  11.7 4.5 %collective-permute-start.6 = (bf16[96,384]{1,0:T(8,128)(2,1)S(1)}, bf16[96,384]{1,0:T(8,128)(2,1)S(1)}, u32[]{:S(2)}, u32[]{:S(2)}) collective-permute-start(bf16[96,384]{1,0:T(8,128)(2,1)S(1)} %get-tuple-element.44), channel_id=1, source_target_pairs={{0,2},{1,3},{2,0},{3,1},{4,6},{5,7},{6,4},{7,5},{8,10},{9,11},{10,... | collective-permute-start | bytes 221192 | tf_op jit(solution)/shard_map/ppermute | solution.py:41
  13.1 4.9 %collective-permute-start.7 = (bf16[96,384]{1,0:T(8,128)(2,1)S(1)}, bf16[96,384]{1,0:T(8,128)(2,1)S(1)}, u32[]{:S(2)}, u32[]{:S(2)}) collective-permute-start(bf16[96,384]{1,0:T(8,128)(2,1)S(1)} %get-tuple-element.45), channel_id=1, source_target_pairs={{0,3},{1,2},{2,1},{3,0},{4,7},{5,6},{6,5},{7,4},{8,11},{9,10},{10,... | collective-permute-start | bytes 221192 | tf_op jit(solution)/shard_map/ppermute | solution.py:41
  18.8 11.7 %collective-permute-start.13 = (bf16[3,96,640]{2,1,0:T(8,128)(2,1)S(1)}, bf16[3,96,640]{2,1,0:T(8,128)(2,1)S(1)}, u32[]{:S(2)}, u32[]{:S(2)}) collective-permute-start(bf16[3,96,640]{2,1,0:T(8,128)(2,1)S(1)} %get-tuple-element.59), channel_id=1, source_target_pairs={{0,4},{1,5},{2,6},{3,7},{4,0},{5,1},{6,2},{7,3},{8,12},{9,13},{10,... | collective-permute-start | bytes 1105928 | tf_op jit(solution)/shard_map/ppermute | solution.py:513
  20.2 10.8 %collective-permute-start.14 = (bf16[3,96,640]{2,1,0:T(8,128)(2,1)S(1)}, bf16[3,96,640]{2,1,0:T(8,128)(2,1)S(1)}, u32[]{:S(2)}, u32[]{:S(2)}) collective-permute-start(bf16[3,96,640]{2,1,0:T(8,128)(2,1)S(1)} %get-tuple-element.60), channel_id=1, source_target_pairs={{0,1},{1,0},{2,3},{3,2},{4,8},{5,9},{6,10},{7,11},{8,4},{9,5},{10,... | collective-permute-start | bytes 1105928 | tf_op jit(solution)/shard_map/ppermute | solution.py:513
  20.9 3.4 %collective-permute-start.3 = (bf16[64,384]{1,0:T(8,128)(2,1)S(1)}, bf16[64,384]{1,0:T(8,128)(2,1)S(1)}, u32[]{:S(2)}, u32[]{:S(2)}) collective-permute-start(bf16[64,384]{1,0:T(8,128)(2,1)S(1)} %get-tuple-element.39), channel_id=1, source_target_pairs={{0,2},{1,3},{2,0},{3,1},{4,6},{5,7},{6,4},{7,5},{8,10},{9,11},{10,... | collective-permute-start | bytes 147464 | tf_op jit(solution)/shard_map/ppermute | solution.py:41
  21.9 3.9 %collective-permute-start.4 = (bf16[64,384]{1,0:T(8,128)(2,1)S(1)}, bf16[64,384]{1,0:T(8,128)(2,1)S(1)}, u32[]{:S(2)}, u32[]{:S(2)}) collective-permute-start(bf16[64,384]{1,0:T(8,128)(2,1)S(1)} %get-tuple-element.40), channel_id=1, source_target_pairs={{0,3},{1,2},{2,1},{3,0},{4,7},{5,6},{6,5},{7,4},{8,11},{9,10},{10,... | collective-permute-start | bytes 147464 | tf_op jit(solution)/shard_map/ppermute | solution.py:41
  26.5 8.4 %collective-permute-start.8 = (bf16[3,64,640]{2,1,0:T(8,128)(2,1)S(1)}, bf16[3,64,640]{2,1,0:T(8,128)(2,1)S(1)}, u32[]{:S(2)}, u32[]{:S(2)}) collective-permute-start(bf16[3,64,640]{2,1,0:T(8,128)(2,1)S(1)} %get-tuple-element.52), channel_id=1, source_target_pairs={{0,4},{1,5},{2,6},{3,7},{4,0},{5,1},{6,2},{7,3},{8,12},{9,13},{10,... | collective-permute-start | bytes 737288 | tf_op jit(solution)/shard_map/ppermute | solution.py:513
  29.1 5.8 %collective-permute-start.9 = (bf16[3,64,640]{2,1,0:T(8,128)(2,1)S(1)}, bf16[3,64,640]{2,1,0:T(8,128)(2,1)S(1)}, u32[]{:S(2)}, u32[]{:S(2)}) collective-permute-start(bf16[3,64,640]{2,1,0:T(8,128)(2,1)S(1)} %get-tuple-element.53), channel_id=1, source_target_pairs={{0,1},{1,0},{2,3},{3,2},{4,8},{5,9},{6,10},{7,11},{8,4},{9,5},{10,... | collective-permute-start | bytes 737288 | tf_op jit(solution)/shard_map/ppermute | solution.py:513
  32.3 6.5 %collective-permute-start.15 = (bf16[180,384]{1,0:T(8,128)(2,1)S(1)}, bf16[180,384]{1,0:T(8,128)(2,1)S(1)}, u32[]{:S(2)}, u32[]{:S(2)}) collective-permute-start(bf16[180,384]{1,0:T(8,128)(2,1)S(1)} %get-tuple-element.61), channel_id=1, source_target_pairs={{0,2},{1,3},{2,0},{3,1},{4,6},{5,7},{6,4},{7,5},{8,10},{9,11},{10,... | collective-permute-start | bytes 414728 | tf_op jit(solution)/shard_map/ppermute | solution.py:41
  33.0 8.2 %collective-permute-start.16 = (bf16[180,384]{1,0:T(8,128)(2,1)S(1)}, bf16[180,384]{1,0:T(8,128)(2,1)S(1)}, u32[]{:S(2)}, u32[]{:S(2)}) collective-permute-start(bf16[180,384]{1,0:T(8,128)(2,1)S(1)} %get-tuple-element.62), channel_id=1, source_target_pairs={{0,3},{1,2},{2,1},{3,0},{4,7},{5,6},{6,5},{7,4},{8,11},{9,10},{10,... | collective-permute-start | bytes 414728 | tf_op jit(solution)/shard_map/ppermute | solution.py:41
  34.0 7.2 %collective-permute-start.17 = (bf16[180,384]{1,0:T(8,128)(2,1)S(1)}, bf16[180,384]{1,0:T(8,128)(2,1)S(1)}, u32[]{:S(2)}, u32[]{:S(2)}) collective-permute-start(bf16[180,384]{1,0:T(8,128)(2,1)S(1)} %get-tuple-element.64), channel_id=1, source_target_pairs={{0,1},{1,0},{2,3},{3,2},{4,5},{5,4},{6,7},{7,6},{8,9},{9,8},{10,11... | collective-permute-start | bytes 414728 | tf_op jit(solution)/shard_map/ppermute | solution.py:41
  36.0 6.8 %collective-permute-start.10 = (bf16[180,256]{1,0:T(8,128)(2,1)S(1)}, bf16[180,256]{1,0:T(8,128)(2,1)S(1)}, u32[]{:S(2)}, u32[]{:S(2)}) collective-permute-start(bf16[180,256]{1,0:T(8,128)(2,1)S(1)} %get-tuple-element.55), channel_id=1, source_target_pairs={{0,2},{1,3},{2,0},{3,1},{4,6},{5,7},{6,4},{7,5},{8,10},{9,11},{10,... | collective-permute-start | bytes 276488 | tf_op jit(solution)/shard_map/ppermute | solution.py:41
  37.8 7.1 %collective-permute-start.11 = (bf16[180,256]{1,0:T(8,128)(2,1)S(1)}, bf16[180,256]{1,0:T(8,128)(2,1)S(1)}, u32[]{:S(2)}, u32[]{:S(2)}) collective-permute-start(bf16[180,256]{1,0:T(8,128)(2,1)S(1)} %get-tuple-element.56), channel_id=1, source_target_pairs={{0,3},{1,2},{2,1},{3,0},{4,7},{5,6},{6,5},{7,4},{8,11},{9,10},{10,... | collective-permute-start | bytes 276488 | tf_op jit(solution)/shard_map/ppermute | solution.py:41
  38.8 6.1 %collective-permute-start.12 = (bf16[180,256]{1,0:T(8,128)(2,1)S(1)}, bf16[180,256]{1,0:T(8,128)(2,1)S(1)}, u32[]{:S(2)}, u32[]{:S(2)}) collective-permute-start(bf16[180,256]{1,0:T(8,128)(2,1)S(1)} %get-tuple-element.58), channel_id=1, source_target_pairs={{0,1},{1,0},{2,3},{3,2},{4,5},{5,4},{6,7},{7,6},{8,9},{9,8},{10,11... | collective-permute-start | bytes 276488 | tf_op jit(solution)/shard_map/ppermute | solution.py:41

commit v3 on v2

--- a/solution.py
+++ b/solution.py
@@ -15,7 +15,6 @@
 HALF = 64
 TERMS = 3
 NEAR = 1
-TOKEN = -1
 VMEM = pltpu.MemorySpace.VMEM
 NO_COST = pl.CostEstimate(flops=0, bytes_accessed=0, transcendentals=0)
 
@@ -182,60 +181,87 @@
     )(conv_out, grad_out, w_in, b_in, w_out, *after)
 
 
-def analysis_kernel(count, rows, chunk, *refs):
-    own_ref, first_ref, second_ref = refs[-3:]
-    start, size = chunk
-    halves = next(h for h in range(1, rows + 1) if refs[h * count].ndim == 3)
-    table_ref = refs[halves * count]
-    ranks = far_first(halves * count, count)
-    pieces = [refs[ranks.index(i)] for i in range(halves * count)]
-    rows_each = rows // halves
-    wide = refs[0].shape[1] // rows_each
+def spectra_of(pieces, channels, table_ref, wide):
+    size = channels[1]
+    rows = pieces[0][0].shape[1] // wide
     window = table_ref.shape[1] - HALF
-    even = lax.rem(lax.axis_index("polar"), 2) == 0
-
-    def columns(row, k):
-        half, row = divmod(row, rows_each)
-        piece = pieces[half * count + k]
-        base = 0 if half == halves - 1 and k > NEAR else start
-        first = row * wide // LANES * LANES
-        return piece[base : base + size, first : first + window]
-
-    shifts = [row % rows_each * wide % LANES for row in range(rows)]
+    shifts = [row * wide % LANES for row in range(rows)]
+    spectra = [None] * rows
     for shift in sorted(set(shifts)):
         group = [row for row in range(rows) if shifts[row] == shift]
         total = None
-        for k in range(count):
-            left = jnp.concatenate([columns(row, k) for row in group], axis=0)
+        for k, (piece, base) in enumerate(pieces):
+            windows = [row * wide // LANES * LANES for row in group]
+            left = jnp.concatenate([piece[base : base + size, at : at + window] for at in windows], axis=0)
             term = dot_nn(left, table_ref[k, HALF - shift : HALF - shift + window, :])
             total = term if total is None else total + term
         for at, row in enumerate(group):
-            mine = total[at * size : (at + 1) * size]
-            own_ref[row] = mine
+            spectra[row] = total[at * size : (at + 1) * size]
+    return spectra
+
+
+def early_kernel(count, wide, *refs):
+    ranks = far_first(count, count)
+    pieces = [(refs[ranks.index(k)], 0) for k in range(count)]
+    table_ref, out_ref = refs[count], refs[-1]
+    for row, spectrum in enumerate(spectra_of(pieces, (0, pieces[0][0].shape[0]), table_ref, wide)):
+        out_ref[row] = spectrum
+
+
+def analyze_early(pieces, table, wide):
+    count = len(pieces)
+    size, across = pieces[0].shape
+    return pl.pallas_call(
+        functools.partial(early_kernel, count, wide),
+        in_specs=[pl.BlockSpec(memory_space=VMEM)] * (count + 1),
+        out_specs=pl.BlockSpec(memory_space=VMEM),
+        out_shape=jax.ShapeDtypeStruct((across // wide, size, table.shape[2]), jnp.float32),
+        compiler_params=pltpu.CompilerParams(vmem_limit_bytes=12 * 2**20),
+        cost_estimate=NO_COST,
+        name="analysis_early",
+    )(*(pieces[k] for k in far_first(count, count)), table)
+
+
+def analysis_kernel(count, rows, wide, chunk, halves, *refs):
+    own_ref, first_ref, second_ref = refs[-3:]
+    start, size = chunk
+    ranks = far_first(count, count)
+    pieces = [(refs[ranks.index(k)], 0 if k > NEAR else start) for k in range(count)]
+    table_ref, early = refs[count], refs[count + 1 : count + halves]
+    per = rows // halves
+    even = lax.rem(lax.axis_index("polar"), 2) == 0
+    for row, spectrum in enumerate(spectra_of(pieces, chunk, table_ref, wide)):
+        own_ref[row] = spectrum
+
+    def row_of(row):
+        half, row = divmod(row, per)
+        return own_ref[row] if half == halves - 1 else early[half][row, start : start + size, :]
 
     def share(above, below):
         for h in range(REACH):
-            above[h] = own_ref[rows - REACH + h].astype(jnp.bfloat16)
-            below[h] = own_ref[h].astype(jnp.bfloat16)
+            above[h] = row_of(rows - REACH + h).astype(jnp.bfloat16)
+            below[h] = row_of(h).astype(jnp.bfloat16)
 
     pl.when(even)(lambda: share(first_ref, second_ref))
     pl.when(jnp.logical_not(even))(lambda: share(second_ref, first_ref))
 
 
-def analyze(pieces, table, rows, chunk, count, after):
+def analyze(pieces, table, early, rows, wide, chunk, after):
+    count = len(pieces)
     size = chunk[1]
     width = table.shape[2]
+    halves = len(early) + 1
     halo = jax.ShapeDtypeStruct((REACH, size, width), jnp.bfloat16)
     return pl.pallas_call(
-        functools.partial(analysis_kernel, count, rows, chunk),
-        in_specs=[pl.BlockSpec(memory_space=VMEM)] * (len(pieces) + 1)
+        functools.partial(analysis_kernel, count, rows, wide, chunk, halves),
+        in_specs=[pl.BlockSpec(memory_space=VMEM)] * (count + halves)
         + [pl.BlockSpec(memory_space=pl.ANY)] * len(after),
         out_specs=[pl.BlockSpec(memory_space=VMEM)] * 3,
-        out_shape=[jax.ShapeDtypeStruct((rows, size, width), jnp.float32), halo, halo],
+        out_shape=[jax.ShapeDtypeStruct((rows // halves, size, width), jnp.float32), halo, halo],
         compiler_params=pltpu.CompilerParams(vmem_limit_bytes=12 * 2**20),
         cost_estimate=NO_COST,
         name="analysis",
-    )(*(pieces[i] for i in far_first(len(pieces), count)), table, *after)
+    )(*(pieces[k] for k in far_first(count, count)), table, *early, *after)
 
 
 def add_row(accs, spectrum, weight, target_row, filter_row, targets):
@@ -265,27 +291,32 @@
     return value[:, :whole], value[:, whole : 2 * whole], value[:, 2 * whole :]
 
 
-def own_kernel(own_ref, weight_ref, target_ref, filter_ref, out_ref):
-    rows, size, width = own_ref.shape
+def own_kernel(start, own_ref, weight_ref, target_ref, filter_ref, *rest):
+    early, out_ref = rest[:-1], rest[-1]
+    rows, size, width = out_ref.shape
+    per = own_ref.shape[0]
     accs = {t: split_tiles(jnp.zeros((size, width), jnp.float32)) for t in range(rows)}
     for row in range(rows):
         at = row + REACH
         targets = [t for t in range(rows) if abs(row - t) <= REACH]
-        add_row(accs, own_ref[row], weight_ref[...], target_ref[at : at + 1, :], filter_ref[at], targets)
+        half = row // per
+        spectrum = early[half][row % per, start : start + size, :] if half < len(early) else own_ref[row % per]
+        add_row(accs, spectrum, weight_ref[...], target_ref[at : at + 1, :], filter_ref[at], targets)
     for t in range(rows):
         out_ref[t] = jnp.concatenate(accs[t], axis=1)
 
 
-def own_terms(own, weight, target, filters):
-    return pl.pallas_call(
-        own_kernel,
-        in_specs=[pl.BlockSpec(memory_space=VMEM)] * 4,
+def own_terms(own, early, start, weight, target, filters):
+    per, size, width = own.shape
+    return pl.pallas_call(
+        functools.partial(own_kernel, start),
+        in_specs=[pl.BlockSpec(memory_space=VMEM)] * (4 + len(early)),
         out_specs=pl.BlockSpec(memory_space=VMEM),
-        out_shape=jax.ShapeDtypeStruct(own.shape, jnp.float32),
+        out_shape=jax.ShapeDtypeStruct((per * (1 + len(early)), size, width), jnp.float32),
         compiler_params=pltpu.CompilerParams(vmem_limit_bytes=12 * 2**20),
         cost_estimate=NO_COST,
         name="own_terms",
-    )(own, weight, target, filters)
+    )(own, weight, target, filters, *early)
 
 
 def add_halo(accs, sides, rows, weight_ref, target_ref, filter_ref):
@@ -330,9 +361,9 @@
     )(own, first, weight, target, filters, *after)
 
 
-def finish_kernel(count, swaps, steps, part_ref, *refs):
+def finish_kernel(count, swaps, part_ref, *refs):
     halos, (weight_ref, target_ref, filter_ref, table_ref) = refs[:swaps], refs[swaps : swaps + 4]
-    outs, stacked_ref = refs[-len(steps) - 1 : -1], refs[-1]
+    outs, stacked_ref = refs[-count - 1 : -1], refs[-1]
     rows, size, width = part_ref.shape
     even = lax.rem(lax.axis_index("polar"), 2) == 0
 
@@ -347,30 +378,22 @@
     pl.when(jnp.logical_not(even))(lambda: combine((-REACH, rows)))
     grid = dot_nt(table_ref[...], stacked_ref[...])
     wide = grid.shape[0] // count
-    for k, out in zip(steps, outs):
+    for k, out in enumerate(outs):
         out[...] = grid[k * wide : k * wide + out.shape[0]].astype(jnp.bfloat16)
 
 
-def finish(own, halos, weight, target, filters, table, count, part, cut, after):
+def finish(own, halos, weight, target, filters, table, count, part):
     rows, size, width = own.shape
-    wide = table.shape[0] // count
-    ends = {k: wide if cut and k == NEAR else part for k in range(count)}
-    if cut:
-        ends[TOKEN] = cut
-    steps = [NEAR if k == TOKEN else k for k in ends]
-    blocks = pl.pallas_call(
-        functools.partial(finish_kernel, count, len(halos), steps),
-        in_specs=[pl.BlockSpec(memory_space=VMEM)] * (5 + len(halos)) + [pl.BlockSpec(memory_space=pl.ANY)] * len(after),
-        out_specs=[pl.BlockSpec(memory_space=VMEM)] * len(ends),
-        out_shape=[
-            jax.ShapeDtypeStruct((end, rows * size), jnp.bfloat16) for end in ends.values()
-        ],
+    return pl.pallas_call(
+        functools.partial(finish_kernel, count, len(halos)),
+        in_specs=[pl.BlockSpec(memory_space=VMEM)] * (5 + len(halos)),
+        out_specs=[pl.BlockSpec(memory_space=VMEM)] * count,
+        out_shape=[jax.ShapeDtypeStruct((part, rows * size), jnp.bfloat16)] * count,
         scratch_shapes=[pltpu.VMEM((rows * size, width), jnp.bfloat16)],
         compiler_params=pltpu.CompilerParams(vmem_limit_bytes=12 * 2**20),
         cost_estimate=NO_COST,
         name="finish",
-    )(own, *halos, weight, target, filters, table, *after)
-    return dict(zip(ends, blocks))
+    )(own, *halos, weight, target, filters, table)
 
 
 def add_kernel(count, chunk, steps, grad_ref, *refs):
@@ -521,47 +544,37 @@
     forth, back = jnp.asarray(forth), jnp.asarray(back)
     owned = channels // count
     halves = 2 if rows % 2 == 0 else 1
-    pieces = []
+    wide = round_up(part, HALF)
+    far = range(NEAR + 1, count)
+    filters, target, forth, back, *weights = prepare(
+        basis_weight, filt, offsets, forth, back, rows, count, chunks
+    )
+    early, order = [], []
     for half in range(halves):
         final = half == halves - 1
-        far = range(NEAR + 1, count)
         sent = [(k, 0, owned) for k in range(count)]
         if final:
             sent[NEAR + 1 :] = [(k,) + chunk for chunk in chunks for k in far]
-        blocks = mlp(conv_out, grad_out, w_in, b_in, w_out, count, half, halves, sent, chunks, pieces[1:2])
-        steps = [] if final else list(far)
-        moved = {k: exchange(blocks[k], k, count) for k in steps + list(range(NEAR + 1))}
-        pieces += [moved[k] for k in sorted(moved)]
-    filters, target, forth, back, *weights = prepare(
-        basis_weight, filt, offsets, forth, back, rows, count, chunks
-    )
-    spectra, terms, grids, returned = {}, {}, {}, {}
-
-    def open_chunk(q, after):
+        blocks = mlp(conv_out, grad_out, w_in, b_in, w_out, count, half, halves, sent, chunks, order)
+        order = blocks[:1]
+        if not final:
+            early.append(analyze_early([exchange(blocks[k], k, count) for k in range(count)], forth, wide))
+    whole = [exchange(blocks[k], k, count) for k in range(NEAR + 1)]
+    spectra, terms, returned = {}, {}, {}
+    for q, (start, size) in enumerate(chunks):
         tail = [exchange(blocks[NEAR + 1 + q * len(far) + i], k, count) for i, k in enumerate(far)]
-        own, first, second = analyze(pieces + tail, forth, rows, chunks[q], count, after)
+        after = [terms[q - 1]] if q else []
+        own, first, second = analyze(whole + tail, forth, early, rows, wide, (start, size), after)
         spectra[q] = halo(first, second)
-        terms[q] = own_terms(own, weights[q], target, filters)
-
-    def close_chunk(q):
-        after = []
-        cut = 0
+        terms[q] = own_terms(own, early, start, weights[q], target, filters)
+    for q in range(len(chunks)):
         halos = spectra[q]
         if q == 0:
             others = [terms[other] for other in terms if other > q]
             terms[q] = side_terms(terms[q], halos[0], weights[q], target, filters, others)
             halos = halos[1:]
-        grids[q] = finish(terms[q], halos, weights[q], target, filters, back, count, part, cut, after)
-        returned[q] = {k: exchange(block, NEAR if k == TOKEN else k, count) for k, block in grids[q].items()}
-
-    last = len(chunks) - 1
-    open_chunk(0, [])
-    if last > 0:
-        open_chunk(1, [terms[0]])
-    for q in range(last + 1):
-        close_chunk(q)
-        if q + 2 <= last:
-            open_chunk(q + 2, [grids[q][0]])
+        grids = finish(terms[q], halos, weights[q], target, filters, back, count, part)
+        returned[q] = {k: exchange(grids[k], k, count) for k in range(count)}
     total = []
     for q, chunk in enumerate(chunks):
         total = [add_chunk(grad_out, returned[q], chunk, count, total)]

time: 46.5 us -> 46.1 us (level)
  waiting for transfers between devices: 11.4 us -> 9.22 us
  starting transfers between devices: 17 us -> 18.3 us
  Pallas kernels: 14.6 us -> 15.1 us
    ppermute x14, waiting for transfers between devices: 10.7 us -> 8.52 us  [exchange(): return lax.ppermute(block, 'azimuth', pairs)]
    ppermute x14, starting transfers between devices: 11.5 us -> 12.5 us  [exchange(): return lax.ppermute(block, 'azimuth', pairs)]
    pallas_call x6 -> x7, Pallas kernels: 5.42 us -> 5.9 us  [the longest x2 2.36 us: finish(): pl.pallas_call(functools.partial(finish_kernel, count, len(halos)), in_sp...]
  transfers between devices with their start and end apart: 18 -> 18, of which waited for: 9 -> 7; matrix products, arithmetic and copies ran while one was open for 0% -> 0% of each run, Pallas kernels for 22% -> 23%
where the time goes in v3:
time: 46.1 us; the launch traced here: 45.7 us
  starting transfers between devices  18.3 us (40%)
  Pallas kernels  15.1 us (33%)
  waiting for transfers between devices  9.22 us (20%)
  local copies, waits for them, and re-layouts  2.77 us (6%)
    ppermute x14, starting transfers between devices, exchange(): return lax.ppermute(block, 'azimuth', pairs)  12.5 us
    ppermute x14, waiting for transfers between devices, exchange(): return lax.ppermute(block, 'azimuth', pairs)  8.52 us
    ppermute x4, starting transfers between devices, halo(): blocks.append(lax.ppermute(block, ('polar', 'azimuth'), pairs))  5.74 us
    pallas_call x2, Pallas kernels, mlp(): pl.pallas_call(functools.partial(mlp_kernel, count, half, sent, chunks),...  5.5 us
    unnamed x18, local copies, waits for them, and re-layouts  2.77 us
    pallas_call x2, Pallas kernels, add_chunk(): pl.pallas_call(functools.partial(add_kernel, count, chunk, [k for k, _ in...  2.47 us
    pallas_call x2, Pallas kernels, finish(): pl.pallas_call(functools.partial(finish_kernel, count, len(halos)), in_sp...  2.36 us
    pallas_call x2, Pallas kernels, own_terms(): pl.pallas_call(functools.partial(own_kernel, start), in_specs=[pl.BlockSp...  1.64 us
  transfers between devices with their start and end apart: 18, of which 7 were waited for; matrix products, arithmetic and copies ran while one was open for 0% of the time, Pallas kernels for 23%

profile of v3, /device:TPU:1, one launch (start us, length us, event | category | flops | bytes accessed | tf_op | source)
XLA Modules:
  0.0 45.7 jit_solution(18429976983289075533)
XLA Ops:
  0.0 0.0 copy-start.1
  0.0 0.0 copy-start.6
  0.0 1.4 %copy.17.grad_ref = bf16[4,180,640]{2,1,0:T(8,128)(2,1)S(1)} copy(bf16[4,180,640]{2,0,1:T(4,128)(2,1)} %param.11) | data formatting | bytes 1843200 | tf_op args[1]
  1.5 1.3 %copy.14.conv_ref = bf16[4,180,640]{2,1,0:T(8,128)(2,1)S(1)} copy(bf16[4,180,640]{2,0,1:T(4,128)(2,1)} %param.10) | data formatting | bytes 1843200 | tf_op args[0]
  2.8 0.0 copy-done.1
  2.8 0.0 copy-done.6
  2.8 0.0 copy-done
  2.8 2.8 %mlp.2 = (bf16[160,384]{1,0:T(8,128)(2,1)S(1)}, bf16[160,384]{1,0:T(8,128)(2,1)S(1)}, bf16[160,384]{1,0:T(8,128)(2,1)S(1)}, bf16[160,384]{1,0:T(8,128)(2,1)S(1)}) custom-call(bf16[4,180,640]{2,1,0:T(8,128)(2,1)S(1)} %copy.14.conv_ref, bf16[4,180,640]{2,1,0:T(8,128)(2,1)S(1)} %copy.17.grad_ref, bf16[640,1280]{1,0:T(8,128)(2,1)S(1)} %copy-done, ...), custom_call_target="tpu_custom_call" | custom-call | tf_op jit(solution)/shard_map/mlp/pallas_call | solution.py:165
  5.5 2.1 %collective-permute-start.3 = (bf16[160,384]{1,0:T(8,128)(2,1)S(1)}, bf16[160,384]{1,0:T(8,128)(2,1)S(1)}, u32[]{:S(2)}, u32[]{:S(2)}) collective-permute-start(bf16[160,384]{1,0:T(8,128)(2,1)S(1)} %get-tuple-element.41), channel_id=1, source_target_pairs={{0,2},{1,3},{2,0},{3,1},{4,6},{5,7},{6,4},{7,5},{8,10},{9,11},{10,... | collective-permute-start | bytes 368648 | tf_op jit(solution)/shard_map/ppermute | solution.py:40
  7.7 0.6 %collective-permute-start.4 = (bf16[160,384]{1,0:T(8,128)(2,1)S(1)}, bf16[160,384]{1,0:T(8,128)(2,1)S(1)}, u32[]{:S(2)}, u32[]{:S(2)}) collective-permute-start(bf16[160,384]{1,0:T(8,128)(2,1)S(1)} %get-tuple-element.42), channel_id=1, source_target_pairs={{0,3},{1,2},{2,1},{3,0},{4,7},{5,6},{6,5},{7,4},{8,11},{9,10},{10,... | collective-permute-start | bytes 368648 | tf_op jit(solution)/shard_map/ppermute | solution.py:40
  8.3 0.3 collective-permute-start.5
  8.6 0.0 copy-start.2
  8.6 0.0 copy-start.3
  8.6 0.0 copy-start.7
  8.6 2.7 %mlp.3 = (bf16[160,384]{1,0:T(8,128)(2,1)S(1)}, bf16[160,384]{1,0:T(8,128)(2,1)S(1)}, bf16[96,384]{1,0:T(8,128)(2,1)S(1)}, bf16[96,384]{1,0:T(8,128)(2,1)S(1)}, ...) custom-call(bf16[4,180,640]{2,1,0:T(8,128)(2,1)S(1)} %copy.14.conv_ref, bf16[4,180,640]{2,1,0:T(8,128)(2,1)S(1)} %copy.17.grad_ref, ...), custom_call_target="tpu_custom_call" | custom-call | tf_op jit(solution)/shard_map/mlp/pallas_call | solution.py:165
  11.4 0.3 collective-permute-start.2
  11.6 1.7 %collective-permute-start.6 = (bf16[96,384]{1,0:T(8,128)(2,1)S(1)}, bf16[96,384]{1,0:T(8,128)(2,1)S(1)}, u32[]{:S(2)}, u32[]{:S(2)}) collective-permute-start(bf16[96,384]{1,0:T(8,128)(2,1)S(1)} %get-tuple-element.44), channel_id=1, source_target_pairs={{0,2},{1,3},{2,0},{3,1},{4,6},{5,7},{6,4},{7,5},{8,10},{9,11},{10,... | collective-permute-start | bytes 221192 | tf_op jit(solution)/shard_map/ppermute | solution.py:40
  13.3 0.0 collective-permute-done.3.refs_0_
  13.3 1.1 %collective-permute-start.7 = (bf16[96,384]{1,0:T(8,128)(2,1)S(1)}, bf16[96,384]{1,0:T(8,128)(2,1)S(1)}, u32[]{:S(2)}, u32[]{:S(2)}) collective-permute-start(bf16[96,384]{1,0:T(8,128)(2,1)S(1)} %get-tuple-element.45), channel_id=1, source_target_pairs={{0,3},{1,2},{2,1},{3,0},{4,7},{5,6},{6,5},{7,4},{8,11},{9,10},{10,... | collective-permute-start | bytes 221192 | tf_op jit(solution)/shard_map/ppermute | solution.py:40
  14.4 0.0 copy-done.2
  14.4 0.0 copy-done.3
  14.4 0.0 copy-done.4
  14.4 0.0 copy-done.5
  14.4 0.0 copy-done.7
  14.4 0.7 %prepare.1 = (bf16[10,32,768]{2,1,0:T(8,128)(2,1)S(1)}, s32[10,32]{1,0:T(8,128)S(1)}, bf16[4,320,640]{2,1,0:T(8,128)(2,1)S(1)}, bf16[768,640]{1,0:T(8,128)(2,1)S...) custom-call(f32[9,640]{1,0:T(8,128)S(1)} %copy-done.5, bf16[9,16,640]{2,1,0:T(8,128)(2,1)S(1)} %copy-done.4, ...), custom_call_target="tpu_custom_call" | custom-call | tf_op jit(solution)/shard_map/prepare/pallas_call | solution.py:514
  15.2 0.0 collective-permute-done.4.refs_1_
  15.2 0.0 collective-permute-done.5.refs_3_
  15.2 0.7 %analysis_early.1.refs_5_.rest_0_ = f32[2,160,640]{2,1,0:T(8,128)S(1)} custom-call(bf16[160,384]{1,0:T(8,128)(2,1)S(1)} %collective-permute-done.3.refs_0_, bf16[160,384]{1,0:T(8,128)(2,1)S(1)} %collective-permute-done.4.refs_1_, bf16[160,384]{1,0:T(8,128)(2,1)S(1)} %get-tuple-element.35.rest_0_.refs_2_, ...), custom_call_target="tpu_custom_call" | custom-call | tf_op jit(solution)/shard_map/analysis_early/pallas_call | solution.py:214
  15.9 0.0 collective-permute-done.6.refs_0_
  15.9 1.7 %collective-permute-done.7.refs_1_ = bf16[96,384]{1,0:T(8,128)(2,1)S(1)} collective-permute-done((bf16[96,384]{1,0:T(8,128)(2,1)S(1)}, bf16[96,384]{1,0:T(8,128)(2,1)S(1)}, u32[]{:S(2)}, u32[]{:S(2)}) %collective-permute-start.7) | collective-permute-done | bytes 73760 | tf_op jit(solution)/shard_map/ppermute | solution.py:40
  17.6 0.0 collective-permute-done.2.refs_3_
  17.6 0.6 %analysis.2 = (f32[2,96,640]{2,1,0:T(8,128)S(1)}, bf16[3,96,640]{2,1,0:T(8,128)(2,1)S(1)}, bf16[3,96,640]{2,1,0:T(8,128)(2,1)S(1)}) custom-call(bf16[96,384]{1,0:T(8,128)(2,1)S(1)} %collective-permute-done.6.refs_0_, bf16[96,384]{1,0:T(8,128)(2,1)S(1)} %collective-permute-done.7.refs_1_, bf16[160,384]{1,0:T(8,128)(2,1)S(1)} %get-tuple-element.38.refs_2_, ...), custom_call_target="tpu_custom_call" | custom-call | tf_op jit(solution)/shard_map/analysis/pallas_call | solution.py:255
  18.2 1.6 %collective-permute-start.13 = (bf16[3,96,640]{2,1,0:T(8,128)(2,1)S(1)}, bf16[3,96,640]{2,1,0:T(8,128)(2,1)S(1)}, u32[]{:S(2)}, u32[]{:S(2)}) collective-permute-start(bf16[3,96,640]{2,1,0:T(8,128)(2,1)S(1)} %get-tuple-element.59), channel_id=1, source_target_pairs={{0,4},{1,5},{2,6},{3,7},{4,0},{5,1},{6,2},{7,3},{8,12},{9,13},{10,... | collective-permute-start | bytes 1105928 | tf_op jit(solution)/shard_map/ppermute | solution.py:536
  19.8 0.7 %collective-permute-start.14 = (bf16[3,96,640]{2,1,0:T(8,128)(2,1)S(1)}, bf16[3,96,640]{2,1,0:T(8,128)(2,1)S(1)}, u32[]{:S(2)}, u32[]{:S(2)}) collective-permute-start(bf16[3,96,640]{2,1,0:T(8,128)(2,1)S(1)} %get-tuple-element.60), channel_id=1, source_target_pairs={{0,1},{1,0},{2,3},{3,2},{4,8},{5,9},{6,10},{7,11},{8,4},{9,5},{10,... | collective-permute-start | bytes 1105928 | tf_op jit(solution)/shard_map/ppermute | solution.py:536
  20.5 1.0 %collective-permute-start = (bf16[64,384]{1,0:T(8,128)(2,1)S(1)}, bf16[64,384]{1,0:T(8,128)(2,1)S(1)}, u32[]{:S(2)}, u32[]{:S(2)}) collective-permute-start(bf16[64,384]{1,0:T(8,128)(2,1)S(1)} %get-tuple-element.36), channel_id=1, source_target_pairs={{0,2},{1,3},{2,0},{3,1},{4,6},{5,7},{6,4},{7,5},{8,10},{9,11},{10,... | collective-permute-start | bytes 147464 | tf_op jit(solution)/shard_map/ppermute | solution.py:40
  21.4 0.7 %collective-permute-start.1 = (bf16[64,384]{1,0:T(8,128)(2,1)S(1)}, bf16[64,384]{1,0:T(8,128)(2,1)S(1)}, u32[]{:S(2)}, u32[]{:S(2)}) collective-permute-start(bf16[64,384]{1,0:T(8,128)(2,1)S(1)} %get-tuple-element.37), channel_id=1, source_target_pairs={{0,3},{1,2},{2,1},{3,0},{4,7},{5,6},{6,5},{7,4},{8,11},{9,10},{10,... | collective-permute-start | bytes 147464 | tf_op jit(solution)/shard_map/ppermute | solution.py:40
  22.1 1.0 %own_terms.2.refs_6_.part_ref = f32[4,96,640]{2,1,0:T(8,128)S(1)} custom-call(f32[2,96,640]{2,1,0:T(8,128)S(1)} %get-tuple-element.46.own_ref, f32[96,32]{1,0:T(8,128)S(1)} %get-tuple-element.47.weight_ref.refs_1_, s32[10,32]{1,0:T(8,128)S(1)} %get-tuple-element.48.target_ref.refs_3_.refs_2_, ...), custom_call_target="tpu_custom_call" | custom-call | tf_op jit(solution)/shard_map/own_terms/pallas_call | solution.py:311
  23.1 0.7 %collective-permute-done.refs_0_ = bf16[64,384]{1,0:T(8,128)(2,1)S(1)} collective-permute-done((bf16[64,384]{1,0:T(8,128)(2,1)S(1)}, bf16[64,384]{1,0:T(8,128)(2,1)S(1)}, u32[]{:S(2)}, u32[]{:S(2)}) %collective-permute-start) | collective-permute-done | bytes 49184 | tf_op jit(solution)/shard_map/ppermute | solution.py:40
  23.9 1.5 %collective-permute-done.1.refs_1_ = bf16[64,384]{1,0:T(8,128)(2,1)S(1)} collective-permute-done((bf16[64,384]{1,0:T(8,128)(2,1)S(1)}, bf16[64,384]{1,0:T(8,128)(2,1)S(1)}, u32[]{:S(2)}, u32[]{:S(2)}) %collective-permute-start.1) | collective-permute-done | bytes 49184 | tf_op jit(solution)/shard_map/ppermute | solution.py:40
  25.4 0.6 %analysis.3 = (f32[2,64,640]{2,1,0:T(8,128)S(1)}, bf16[3,64,640]{2,1,0:T(8,128)(2,1)S(1)}, bf16[3,64,640]{2,1,0:T(8,128)(2,1)S(1)}) custom-call(bf16[64,384]{1,0:T(8,128)(2,1)S(1)} %collective-permute-done.refs_0_, bf16[64,384]{1,0:T(8,128)(2,1)S(1)} %collective-permute-done.1.refs_1_, bf16[160,384]{1,0:T(8,128)(2,1)S(1)} %get-tuple-element.38.refs_2_, ...), custom_call_target="tpu_custom_call" | custom-call | tf_op jit(solution)/shard_map/analysis/pallas_call | solution.py:255
  25.9 2.7 %collective-permute-start.8 = (bf16[3,64,640]{2,1,0:T(8,128)(2,1)S(1)}, bf16[3,64,640]{2,1,0:T(8,128)(2,1)S(1)}, u32[]{:S(2)}, u32[]{:S(2)}) collective-permute-start(bf16[3,64,640]{2,1,0:T(8,128)(2,1)S(1)} %get-tuple-element.52), channel_id=1, source_target_pairs={{0,4},{1,5},{2,6},{3,7},{4,0},{5,1},{6,2},{7,3},{8,12},{9,13},{10,... | collective-permute-start | bytes 737288 | tf_op jit(solution)/shard_map/ppermute | solution.py:536
  28.6 0.8 %collective-permute-start.9 = (bf16[3,64,640]{2,1,0:T(8,128)(2,1)S(1)}, bf16[3,64,640]{2,1,0:T(8,128)(2,1)S(1)}, u32[]{:S(2)}, u32[]{:S(2)}) collective-permute-start(bf16[3,64,640]{2,1,0:T(8,128)(2,1)S(1)} %get-tuple-element.53), channel_id=1, source_target_pairs={{0,1},{1,0},{2,3},{3,2},{4,8},{5,9},{6,10},{7,11},{8,4},{9,5},{10,... | collective-permute-start | bytes 737288 | tf_op jit(solution)/shard_map/ppermute | solution.py:536
  29.4 0.6 %own_terms.3.part_ref.rest_0_ = f32[4,64,640]{2,1,0:T(8,128)S(1)} custom-call(f32[2,64,640]{2,1,0:T(8,128)S(1)} %get-tuple-element.50.own_ref, f32[64,32]{1,0:T(8,128)S(1)} %get-tuple-element.51.weight_ref.refs_2_, s32[10,32]{1,0:T(8,128)S(1)} %get-tuple-element.48.target_ref.refs_3_.refs_2_, ...), custom_call_target="tpu_custom_call" | custom-call | tf_op jit(solution)/shard_map/own_terms/pallas_call | solution.py:311
  30.1 0.0 collective-permute-done.13.first_ref
  30.1 0.5 %side_terms.1.part_ref = f32[4,96,640]{2,1,0:T(8,128)S(1)} custom-call(f32[4,96,640]{2,1,0:T(8,128)S(1)} %own_terms.2.refs_6_.part_ref, bf16[3,96,640]{2,1,0:T(8,128)(2,1)S(1)} %collective-permute-done.13.first_ref, f32[96,32]{1,0:T(8,128)S(1)} %get-tuple-element.47.weight_ref.refs_1_, s32[10,32]{1,0:T(8,128)S(1)} %get-tuple-element.48.target_ref.refs_3_.refs_2_, ...), custom_call_target="tpu_custom_call" | custom-call | tf_op jit(solution)/shard_map/side_terms/pallas_call | solution.py:353
  30.6 0.0 collective-permute-done.14.refs_0_
  30.6 1.3 %finish.3 = (bf16[180,384]{1,0:T(8,128)(2,1)S(1)}, bf16[180,384]{1,0:T(8,128)(2,1)S(1)}, bf16[180,384]{1,0:T(8,128)(2,1)S(1)}, bf16[180,384]{1,0:T(8,128)(2,1)S(1)}) custom-call(f32[4,96,640]{2,1,0:T(8,128)S(1)} %side_terms.1.part_ref, bf16[3,96,640]{2,1,0:T(8,128)(2,1)S(1)} %collective-permute-done.14.refs_0_, ...), custom_call_target="tpu_custom_call" | custom-call | tf_op jit(solution)/shard_map/finish/pallas_call | solution.py:387
  31.9 0.7 %collective-permute-start.15 = (bf16[180,384]{1,0:T(8,128)(2,1)S(1)}, bf16[180,384]{1,0:T(8,128)(2,1)S(1)}, u32[]{:S(2)}, u32[]{:S(2)}) collective-permute-start(bf16[180,384]{1,0:T(8,128)(2,1)S(1)} %get-tuple-element.61), channel_id=1, source_target_pairs={{0,2},{1,3},{2,0},{3,1},{4,6},{5,7},{6,4},{7,5},{8,10},{9,11},{10,... | collective-permute-start | bytes 414728 | tf_op jit(solution)/shard_map/ppermute | solution.py:40
  32.6 1.0 %collective-permute-start.16 = (bf16[180,384]{1,0:T(8,128)(2,1)S(1)}, bf16[180,384]{1,0:T(8,128)(2,1)S(1)}, u32[]{:S(2)}, u32[]{:S(2)}) collective-permute-start(bf16[180,384]{1,0:T(8,128)(2,1)S(1)} %get-tuple-element.62), channel_id=1, source_target_pairs={{0,3},{1,2},{2,1},{3,0},{4,7},{5,6},{6,5},{7,4},{8,11},{9,10},{10,... | collective-permute-start | bytes 414728 | tf_op jit(solution)/shard_map/ppermute | solution.py:40
  33.6 0.2 collective-permute-start.17
  33.8 0.7 %collective-permute-done.8.refs_0_ = bf16[3,64,640]{2,1,0:T(8,128)(2,1)S(1)} collective-permute-done((bf16[3,64,640]{2,1,0:T(8,128)(2,1)S(1)}, bf16[3,64,640]{2,1,0:T(8,128)(2,1)S(1)}, u32[]{:S(2)}, u32[]{:S(2)}) %collective-permute-start.8) | collective-permute-done | bytes 245792 | tf_op jit(solution)/shard_map/ppermute | solution.py:536
  34.5 0.0 collective-permute-done.9.refs_1_
  34.5 1.1 %finish.2 = (bf16[180,256]{1,0:T(8,128)(2,1)S(1)}, bf16[180,256]{1,0:T(8,128)(2,1)S(1)}, bf16[180,256]{1,0:T(8,128)(2,1)S(1)}, bf16[180,256]{1,0:T(8,128)(2,1)S(1)}) custom-call(f32[4,64,640]{2,1,0:T(8,128)S(1)} %own_terms.3.part_ref.rest_0_, bf16[3,64,640]{2,1,0:T(8,128)(2,1)S(1)} %collective-permute-done.8.refs_0_, ...), custom_call_target="tpu_custom_call" | custom-call | tf_op jit(solution)/shard_map/finish/pallas_call | solution.py:387
  35.6 1.5 %collective-permute-start.10 = (bf16[180,256]{1,0:T(8,128)(2,1)S(1)}, bf16[180,256]{1,0:T(8,128)(2,1)S(1)}, u32[]{:S(2)}, u32[]{:S(2)}) collective-permute-start(bf16[180,256]{1,0:T(8,128)(2,1)S(1)} %get-tuple-element.55), channel_id=1, source_target_pairs={{0,2},{1,3},{2,0},{3,1},{4,6},{5,7},{6,4},{7,5},{8,10},{9,11},{10,... | collective-permute-start | bytes 276488 | tf_op jit(solution)/shard_map/ppermute | solution.py:40
  37.1 1.2 %collective-permute-start.11 = (bf16[180,256]{1,0:T(8,128)(2,1)S(1)}, bf16[180,256]{1,0:T(8,128)(2,1)S(1)}, u32[]{:S(2)}, u32[]{:S(2)}) collective-permute-start(bf16[180,256]{1,0:T(8,128)(2,1)S(1)} %get-tuple-element.56), channel_id=1, source_target_pairs={{0,3},{1,2},{2,1},{3,0},{4,7},{5,6},{6,5},{7,4},{8,11},{9,10},{10,... | collective-permute-start | bytes 276488 | tf_op jit(solution)/shard_map/ppermute | solution.py:40
  38.3 0.0 collective-permute-done.15.refs_0_
  38.4 0.1 collective-permute-start.12
  38.5 2.3 %collective-permute-done.16.refs_1_ = bf16[180,384]{1,0:T(8,128)(2,1)S(1)} collective-permute-done((bf16[180,384]{1,0:T(8,128)(2,1)S(1)}, bf16[180,384]{1,0:T(8,128)(2,1)S(1)}, u32[]{:S(2)}, u32[]{:S(2)}) %collective-permute-start.16) | collective-permute-done | bytes 138272 | tf_op jit(solution)/shard_map/ppermute | solution.py:40
  40.8 0.0 collective-permute-done.17.refs_3_
  40.8 1.4 %add_chunk.2.refs_4_ = bf16[180,4,640]{2,1,0:T(4,128)(2,1)} custom-call(bf16[4,180,640]{2,1,0:T(8,128)(2,1)S(1)} %copy.17.grad_ref, bf16[180,384]{1,0:T(8,128)(2,1)S(1)} %collective-permute-done.15.refs_0_, bf16[180,384]{1,0:T(8,128)(2,1)S(1)} %collective-permute-done.16.refs_1_, bf16[180,384]{1,0:T(8,128)(2,1)S(1)} %get-tuple-element.63.refs_2_, ...), custom_call_target="tpu_custom_call" | custom-call | tf_op jit(solution)/shard_map/add_chunk/pallas_call | solution.py:438
  42.2 0.1 collective-permute-done.10.refs_0_
  42.4 2.1 %collective-permute-done.11.refs_1_ = bf16[180,256]{1,0:T(8,128)(2,1)S(1)} collective-permute-done((bf16[180,256]{1,0:T(8,128)(2,1)S(1)}, bf16[180,256]{1,0:T(8,128)(2,1)S(1)}, u32[]{:S(2)}, u32[]{:S(2)}) %collective-permute-start.11) | collective-permute-done | bytes 92192 | tf_op jit(solution)/shard_map/ppermute | solution.py:40
  44.5 0.0 collective-permute-done.12.refs_3_
  44.5 1.1 %add_chunk.3 = bf16[180,4,640]{2,1,0:T(4,128)(2,1)} custom-call(bf16[4,180,640]{2,1,0:T(8,128)(2,1)S(1)} %copy.17.grad_ref, bf16[180,256]{1,0:T(8,128)(2,1)S(1)} %collective-permute-done.10.refs_0_, bf16[180,256]{1,0:T(8,128)(2,1)S(1)} %collective-permute-done.11.refs_1_, ...), custom_call_target="tpu_custom_call", output_to_operand_aliasing={{}: (5, {})} | custom-call | tf_op jit(solution)/shard_map/add_chunk/pallas_call | solution.py:438
  (3 shorter events, 0.0 us)
Async XLA Ops:
  0.0 2.8 %copy-start.1 = (bf16[1280,640]{1,0:T(8,128)(2,1)S(1)}, bf16[1280,640]{1,0:T(8,128)(2,1)}, u32[]{:S(2)}) copy-start(bf16[1280,640]{1,0:T(8,128)(2,1)} %wout_ref.3) | copy-start | bytes 4915204
  0.0 2.8 %copy-start.6 = (f32[1280]{0:T(1024)S(1)}, f32[1280]{0:T(1024)}, u32[]{:S(2)}) copy-start(f32[1280]{0:T(1024)} %bias_ref.3) | copy-start | bytes 15364
  0.0 2.8 %copy-start = (bf16[640,1280]{1,0:T(8,128)(2,1)S(1)}, bf16[640,1280]{1,0:T(8,128)(2,1)}, u32[]{:S(2)}) copy-start(bf16[640,1280]{1,0:T(8,128)(2,1)} %win_ref.3) | copy-start | bytes 4915204
  5.5 7.8 %collective-permute-start.3 = (bf16[160,384]{1,0:T(8,128)(2,1)S(1)}, bf16[160,384]{1,0:T(8,128)(2,1)S(1)}, u32[]{:S(2)}, u32[]{:S(2)}) collective-permute-start(bf16[160,384]{1,0:T(8,128)(2,1)S(1)} %get-tuple-element.41), channel_id=1, source_target_pairs={{0,2},{1,3},{2,0},{3,1},{4,6},{5,7},{6,4},{7,5},{8,10},{9,11},{10,... | collective-permute-start | bytes 368648 | tf_op jit(solution)/shard_map/ppermute | solution.py:40
  7.7 7.5 %collective-permute-start.4 = (bf16[160,384]{1,0:T(8,128)(2,1)S(1)}, bf16[160,384]{1,0:T(8,128)(2,1)S(1)}, u32[]{:S(2)}, u32[]{:S(2)}) collective-permute-start(bf16[160,384]{1,0:T(8,128)(2,1)S(1)} %get-tuple-element.42), channel_id=1, source_target_pairs={{0,3},{1,2},{2,1},{3,0},{4,7},{5,6},{6,5},{7,4},{8,11},{9,10},{10,... | collective-permute-start | bytes 368648 | tf_op jit(solution)/shard_map/ppermute | solution.py:40
  8.3 6.9 %collective-permute-start.5 = (bf16[160,384]{1,0:T(8,128)(2,1)S(1)}, bf16[160,384]{1,0:T(8,128)(2,1)S(1)}, u32[]{:S(2)}, u32[]{:S(2)}) collective-permute-start(bf16[160,384]{1,0:T(8,128)(2,1)S(1)} %get-tuple-element.43), channel_id=1, source_target_pairs={{0,1},{1,0},{2,3},{3,2},{4,5},{5,4},{6,7},{7,6},{8,9},{9,8},{10,11... | collective-permute-start | bytes 368648 | tf_op jit(solution)/shard_map/ppermute | solution.py:40
  8.6 5.8 %copy-start.2 = (bf16[4,320,640]{2,1,0:T(8,128)(2,1)S(1)}, bf16[4,320,640]{2,1,0:T(8,128)(2,1)}, u32[]{:S(2)}) copy-start(bf16[4,320,640]{2,1,0:T(8,128)(2,1)} %constant.4.clone.forth_ref) | copy-start | bytes 4915204
  8.6 5.8 %copy-start.3 = (bf16[768,640]{1,0:T(8,128)(2,1)S(1)}, bf16[768,640]{1,0:T(8,128)(2,1)}, u32[]{:S(2)}) copy-start(bf16[768,640]{1,0:T(8,128)(2,1)} %constant.5.clone.back_ref) | copy-start | bytes 2949124
  8.6 5.8 %copy-start.4 = (bf16[9,16,640]{2,1,0:T(8,128)(2,1)S(1)}, bf16[9,16,640]{2,1,0:T(8,128)(2,1)}, u32[]{:S(2)}) copy-start(bf16[9,16,640]{2,1,0:T(8,128)(2,1)} %filt_ref.1) | copy-start | bytes 552964
  8.6 5.8 %copy-start.5 = (f32[9,640]{1,0:T(8,128)S(1)}, f32[9,640]{1,0:T(8,128)}, u32[]{:S(2)}) copy-start(f32[9,640]{1,0:T(8,128)} %weight_ref.1) | copy-start | bytes 69124
  8.6 5.8 %copy-start.7 = (s32[16,9]{1,0:T(8,128)S(1)}, s32[16,9]{1,0:T(8,128)}, u32[]{:S(2)}) copy-start(s32[16,9]{1,0:T(8,128)} %offset_ref.1) | copy-start | bytes 1732
  11.4 6.2 %collective-permute-start.2 = (bf16[160,384]{1,0:T(8,128)(2,1)S(1)}, bf16[160,384]{1,0:T(8,128)(2,1)S(1)}, u32[]{:S(2)}, u32[]{:S(2)}) collective-permute-start(bf16[160,384]{1,0:T(8,128)(2,1)S(1)} %get-tuple-element.39), channel_id=1, source_target_pairs={{0,1},{1,0},{2,3},{3,2},{4,5},{5,4},{6,7},{7,6},{8,9},{9,8},{10,11... | collective-permute-start | bytes 368648 | tf_op jit(solution)/shard_map/ppermute | solution.py:40
  11.6 4.2 %collective-permute-start.6 = (bf16[96,384]{1,0:T(8,128)(2,1)S(1)}, bf16[96,384]{1,0:T(8,128)(2,1)S(1)}, u32[]{:S(2)}, u32[]{:S(2)}) collective-permute-start(bf16[96,384]{1,0:T(8,128)(2,1)S(1)} %get-tuple-element.44), channel_id=1, source_target_pairs={{0,2},{1,3},{2,0},{3,1},{4,6},{5,7},{6,4},{7,5},{8,10},{9,11},{10,... | collective-permute-start | bytes 221192 | tf_op jit(solution)/shard_map/ppermute | solution.py:40
  13.3 4.2 %collective-permute-start.7 = (bf16[96,384]{1,0:T(8,128)(2,1)S(1)}, bf16[96,384]{1,0:T(8,128)(2,1)S(1)}, u32[]{:S(2)}, u32[]{:S(2)}) collective-permute-start(bf16[96,384]{1,0:T(8,128)(2,1)S(1)} %get-tuple-element.45), channel_id=1, source_target_pairs={{0,3},{1,2},{2,1},{3,0},{4,7},{5,6},{6,5},{7,4},{8,11},{9,10},{10,... | collective-permute-start | bytes 221192 | tf_op jit(solution)/shard_map/ppermute | solution.py:40
  18.2 11.9 %collective-permute-start.13 = (bf16[3,96,640]{2,1,0:T(8,128)(2,1)S(1)}, bf16[3,96,640]{2,1,0:T(8,128)(2,1)S(1)}, u32[]{:S(2)}, u32[]{:S(2)}) collective-permute-start(bf16[3,96,640]{2,1,0:T(8,128)(2,1)S(1)} %get-tuple-element.59), channel_id=1, source_target_pairs={{0,4},{1,5},{2,6},{3,7},{4,0},{5,1},{6,2},{7,3},{8,12},{9,13},{10,... | collective-permute-start | bytes 1105928 | tf_op jit(solution)/shard_map/ppermute | solution.py:536
  19.8 10.8 %collective-permute-start.14 = (bf16[3,96,640]{2,1,0:T(8,128)(2,1)S(1)}, bf16[3,96,640]{2,1,0:T(8,128)(2,1)S(1)}, u32[]{:S(2)}, u32[]{:S(2)}) collective-permute-start(bf16[3,96,640]{2,1,0:T(8,128)(2,1)S(1)} %get-tuple-element.60), channel_id=1, source_target_pairs={{0,1},{1,0},{2,3},{3,2},{4,8},{5,9},{6,10},{7,11},{8,4},{9,5},{10,... | collective-permute-start | bytes 1105928 | tf_op jit(solution)/shard_map/ppermute | solution.py:536
  20.5 3.4 %collective-permute-start = (bf16[64,384]{1,0:T(8,128)(2,1)S(1)}, bf16[64,384]{1,0:T(8,128)(2,1)S(1)}, u32[]{:S(2)}, u32[]{:S(2)}) collective-permute-start(bf16[64,384]{1,0:T(8,128)(2,1)S(1)} %get-tuple-element.36), channel_id=1, source_target_pairs={{0,2},{1,3},{2,0},{3,1},{4,6},{5,7},{6,4},{7,5},{8,10},{9,11},{10,... | collective-permute-start | bytes 147464 | tf_op jit(solution)/shard_map/ppermute | solution.py:40
  21.4 3.9 %collective-permute-start.1 = (bf16[64,384]{1,0:T(8,128)(2,1)S(1)}, bf16[64,384]{1,0:T(8,128)(2,1)S(1)}, u32[]{:S(2)}, u32[]{:S(2)}) collective-permute-start(bf16[64,384]{1,0:T(8,128)(2,1)S(1)} %get-tuple-element.37), channel_id=1, source_target_pairs={{0,3},{1,2},{2,1},{3,0},{4,7},{5,6},{6,5},{7,4},{8,11},{9,10},{10,... | collective-permute-start | bytes 147464 | tf_op jit(solution)/shard_map/ppermute | solution.py:40
  25.9 8.6 %collective-permute-start.8 = (bf16[3,64,640]{2,1,0:T(8,128)(2,1)S(1)}, bf16[3,64,640]{2,1,0:T(8,128)(2,1)S(1)}, u32[]{:S(2)}, u32[]{:S(2)}) collective-permute-start(bf16[3,64,640]{2,1,0:T(8,128)(2,1)S(1)} %get-tuple-element.52), channel_id=1, source_target_pairs={{0,4},{1,5},{2,6},{3,7},{4,0},{5,1},{6,2},{7,3},{8,12},{9,13},{10,... | collective-permute-start | bytes 737288 | tf_op jit(solution)/shard_map/ppermute | solution.py:536
  28.6 5.9 %collective-permute-start.9 = (bf16[3,64,640]{2,1,0:T(8,128)(2,1)S(1)}, bf16[3,64,640]{2,1,0:T(8,128)(2,1)S(1)}, u32[]{:S(2)}, u32[]{:S(2)}) collective-permute-start(bf16[3,64,640]{2,1,0:T(8,128)(2,1)S(1)} %get-tuple-element.53), channel_id=1, source_target_pairs={{0,1},{1,0},{2,3},{3,2},{4,8},{5,9},{6,10},{7,11},{8,4},{9,5},{10,... | collective-permute-start | bytes 737288 | tf_op jit(solution)/shard_map/ppermute | solution.py:536
  31.9 6.4 %collective-permute-start.15 = (bf16[180,384]{1,0:T(8,128)(2,1)S(1)}, bf16[180,384]{1,0:T(8,128)(2,1)S(1)}, u32[]{:S(2)}, u32[]{:S(2)}) collective-permute-start(bf16[180,384]{1,0:T(8,128)(2,1)S(1)} %get-tuple-element.61), channel_id=1, source_target_pairs={{0,2},{1,3},{2,0},{3,1},{4,6},{5,7},{6,4},{7,5},{8,10},{9,11},{10,... | collective-permute-start | bytes 414728 | tf_op jit(solution)/shard_map/ppermute | solution.py:40
  32.6 8.2 %collective-permute-start.16 = (bf16[180,384]{1,0:T(8,128)(2,1)S(1)}, bf16[180,384]{1,0:T(8,128)(2,1)S(1)}, u32[]{:S(2)}, u32[]{:S(2)}) collective-permute-start(bf16[180,384]{1,0:T(8,128)(2,1)S(1)} %get-tuple-element.62), channel_id=1, source_target_pairs={{0,3},{1,2},{2,1},{3,0},{4,7},{5,6},{6,5},{7,4},{8,11},{9,10},{10,... | collective-permute-start | bytes 414728 | tf_op jit(solution)/shard_map/ppermute | solution.py:40
  33.6 7.2 %collective-permute-start.17 = (bf16[180,384]{1,0:T(8,128)(2,1)S(1)}, bf16[180,384]{1,0:T(8,128)(2,1)S(1)}, u32[]{:S(2)}, u32[]{:S(2)}) collective-permute-start(bf16[180,384]{1,0:T(8,128)(2,1)S(1)} %get-tuple-element.64), channel_id=1, source_target_pairs={{0,1},{1,0},{2,3},{3,2},{4,5},{5,4},{6,7},{7,6},{8,9},{9,8},{10,11... | collective-permute-start | bytes 414728 | tf_op jit(solution)/shard_map/ppermute | solution.py:40
  35.6 6.8 %collective-permute-start.10 = (bf16[180,256]{1,0:T(8,128)(2,1)S(1)}, bf16[180,256]{1,0:T(8,128)(2,1)S(1)}, u32[]{:S(2)}, u32[]{:S(2)}) collective-permute-start(bf16[180,256]{1,0:T(8,128)(2,1)S(1)} %get-tuple-element.55), channel_id=1, source_target_pairs={{0,2},{1,3},{2,0},{3,1},{4,6},{5,7},{6,4},{7,5},{8,10},{9,11},{10,... | collective-permute-start | bytes 276488 | tf_op jit(solution)/shard_map/ppermute | solution.py:40
  37.1 7.3 %collective-permute-start.11 = (bf16[180,256]{1,0:T(8,128)(2,1)S(1)}, bf16[180,256]{1,0:T(8,128)(2,1)S(1)}, u32[]{:S(2)}, u32[]{:S(2)}) collective-permute-start(bf16[180,256]{1,0:T(8,128)(2,1)S(1)} %get-tuple-element.56), channel_id=1, source_target_pairs={{0,3},{1,2},{2,1},{3,0},{4,7},{5,6},{6,5},{7,4},{8,11},{9,10},{10,... | collective-permute-start | bytes 276488 | tf_op jit(solution)/shard_map/ppermute | solution.py:40
  38.4 6.1 %collective-permute-start.12 = (bf16[180,256]{1,0:T(8,128)(2,1)S(1)}, bf16[180,256]{1,0:T(8,128)(2,1)S(1)}, u32[]{:S(2)}, u32[]{:S(2)}) collective-permute-start(bf16[180,256]{1,0:T(8,128)(2,1)S(1)} %get-tuple-element.58), channel_id=1, source_target_pairs={{0,1},{1,0},{2,3},{3,2},{4,5},{5,4},{6,7},{7,6},{8,9},{9,8},{10,11... | collective-permute-start | bytes 276488 | tf_op jit(solution)/shard_map/ppermute | solution.py:40

commit v4 on v3

--- a/solution.py
+++ b/solution.py
@@ -226,7 +226,7 @@
     own_ref, first_ref, second_ref = refs[-3:]
     start, size = chunk
     ranks = far_first(count, count)
-    pieces = [(refs[ranks.index(k)], 0 if k > NEAR else start) for k in range(count)]
+    pieces = [(refs[ranks.index(k)], 0 if k else start) for k in range(count)]
     table_ref, early = refs[count], refs[count + 1 : count + halves]
     per = rows // halves
     even = lax.rem(lax.axis_index("polar"), 2) == 0
@@ -545,7 +545,6 @@
     owned = channels // count
     halves = 2 if rows % 2 == 0 else 1
     wide = round_up(part, HALF)
-    far = range(NEAR + 1, count)
     filters, target, forth, back, *weights = prepare(
         basis_weight, filt, offsets, forth, back, rows, count, chunks
     )
@@ -554,17 +553,17 @@
         final = half == halves - 1
         sent = [(k, 0, owned) for k in range(count)]
         if final:
-            sent[NEAR + 1 :] = [(k,) + chunk for chunk in chunks for k in far]
+            sent[1:] = [(k,) + chunk for chunk in chunks for k in range(1, count)]
         blocks = mlp(conv_out, grad_out, w_in, b_in, w_out, count, half, halves, sent, chunks, order)
         order = blocks[:1]
         if not final:
             early.append(analyze_early([exchange(blocks[k], k, count) for k in range(count)], forth, wide))
-    whole = [exchange(blocks[k], k, count) for k in range(NEAR + 1)]
     spectra, terms, returned = {}, {}, {}
     for q, (start, size) in enumerate(chunks):
-        tail = [exchange(blocks[NEAR + 1 + q * len(far) + i], k, count) for i, k in enumerate(far)]
+        mine = blocks[1 + q * (count - 1) : 1 + (q + 1) * (count - 1)]
+        pieces = [blocks[0]] + [exchange(block, k, count) for k, block in enumerate(mine, 1)]
         after = [terms[q - 1]] if q else []
-        own, first, second = analyze(whole + tail, forth, early, rows, wide, (start, size), after)
+        own, first, second = analyze(pieces, forth, early, rows, wide, (start, size), after)
         spectra[q] = halo(first, second)
         terms[q] = own_terms(own, early, start, weights[q], target, filters)
     for q in range(len(chunks)):

time: 46.1 us -> 45.3 us (0.983)
  starting transfers between devices: 18.3 us -> 16.5 us
  waiting for transfers between devices: 9.22 us -> 10.4 us
    ppermute x14 -> x15, starting transfers between devices: 12.5 us -> 11.3 us  [exchange(): return lax.ppermute(block, 'azimuth', pairs)]
    ppermute x4, waiting for transfers between devices: 0.7 us -> 1.72 us  [halo(): blocks.append(lax.ppermute(block, ('polar', 'azimuth'), pairs))]
    ppermute x4, starting transfers between devices: 5.74 us -> 5.16 us  [halo(): blocks.append(lax.ppermute(block, ('polar', 'azimuth'), pairs))]
    ppermute x14 -> x15, waiting for transfers between devices: 8.52 us -> 8.68 us  [exchange(): return lax.ppermute(block, 'azimuth', pairs)]
  transfers between devices with their start and end apart: 18 -> 19, of which waited for: 7 -> 7; matrix products, arithmetic and copies ran while one was open for 0% -> 0% of each run, Pallas kernels for 23% -> 24%
where the time goes in v4:
time: 45.3 us; the launch traced here: 45.2 us
  starting transfers between devices  16.5 us (36%)
  Pallas kernels  15.1 us (33%)
  waiting for transfers between devices  10.4 us (23%)
  local copies, waits for them, and re-layouts  2.77 us (6%)
    ppermute x15, starting transfers between devices, exchange(): return lax.ppermute(block, 'azimuth', pairs)  11.3 us
    ppermute x15, waiting for transfers between devices, exchange(): return lax.ppermute(block, 'azimuth', pairs)  8.68 us
    pallas_call x2, Pallas kernels, mlp(): pl.pallas_call(functools.partial(mlp_kernel, count, half, sent, chunks),...  5.5 us
    ppermute x4, starting transfers between devices, halo(): blocks.append(lax.ppermute(block, ('polar', 'azimuth'), pairs))  5.16 us
    unnamed x18, local copies, waits for them, and re-layouts  2.77 us
    pallas_call x2, Pallas kernels, add_chunk(): pl.pallas_call(functools.partial(add_kernel, count, chunk, [k for k, _ in...  2.46 us
    pallas_call x2, Pallas kernels, finish(): pl.pallas_call(functools.partial(finish_kernel, count, len(halos)), in_sp...  2.37 us
    ppermute x4, waiting for transfers between devices, halo(): blocks.append(lax.ppermute(block, ('polar', 'azimuth'), pairs))  1.72 us
  transfers between devices with their start and end apart: 19, of which 7 were waited for; matrix products, arithmetic and copies ran while one was open for 0% of the time, Pallas kernels for 24%

profile of v4, /device:TPU:1, one launch (start us, length us, event | category | flops | bytes accessed | tf_op | source)
XLA Modules:
  0.0 45.2 jit_solution(7522957696629321956)
XLA Ops:
  0.0 0.0 copy-start.1
  0.0 0.0 copy-start.6
  0.0 1.4 %copy.17.grad_ref = bf16[4,180,640]{2,1,0:T(8,128)(2,1)S(1)} copy(bf16[4,180,640]{2,0,1:T(4,128)(2,1)} %param.11) | data formatting | bytes 1843200 | tf_op args[1]
  1.5 1.3 %copy.14.conv_ref = bf16[4,180,640]{2,1,0:T(8,128)(2,1)S(1)} copy(bf16[4,180,640]{2,0,1:T(4,128)(2,1)} %param.10) | data formatting | bytes 1843200 | tf_op args[0]
  2.8 0.0 copy-done.1
  2.8 0.0 copy-done.6
  2.8 0.0 copy-done
  2.8 2.8 %mlp.2 = (bf16[160,384]{1,0:T(8,128)(2,1)S(1)}, bf16[160,384]{1,0:T(8,128)(2,1)S(1)}, bf16[160,384]{1,0:T(8,128)(2,1)S(1)}, bf16[160,384]{1,0:T(8,128)(2,1)S(1)}) custom-call(bf16[4,180,640]{2,1,0:T(8,128)(2,1)S(1)} %copy.14.conv_ref, bf16[4,180,640]{2,1,0:T(8,128)(2,1)S(1)} %copy.17.grad_ref, bf16[640,1280]{1,0:T(8,128)(2,1)S(1)} %copy-done, ...), custom_call_target="tpu_custom_call" | custom-call | tf_op jit(solution)/shard_map/mlp/pallas_call | solution.py:165
  5.5 2.1 %collective-permute-start.3 = (bf16[160,384]{1,0:T(8,128)(2,1)S(1)}, bf16[160,384]{1,0:T(8,128)(2,1)S(1)}, u32[]{:S(2)}, u32[]{:S(2)}) collective-permute-start(bf16[160,384]{1,0:T(8,128)(2,1)S(1)} %get-tuple-element.42), channel_id=1, source_target_pairs={{0,2},{1,3},{2,0},{3,1},{4,6},{5,7},{6,4},{7,5},{8,10},{9,11},{10,... | collective-permute-start | bytes 368648 | tf_op jit(solution)/shard_map/ppermute | solution.py:40
  7.7 0.6 %collective-permute-start.4 = (bf16[160,384]{1,0:T(8,128)(2,1)S(1)}, bf16[160,384]{1,0:T(8,128)(2,1)S(1)}, u32[]{:S(2)}, u32[]{:S(2)}) collective-permute-start(bf16[160,384]{1,0:T(8,128)(2,1)S(1)} %get-tuple-element.43), channel_id=1, source_target_pairs={{0,3},{1,2},{2,1},{3,0},{4,7},{5,6},{6,5},{7,4},{8,11},{9,10},{10,... | collective-permute-start | bytes 368648 | tf_op jit(solution)/shard_map/ppermute | solution.py:40
  8.3 0.3 collective-permute-start.5
  8.6 0.0 copy-start.7
  8.6 2.7 %mlp.3 = (bf16[160,384]{1,0:T(8,128)(2,1)S(1)}, bf16[96,384]{1,0:T(8,128)(2,1)S(1)}, bf16[96,384]{1,0:T(8,128)(2,1)S(1)}, bf16[96,384]{1,0:T(8,128)(2,1)S(1)}, b...) custom-call(bf16[4,180,640]{2,1,0:T(8,128)(2,1)S(1)} %copy.14.conv_ref, ...), custom_call_target="tpu_custom_call" | custom-call | tf_op jit(solution)/shard_map/mlp/pallas_call | solution.py:165
  11.4 1.5 %collective-permute-start.6 = (bf16[96,384]{1,0:T(8,128)(2,1)S(1)}, bf16[96,384]{1,0:T(8,128)(2,1)S(1)}, u32[]{:S(2)}, u32[]{:S(2)}) collective-permute-start(bf16[96,384]{1,0:T(8,128)(2,1)S(1)} %get-tuple-element.45), channel_id=1, source_target_pairs={{0,2},{1,3},{2,0},{3,1},{4,6},{5,7},{6,4},{7,5},{8,10},{9,11},{10,... | collective-permute-start | bytes 221192 | tf_op jit(solution)/shard_map/ppermute | solution.py:40
  12.8 0.4 collective-permute-start.7
  13.3 0.0 collective-permute-done.3.refs_0_
  13.3 0.3 collective-permute-start.8
  13.6 0.0 copy-done.2
  13.6 0.0 copy-done.3
  13.6 0.0 copy-done.4
  13.6 0.0 copy-done.5
  13.6 0.0 copy-done.7
  13.6 0.7 %prepare.1 = (bf16[10,32,768]{2,1,0:T(8,128)(2,1)S(1)}, s32[10,32]{1,0:T(8,128)S(1)}, bf16[4,320,640]{2,1,0:T(8,128)(2,1)S(1)}, bf16[768,640]{1,0:T(8,128)(2,1)S...) custom-call(f32[9,640]{1,0:T(8,128)S(1)} %copy-done.5, bf16[9,16,640]{2,1,0:T(8,128)(2,1)S(1)} %copy-done.4, ...), custom_call_target="tpu_custom_call" | custom-call | tf_op jit(solution)/shard_map/prepare/pallas_call | solution.py:514
  14.3 0.0 collective-permute-done.4.refs_1_
  14.3 0.0 collective-permute-done.5.refs_3_
  14.4 0.7 %analysis_early.1.refs_5_.rest_0_ = f32[2,160,640]{2,1,0:T(8,128)S(1)} custom-call(bf16[160,384]{1,0:T(8,128)(2,1)S(1)} %collective-permute-done.3.refs_0_, bf16[160,384]{1,0:T(8,128)(2,1)S(1)} %collective-permute-done.4.refs_1_, bf16[160,384]{1,0:T(8,128)(2,1)S(1)} %get-tuple-element.36.rest_0_.refs_2_, ...), custom_call_target="tpu_custom_call" | custom-call | tf_op jit(solution)/shard_map/analysis_early/pallas_call | solution.py:214
  15.0 0.1 collective-permute-done.6.refs_0_
  15.2 2.5 %collective-permute-done.7.refs_1_ = bf16[96,384]{1,0:T(8,128)(2,1)S(1)} collective-permute-done((bf16[96,384]{1,0:T(8,128)(2,1)S(1)}, bf16[96,384]{1,0:T(8,128)(2,1)S(1)}, u32[]{:S(2)}, u32[]{:S(2)}) %collective-permute-start.7) | collective-permute-done | bytes 73760 | tf_op jit(solution)/shard_map/ppermute | solution.py:40
  17.6 0.0 collective-permute-done.8.refs_3_
  17.6 0.6 %analysis.2 = (f32[2,96,640]{2,1,0:T(8,128)S(1)}, bf16[3,96,640]{2,1,0:T(8,128)(2,1)S(1)}, bf16[3,96,640]{2,1,0:T(8,128)(2,1)S(1)}) custom-call(bf16[96,384]{1,0:T(8,128)(2,1)S(1)} %collective-permute-done.6.refs_0_, bf16[96,384]{1,0:T(8,128)(2,1)S(1)} %collective-permute-done.7.refs_1_, bf16[160,384]{1,0:T(8,128)(2,1)S(1)} %get-tuple-element.39.refs_2_, ...), custom_call_target="tpu_custom_call" | custom-call | tf_op jit(solution)/shard_map/analysis/pallas_call | solution.py:255
  18.3 1.4 %collective-permute-start.14 = (bf16[3,96,640]{2,1,0:T(8,128)(2,1)S(1)}, bf16[3,96,640]{2,1,0:T(8,128)(2,1)S(1)}, u32[]{:S(2)}, u32[]{:S(2)}) collective-permute-start(bf16[3,96,640]{2,1,0:T(8,128)(2,1)S(1)} %get-tuple-element.61), channel_id=1, source_target_pairs={{0,4},{1,5},{2,6},{3,7},{4,0},{5,1},{6,2},{7,3},{8,12},{9,13},{10,... | collective-permute-start | bytes 1105928 | tf_op jit(solution)/shard_map/ppermute | solution.py:536
  19.6 0.7 %collective-permute-start.15 = (bf16[3,96,640]{2,1,0:T(8,128)(2,1)S(1)}, bf16[3,96,640]{2,1,0:T(8,128)(2,1)S(1)}, u32[]{:S(2)}, u32[]{:S(2)}) collective-permute-start(bf16[3,96,640]{2,1,0:T(8,128)(2,1)S(1)} %get-tuple-element.62), channel_id=1, source_target_pairs={{0,1},{1,0},{2,3},{3,2},{4,8},{5,9},{6,10},{7,11},{8,4},{9,5},{10,... | collective-permute-start | bytes 1105928 | tf_op jit(solution)/shard_map/ppermute | solution.py:536
  20.4 0.3 collective-permute-start
  20.7 1.3 %collective-permute-start.1 = (bf16[64,384]{1,0:T(8,128)(2,1)S(1)}, bf16[64,384]{1,0:T(8,128)(2,1)S(1)}, u32[]{:S(2)}, u32[]{:S(2)}) collective-permute-start(bf16[64,384]{1,0:T(8,128)(2,1)S(1)} %get-tuple-element.38), channel_id=1, source_target_pairs={{0,3},{1,2},{2,1},{3,0},{4,7},{5,6},{6,5},{7,4},{8,11},{9,10},{10,... | collective-permute-start | bytes 147464 | tf_op jit(solution)/shard_map/ppermute | solution.py:40
  22.0 0.2 collective-permute-start.2
  22.2 1.0 %own_terms.2.refs_6_.part_ref = f32[4,96,640]{2,1,0:T(8,128)S(1)} custom-call(f32[2,96,640]{2,1,0:T(8,128)S(1)} %get-tuple-element.48.own_ref, f32[96,32]{1,0:T(8,128)S(1)} %get-tuple-element.49.weight_ref.refs_1_, s32[10,32]{1,0:T(8,128)S(1)} %get-tuple-element.50.target_ref.refs_3_.refs_2_, ...), custom_call_target="tpu_custom_call" | custom-call | tf_op jit(solution)/shard_map/own_terms/pallas_call | solution.py:311
  23.3 0.5 %collective-permute-done.refs_0_ = bf16[64,384]{1,0:T(8,128)(2,1)S(1)} collective-permute-done((bf16[64,384]{1,0:T(8,128)(2,1)S(1)}, bf16[64,384]{1,0:T(8,128)(2,1)S(1)}, u32[]{:S(2)}, u32[]{:S(2)}) %collective-permute-start) | collective-permute-done | bytes 49184 | tf_op jit(solution)/shard_map/ppermute | solution.py:40
  23.8 1.4 %collective-permute-done.1.refs_1_ = bf16[64,384]{1,0:T(8,128)(2,1)S(1)} collective-permute-done((bf16[64,384]{1,0:T(8,128)(2,1)S(1)}, bf16[64,384]{1,0:T(8,128)(2,1)S(1)}, u32[]{:S(2)}, u32[]{:S(2)}) %collective-permute-start.1) | collective-permute-done | bytes 49184 | tf_op jit(solution)/shard_map/ppermute | solution.py:40
  25.2 0.0 collective-permute-done.2.refs_3_
  25.2 0.6 %analysis.3 = (f32[2,64,640]{2,1,0:T(8,128)S(1)}, bf16[3,64,640]{2,1,0:T(8,128)(2,1)S(1)}, bf16[3,64,640]{2,1,0:T(8,128)(2,1)S(1)}) custom-call(bf16[64,384]{1,0:T(8,128)(2,1)S(1)} %collective-permute-done.refs_0_, bf16[64,384]{1,0:T(8,128)(2,1)S(1)} %collective-permute-done.1.refs_1_, bf16[160,384]{1,0:T(8,128)(2,1)S(1)} %get-tuple-element.39.refs_2_, ...), custom_call_target="tpu_custom_call" | custom-call | tf_op jit(solution)/shard_map/analysis/pallas_call | solution.py:255
  25.8 2.9 %collective-permute-start.9 = (bf16[3,64,640]{2,1,0:T(8,128)(2,1)S(1)}, bf16[3,64,640]{2,1,0:T(8,128)(2,1)S(1)}, u32[]{:S(2)}, u32[]{:S(2)}) collective-permute-start(bf16[3,64,640]{2,1,0:T(8,128)(2,1)S(1)} %get-tuple-element.54), channel_id=1, source_target_pairs={{0,4},{1,5},{2,6},{3,7},{4,0},{5,1},{6,2},{7,3},{8,12},{9,13},{10,... | collective-permute-start | bytes 737288 | tf_op jit(solution)/shard_map/ppermute | solution.py:536
  28.7 0.2 collective-permute-start.10
  28.8 0.7 %own_terms.3.part_ref.rest_0_ = f32[4,64,640]{2,1,0:T(8,128)S(1)} custom-call(f32[2,64,640]{2,1,0:T(8,128)S(1)} %get-tuple-element.52.own_ref, f32[64,32]{1,0:T(8,128)S(1)} %get-tuple-element.53.weight_ref.refs_2_, s32[10,32]{1,0:T(8,128)S(1)} %get-tuple-element.50.target_ref.refs_3_.refs_2_, ...), custom_call_target="tpu_custom_call" | custom-call | tf_op jit(solution)/shard_map/own_terms/pallas_call | solution.py:311
  29.5 0.0 collective-permute-done.14.first_ref
  29.5 0.5 %side_terms.1.part_ref = f32[4,96,640]{2,1,0:T(8,128)S(1)} custom-call(f32[4,96,640]{2,1,0:T(8,128)S(1)} %own_terms.2.refs_6_.part_ref, bf16[3,96,640]{2,1,0:T(8,128)(2,1)S(1)} %collective-permute-done.14.first_ref, f32[96,32]{1,0:T(8,128)S(1)} %get-tuple-element.49.weight_ref.refs_1_, s32[10,32]{1,0:T(8,128)S(1)} %get-tuple-element.50.target_ref.refs_3_.refs_2_, ...), custom_call_target="tpu_custom_call" | custom-call | tf_op jit(solution)/shard_map/side_terms/pallas_call | solution.py:353
  30.1 0.0 collective-permute-done.15.refs_0_
  30.1 1.3 %finish.3 = (bf16[180,384]{1,0:T(8,128)(2,1)S(1)}, bf16[180,384]{1,0:T(8,128)(2,1)S(1)}, bf16[180,384]{1,0:T(8,128)(2,1)S(1)}, bf16[180,384]{1,0:T(8,128)(2,1)S(1)}) custom-call(f32[4,96,640]{2,1,0:T(8,128)S(1)} %side_terms.1.part_ref, bf16[3,96,640]{2,1,0:T(8,128)(2,1)S(1)} %collective-permute-done.15.refs_0_, ...), custom_call_target="tpu_custom_call" | custom-call | tf_op jit(solution)/shard_map/finish/pallas_call | solution.py:387
  31.4 0.9 %collective-permute-start.16 = (bf16[180,384]{1,0:T(8,128)(2,1)S(1)}, bf16[180,384]{1,0:T(8,128)(2,1)S(1)}, u32[]{:S(2)}, u32[]{:S(2)}) collective-permute-start(bf16[180,384]{1,0:T(8,128)(2,1)S(1)} %get-tuple-element.63), channel_id=1, source_target_pairs={{0,2},{1,3},{2,0},{3,1},{4,6},{5,7},{6,4},{7,5},{8,10},{9,11},{10,... | collective-permute-start | bytes 414728 | tf_op jit(solution)/shard_map/ppermute | solution.py:40
  32.2 1.2 %collective-permute-start.17 = (bf16[180,384]{1,0:T(8,128)(2,1)S(1)}, bf16[180,384]{1,0:T(8,128)(2,1)S(1)}, u32[]{:S(2)}, u32[]{:S(2)}) collective-permute-start(bf16[180,384]{1,0:T(8,128)(2,1)S(1)} %get-tuple-element.64), channel_id=1, source_target_pairs={{0,3},{1,2},{2,1},{3,0},{4,7},{5,6},{6,5},{7,4},{8,11},{9,10},{10,... | collective-permute-start | bytes 414728 | tf_op jit(solution)/shard_map/ppermute | solution.py:40
  33.4 0.0 collective-permute-start.18
  33.4 1.7 %collective-permute-done.9.refs_0_ = bf16[3,64,640]{2,1,0:T(8,128)(2,1)S(1)} collective-permute-done((bf16[3,64,640]{2,1,0:T(8,128)(2,1)S(1)}, bf16[3,64,640]{2,1,0:T(8,128)(2,1)S(1)}, u32[]{:S(2)}, u32[]{:S(2)}) %collective-permute-start.9) | collective-permute-done | bytes 245792 | tf_op jit(solution)/shard_map/ppermute | solution.py:536
  35.1 0.0 collective-permute-done.10.refs_1_
  35.1 1.1 %finish.2 = (bf16[180,256]{1,0:T(8,128)(2,1)S(1)}, bf16[180,256]{1,0:T(8,128)(2,1)S(1)}, bf16[180,256]{1,0:T(8,128)(2,1)S(1)}, bf16[180,256]{1,0:T(8,128)(2,1)S(1)}) custom-call(f32[4,64,640]{2,1,0:T(8,128)S(1)} %own_terms.3.part_ref.rest_0_, bf16[3,64,640]{2,1,0:T(8,128)(2,1)S(1)} %collective-permute-done.9.refs_0_, ...), custom_call_target="tpu_custom_call" | custom-call | tf_op jit(solution)/shard_map/finish/pallas_call | solution.py:387
  36.2 0.1 collective-permute-start.11
  36.3 2.1 %collective-permute-start.12 = (bf16[180,256]{1,0:T(8,128)(2,1)S(1)}, bf16[180,256]{1,0:T(8,128)(2,1)S(1)}, u32[]{:S(2)}, u32[]{:S(2)}) collective-permute-start(bf16[180,256]{1,0:T(8,128)(2,1)S(1)} %get-tuple-element.58), channel_id=1, source_target_pairs={{0,3},{1,2},{2,1},{3,0},{4,7},{5,6},{6,5},{7,4},{8,11},{9,10},{10,... | collective-permute-start | bytes 276488 | tf_op jit(solution)/shard_map/ppermute | solution.py:40
  38.4 0.0 collective-permute-done.16.refs_0_
  38.4 0.0 collective-permute-start.13
  38.4 2.3 %collective-permute-done.17.refs_1_ = bf16[180,384]{1,0:T(8,128)(2,1)S(1)} collective-permute-done((bf16[180,384]{1,0:T(8,128)(2,1)S(1)}, bf16[180,384]{1,0:T(8,128)(2,1)S(1)}, u32[]{:S(2)}, u32[]{:S(2)}) %collective-permute-start.17) | collective-permute-done | bytes 138272 | tf_op jit(solution)/shard_map/ppermute | solution.py:40
  40.7 0.0 collective-permute-done.18.refs_3_
  40.7 1.4 %add_chunk.2.refs_4_ = bf16[180,4,640]{2,1,0:T(4,128)(2,1)} custom-call(bf16[4,180,640]{2,1,0:T(8,128)(2,1)S(1)} %copy.17.grad_ref, bf16[180,384]{1,0:T(8,128)(2,1)S(1)} %collective-permute-done.16.refs_0_, bf16[180,384]{1,0:T(8,128)(2,1)S(1)} %collective-permute-done.17.refs_1_, bf16[180,384]{1,0:T(8,128)(2,1)S(1)} %get-tuple-element.65.refs_2_, ...), custom_call_target="tpu_custom_call" | custom-call | tf_op jit(solution)/shard_map/add_chunk/pallas_call | solution.py:438
  42.1 0.0 collective-permute-done.11.refs_0_
  42.1 1.8 %collective-permute-done.12.refs_1_ = bf16[180,256]{1,0:T(8,128)(2,1)S(1)} collective-permute-done((bf16[180,256]{1,0:T(8,128)(2,1)S(1)}, bf16[180,256]{1,0:T(8,128)(2,1)S(1)}, u32[]{:S(2)}, u32[]{:S(2)}) %collective-permute-start.12) | collective-permute-done | bytes 92192 | tf_op jit(solution)/shard_map/ppermute | solution.py:40
  43.9 0.0 collective-permute-done.13.refs_3_
  43.9 1.1 %add_chunk.3 = bf16[180,4,640]{2,1,0:T(4,128)(2,1)} custom-call(bf16[4,180,640]{2,1,0:T(8,128)(2,1)S(1)} %copy.17.grad_ref, bf16[180,256]{1,0:T(8,128)(2,1)S(1)} %collective-permute-done.11.refs_0_, bf16[180,256]{1,0:T(8,128)(2,1)S(1)} %collective-permute-done.12.refs_1_, ...), custom_call_target="tpu_custom_call", output_to_operand_aliasing={{}: (5, {})} | custom-call | tf_op jit(solution)/shard_map/add_chunk/pallas_call | solution.py:438
  (5 shorter events, 0.0 us)
Async XLA Ops:
  0.0 2.8 %copy-start.1 = (bf16[1280,640]{1,0:T(8,128)(2,1)S(1)}, bf16[1280,640]{1,0:T(8,128)(2,1)}, u32[]{:S(2)}) copy-start(bf16[1280,640]{1,0:T(8,128)(2,1)} %wout_ref.3) | copy-start | bytes 4915204
  0.0 2.8 %copy-start.6 = (f32[1280]{0:T(1024)S(1)}, f32[1280]{0:T(1024)}, u32[]{:S(2)}) copy-start(f32[1280]{0:T(1024)} %bias_ref.3) | copy-start | bytes 15364
  0.0 2.8 %copy-start = (bf16[640,1280]{1,0:T(8,128)(2,1)S(1)}, bf16[640,1280]{1,0:T(8,128)(2,1)}, u32[]{:S(2)}) copy-start(bf16[640,1280]{1,0:T(8,128)(2,1)} %win_ref.3) | copy-start | bytes 4915204
  5.5 7.7 %collective-permute-start.3 = (bf16[160,384]{1,0:T(8,128)(2,1)S(1)}, bf16[160,384]{1,0:T(8,128)(2,1)S(1)}, u32[]{:S(2)}, u32[]{:S(2)}) collective-permute-start(bf16[160,384]{1,0:T(8,128)(2,1)S(1)} %get-tuple-element.42), channel_id=1, source_target_pairs={{0,2},{1,3},{2,0},{3,1},{4,6},{5,7},{6,4},{7,5},{8,10},{9,11},{10,... | collective-permute-start | bytes 368648 | tf_op jit(solution)/shard_map/ppermute | solution.py:40
  7.7 6.7 %collective-permute-start.4 = (bf16[160,384]{1,0:T(8,128)(2,1)S(1)}, bf16[160,384]{1,0:T(8,128)(2,1)S(1)}, u32[]{:S(2)}, u32[]{:S(2)}) collective-permute-start(bf16[160,384]{1,0:T(8,128)(2,1)S(1)} %get-tuple-element.43), channel_id=1, source_target_pairs={{0,3},{1,2},{2,1},{3,0},{4,7},{5,6},{6,5},{7,4},{8,11},{9,10},{10,... | collective-permute-start | bytes 368648 | tf_op jit(solution)/shard_map/ppermute | solution.py:40
  8.3 6.1 %collective-permute-start.5 = (bf16[160,384]{1,0:T(8,128)(2,1)S(1)}, bf16[160,384]{1,0:T(8,128)(2,1)S(1)}, u32[]{:S(2)}, u32[]{:S(2)}) collective-permute-start(bf16[160,384]{1,0:T(8,128)(2,1)S(1)} %get-tuple-element.44), channel_id=1, source_target_pairs={{0,1},{1,0},{2,3},{3,2},{4,5},{5,4},{6,7},{7,6},{8,9},{9,8},{10,11... | collective-permute-start | bytes 368648 | tf_op jit(solution)/shard_map/ppermute | solution.py:40
  8.6 5.0 %copy-start.2 = (bf16[4,320,640]{2,1,0:T(8,128)(2,1)S(1)}, bf16[4,320,640]{2,1,0:T(8,128)(2,1)}, u32[]{:S(2)}) copy-start(bf16[4,320,640]{2,1,0:T(8,128)(2,1)} %constant.4.clone.forth_ref) | copy-start | bytes 4915204
  8.6 5.0 %copy-start.3 = (bf16[768,640]{1,0:T(8,128)(2,1)S(1)}, bf16[768,640]{1,0:T(8,128)(2,1)}, u32[]{:S(2)}) copy-start(bf16[768,640]{1,0:T(8,128)(2,1)} %constant.5.clone.back_ref) | copy-start | bytes 2949124
  8.6 5.0 %copy-start.4 = (bf16[9,16,640]{2,1,0:T(8,128)(2,1)S(1)}, bf16[9,16,640]{2,1,0:T(8,128)(2,1)}, u32[]{:S(2)}) copy-start(bf16[9,16,640]{2,1,0:T(8,128)(2,1)} %filt_ref.1) | copy-start | bytes 552964
  8.6 5.0 %copy-start.5 = (f32[9,640]{1,0:T(8,128)S(1)}, f32[9,640]{1,0:T(8,128)}, u32[]{:S(2)}) copy-start(f32[9,640]{1,0:T(8,128)} %weight_ref.1) | copy-start | bytes 69124
  8.6 5.0 %copy-start.7 = (s32[16,9]{1,0:T(8,128)S(1)}, s32[16,9]{1,0:T(8,128)}, u32[]{:S(2)}) copy-start(s32[16,9]{1,0:T(8,128)} %offset_ref.1) | copy-start | bytes 1732
  11.4 3.8 %collective-permute-start.6 = (bf16[96,384]{1,0:T(8,128)(2,1)S(1)}, bf16[96,384]{1,0:T(8,128)(2,1)S(1)}, u32[]{:S(2)}, u32[]{:S(2)}) collective-permute-start(bf16[96,384]{1,0:T(8,128)(2,1)S(1)} %get-tuple-element.45), channel_id=1, source_target_pairs={{0,2},{1,3},{2,0},{3,1},{4,6},{5,7},{6,4},{7,5},{8,10},{9,11},{10,... | collective-permute-start | bytes 221192 | tf_op jit(solution)/shard_map/ppermute | solution.py:40
  12.8 4.8 %collective-permute-start.7 = (bf16[96,384]{1,0:T(8,128)(2,1)S(1)}, bf16[96,384]{1,0:T(8,128)(2,1)S(1)}, u32[]{:S(2)}, u32[]{:S(2)}) collective-permute-start(bf16[96,384]{1,0:T(8,128)(2,1)S(1)} %get-tuple-element.46), channel_id=1, source_target_pairs={{0,3},{1,2},{2,1},{3,0},{4,7},{5,6},{6,5},{7,4},{8,11},{9,10},{10,... | collective-permute-start | bytes 221192 | tf_op jit(solution)/shard_map/ppermute | solution.py:40
  13.3 4.4 %collective-permute-start.8 = (bf16[96,384]{1,0:T(8,128)(2,1)S(1)}, bf16[96,384]{1,0:T(8,128)(2,1)S(1)}, u32[]{:S(2)}, u32[]{:S(2)}) collective-permute-start(bf16[96,384]{1,0:T(8,128)(2,1)S(1)} %get-tuple-element.47), channel_id=1, source_target_pairs={{0,1},{1,0},{2,3},{3,2},{4,5},{5,4},{6,7},{7,6},{8,9},{9,8},{10,11... | collective-permute-start | bytes 221192 | tf_op jit(solution)/shard_map/ppermute | solution.py:40
  18.3 11.3 %collective-permute-start.14 = (bf16[3,96,640]{2,1,0:T(8,128)(2,1)S(1)}, bf16[3,96,640]{2,1,0:T(8,128)(2,1)S(1)}, u32[]{:S(2)}, u32[]{:S(2)}) collective-permute-start(bf16[3,96,640]{2,1,0:T(8,128)(2,1)S(1)} %get-tuple-element.61), channel_id=1, source_target_pairs={{0,4},{1,5},{2,6},{3,7},{4,0},{5,1},{6,2},{7,3},{8,12},{9,13},{10,... | collective-permute-start | bytes 1105928 | tf_op jit(solution)/shard_map/ppermute | solution.py:536
  19.6 10.4 %collective-permute-start.15 = (bf16[3,96,640]{2,1,0:T(8,128)(2,1)S(1)}, bf16[3,96,640]{2,1,0:T(8,128)(2,1)S(1)}, u32[]{:S(2)}, u32[]{:S(2)}) collective-permute-start(bf16[3,96,640]{2,1,0:T(8,128)(2,1)S(1)} %get-tuple-element.62), channel_id=1, source_target_pairs={{0,1},{1,0},{2,3},{3,2},{4,8},{5,9},{6,10},{7,11},{8,4},{9,5},{10,... | collective-permute-start | bytes 1105928 | tf_op jit(solution)/shard_map/ppermute | solution.py:536
  20.4 3.4 %collective-permute-start = (bf16[64,384]{1,0:T(8,128)(2,1)S(1)}, bf16[64,384]{1,0:T(8,128)(2,1)S(1)}, u32[]{:S(2)}, u32[]{:S(2)}) collective-permute-start(bf16[64,384]{1,0:T(8,128)(2,1)S(1)} %get-tuple-element.37), channel_id=1, source_target_pairs={{0,2},{1,3},{2,0},{3,1},{4,6},{5,7},{6,4},{7,5},{8,10},{9,11},{10,... | collective-permute-start | bytes 147464 | tf_op jit(solution)/shard_map/ppermute | solution.py:40
  20.7 4.5 %collective-permute-start.1 = (bf16[64,384]{1,0:T(8,128)(2,1)S(1)}, bf16[64,384]{1,0:T(8,128)(2,1)S(1)}, u32[]{:S(2)}, u32[]{:S(2)}) collective-permute-start(bf16[64,384]{1,0:T(8,128)(2,1)S(1)} %get-tuple-element.38), channel_id=1, source_target_pairs={{0,3},{1,2},{2,1},{3,0},{4,7},{5,6},{6,5},{7,4},{8,11},{9,10},{10,... | collective-permute-start | bytes 147464 | tf_op jit(solution)/shard_map/ppermute | solution.py:40
  22.0 3.2 %collective-permute-start.2 = (bf16[64,384]{1,0:T(8,128)(2,1)S(1)}, bf16[64,384]{1,0:T(8,128)(2,1)S(1)}, u32[]{:S(2)}, u32[]{:S(2)}) collective-permute-start(bf16[64,384]{1,0:T(8,128)(2,1)S(1)} %get-tuple-element.40), channel_id=1, source_target_pairs={{0,1},{1,0},{2,3},{3,2},{4,5},{5,4},{6,7},{7,6},{8,9},{9,8},{10,11... | collective-permute-start | bytes 147464 | tf_op jit(solution)/shard_map/ppermute | solution.py:40
  25.8 9.3 %collective-permute-start.9 = (bf16[3,64,640]{2,1,0:T(8,128)(2,1)S(1)}, bf16[3,64,640]{2,1,0:T(8,128)(2,1)S(1)}, u32[]{:S(2)}, u32[]{:S(2)}) collective-permute-start(bf16[3,64,640]{2,1,0:T(8,128)(2,1)S(1)} %get-tuple-element.54), channel_id=1, source_target_pairs={{0,4},{1,5},{2,6},{3,7},{4,0},{5,1},{6,2},{7,3},{8,12},{9,13},{10,... | collective-permute-start | bytes 737288 | tf_op jit(solution)/shard_map/ppermute | solution.py:536
  28.7 6.5 %collective-permute-start.10 = (bf16[3,64,640]{2,1,0:T(8,128)(2,1)S(1)}, bf16[3,64,640]{2,1,0:T(8,128)(2,1)S(1)}, u32[]{:S(2)}, u32[]{:S(2)}) collective-permute-start(bf16[3,64,640]{2,1,0:T(8,128)(2,1)S(1)} %get-tuple-element.55), channel_id=1, source_target_pairs={{0,1},{1,0},{2,3},{3,2},{4,8},{5,9},{6,10},{7,11},{8,4},{9,5},{10,... | collective-permute-start | bytes 737288 | tf_op jit(solution)/shard_map/ppermute | solution.py:536
  31.4 7.0 %collective-permute-start.16 = (bf16[180,384]{1,0:T(8,128)(2,1)S(1)}, bf16[180,384]{1,0:T(8,128)(2,1)S(1)}, u32[]{:S(2)}, u32[]{:S(2)}) collective-permute-start(bf16[180,384]{1,0:T(8,128)(2,1)S(1)} %get-tuple-element.63), channel_id=1, source_target_pairs={{0,2},{1,3},{2,0},{3,1},{4,6},{5,7},{6,4},{7,5},{8,10},{9,11},{10,... | collective-permute-start | bytes 414728 | tf_op jit(solution)/shard_map/ppermute | solution.py:40
  32.2 8.4 %collective-permute-start.17 = (bf16[180,384]{1,0:T(8,128)(2,1)S(1)}, bf16[180,384]{1,0:T(8,128)(2,1)S(1)}, u32[]{:S(2)}, u32[]{:S(2)}) collective-permute-start(bf16[180,384]{1,0:T(8,128)(2,1)S(1)} %get-tuple-element.64), channel_id=1, source_target_pairs={{0,3},{1,2},{2,1},{3,0},{4,7},{5,6},{6,5},{7,4},{8,11},{9,10},{10,... | collective-permute-start | bytes 414728 | tf_op jit(solution)/shard_map/ppermute | solution.py:40
  33.4 7.3 %collective-permute-start.18 = (bf16[180,384]{1,0:T(8,128)(2,1)S(1)}, bf16[180,384]{1,0:T(8,128)(2,1)S(1)}, u32[]{:S(2)}, u32[]{:S(2)}) collective-permute-start(bf16[180,384]{1,0:T(8,128)(2,1)S(1)} %get-tuple-element.66), channel_id=1, source_target_pairs={{0,1},{1,0},{2,3},{3,2},{4,5},{5,4},{6,7},{7,6},{8,9},{9,8},{10,11... | collective-permute-start | bytes 414728 | tf_op jit(solution)/shard_map/ppermute | solution.py:40
  36.2 5.9 %collective-permute-start.11 = (bf16[180,256]{1,0:T(8,128)(2,1)S(1)}, bf16[180,256]{1,0:T(8,128)(2,1)S(1)}, u32[]{:S(2)}, u32[]{:S(2)}) collective-permute-start(bf16[180,256]{1,0:T(8,128)(2,1)S(1)} %get-tuple-element.57), channel_id=1, source_target_pairs={{0,2},{1,3},{2,0},{3,1},{4,6},{5,7},{6,4},{7,5},{8,10},{9,11},{10,... | collective-permute-start | bytes 276488 | tf_op jit(solution)/shard_map/ppermute | solution.py:40
  36.3 7.6 %collective-permute-start.12 = (bf16[180,256]{1,0:T(8,128)(2,1)S(1)}, bf16[180,256]{1,0:T(8,128)(2,1)S(1)}, u32[]{:S(2)}, u32[]{:S(2)}) collective-permute-start(bf16[180,256]{1,0:T(8,128)(2,1)S(1)} %get-tuple-element.58), channel_id=1, source_target_pairs={{0,3},{1,2},{2,1},{3,0},{4,7},{5,6},{6,5},{7,4},{8,11},{9,10},{10,... | collective-permute-start | bytes 276488 | tf_op jit(solution)/shard_map/ppermute | solution.py:40
  38.4 5.6 %collective-permute-start.13 = (bf16[180,256]{1,0:T(8,128)(2,1)S(1)}, bf16[180,256]{1,0:T(8,128)(2,1)S(1)}, u32[]{:S(2)}, u32[]{:S(2)}) collective-permute-start(bf16[180,256]{1,0:T(8,128)(2,1)S(1)} %get-tuple-element.60), channel_id=1, source_target_pairs={{0,1},{1,0},{2,3},{3,2},{4,5},{5,4},{6,7},{7,6},{8,9},{9,8},{10,11... | collective-permute-start | bytes 276488 | tf_op jit(solution)/shard_map/ppermute | solution.py:40

commit v5 on v4

--- a/solution.py
+++ b/solution.py
@@ -138,7 +138,7 @@
         if step + 1 < steps:
             project_pre(step + 1)
         slope(step, thirds[0], thirds[1])
-        if step - gathered == 2:
+        if step - gathered == 3:
             gather(gathered, step)
             gathered = step
         slope(step, thirds[1], thirds[2])
@@ -203,9 +203,10 @@
 def early_kernel(count, wide, *refs):
     ranks = far_first(count, count)
     pieces = [(refs[ranks.index(k)], 0) for k in range(count)]
-    table_ref, out_ref = refs[count], refs[-1]
+    table_ref, (out_ref, sent_ref) = refs[count], refs[-2:]
     for row, spectrum in enumerate(spectra_of(pieces, (0, pieces[0][0].shape[0]), table_ref, wide)):
         out_ref[row] = spectrum
+        sent_ref[row] = spectrum.astype(jnp.bfloat16)
 
 
 def analyze_early(pieces, table, wide):
@@ -214,8 +215,10 @@
     return pl.pallas_call(
         functools.partial(early_kernel, count, wide),
         in_specs=[pl.BlockSpec(memory_space=VMEM)] * (count + 1),
-        out_specs=pl.BlockSpec(memory_space=VMEM),
-        out_shape=jax.ShapeDtypeStruct((across // wide, size, table.shape[2]), jnp.float32),
+        out_specs=[pl.BlockSpec(memory_space=VMEM)] * 2,
+        out_shape=[
+            jax.ShapeDtypeStruct((across // wide, size, table.shape[2]), kind) for kind in (jnp.float32, jnp.bfloat16)
+        ],
         compiler_params=pltpu.CompilerParams(vmem_limit_bytes=12 * 2**20),
         cost_estimate=NO_COST,
         name="analysis_early",
@@ -223,7 +226,7 @@
 
 
 def analysis_kernel(count, rows, wide, chunk, halves, *refs):
-    own_ref, first_ref, second_ref = refs[-3:]
+    own_ref, first_ref, second_ref, sent_ref = refs[-4:]
     start, size = chunk
     ranks = far_first(count, count)
     pieces = [(refs[ranks.index(k)], 0 if k else start) for k in range(count)]
@@ -232,15 +235,16 @@
     even = lax.rem(lax.axis_index("polar"), 2) == 0
     for row, spectrum in enumerate(spectra_of(pieces, chunk, table_ref, wide)):
         own_ref[row] = spectrum
+        sent_ref[row] = spectrum.astype(jnp.bfloat16)
 
     def row_of(row):
         half, row = divmod(row, per)
-        return own_ref[row] if half == halves - 1 else early[half][row, start : start + size, :]
+        return sent_ref[row] if half == halves - 1 else early[half][row, start : start + size, :]
 
     def share(above, below):
         for h in range(REACH):
-            above[h] = row_of(rows - REACH + h).astype(jnp.bfloat16)
-            below[h] = row_of(h).astype(jnp.bfloat16)
+            above[h] = row_of(rows - REACH + h)
+            below[h] = row_of(h)
 
     pl.when(even)(lambda: share(first_ref, second_ref))
     pl.when(jnp.logical_not(even))(lambda: share(second_ref, first_ref))
@@ -258,6 +262,7 @@
         + [pl.BlockSpec(memory_space=pl.ANY)] * len(after),
         out_specs=[pl.BlockSpec(memory_space=VMEM)] * 3,
         out_shape=[jax.ShapeDtypeStruct((rows // halves, size, width), jnp.float32), halo, halo],
+        scratch_shapes=[pltpu.VMEM((rows // halves, size, width), jnp.bfloat16)],
         compiler_params=pltpu.CompilerParams(vmem_limit_bytes=12 * 2**20),
         cost_estimate=NO_COST,
         name="analysis",
@@ -563,9 +568,9 @@
         mine = blocks[1 + q * (count - 1) : 1 + (q + 1) * (count - 1)]
         pieces = [blocks[0]] + [exchange(block, k, count) for k, block in enumerate(mine, 1)]
         after = [terms[q - 1]] if q else []
-        own, first, second = analyze(pieces, forth, early, rows, wide, (start, size), after)
+        own, first, second = analyze(pieces, forth, [sent for _, sent in early], rows, wide, (start, size), after)
         spectra[q] = halo(first, second)
-        terms[q] = own_terms(own, early, start, weights[q], target, filters)
+        terms[q] = own_terms(own, [spectrum for spectrum, _ in early], start, weights[q], target, filters)
     for q in range(len(chunks)):
         halos = spectra[q]
         if q == 0:

time: 45.3 us -> 45.5 us (level)
  no operation moved by 1% of the time
where the time goes in v5:
time: 45.5 us; the launch traced here: 45.3 us
  starting transfers between devices  16.6 us (36%)
  Pallas kernels  15.3 us (34%)
  waiting for transfers between devices  10.3 us (23%)
  local copies, waits for them, and re-layouts  2.77 us (6%)
    ppermute x15, starting transfers between devices, exchange(): return lax.ppermute(block, 'azimuth', pairs)  11.4 us
    ppermute x15, waiting for transfers between devices, exchange(): return lax.ppermute(block, 'azimuth', pairs)  8.7 us
    pallas_call x2, Pallas kernels, mlp(): pl.pallas_call(functools.partial(mlp_kernel, count, half, sent, chunks),...  5.46 us
    ppermute x4, starting transfers between devices, halo(): blocks.append(lax.ppermute(block, ('polar', 'azimuth'), pairs))  5.15 us
    unnamed x18, local copies, waits for them, and re-layouts  2.77 us
    pallas_call x2, Pallas kernels, finish(): pl.pallas_call(functools.partial(finish_kernel, count, len(halos)), in_sp...  2.57 us
    pallas_call x2, Pallas kernels, add_chunk(): pl.pallas_call(functools.partial(add_kernel, count, chunk, [k for k, _ in...  2.47 us
    pallas_call x2, Pallas kernels, own_terms(): pl.pallas_call(functools.partial(own_kernel, start), in_specs=[pl.BlockSp...  1.71 us
  transfers between devices with their start and end apart: 19, of which 7 were waited for; matrix products, arithmetic and copies ran while one was open for 0% of the time, Pallas kernels for 24%

profile of v5, /device:TPU:1, one launch (start us, length us, event | category | flops | bytes accessed | tf_op | source)
XLA Modules:
  0.0 45.3 jit_solution(1942056553898703234)
XLA Ops:
  0.0 0.0 copy-start.1
  0.0 0.0 copy-start.6
  0.0 1.4 %copy.17.grad_ref = bf16[4,180,640]{2,1,0:T(8,128)(2,1)S(1)} copy(bf16[4,180,640]{2,0,1:T(4,128)(2,1)} %param.11) | data formatting | bytes 1843200 | tf_op args[1]
  1.5 1.3 %copy.14.conv_ref = bf16[4,180,640]{2,1,0:T(8,128)(2,1)S(1)} copy(bf16[4,180,640]{2,0,1:T(4,128)(2,1)} %param.10) | data formatting | bytes 1843200 | tf_op args[0]
  2.8 0.0 copy-done.1
  2.8 0.0 copy-done.6
  2.8 0.0 copy-done
  2.8 2.7 %mlp.2 = (bf16[160,384]{1,0:T(8,128)(2,1)S(1)}, bf16[160,384]{1,0:T(8,128)(2,1)S(1)}, bf16[160,384]{1,0:T(8,128)(2,1)S(1)}, bf16[160,384]{1,0:T(8,128)(2,1)S(1)}) custom-call(bf16[4,180,640]{2,1,0:T(8,128)(2,1)S(1)} %copy.14.conv_ref, bf16[4,180,640]{2,1,0:T(8,128)(2,1)S(1)} %copy.17.grad_ref, bf16[640,1280]{1,0:T(8,128)(2,1)S(1)} %copy-done, ...), custom_call_target="tpu_custom_call" | custom-call | tf_op jit(solution)/shard_map/mlp/pallas_call | solution.py:165
  5.5 2.1 %collective-permute-start.3 = (bf16[160,384]{1,0:T(8,128)(2,1)S(1)}, bf16[160,384]{1,0:T(8,128)(2,1)S(1)}, u32[]{:S(2)}, u32[]{:S(2)}) collective-permute-start(bf16[160,384]{1,0:T(8,128)(2,1)S(1)} %get-tuple-element.44), channel_id=1, source_target_pairs={{0,2},{1,3},{2,0},{3,1},{4,6},{5,7},{6,4},{7,5},{8,10},{9,11},{10,... | collective-permute-start | bytes 368648 | tf_op jit(solution)/shard_map/ppermute | solution.py:40
  7.6 0.6 %collective-permute-start.4 = (bf16[160,384]{1,0:T(8,128)(2,1)S(1)}, bf16[160,384]{1,0:T(8,128)(2,1)S(1)}, u32[]{:S(2)}, u32[]{:S(2)}) collective-permute-start(bf16[160,384]{1,0:T(8,128)(2,1)S(1)} %get-tuple-element.45), channel_id=1, source_target_pairs={{0,3},{1,2},{2,1},{3,0},{4,7},{5,6},{6,5},{7,4},{8,11},{9,10},{10,... | collective-permute-start | bytes 368648 | tf_op jit(solution)/shard_map/ppermute | solution.py:40
  8.3 0.3 collective-permute-start.5
  8.6 0.0 copy-start.7
  8.6 2.7 %mlp.3 = (bf16[160,384]{1,0:T(8,128)(2,1)S(1)}, bf16[96,384]{1,0:T(8,128)(2,1)S(1)}, bf16[96,384]{1,0:T(8,128)(2,1)S(1)}, bf16[96,384]{1,0:T(8,128)(2,1)S(1)}, b...) custom-call(bf16[4,180,640]{2,1,0:T(8,128)(2,1)S(1)} %copy.14.conv_ref, ...), custom_call_target="tpu_custom_call" | custom-call | tf_op jit(solution)/shard_map/mlp/pallas_call | solution.py:165
  11.4 1.4 %collective-permute-start.6 = (bf16[96,384]{1,0:T(8,128)(2,1)S(1)}, bf16[96,384]{1,0:T(8,128)(2,1)S(1)}, u32[]{:S(2)}, u32[]{:S(2)}) collective-permute-start(bf16[96,384]{1,0:T(8,128)(2,1)S(1)} %get-tuple-element.48), channel_id=1, source_target_pairs={{0,2},{1,3},{2,0},{3,1},{4,6},{5,7},{6,4},{7,5},{8,10},{9,11},{10,... | collective-permute-start | bytes 221192 | tf_op jit(solution)/shard_map/ppermute | solution.py:40
  12.8 0.4 collective-permute-start.7
  13.2 0.0 collective-permute-done.3.refs_0_
  13.2 0.3 collective-permute-start.8
  13.6 0.0 copy-done.2
  13.6 0.0 copy-done.3
  13.6 0.0 copy-done.4
  13.6 0.0 copy-done.5
  13.6 0.0 copy-done.7
  13.6 0.7 %prepare.1 = (bf16[10,32,768]{2,1,0:T(8,128)(2,1)S(1)}, s32[10,32]{1,0:T(8,128)S(1)}, bf16[4,320,640]{2,1,0:T(8,128)(2,1)S(1)}, bf16[768,640]{1,0:T(8,128)(2,1)S...) custom-call(f32[9,640]{1,0:T(8,128)S(1)} %copy-done.5, bf16[9,16,640]{2,1,0:T(8,128)(2,1)S(1)} %copy-done.4, ...), custom_call_target="tpu_custom_call" | custom-call | tf_op jit(solution)/shard_map/prepare/pallas_call | solution.py:519
  14.3 0.0 collective-permute-done.4.refs_1_
  14.3 0.0 collective-permute-done.5.refs_3_
  14.3 0.7 %analysis_early.1 = (f32[2,160,640]{2,1,0:T(8,128)S(1)}, bf16[2,160,640]{2,1,0:T(8,128)(2,1)S(1)}) custom-call(bf16[160,384]{1,0:T(8,128)(2,1)S(1)} %collective-permute-done.3.refs_0_, bf16[160,384]{1,0:T(8,128)(2,1)S(1)} %collective-permute-done.4.refs_1_, bf16[160,384]{1,0:T(8,128)(2,1)S(1)} %get-tuple-element.38.rest_0_.refs_2_, ...), custom_call_target="tpu_custom_call" | custom-call | tf_op jit(solution)/shard_map/analysis_early/pallas_call | solution.py:215
  15.0 0.2 collective-permute-done.6.refs_0_
  15.2 2.4 %collective-permute-done.7.refs_1_ = bf16[96,384]{1,0:T(8,128)(2,1)S(1)} collective-permute-done((bf16[96,384]{1,0:T(8,128)(2,1)S(1)}, bf16[96,384]{1,0:T(8,128)(2,1)S(1)}, u32[]{:S(2)}, u32[]{:S(2)}) %collective-permute-start.7) | collective-permute-done | bytes 73760 | tf_op jit(solution)/shard_map/ppermute | solution.py:40
  17.6 0.0 collective-permute-done.8.refs_3_
  17.6 0.7 %analysis.2 = (f32[2,96,640]{2,1,0:T(8,128)S(1)}, bf16[3,96,640]{2,1,0:T(8,128)(2,1)S(1)}, bf16[3,96,640]{2,1,0:T(8,128)(2,1)S(1)}) custom-call(bf16[96,384]{1,0:T(8,128)(2,1)S(1)} %collective-permute-done.6.refs_0_, bf16[96,384]{1,0:T(8,128)(2,1)S(1)} %collective-permute-done.7.refs_1_, bf16[160,384]{1,0:T(8,128)(2,1)S(1)} %get-tuple-element.41.refs_2_, ...), custom_call_target="tpu_custom_call" | custom-call | tf_op jit(solution)/shard_map/analysis/pallas_call | solution.py:259
  18.3 1.4 %collective-permute-start.14 = (bf16[3,96,640]{2,1,0:T(8,128)(2,1)S(1)}, bf16[3,96,640]{2,1,0:T(8,128)(2,1)S(1)}, u32[]{:S(2)}, u32[]{:S(2)}) collective-permute-start(bf16[3,96,640]{2,1,0:T(8,128)(2,1)S(1)} %get-tuple-element.65), channel_id=1, source_target_pairs={{0,4},{1,5},{2,6},{3,7},{4,0},{5,1},{6,2},{7,3},{8,12},{9,13},{10,... | collective-permute-start | bytes 1105928 | tf_op jit(solution)/shard_map/ppermute | solution.py:541
  19.6 0.7 %collective-permute-start.15 = (bf16[3,96,640]{2,1,0:T(8,128)(2,1)S(1)}, bf16[3,96,640]{2,1,0:T(8,128)(2,1)S(1)}, u32[]{:S(2)}, u32[]{:S(2)}) collective-permute-start(bf16[3,96,640]{2,1,0:T(8,128)(2,1)S(1)} %get-tuple-element.66), channel_id=1, source_target_pairs={{0,1},{1,0},{2,3},{3,2},{4,8},{5,9},{6,10},{7,11},{8,4},{9,5},{10,... | collective-permute-start | bytes 1105928 | tf_op jit(solution)/shard_map/ppermute | solution.py:541
  20.4 0.3 collective-permute-start
  20.7 1.3 %collective-permute-start.1 = (bf16[64,384]{1,0:T(8,128)(2,1)S(1)}, bf16[64,384]{1,0:T(8,128)(2,1)S(1)}, u32[]{:S(2)}, u32[]{:S(2)}) collective-permute-start(bf16[64,384]{1,0:T(8,128)(2,1)S(1)} %get-tuple-element.40), channel_id=1, source_target_pairs={{0,3},{1,2},{2,1},{3,0},{4,7},{5,6},{6,5},{7,4},{8,11},{9,10},{10,... | collective-permute-start | bytes 147464 | tf_op jit(solution)/shard_map/ppermute | solution.py:40
  22.0 0.2 collective-permute-start.2
  22.2 1.0 %own_terms.2.refs_6_.part_ref = f32[4,96,640]{2,1,0:T(8,128)S(1)} custom-call(f32[2,96,640]{2,1,0:T(8,128)S(1)} %get-tuple-element.51.own_ref, f32[96,32]{1,0:T(8,128)S(1)} %get-tuple-element.52.weight_ref.refs_1_, s32[10,32]{1,0:T(8,128)S(1)} %get-tuple-element.53.target_ref.refs_3_.refs_2_, ...), custom_call_target="tpu_custom_call" | custom-call | tf_op jit(solution)/shard_map/own_terms/pallas_call | solution.py:316
  23.3 0.5 %collective-permute-done.refs_0_ = bf16[64,384]{1,0:T(8,128)(2,1)S(1)} collective-permute-done((bf16[64,384]{1,0:T(8,128)(2,1)S(1)}, bf16[64,384]{1,0:T(8,128)(2,1)S(1)}, u32[]{:S(2)}, u32[]{:S(2)}) %collective-permute-start) | collective-permute-done | bytes 49184 | tf_op jit(solution)/shard_map/ppermute | solution.py:40
  23.7 1.4 %collective-permute-done.1.refs_1_ = bf16[64,384]{1,0:T(8,128)(2,1)S(1)} collective-permute-done((bf16[64,384]{1,0:T(8,128)(2,1)S(1)}, bf16[64,384]{1,0:T(8,128)(2,1)S(1)}, u32[]{:S(2)}, u32[]{:S(2)}) %collective-permute-start.1) | collective-permute-done | bytes 49184 | tf_op jit(solution)/shard_map/ppermute | solution.py:40
  25.2 0.0 collective-permute-done.2.refs_3_
  25.2 0.6 %analysis.3 = (f32[2,64,640]{2,1,0:T(8,128)S(1)}, bf16[3,64,640]{2,1,0:T(8,128)(2,1)S(1)}, bf16[3,64,640]{2,1,0:T(8,128)(2,1)S(1)}) custom-call(bf16[64,384]{1,0:T(8,128)(2,1)S(1)} %collective-permute-done.refs_0_, bf16[64,384]{1,0:T(8,128)(2,1)S(1)} %collective-permute-done.1.refs_1_, bf16[160,384]{1,0:T(8,128)(2,1)S(1)} %get-tuple-element.41.refs_2_, ...), custom_call_target="tpu_custom_call" | custom-call | tf_op jit(solution)/shard_map/analysis/pallas_call | solution.py:259
  25.8 2.9 %collective-permute-start.9 = (bf16[3,64,640]{2,1,0:T(8,128)(2,1)S(1)}, bf16[3,64,640]{2,1,0:T(8,128)(2,1)S(1)}, u32[]{:S(2)}, u32[]{:S(2)}) collective-permute-start(bf16[3,64,640]{2,1,0:T(8,128)(2,1)S(1)} %get-tuple-element.58), channel_id=1, source_target_pairs={{0,4},{1,5},{2,6},{3,7},{4,0},{5,1},{6,2},{7,3},{8,12},{9,13},{10,... | collective-permute-start | bytes 737288 | tf_op jit(solution)/shard_map/ppermute | solution.py:541
  28.7 0.2 collective-permute-start.10
  28.8 0.7 %own_terms.3.part_ref.rest_0_ = f32[4,64,640]{2,1,0:T(8,128)S(1)} custom-call(f32[2,64,640]{2,1,0:T(8,128)S(1)} %get-tuple-element.56.own_ref, f32[64,32]{1,0:T(8,128)S(1)} %get-tuple-element.57.weight_ref.refs_2_, s32[10,32]{1,0:T(8,128)S(1)} %get-tuple-element.53.target_ref.refs_3_.refs_2_, ...), custom_call_target="tpu_custom_call" | custom-call | tf_op jit(solution)/shard_map/own_terms/pallas_call | solution.py:316
  29.5 0.0 collective-permute-done.14.first_ref
  29.5 0.5 %side_terms.1.part_ref = f32[4,96,640]{2,1,0:T(8,128)S(1)} custom-call(f32[4,96,640]{2,1,0:T(8,128)S(1)} %own_terms.2.refs_6_.part_ref, bf16[3,96,640]{2,1,0:T(8,128)(2,1)S(1)} %collective-permute-done.14.first_ref, f32[96,32]{1,0:T(8,128)S(1)} %get-tuple-element.52.weight_ref.refs_1_, s32[10,32]{1,0:T(8,128)S(1)} %get-tuple-element.53.target_ref.refs_3_.refs_2_, ...), custom_call_target="tpu_custom_call" | custom-call | tf_op jit(solution)/shard_map/side_terms/pallas_call | solution.py:358
  30.1 0.0 collective-permute-done.15.refs_0_
  30.1 1.4 %finish.3 = (bf16[180,384]{1,0:T(8,128)(2,1)S(1)}, bf16[180,384]{1,0:T(8,128)(2,1)S(1)}, bf16[180,384]{1,0:T(8,128)(2,1)S(1)}, bf16[180,384]{1,0:T(8,128)(2,1)S(1)}) custom-call(f32[4,96,640]{2,1,0:T(8,128)S(1)} %side_terms.1.part_ref, bf16[3,96,640]{2,1,0:T(8,128)(2,1)S(1)} %collective-permute-done.15.refs_0_, ...), custom_call_target="tpu_custom_call" | custom-call | tf_op jit(solution)/shard_map/finish/pallas_call | solution.py:392
  31.5 0.9 %collective-permute-start.16 = (bf16[180,384]{1,0:T(8,128)(2,1)S(1)}, bf16[180,384]{1,0:T(8,128)(2,1)S(1)}, u32[]{:S(2)}, u32[]{:S(2)}) collective-permute-start(bf16[180,384]{1,0:T(8,128)(2,1)S(1)} %get-tuple-element.67), channel_id=1, source_target_pairs={{0,2},{1,3},{2,0},{3,1},{4,6},{5,7},{6,4},{7,5},{8,10},{9,11},{10,... | collective-permute-start | bytes 414728 | tf_op jit(solution)/shard_map/ppermute | solution.py:40
  32.4 1.2 %collective-permute-start.17 = (bf16[180,384]{1,0:T(8,128)(2,1)S(1)}, bf16[180,384]{1,0:T(8,128)(2,1)S(1)}, u32[]{:S(2)}, u32[]{:S(2)}) collective-permute-start(bf16[180,384]{1,0:T(8,128)(2,1)S(1)} %get-tuple-element.68), channel_id=1, source_target_pairs={{0,3},{1,2},{2,1},{3,0},{4,7},{5,6},{6,5},{7,4},{8,11},{9,10},{10,... | collective-permute-start | bytes 414728 | tf_op jit(solution)/shard_map/ppermute | solution.py:40
  33.6 0.0 collective-permute-start.18
  33.6 1.5 %collective-permute-done.9.refs_0_ = bf16[3,64,640]{2,1,0:T(8,128)(2,1)S(1)} collective-permute-done((bf16[3,64,640]{2,1,0:T(8,128)(2,1)S(1)}, bf16[3,64,640]{2,1,0:T(8,128)(2,1)S(1)}, u32[]{:S(2)}, u32[]{:S(2)}) %collective-permute-start.9) | collective-permute-done | bytes 245792 | tf_op jit(solution)/shard_map/ppermute | solution.py:541
  35.1 0.0 collective-permute-done.10.refs_1_
  35.1 1.1 %finish.2 = (bf16[180,256]{1,0:T(8,128)(2,1)S(1)}, bf16[180,256]{1,0:T(8,128)(2,1)S(1)}, bf16[180,256]{1,0:T(8,128)(2,1)S(1)}, bf16[180,256]{1,0:T(8,128)(2,1)S(1)}) custom-call(f32[4,64,640]{2,1,0:T(8,128)S(1)} %own_terms.3.part_ref.rest_0_, bf16[3,64,640]{2,1,0:T(8,128)(2,1)S(1)} %collective-permute-done.9.refs_0_, ...), custom_call_target="tpu_custom_call" | custom-call | tf_op jit(solution)/shard_map/finish/pallas_call | solution.py:392
  36.3 0.1 collective-permute-start.11
  36.3 2.1 %collective-permute-start.12 = (bf16[180,256]{1,0:T(8,128)(2,1)S(1)}, bf16[180,256]{1,0:T(8,128)(2,1)S(1)}, u32[]{:S(2)}, u32[]{:S(2)}) collective-permute-start(bf16[180,256]{1,0:T(8,128)(2,1)S(1)} %get-tuple-element.62), channel_id=1, source_target_pairs={{0,3},{1,2},{2,1},{3,0},{4,7},{5,6},{6,5},{7,4},{8,11},{9,10},{10,... | collective-permute-start | bytes 276488 | tf_op jit(solution)/shard_map/ppermute | solution.py:40
  38.4 0.0 collective-permute-done.16.refs_0_
  38.4 0.1 collective-permute-start.13
  38.5 2.3 %collective-permute-done.17.refs_1_ = bf16[180,384]{1,0:T(8,128)(2,1)S(1)} collective-permute-done((bf16[180,384]{1,0:T(8,128)(2,1)S(1)}, bf16[180,384]{1,0:T(8,128)(2,1)S(1)}, u32[]{:S(2)}, u32[]{:S(2)}) %collective-permute-start.17) | collective-permute-done | bytes 138272 | tf_op jit(solution)/shard_map/ppermute | solution.py:40
  40.8 0.0 collective-permute-done.18.refs_3_
  40.8 1.4 %add_chunk.2.refs_4_ = bf16[180,4,640]{2,1,0:T(4,128)(2,1)} custom-call(bf16[4,180,640]{2,1,0:T(8,128)(2,1)S(1)} %copy.17.grad_ref, bf16[180,384]{1,0:T(8,128)(2,1)S(1)} %collective-permute-done.16.refs_0_, bf16[180,384]{1,0:T(8,128)(2,1)S(1)} %collective-permute-done.17.refs_1_, bf16[180,384]{1,0:T(8,128)(2,1)S(1)} %get-tuple-element.69.refs_2_, ...), custom_call_target="tpu_custom_call" | custom-call | tf_op jit(solution)/shard_map/add_chunk/pallas_call | solution.py:443
  42.2 0.0 collective-permute-done.11.refs_0_
  42.3 1.8 %collective-permute-done.12.refs_1_ = bf16[180,256]{1,0:T(8,128)(2,1)S(1)} collective-permute-done((bf16[180,256]{1,0:T(8,128)(2,1)S(1)}, bf16[180,256]{1,0:T(8,128)(2,1)S(1)}, u32[]{:S(2)}, u32[]{:S(2)}) %collective-permute-start.12) | collective-permute-done | bytes 92192 | tf_op jit(solution)/shard_map/ppermute | solution.py:40
  44.1 0.0 collective-permute-done.13.refs_3_
  44.1 1.1 %add_chunk.3 = bf16[180,4,640]{2,1,0:T(4,128)(2,1)} custom-call(bf16[4,180,640]{2,1,0:T(8,128)(2,1)S(1)} %copy.17.grad_ref, bf16[180,256]{1,0:T(8,128)(2,1)S(1)} %collective-permute-done.11.refs_0_, bf16[180,256]{1,0:T(8,128)(2,1)S(1)} %collective-permute-done.12.refs_1_, ...), custom_call_target="tpu_custom_call", output_to_operand_aliasing={{}: (5, {})} | custom-call | tf_op jit(solution)/shard_map/add_chunk/pallas_call | solution.py:443
  (5 shorter events, 0.0 us)
Async XLA Ops:
  0.0 2.8 %copy-start.1 = (bf16[1280,640]{1,0:T(8,128)(2,1)S(1)}, bf16[1280,640]{1,0:T(8,128)(2,1)}, u32[]{:S(2)}) copy-start(bf16[1280,640]{1,0:T(8,128)(2,1)} %wout_ref.3) | copy-start | bytes 4915204
  0.0 2.8 %copy-start.6 = (f32[1280]{0:T(1024)S(1)}, f32[1280]{0:T(1024)}, u32[]{:S(2)}) copy-start(f32[1280]{0:T(1024)} %bias_ref.3) | copy-start | bytes 15364
  0.0 2.8 %copy-start = (bf16[640,1280]{1,0:T(8,128)(2,1)S(1)}, bf16[640,1280]{1,0:T(8,128)(2,1)}, u32[]{:S(2)}) copy-start(bf16[640,1280]{1,0:T(8,128)(2,1)} %win_ref.3) | copy-start | bytes 4915204
  5.5 7.7 %collective-permute-start.3 = (bf16[160,384]{1,0:T(8,128)(2,1)S(1)}, bf16[160,384]{1,0:T(8,128)(2,1)S(1)}, u32[]{:S(2)}, u32[]{:S(2)}) collective-permute-start(bf16[160,384]{1,0:T(8,128)(2,1)S(1)} %get-tuple-element.44), channel_id=1, source_target_pairs={{0,2},{1,3},{2,0},{3,1},{4,6},{5,7},{6,4},{7,5},{8,10},{9,11},{10,... | collective-permute-start | bytes 368648 | tf_op jit(solution)/shard_map/ppermute | solution.py:40
  7.6 6.6 %collective-permute-start.4 = (bf16[160,384]{1,0:T(8,128)(2,1)S(1)}, bf16[160,384]{1,0:T(8,128)(2,1)S(1)}, u32[]{:S(2)}, u32[]{:S(2)}) collective-permute-start(bf16[160,384]{1,0:T(8,128)(2,1)S(1)} %get-tuple-element.45), channel_id=1, source_target_pairs={{0,3},{1,2},{2,1},{3,0},{4,7},{5,6},{6,5},{7,4},{8,11},{9,10},{10,... | collective-permute-start | bytes 368648 | tf_op jit(solution)/shard_map/ppermute | solution.py:40
  8.3 6.0 %collective-permute-start.5 = (bf16[160,384]{1,0:T(8,128)(2,1)S(1)}, bf16[160,384]{1,0:T(8,128)(2,1)S(1)}, u32[]{:S(2)}, u32[]{:S(2)}) collective-permute-start(bf16[160,384]{1,0:T(8,128)(2,1)S(1)} %get-tuple-element.46), channel_id=1, source_target_pairs={{0,1},{1,0},{2,3},{3,2},{4,5},{5,4},{6,7},{7,6},{8,9},{9,8},{10,11... | collective-permute-start | bytes 368648 | tf_op jit(solution)/shard_map/ppermute | solution.py:40
  8.6 5.0 %copy-start.2 = (bf16[4,320,640]{2,1,0:T(8,128)(2,1)S(1)}, bf16[4,320,640]{2,1,0:T(8,128)(2,1)}, u32[]{:S(2)}) copy-start(bf16[4,320,640]{2,1,0:T(8,128)(2,1)} %constant.4.clone.forth_ref) | copy-start | bytes 4915204
  8.6 5.0 %copy-start.3 = (bf16[768,640]{1,0:T(8,128)(2,1)S(1)}, bf16[768,640]{1,0:T(8,128)(2,1)}, u32[]{:S(2)}) copy-start(bf16[768,640]{1,0:T(8,128)(2,1)} %constant.5.clone.back_ref) | copy-start | bytes 2949124
  8.6 5.0 %copy-start.4 = (bf16[9,16,640]{2,1,0:T(8,128)(2,1)S(1)}, bf16[9,16,640]{2,1,0:T(8,128)(2,1)}, u32[]{:S(2)}) copy-start(bf16[9,16,640]{2,1,0:T(8,128)(2,1)} %filt_ref.1) | copy-start | bytes 552964
  8.6 5.0 %copy-start.5 = (f32[9,640]{1,0:T(8,128)S(1)}, f32[9,640]{1,0:T(8,128)}, u32[]{:S(2)}) copy-start(f32[9,640]{1,0:T(8,128)} %weight_ref.1) | copy-start | bytes 69124
  8.6 5.0 %copy-start.7 = (s32[16,9]{1,0:T(8,128)S(1)}, s32[16,9]{1,0:T(8,128)}, u32[]{:S(2)}) copy-start(s32[16,9]{1,0:T(8,128)} %offset_ref.1) | copy-start | bytes 1732
  11.4 3.8 %collective-permute-start.6 = (bf16[96,384]{1,0:T(8,128)(2,1)S(1)}, bf16[96,384]{1,0:T(8,128)(2,1)S(1)}, u32[]{:S(2)}, u32[]{:S(2)}) collective-permute-start(bf16[96,384]{1,0:T(8,128)(2,1)S(1)} %get-tuple-element.48), channel_id=1, source_target_pairs={{0,2},{1,3},{2,0},{3,1},{4,6},{5,7},{6,4},{7,5},{8,10},{9,11},{10,... | collective-permute-start | bytes 221192 | tf_op jit(solution)/shard_map/ppermute | solution.py:40
  12.8 4.8 %collective-permute-start.7 = (bf16[96,384]{1,0:T(8,128)(2,1)S(1)}, bf16[96,384]{1,0:T(8,128)(2,1)S(1)}, u32[]{:S(2)}, u32[]{:S(2)}) collective-permute-start(bf16[96,384]{1,0:T(8,128)(2,1)S(1)} %get-tuple-element.49), channel_id=1, source_target_pairs={{0,3},{1,2},{2,1},{3,0},{4,7},{5,6},{6,5},{7,4},{8,11},{9,10},{10,... | collective-permute-start | bytes 221192 | tf_op jit(solution)/shard_map/ppermute | solution.py:40
  13.2 4.4 %collective-permute-start.8 = (bf16[96,384]{1,0:T(8,128)(2,1)S(1)}, bf16[96,384]{1,0:T(8,128)(2,1)S(1)}, u32[]{:S(2)}, u32[]{:S(2)}) collective-permute-start(bf16[96,384]{1,0:T(8,128)(2,1)S(1)} %get-tuple-element.50), channel_id=1, source_target_pairs={{0,1},{1,0},{2,3},{3,2},{4,5},{5,4},{6,7},{7,6},{8,9},{9,8},{10,11... | collective-permute-start | bytes 221192 | tf_op jit(solution)/shard_map/ppermute | solution.py:40
  18.3 11.3 %collective-permute-start.14 = (bf16[3,96,640]{2,1,0:T(8,128)(2,1)S(1)}, bf16[3,96,640]{2,1,0:T(8,128)(2,1)S(1)}, u32[]{:S(2)}, u32[]{:S(2)}) collective-permute-start(bf16[3,96,640]{2,1,0:T(8,128)(2,1)S(1)} %get-tuple-element.65), channel_id=1, source_target_pairs={{0,4},{1,5},{2,6},{3,7},{4,0},{5,1},{6,2},{7,3},{8,12},{9,13},{10,... | collective-permute-start | bytes 1105928 | tf_op jit(solution)/shard_map/ppermute | solution.py:541
  19.6 10.4 %collective-permute-start.15 = (bf16[3,96,640]{2,1,0:T(8,128)(2,1)S(1)}, bf16[3,96,640]{2,1,0:T(8,128)(2,1)S(1)}, u32[]{:S(2)}, u32[]{:S(2)}) collective-permute-start(bf16[3,96,640]{2,1,0:T(8,128)(2,1)S(1)} %get-tuple-element.66), channel_id=1, source_target_pairs={{0,1},{1,0},{2,3},{3,2},{4,8},{5,9},{6,10},{7,11},{8,4},{9,5},{10,... | collective-permute-start | bytes 1105928 | tf_op jit(solution)/shard_map/ppermute | solution.py:541
  20.4 3.4 %collective-permute-start = (bf16[64,384]{1,0:T(8,128)(2,1)S(1)}, bf16[64,384]{1,0:T(8,128)(2,1)S(1)}, u32[]{:S(2)}, u32[]{:S(2)}) collective-permute-start(bf16[64,384]{1,0:T(8,128)(2,1)S(1)} %get-tuple-element.39), channel_id=1, source_target_pairs={{0,2},{1,3},{2,0},{3,1},{4,6},{5,7},{6,4},{7,5},{8,10},{9,11},{10,... | collective-permute-start | bytes 147464 | tf_op jit(solution)/shard_map/ppermute | solution.py:40
  20.7 4.5 %collective-permute-start.1 = (bf16[64,384]{1,0:T(8,128)(2,1)S(1)}, bf16[64,384]{1,0:T(8,128)(2,1)S(1)}, u32[]{:S(2)}, u32[]{:S(2)}) collective-permute-start(bf16[64,384]{1,0:T(8,128)(2,1)S(1)} %get-tuple-element.40), channel_id=1, source_target_pairs={{0,3},{1,2},{2,1},{3,0},{4,7},{5,6},{6,5},{7,4},{8,11},{9,10},{10,... | collective-permute-start | bytes 147464 | tf_op jit(solution)/shard_map/ppermute | solution.py:40
  22.0 3.2 %collective-permute-start.2 = (bf16[64,384]{1,0:T(8,128)(2,1)S(1)}, bf16[64,384]{1,0:T(8,128)(2,1)S(1)}, u32[]{:S(2)}, u32[]{:S(2)}) collective-permute-start(bf16[64,384]{1,0:T(8,128)(2,1)S(1)} %get-tuple-element.42), channel_id=1, source_target_pairs={{0,1},{1,0},{2,3},{3,2},{4,5},{5,4},{6,7},{7,6},{8,9},{9,8},{10,11... | collective-permute-start | bytes 147464 | tf_op jit(solution)/shard_map/ppermute | solution.py:40
  25.8 9.3 %collective-permute-start.9 = (bf16[3,64,640]{2,1,0:T(8,128)(2,1)S(1)}, bf16[3,64,640]{2,1,0:T(8,128)(2,1)S(1)}, u32[]{:S(2)}, u32[]{:S(2)}) collective-permute-start(bf16[3,64,640]{2,1,0:T(8,128)(2,1)S(1)} %get-tuple-element.58), channel_id=1, source_target_pairs={{0,4},{1,5},{2,6},{3,7},{4,0},{5,1},{6,2},{7,3},{8,12},{9,13},{10,... | collective-permute-start | bytes 737288 | tf_op jit(solution)/shard_map/ppermute | solution.py:541
  28.7 6.5 %collective-permute-start.10 = (bf16[3,64,640]{2,1,0:T(8,128)(2,1)S(1)}, bf16[3,64,640]{2,1,0:T(8,128)(2,1)S(1)}, u32[]{:S(2)}, u32[]{:S(2)}) collective-permute-start(bf16[3,64,640]{2,1,0:T(8,128)(2,1)S(1)} %get-tuple-element.59), channel_id=1, source_target_pairs={{0,1},{1,0},{2,3},{3,2},{4,8},{5,9},{6,10},{7,11},{8,4},{9,5},{10,... | collective-permute-start | bytes 737288 | tf_op jit(solution)/shard_map/ppermute | solution.py:541
  31.5 6.9 %collective-permute-start.16 = (bf16[180,384]{1,0:T(8,128)(2,1)S(1)}, bf16[180,384]{1,0:T(8,128)(2,1)S(1)}, u32[]{:S(2)}, u32[]{:S(2)}) collective-permute-start(bf16[180,384]{1,0:T(8,128)(2,1)S(1)} %get-tuple-element.67), channel_id=1, source_target_pairs={{0,2},{1,3},{2,0},{3,1},{4,6},{5,7},{6,4},{7,5},{8,10},{9,11},{10,... | collective-permute-start | bytes 414728 | tf_op jit(solution)/shard_map/ppermute | solution.py:40
  32.4 8.4 %collective-permute-start.17 = (bf16[180,384]{1,0:T(8,128)(2,1)S(1)}, bf16[180,384]{1,0:T(8,128)(2,1)S(1)}, u32[]{:S(2)}, u32[]{:S(2)}) collective-permute-start(bf16[180,384]{1,0:T(8,128)(2,1)S(1)} %get-tuple-element.68), channel_id=1, source_target_pairs={{0,3},{1,2},{2,1},{3,0},{4,7},{5,6},{6,5},{7,4},{8,11},{9,10},{10,... | collective-permute-start | bytes 414728 | tf_op jit(solution)/shard_map/ppermute | solution.py:40
  33.6 7.3 %collective-permute-start.18 = (bf16[180,384]{1,0:T(8,128)(2,1)S(1)}, bf16[180,384]{1,0:T(8,128)(2,1)S(1)}, u32[]{:S(2)}, u32[]{:S(2)}) collective-permute-start(bf16[180,384]{1,0:T(8,128)(2,1)S(1)} %get-tuple-element.70), channel_id=1, source_target_pairs={{0,1},{1,0},{2,3},{3,2},{4,5},{5,4},{6,7},{7,6},{8,9},{9,8},{10,11... | collective-permute-start | bytes 414728 | tf_op jit(solution)/shard_map/ppermute | solution.py:40
  36.3 6.0 %collective-permute-start.11 = (bf16[180,256]{1,0:T(8,128)(2,1)S(1)}, bf16[180,256]{1,0:T(8,128)(2,1)S(1)}, u32[]{:S(2)}, u32[]{:S(2)}) collective-permute-start(bf16[180,256]{1,0:T(8,128)(2,1)S(1)} %get-tuple-element.61), channel_id=1, source_target_pairs={{0,2},{1,3},{2,0},{3,1},{4,6},{5,7},{6,4},{7,5},{8,10},{9,11},{10,... | collective-permute-start | bytes 276488 | tf_op jit(solution)/shard_map/ppermute | solution.py:40
  36.3 7.8 %collective-permute-start.12 = (bf16[180,256]{1,0:T(8,128)(2,1)S(1)}, bf16[180,256]{1,0:T(8,128)(2,1)S(1)}, u32[]{:S(2)}, u32[]{:S(2)}) collective-permute-start(bf16[180,256]{1,0:T(8,128)(2,1)S(1)} %get-tuple-element.62), channel_id=1, source_target_pairs={{0,3},{1,2},{2,1},{3,0},{4,7},{5,6},{6,5},{7,4},{8,11},{9,10},{10,... | collective-permute-start | bytes 276488 | tf_op jit(solution)/shard_map/ppermute | solution.py:40
  38.4 5.7 %collective-permute-start.13 = (bf16[180,256]{1,0:T(8,128)(2,1)S(1)}, bf16[180,256]{1,0:T(8,128)(2,1)S(1)}, u32[]{:S(2)}, u32[]{:S(2)}) collective-permute-start(bf16[180,256]{1,0:T(8,128)(2,1)S(1)} %get-tuple-element.64), channel_id=1, source_target_pairs={{0,1},{1,0},{2,3},{3,2},{4,5},{5,4},{6,7},{7,6},{8,9},{9,8},{10,11... | collective-permute-start | bytes 276488 | tf_op jit(solution)/shard_map/ppermute | solution.py:40

commit v6 on v4

--- a/solution.py
+++ b/solution.py
@@ -396,54 +396,64 @@
     )(own, *halos, weight, target, filters, table)
 
 
-def add_kernel(count, chunk, steps, grad_ref, *refs):
+def add_kernel(count, chunk, steps, tiles, grad_ref, *refs):
     out_ref, tall_ref, done_ref, sems = refs[-4:]
     pieces = dict(zip(steps, refs))
-    tiles, part, rows, _ = done_ref.shape
+    _, part, rows, _ = done_ref.shape
     start, size = chunk
     me = lax.axis_index("azimuth")
 
-    def add(tile, mine):
+    def add(mine):
         order = [[k for k in range(count) if partner_static(mine, k, count, -1) == s][0] for s in range(count)]
-        lanes = range(tile * LANES, (tile + 1) * LANES)
-        for row in range(rows):
-            parts = []
-            for s in range(lanes[0] // size, lanes[-1] // size + 1):
-                low, high = max(lanes[0], s * size) - s * size, min(lanes[-1] + 1, (s + 1) * size) - s * size
-                parts.append(pieces[order[s]][:part, row * size + low : row * size + high])
-            conv = jnp.concatenate(parts, axis=1).astype(jnp.float32)
+        copies = []
+        for at, tile in enumerate(tiles[mine]):
+            lanes = range(tile * LANES, (tile + 1) * LANES)
             first = count * start + tile * LANES
-            total = grad_ref[row, :, first : first + LANES].astype(jnp.float32) + conv
-            tall_ref[tile, pl.ds(row, part, stride=rows), :] = total
-        done_ref[tile] = tall_ref[tile].reshape(part, rows, LANES).astype(jnp.bfloat16)
-
-    copies = []
-    for tile in range(tiles):
-        for mine in range(count):
-            pl.when(me == mine)(functools.partial(add, tile, mine))
-        lanes = pl.ds(count * start + tile * LANES, LANES)
-        copies.append(pltpu.make_async_copy(done_ref.at[tile], out_ref.at[:, :, lanes], sems.at[tile]))
-        copies[-1].start()
-    for copy in copies:
-        copy.wait()
-
-
-def add_chunk(grad_out, pieces, chunk, count, before):
+            for row in range(rows):
+                parts = []
+                for s in owners(tile, size):
+                    low, high = max(lanes[0], s * size) - s * size, min(lanes[-1] + 1, (s + 1) * size) - s * size
+                    parts.append(pieces[order[s]][:, row * size + low : row * size + high])
+                conv = jnp.concatenate(parts, axis=1).astype(jnp.float32)
+                total = grad_ref[row, :, first : first + LANES].astype(jnp.float32) + conv
+                tall_ref[at, pl.ds(row, part, stride=rows), :] = total
+            done_ref[at] = tall_ref[at].reshape(part, rows, LANES).astype(jnp.bfloat16)
+            copies.append(pltpu.make_async_copy(done_ref.at[at], out_ref.at[:, :, pl.ds(first, LANES)], sems.at[at]))
+            copies[-1].start()
+        for copy in copies:
+            copy.wait()
+
+    for mine in range(count):
+        pl.when(me == mine)(functools.partial(add, mine))
+
+
+def owners(tile, size):
+    return range(tile * LANES // size, ((tile + 1) * LANES - 1) // size + 1)
+
+
+def add_chunk(grad_out, pieces, chunk, count, tiles, before):
     rows, part, channels = grad_out.shape
-    start, size = chunk
-    tiles = count * size // LANES
-    pieces = sorted(pieces.items(), key=lambda item: item[0] <= NEAR)
+    number = max(len(some) for some in tiles)
+    needed = {
+        k
+        for mine in range(count)
+        for tile in tiles[mine]
+        for s in owners(tile, chunk[1])
+        for k in range(count)
+        if partner_static(mine, k, count, -1) == s
+    }
+    pieces = sorted(((k, pieces[k]) for k in needed), key=lambda item: item[0] <= NEAR)
     vmem = pl.BlockSpec(memory_space=VMEM)
     anywhere = pl.BlockSpec(memory_space=pl.ANY)
     return pl.pallas_call(
-        functools.partial(add_kernel, count, chunk, [k for k, _ in pieces]),
+        functools.partial(add_kernel, count, chunk, [k for k, _ in pieces], tiles),
         in_specs=[vmem] * (1 + len(pieces)) + [anywhere] * len(before),
         out_specs=anywhere,
         out_shape=jax.ShapeDtypeStruct((part, rows, channels), jnp.bfloat16),
         scratch_shapes=[
-            pltpu.VMEM((tiles, rows * part, LANES), jnp.float32),
-            pltpu.VMEM((tiles, part, rows, LANES), jnp.bfloat16),
-            pltpu.SemaphoreType.DMA((tiles,)),
+            pltpu.VMEM((number, rows * part, LANES), jnp.float32),
+            pltpu.VMEM((number, part, rows, LANES), jnp.bfloat16),
+            pltpu.SemaphoreType.DMA((number,)),
         ],
         input_output_aliases={1 + len(pieces): 0} if before else {},
         compiler_params=pltpu.CompilerParams(vmem_limit_bytes=12 * 2**20),
@@ -576,7 +586,14 @@
         returned[q] = {k: exchange(grids[k], k, count) for k in range(count)}
     total = []
     for q, chunk in enumerate(chunks):
-        total = [add_chunk(grad_out, returned[q], chunk, count, total)]
+        tiles = [list(range(count * chunk[1] // LANES)) for _ in range(count)]
+        if q == len(chunks) - 1:
+            chip = [{mine, partner_static(mine, NEAR, count, -1)} for mine in range(count)]
+            close = [[t for t in tiles[mine] if set(owners(t, chunk[1])) <= chip[mine]] for mine in range(count)]
+            if any(close):
+                total = [add_chunk(grad_out, returned[q], chunk, count, close, total)]
+                tiles = [[t for t in tiles[mine] if t not in close[mine]] for mine in range(count)]
+        total = [add_chunk(grad_out, returned[q], chunk, count, tiles, total)]
     return jnp.transpose(total[0], (1, 0, 2))
 
 

time: 45.3 us -> 45.1 us (level)
  waiting for transfers between devices: 10.4 us -> 9.46 us
  Pallas kernels: 15.1 us -> 15.6 us
    ppermute x15, waiting for transfers between devices: 8.68 us -> 7.74 us  [exchange(): return lax.ppermute(block, 'azimuth', pairs)]
    pallas_call x2 -> x3, Pallas kernels: 2.46 us -> 2.92 us  [add_chunk(): pl.pallas_call(functools.partial(add_kernel, count, chunk, [k for k, _ in...]
  transfers between devices with their start and end apart: 19 -> 19, of which waited for: 7 -> 7; matrix products, arithmetic and copies ran while one was open for 0% -> 0% of each run, Pallas kernels for 24% -> 25%
where the time goes in v6:
time: 45.1 us; the launch traced here: 44.9 us
  starting transfers between devices  16.8 us (37%)
  Pallas kernels  15.6 us (35%)
  waiting for transfers between devices  9.46 us (21%)
  local copies, waits for them, and re-layouts  2.77 us (6%)
    ppermute x15, starting transfers between devices, exchange(): return lax.ppermute(block, 'azimuth', pairs)  11.6 us
    ppermute x15, waiting for transfers between devices, exchange(): return lax.ppermute(block, 'azimuth', pairs)  7.74 us
    pallas_call x2, Pallas kernels, mlp(): pl.pallas_call(functools.partial(mlp_kernel, count, half, sent, chunks),...  5.5 us
    ppermute x4, starting transfers between devices, halo(): blocks.append(lax.ppermute(block, ('polar', 'azimuth'), pairs))  5.16 us
    pallas_call x3, Pallas kernels, add_chunk(): pl.pallas_call(functools.partial(add_kernel, count, chunk, [k for k, _ in...  2.92 us
    unnamed x18, local copies, waits for them, and re-layouts  2.77 us
    pallas_call x2, Pallas kernels, finish(): pl.pallas_call(functools.partial(finish_kernel, count, len(halos)), in_sp...  2.37 us
    ppermute x4, waiting for transfers between devices, halo(): blocks.append(lax.ppermute(block, ('polar', 'azimuth'), pairs))  1.72 us
  transfers between devices with their start and end apart: 19, of which 7 were waited for; matrix products, arithmetic and copies ran while one was open for 0% of the time, Pallas kernels for 25%

profile of v6, /device:TPU:1, one launch (start us, length us, event | category | flops | bytes accessed | tf_op | source)
XLA Modules:
  0.0 44.9 jit_solution(11497741594561188902)
XLA Ops:
  0.0 0.0 copy-start.1
  0.0 1.4 %copy.19.grad_ref = bf16[4,180,640]{2,1,0:T(8,128)(2,1)S(1)} copy(bf16[4,180,640]{2,0,1:T(4,128)(2,1)} %param.11) | data formatting | bytes 1843200 | tf_op args[1]
  1.5 1.3 %copy.15.conv_ref = bf16[4,180,640]{2,1,0:T(8,128)(2,1)S(1)} copy(bf16[4,180,640]{2,0,1:T(4,128)(2,1)} %param.10) | data formatting | bytes 1843200 | tf_op args[0]
  2.8 0.0 copy-done.1
  2.8 0.0 copy-done.6
  2.8 0.0 copy-done
  2.8 2.8 %mlp.2 = (bf16[160,384]{1,0:T(8,128)(2,1)S(1)}, bf16[160,384]{1,0:T(8,128)(2,1)S(1)}, bf16[160,384]{1,0:T(8,128)(2,1)S(1)}, bf16[160,384]{1,0:T(8,128)(2,1)S(1)}) custom-call(bf16[4,180,640]{2,1,0:T(8,128)(2,1)S(1)} %copy.15.conv_ref, bf16[4,180,640]{2,1,0:T(8,128)(2,1)S(1)} %copy.19.grad_ref, bf16[640,1280]{1,0:T(8,128)(2,1)S(1)} %copy-done, ...), custom_call_target="tpu_custom_call" | custom-call | tf_op jit(solution)/shard_map/mlp/pallas_call | solution.py:165
  5.5 2.1 %collective-permute-start.3 = (bf16[160,384]{1,0:T(8,128)(2,1)S(1)}, bf16[160,384]{1,0:T(8,128)(2,1)S(1)}, u32[]{:S(2)}, u32[]{:S(2)}) collective-permute-start(bf16[160,384]{1,0:T(8,128)(2,1)S(1)} %get-tuple-element.42), channel_id=1, source_target_pairs={{0,2},{1,3},{2,0},{3,1},{4,6},{5,7},{6,4},{7,5},{8,10},{9,11},{10,... | collective-permute-start | bytes 368648 | tf_op jit(solution)/shard_map/ppermute | solution.py:40
  7.7 0.6 %collective-permute-start.4 = (bf16[160,384]{1,0:T(8,128)(2,1)S(1)}, bf16[160,384]{1,0:T(8,128)(2,1)S(1)}, u32[]{:S(2)}, u32[]{:S(2)}) collective-permute-start(bf16[160,384]{1,0:T(8,128)(2,1)S(1)} %get-tuple-element.43), channel_id=1, source_target_pairs={{0,3},{1,2},{2,1},{3,0},{4,7},{5,6},{6,5},{7,4},{8,11},{9,10},{10,... | collective-permute-start | bytes 368648 | tf_op jit(solution)/shard_map/ppermute | solution.py:40
  8.3 0.3 collective-permute-start.5
  8.6 0.0 copy-start.7
  8.6 2.7 %mlp.3 = (bf16[160,384]{1,0:T(8,128)(2,1)S(1)}, bf16[96,384]{1,0:T(8,128)(2,1)S(1)}, bf16[96,384]{1,0:T(8,128)(2,1)S(1)}, bf16[96,384]{1,0:T(8,128)(2,1)S(1)}, b...) custom-call(bf16[4,180,640]{2,1,0:T(8,128)(2,1)S(1)} %copy.15.conv_ref, ...), custom_call_target="tpu_custom_call" | custom-call | tf_op jit(solution)/shard_map/mlp/pallas_call | solution.py:165
  11.4 1.5 %collective-permute-start.6 = (bf16[96,384]{1,0:T(8,128)(2,1)S(1)}, bf16[96,384]{1,0:T(8,128)(2,1)S(1)}, u32[]{:S(2)}, u32[]{:S(2)}) collective-permute-start(bf16[96,384]{1,0:T(8,128)(2,1)S(1)} %get-tuple-element.45), channel_id=1, source_target_pairs={{0,2},{1,3},{2,0},{3,1},{4,6},{5,7},{6,4},{7,5},{8,10},{9,11},{10,... | collective-permute-start | bytes 221192 | tf_op jit(solution)/shard_map/ppermute | solution.py:40
  12.8 0.4 collective-permute-start.7
  13.3 0.0 collective-permute-done.3.refs_0_
  13.3 0.3 collective-permute-start.8
  13.6 0.0 copy-done.2
  13.6 0.0 copy-done.3
  13.6 0.0 copy-done.4
  13.6 0.0 copy-done.5
  13.6 0.0 copy-done.7
  13.6 0.7 %prepare.1 = (bf16[10,32,768]{2,1,0:T(8,128)(2,1)S(1)}, s32[10,32]{1,0:T(8,128)S(1)}, bf16[4,320,640]{2,1,0:T(8,128)(2,1)S(1)}, bf16[768,640]{1,0:T(8,128)(2,1)S...) custom-call(f32[9,640]{1,0:T(8,128)S(1)} %copy-done.5, bf16[9,16,640]{2,1,0:T(8,128)(2,1)S(1)} %copy-done.4, ...), custom_call_target="tpu_custom_call" | custom-call | tf_op jit(solution)/shard_map/prepare/pallas_call | solution.py:524
  14.3 0.0 collective-permute-done.4.refs_1_
  14.3 0.0 collective-permute-done.5.refs_3_
  14.4 0.7 %analysis_early.1.refs_5_.rest_0_ = f32[2,160,640]{2,1,0:T(8,128)S(1)} custom-call(bf16[160,384]{1,0:T(8,128)(2,1)S(1)} %collective-permute-done.3.refs_0_, bf16[160,384]{1,0:T(8,128)(2,1)S(1)} %collective-permute-done.4.refs_1_, bf16[160,384]{1,0:T(8,128)(2,1)S(1)} %get-tuple-element.36.rest_0_.refs_2_, ...), custom_call_target="tpu_custom_call" | custom-call | tf_op jit(solution)/shard_map/analysis_early/pallas_call | solution.py:214
  15.0 0.1 collective-permute-done.6.refs_0_
  15.2 2.5 %collective-permute-done.7.refs_1_ = bf16[96,384]{1,0:T(8,128)(2,1)S(1)} collective-permute-done((bf16[96,384]{1,0:T(8,128)(2,1)S(1)}, bf16[96,384]{1,0:T(8,128)(2,1)S(1)}, u32[]{:S(2)}, u32[]{:S(2)}) %collective-permute-start.7) | collective-permute-done | bytes 73760 | tf_op jit(solution)/shard_map/ppermute | solution.py:40
  17.6 0.0 collective-permute-done.8.refs_3_
  17.6 0.6 %analysis.2 = (f32[2,96,640]{2,1,0:T(8,128)S(1)}, bf16[3,96,640]{2,1,0:T(8,128)(2,1)S(1)}, bf16[3,96,640]{2,1,0:T(8,128)(2,1)S(1)}) custom-call(bf16[96,384]{1,0:T(8,128)(2,1)S(1)} %collective-permute-done.6.refs_0_, bf16[96,384]{1,0:T(8,128)(2,1)S(1)} %collective-permute-done.7.refs_1_, bf16[160,384]{1,0:T(8,128)(2,1)S(1)} %get-tuple-element.39.refs_2_, ...), custom_call_target="tpu_custom_call" | custom-call | tf_op jit(solution)/shard_map/analysis/pallas_call | solution.py:255
  18.3 1.4 %collective-permute-start.14 = (bf16[3,96,640]{2,1,0:T(8,128)(2,1)S(1)}, bf16[3,96,640]{2,1,0:T(8,128)(2,1)S(1)}, u32[]{:S(2)}, u32[]{:S(2)}) collective-permute-start(bf16[3,96,640]{2,1,0:T(8,128)(2,1)S(1)} %get-tuple-element.61), channel_id=1, source_target_pairs={{0,4},{1,5},{2,6},{3,7},{4,0},{5,1},{6,2},{7,3},{8,12},{9,13},{10,... | collective-permute-start | bytes 1105928 | tf_op jit(solution)/shard_map/ppermute | solution.py:546
  19.6 0.7 %collective-permute-start.15 = (bf16[3,96,640]{2,1,0:T(8,128)(2,1)S(1)}, bf16[3,96,640]{2,1,0:T(8,128)(2,1)S(1)}, u32[]{:S(2)}, u32[]{:S(2)}) collective-permute-start(bf16[3,96,640]{2,1,0:T(8,128)(2,1)S(1)} %get-tuple-element.62), channel_id=1, source_target_pairs={{0,1},{1,0},{2,3},{3,2},{4,8},{5,9},{6,10},{7,11},{8,4},{9,5},{10,... | collective-permute-start | bytes 1105928 | tf_op jit(solution)/shard_map/ppermute | solution.py:546
  20.4 0.3 collective-permute-start
  20.7 1.3 %collective-permute-start.1 = (bf16[64,384]{1,0:T(8,128)(2,1)S(1)}, bf16[64,384]{1,0:T(8,128)(2,1)S(1)}, u32[]{:S(2)}, u32[]{:S(2)}) collective-permute-start(bf16[64,384]{1,0:T(8,128)(2,1)S(1)} %get-tuple-element.38), channel_id=1, source_target_pairs={{0,3},{1,2},{2,1},{3,0},{4,7},{5,6},{6,5},{7,4},{8,11},{9,10},{10,... | collective-permute-start | bytes 147464 | tf_op jit(solution)/shard_map/ppermute | solution.py:40
  22.0 0.2 collective-permute-start.2
  22.2 1.0 %own_terms.2.refs_6_.part_ref = f32[4,96,640]{2,1,0:T(8,128)S(1)} custom-call(f32[2,96,640]{2,1,0:T(8,128)S(1)} %get-tuple-element.48.own_ref, f32[96,32]{1,0:T(8,128)S(1)} %get-tuple-element.49.weight_ref.refs_1_, s32[10,32]{1,0:T(8,128)S(1)} %get-tuple-element.50.target_ref.refs_3_.refs_2_, ...), custom_call_target="tpu_custom_call" | custom-call | tf_op jit(solution)/shard_map/own_terms/pallas_call | solution.py:311
  23.3 0.5 %collective-permute-done.refs_0_ = bf16[64,384]{1,0:T(8,128)(2,1)S(1)} collective-permute-done((bf16[64,384]{1,0:T(8,128)(2,1)S(1)}, bf16[64,384]{1,0:T(8,128)(2,1)S(1)}, u32[]{:S(2)}, u32[]{:S(2)}) %collective-permute-start) | collective-permute-done | bytes 49184 | tf_op jit(solution)/shard_map/ppermute | solution.py:40
  23.8 1.4 %collective-permute-done.1.refs_1_ = bf16[64,384]{1,0:T(8,128)(2,1)S(1)} collective-permute-done((bf16[64,384]{1,0:T(8,128)(2,1)S(1)}, bf16[64,384]{1,0:T(8,128)(2,1)S(1)}, u32[]{:S(2)}, u32[]{:S(2)}) %collective-permute-start.1) | collective-permute-done | bytes 49184 | tf_op jit(solution)/shard_map/ppermute | solution.py:40
  25.2 0.0 collective-permute-done.2.refs_3_
  25.2 0.6 %analysis.3 = (f32[2,64,640]{2,1,0:T(8,128)S(1)}, bf16[3,64,640]{2,1,0:T(8,128)(2,1)S(1)}, bf16[3,64,640]{2,1,0:T(8,128)(2,1)S(1)}) custom-call(bf16[64,384]{1,0:T(8,128)(2,1)S(1)} %collective-permute-done.refs_0_, bf16[64,384]{1,0:T(8,128)(2,1)S(1)} %collective-permute-done.1.refs_1_, bf16[160,384]{1,0:T(8,128)(2,1)S(1)} %get-tuple-element.39.refs_2_, ...), custom_call_target="tpu_custom_call" | custom-call | tf_op jit(solution)/shard_map/analysis/pallas_call | solution.py:255
  25.8 2.9 %collective-permute-start.9 = (bf16[3,64,640]{2,1,0:T(8,128)(2,1)S(1)}, bf16[3,64,640]{2,1,0:T(8,128)(2,1)S(1)}, u32[]{:S(2)}, u32[]{:S(2)}) collective-permute-start(bf16[3,64,640]{2,1,0:T(8,128)(2,1)S(1)} %get-tuple-element.54), channel_id=1, source_target_pairs={{0,4},{1,5},{2,6},{3,7},{4,0},{5,1},{6,2},{7,3},{8,12},{9,13},{10,... | collective-permute-start | bytes 737288 | tf_op jit(solution)/shard_map/ppermute | solution.py:546
  28.7 0.2 collective-permute-start.10
  28.8 0.7 %own_terms.3.part_ref.rest_0_ = f32[4,64,640]{2,1,0:T(8,128)S(1)} custom-call(f32[2,64,640]{2,1,0:T(8,128)S(1)} %get-tuple-element.52.own_ref, f32[64,32]{1,0:T(8,128)S(1)} %get-tuple-element.53.weight_ref.refs_2_, s32[10,32]{1,0:T(8,128)S(1)} %get-tuple-element.50.target_ref.refs_3_.refs_2_, ...), custom_call_target="tpu_custom_call" | custom-call | tf_op jit(solution)/shard_map/own_terms/pallas_call | solution.py:311
  29.5 0.0 collective-permute-done.14.first_ref
  29.5 0.5 %side_terms.1.part_ref = f32[4,96,640]{2,1,0:T(8,128)S(1)} custom-call(f32[4,96,640]{2,1,0:T(8,128)S(1)} %own_terms.2.refs_6_.part_ref, bf16[3,96,640]{2,1,0:T(8,128)(2,1)S(1)} %collective-permute-done.14.first_ref, f32[96,32]{1,0:T(8,128)S(1)} %get-tuple-element.49.weight_ref.refs_1_, s32[10,32]{1,0:T(8,128)S(1)} %get-tuple-element.50.target_ref.refs_3_.refs_2_, ...), custom_call_target="tpu_custom_call" | custom-call | tf_op jit(solution)/shard_map/side_terms/pallas_call | solution.py:353
  30.1 0.0 collective-permute-done.15.refs_0_
  30.1 1.3 %finish.3 = (bf16[180,384]{1,0:T(8,128)(2,1)S(1)}, bf16[180,384]{1,0:T(8,128)(2,1)S(1)}, bf16[180,384]{1,0:T(8,128)(2,1)S(1)}, bf16[180,384]{1,0:T(8,128)(2,1)S(1)}) custom-call(f32[4,96,640]{2,1,0:T(8,128)S(1)} %side_terms.1.part_ref, bf16[3,96,640]{2,1,0:T(8,128)(2,1)S(1)} %collective-permute-done.15.refs_0_, ...), custom_call_target="tpu_custom_call" | custom-call | tf_op jit(solution)/shard_map/finish/pallas_call | solution.py:387
  31.4 0.9 %collective-permute-start.16 = (bf16[180,384]{1,0:T(8,128)(2,1)S(1)}, bf16[180,384]{1,0:T(8,128)(2,1)S(1)}, u32[]{:S(2)}, u32[]{:S(2)}) collective-permute-start(bf16[180,384]{1,0:T(8,128)(2,1)S(1)} %get-tuple-element.63), channel_id=1, source_target_pairs={{0,2},{1,3},{2,0},{3,1},{4,6},{5,7},{6,4},{7,5},{8,10},{9,11},{10,... | collective-permute-start | bytes 414728 | tf_op jit(solution)/shard_map/ppermute | solution.py:40
  32.2 1.2 %collective-permute-start.17 = (bf16[180,384]{1,0:T(8,128)(2,1)S(1)}, bf16[180,384]{1,0:T(8,128)(2,1)S(1)}, u32[]{:S(2)}, u32[]{:S(2)}) collective-permute-start(bf16[180,384]{1,0:T(8,128)(2,1)S(1)} %get-tuple-element.64), channel_id=1, source_target_pairs={{0,3},{1,2},{2,1},{3,0},{4,7},{5,6},{6,5},{7,4},{8,11},{9,10},{10,... | collective-permute-start | bytes 414728 | tf_op jit(solution)/shard_map/ppermute | solution.py:40
  33.4 0.0 collective-permute-start.18
  33.4 1.7 %collective-permute-done.9.refs_0_ = bf16[3,64,640]{2,1,0:T(8,128)(2,1)S(1)} collective-permute-done((bf16[3,64,640]{2,1,0:T(8,128)(2,1)S(1)}, bf16[3,64,640]{2,1,0:T(8,128)(2,1)S(1)}, u32[]{:S(2)}, u32[]{:S(2)}) %collective-permute-start.9) | collective-permute-done | bytes 245792 | tf_op jit(solution)/shard_map/ppermute | solution.py:546
  35.1 0.0 collective-permute-done.10.refs_1_
  35.1 1.1 %finish.2 = (bf16[180,256]{1,0:T(8,128)(2,1)S(1)}, bf16[180,256]{1,0:T(8,128)(2,1)S(1)}, bf16[180,256]{1,0:T(8,128)(2,1)S(1)}, bf16[180,256]{1,0:T(8,128)(2,1)S(1)}) custom-call(f32[4,64,640]{2,1,0:T(8,128)S(1)} %own_terms.3.part_ref.rest_0_, bf16[3,64,640]{2,1,0:T(8,128)(2,1)S(1)} %collective-permute-done.9.refs_0_, ...), custom_call_target="tpu_custom_call" | custom-call | tf_op jit(solution)/shard_map/finish/pallas_call | solution.py:387
  36.2 0.5 %collective-permute-start.13 = (bf16[180,256]{1,0:T(8,128)(2,1)S(1)}, bf16[180,256]{1,0:T(8,128)(2,1)S(1)}, u32[]{:S(2)}, u32[]{:S(2)}) collective-permute-start(bf16[180,256]{1,0:T(8,128)(2,1)S(1)} %get-tuple-element.60), channel_id=1, source_target_pairs={{0,1},{1,0},{2,3},{3,2},{4,5},{5,4},{6,7},{7,6},{8,9},{9,8},{10,11... | collective-permute-start | bytes 276488 | tf_op jit(solution)/shard_map/ppermute | solution.py:40
  36.7 0.0 collective-permute-start.11
  36.7 0.0 collective-permute-done.16.refs_0_
  36.7 1.9 %collective-permute-start.12 = (bf16[180,256]{1,0:T(8,128)(2,1)S(1)}, bf16[180,256]{1,0:T(8,128)(2,1)S(1)}, u32[]{:S(2)}, u32[]{:S(2)}) collective-permute-start(bf16[180,256]{1,0:T(8,128)(2,1)S(1)} %get-tuple-element.58), channel_id=1, source_target_pairs={{0,3},{1,2},{2,1},{3,0},{4,7},{5,6},{6,5},{7,4},{8,11},{9,10},{10,... | collective-permute-start | bytes 276488 | tf_op jit(solution)/shard_map/ppermute | solution.py:40
  38.6 1.9 %collective-permute-done.17.refs_1_ = bf16[180,384]{1,0:T(8,128)(2,1)S(1)} collective-permute-done((bf16[180,384]{1,0:T(8,128)(2,1)S(1)}, bf16[180,384]{1,0:T(8,128)(2,1)S(1)}, u32[]{:S(2)}, u32[]{:S(2)}) %collective-permute-start.17) | collective-permute-done | bytes 138272 | tf_op jit(solution)/shard_map/ppermute | solution.py:40
  40.6 0.0 collective-permute-done.18.refs_3_
  40.6 1.2 %add_chunk.3.refs_2_ = bf16[180,4,640]{2,1,0:T(4,128)(2,1)} custom-call(bf16[4,180,640]{2,1,0:T(8,128)(2,1)S(1)} %copy.19.grad_ref, bf16[180,384]{1,0:T(8,128)(2,1)S(1)} %collective-permute-done.16.refs_0_, bf16[180,384]{1,0:T(8,128)(2,1)S(1)} %collective-permute-done.17.refs_1_, bf16[180,384]{1,0:T(8,128)(2,1)S(1)} %get-tuple-element.65.refs_2_, ...), custom_call_target="tpu_custom_call" | custom-call | tf_op jit(solution)/shard_map/add_chunk/pallas_call | solution.py:448
  41.8 0.0 collective-permute-done.13.refs_1_
  41.8 0.9 %add_chunk.4.refs_2_ = bf16[180,4,640]{2,1,0:T(4,128)(2,1)} custom-call(bf16[4,180,640]{2,1,0:T(8,128)(2,1)S(1)} %copy.19.grad_ref, bf16[180,256]{1,0:T(8,128)(2,1)S(1)} %get-tuple-element.59.refs_0_, bf16[180,256]{1,0:T(8,128)(2,1)S(1)} %collective-permute-done.13.refs_1_, bf16[180,4,640]{2,1,0:T(4,128)(2,1)} %add_chunk.3.refs_2_), custom_call_target="tpu_custom_call", output_to_operand_aliasing={{}: (3, {})} | custom-call | tf_op jit(solution)/shard_map/add_chunk/pallas_call | solution.py:448
  42.6 0.0 collective-permute-done.11.refs_0_
  42.7 1.3 %collective-permute-done.12.refs_1_ = bf16[180,256]{1,0:T(8,128)(2,1)S(1)} collective-permute-done((bf16[180,256]{1,0:T(8,128)(2,1)S(1)}, bf16[180,256]{1,0:T(8,128)(2,1)S(1)}, u32[]{:S(2)}, u32[]{:S(2)}) %collective-permute-start.12) | collective-permute-done | bytes 92192 | tf_op jit(solution)/shard_map/ppermute | solution.py:40
  43.9 0.9 %add_chunk.5 = bf16[180,4,640]{2,1,0:T(4,128)(2,1)} custom-call(bf16[4,180,640]{2,1,0:T(8,128)(2,1)S(1)} %copy.19.grad_ref, bf16[180,256]{1,0:T(8,128)(2,1)S(1)} %collective-permute-done.11.refs_0_, bf16[180,256]{1,0:T(8,128)(2,1)S(1)} %collective-permute-done.12.refs_1_, bf16[180,4,640]{2,1,0:T(4,128)(2,1)} %add_chunk.4.refs_2_), custom_call_target="tpu_custom_call", output_to_operand_aliasing={{}: (3, {})} | custom-call | tf_op jit(solution)/shard_map/add_chunk/pallas_call | solution.py:448
  (6 shorter events, 0.0 us)
Async XLA Ops:
  0.0 2.8 %copy-start.1 = (bf16[1280,640]{1,0:T(8,128)(2,1)S(1)}, bf16[1280,640]{1,0:T(8,128)(2,1)}, u32[]{:S(2)}) copy-start(bf16[1280,640]{1,0:T(8,128)(2,1)} %wout_ref.3) | copy-start | bytes 4915204
  0.0 2.8 %copy-start.6 = (f32[1280]{0:T(1024)S(1)}, f32[1280]{0:T(1024)}, u32[]{:S(2)}) copy-start(f32[1280]{0:T(1024)} %bias_ref.3) | copy-start | bytes 15364
  0.0 2.8 %copy-start = (bf16[640,1280]{1,0:T(8,128)(2,1)S(1)}, bf16[640,1280]{1,0:T(8,128)(2,1)}, u32[]{:S(2)}) copy-start(bf16[640,1280]{1,0:T(8,128)(2,1)} %win_ref.3) | copy-start | bytes 4915204
  5.5 7.7 %collective-permute-start.3 = (bf16[160,384]{1,0:T(8,128)(2,1)S(1)}, bf16[160,384]{1,0:T(8,128)(2,1)S(1)}, u32[]{:S(2)}, u32[]{:S(2)}) collective-permute-start(bf16[160,384]{1,0:T(8,128)(2,1)S(1)} %get-tuple-element.42), channel_id=1, source_target_pairs={{0,2},{1,3},{2,0},{3,1},{4,6},{5,7},{6,4},{7,5},{8,10},{9,11},{10,... | collective-permute-start | bytes 368648 | tf_op jit(solution)/shard_map/ppermute | solution.py:40
  7.7 6.7 %collective-permute-start.4 = (bf16[160,384]{1,0:T(8,128)(2,1)S(1)}, bf16[160,384]{1,0:T(8,128)(2,1)S(1)}, u32[]{:S(2)}, u32[]{:S(2)}) collective-permute-start(bf16[160,384]{1,0:T(8,128)(2,1)S(1)} %get-tuple-element.43), channel_id=1, source_target_pairs={{0,3},{1,2},{2,1},{3,0},{4,7},{5,6},{6,5},{7,4},{8,11},{9,10},{10,... | collective-permute-start | bytes 368648 | tf_op jit(solution)/shard_map/ppermute | solution.py:40
  8.3 6.1 %collective-permute-start.5 = (bf16[160,384]{1,0:T(8,128)(2,1)S(1)}, bf16[160,384]{1,0:T(8,128)(2,1)S(1)}, u32[]{:S(2)}, u32[]{:S(2)}) collective-permute-start(bf16[160,384]{1,0:T(8,128)(2,1)S(1)} %get-tuple-element.44), channel_id=1, source_target_pairs={{0,1},{1,0},{2,3},{3,2},{4,5},{5,4},{6,7},{7,6},{8,9},{9,8},{10,11... | collective-permute-start | bytes 368648 | tf_op jit(solution)/shard_map/ppermute | solution.py:40
  8.6 5.0 %copy-start.2 = (bf16[4,320,640]{2,1,0:T(8,128)(2,1)S(1)}, bf16[4,320,640]{2,1,0:T(8,128)(2,1)}, u32[]{:S(2)}) copy-start(bf16[4,320,640]{2,1,0:T(8,128)(2,1)} %constant.4.clone.forth_ref) | copy-start | bytes 4915204
  8.6 5.0 %copy-start.3 = (bf16[768,640]{1,0:T(8,128)(2,1)S(1)}, bf16[768,640]{1,0:T(8,128)(2,1)}, u32[]{:S(2)}) copy-start(bf16[768,640]{1,0:T(8,128)(2,1)} %constant.5.clone.back_ref) | copy-start | bytes 2949124
  8.6 5.0 %copy-start.4 = (bf16[9,16,640]{2,1,0:T(8,128)(2,1)S(1)}, bf16[9,16,640]{2,1,0:T(8,128)(2,1)}, u32[]{:S(2)}) copy-start(bf16[9,16,640]{2,1,0:T(8,128)(2,1)} %filt_ref.1) | copy-start | bytes 552964
  8.6 5.0 %copy-start.5 = (f32[9,640]{1,0:T(8,128)S(1)}, f32[9,640]{1,0:T(8,128)}, u32[]{:S(2)}) copy-start(f32[9,640]{1,0:T(8,128)} %weight_ref.1) | copy-start | bytes 69124
  8.6 5.0 %copy-start.7 = (s32[16,9]{1,0:T(8,128)S(1)}, s32[16,9]{1,0:T(8,128)}, u32[]{:S(2)}) copy-start(s32[16,9]{1,0:T(8,128)} %offset_ref.1) | copy-start | bytes 1732
  11.4 3.8 %collective-permute-start.6 = (bf16[96,384]{1,0:T(8,128)(2,1)S(1)}, bf16[96,384]{1,0:T(8,128)(2,1)S(1)}, u32[]{:S(2)}, u32[]{:S(2)}) collective-permute-start(bf16[96,384]{1,0:T(8,128)(2,1)S(1)} %get-tuple-element.45), channel_id=1, source_target_pairs={{0,2},{1,3},{2,0},{3,1},{4,6},{5,7},{6,4},{7,5},{8,10},{9,11},{10,... | collective-permute-start | bytes 221192 | tf_op jit(solution)/shard_map/ppermute | solution.py:40
  12.8 4.8 %collective-permute-start.7 = (bf16[96,384]{1,0:T(8,128)(2,1)S(1)}, bf16[96,384]{1,0:T(8,128)(2,1)S(1)}, u32[]{:S(2)}, u32[]{:S(2)}) collective-permute-start(bf16[96,384]{1,0:T(8,128)(2,1)S(1)} %get-tuple-element.46), channel_id=1, source_target_pairs={{0,3},{1,2},{2,1},{3,0},{4,7},{5,6},{6,5},{7,4},{8,11},{9,10},{10,... | collective-permute-start | bytes 221192 | tf_op jit(solution)/shard_map/ppermute | solution.py:40
  13.3 4.4 %collective-permute-start.8 = (bf16[96,384]{1,0:T(8,128)(2,1)S(1)}, bf16[96,384]{1,0:T(8,128)(2,1)S(1)}, u32[]{:S(2)}, u32[]{:S(2)}) collective-permute-start(bf16[96,384]{1,0:T(8,128)(2,1)S(1)} %get-tuple-element.47), channel_id=1, source_target_pairs={{0,1},{1,0},{2,3},{3,2},{4,5},{5,4},{6,7},{7,6},{8,9},{9,8},{10,11... | collective-permute-start | bytes 221192 | tf_op jit(solution)/shard_map/ppermute | solution.py:40
  18.3 11.3 %collective-permute-start.14 = (bf16[3,96,640]{2,1,0:T(8,128)(2,1)S(1)}, bf16[3,96,640]{2,1,0:T(8,128)(2,1)S(1)}, u32[]{:S(2)}, u32[]{:S(2)}) collective-permute-start(bf16[3,96,640]{2,1,0:T(8,128)(2,1)S(1)} %get-tuple-element.61), channel_id=1, source_target_pairs={{0,4},{1,5},{2,6},{3,7},{4,0},{5,1},{6,2},{7,3},{8,12},{9,13},{10,... | collective-permute-start | bytes 1105928 | tf_op jit(solution)/shard_map/ppermute | solution.py:546
  19.6 10.4 %collective-permute-start.15 = (bf16[3,96,640]{2,1,0:T(8,128)(2,1)S(1)}, bf16[3,96,640]{2,1,0:T(8,128)(2,1)S(1)}, u32[]{:S(2)}, u32[]{:S(2)}) collective-permute-start(bf16[3,96,640]{2,1,0:T(8,128)(2,1)S(1)} %get-tuple-element.62), channel_id=1, source_target_pairs={{0,1},{1,0},{2,3},{3,2},{4,8},{5,9},{6,10},{7,11},{8,4},{9,5},{10,... | collective-permute-start | bytes 1105928 | tf_op jit(solution)/shard_map/ppermute | solution.py:546
  20.4 3.4 %collective-permute-start = (bf16[64,384]{1,0:T(8,128)(2,1)S(1)}, bf16[64,384]{1,0:T(8,128)(2,1)S(1)}, u32[]{:S(2)}, u32[]{:S(2)}) collective-permute-start(bf16[64,384]{1,0:T(8,128)(2,1)S(1)} %get-tuple-element.37), channel_id=1, source_target_pairs={{0,2},{1,3},{2,0},{3,1},{4,6},{5,7},{6,4},{7,5},{8,10},{9,11},{10,... | collective-permute-start | bytes 147464 | tf_op jit(solution)/shard_map/ppermute | solution.py:40
  20.7 4.5 %collective-permute-start.1 = (bf16[64,384]{1,0:T(8,128)(2,1)S(1)}, bf16[64,384]{1,0:T(8,128)(2,1)S(1)}, u32[]{:S(2)}, u32[]{:S(2)}) collective-permute-start(bf16[64,384]{1,0:T(8,128)(2,1)S(1)} %get-tuple-element.38), channel_id=1, source_target_pairs={{0,3},{1,2},{2,1},{3,0},{4,7},{5,6},{6,5},{7,4},{8,11},{9,10},{10,... | collective-permute-start | bytes 147464 | tf_op jit(solution)/shard_map/ppermute | solution.py:40
  22.0 3.2 %collective-permute-start.2 = (bf16[64,384]{1,0:T(8,128)(2,1)S(1)}, bf16[64,384]{1,0:T(8,128)(2,1)S(1)}, u32[]{:S(2)}, u32[]{:S(2)}) collective-permute-start(bf16[64,384]{1,0:T(8,128)(2,1)S(1)} %get-tuple-element.40), channel_id=1, source_target_pairs={{0,1},{1,0},{2,3},{3,2},{4,5},{5,4},{6,7},{7,6},{8,9},{9,8},{10,11... | collective-permute-start | bytes 147464 | tf_op jit(solution)/shard_map/ppermute | solution.py:40
  25.8 9.3 %collective-permute-start.9 = (bf16[3,64,640]{2,1,0:T(8,128)(2,1)S(1)}, bf16[3,64,640]{2,1,0:T(8,128)(2,1)S(1)}, u32[]{:S(2)}, u32[]{:S(2)}) collective-permute-start(bf16[3,64,640]{2,1,0:T(8,128)(2,1)S(1)} %get-tuple-element.54), channel_id=1, source_target_pairs={{0,4},{1,5},{2,6},{3,7},{4,0},{5,1},{6,2},{7,3},{8,12},{9,13},{10,... | collective-permute-start | bytes 737288 | tf_op jit(solution)/shard_map/ppermute | solution.py:546
  28.7 6.5 %collective-permute-start.10 = (bf16[3,64,640]{2,1,0:T(8,128)(2,1)S(1)}, bf16[3,64,640]{2,1,0:T(8,128)(2,1)S(1)}, u32[]{:S(2)}, u32[]{:S(2)}) collective-permute-start(bf16[3,64,640]{2,1,0:T(8,128)(2,1)S(1)} %get-tuple-element.55), channel_id=1, source_target_pairs={{0,1},{1,0},{2,3},{3,2},{4,8},{5,9},{6,10},{7,11},{8,4},{9,5},{10,... | collective-permute-start | bytes 737288 | tf_op jit(solution)/shard_map/ppermute | solution.py:546
  31.4 5.4 %collective-permute-start.16 = (bf16[180,384]{1,0:T(8,128)(2,1)S(1)}, bf16[180,384]{1,0:T(8,128)(2,1)S(1)}, u32[]{:S(2)}, u32[]{:S(2)}) collective-permute-start(bf16[180,384]{1,0:T(8,128)(2,1)S(1)} %get-tuple-element.63), channel_id=1, source_target_pairs={{0,2},{1,3},{2,0},{3,1},{4,6},{5,7},{6,4},{7,5},{8,10},{9,11},{10,... | collective-permute-start | bytes 414728 | tf_op jit(solution)/shard_map/ppermute | solution.py:40
  32.2 8.3 %collective-permute-start.17 = (bf16[180,384]{1,0:T(8,128)(2,1)S(1)}, bf16[180,384]{1,0:T(8,128)(2,1)S(1)}, u32[]{:S(2)}, u32[]{:S(2)}) collective-permute-start(bf16[180,384]{1,0:T(8,128)(2,1)S(1)} %get-tuple-element.64), channel_id=1, source_target_pairs={{0,3},{1,2},{2,1},{3,0},{4,7},{5,6},{6,5},{7,4},{8,11},{9,10},{10,... | collective-permute-start | bytes 414728 | tf_op jit(solution)/shard_map/ppermute | solution.py:40
  33.4 7.2 %collective-permute-start.18 = (bf16[180,384]{1,0:T(8,128)(2,1)S(1)}, bf16[180,384]{1,0:T(8,128)(2,1)S(1)}, u32[]{:S(2)}, u32[]{:S(2)}) collective-permute-start(bf16[180,384]{1,0:T(8,128)(2,1)S(1)} %get-tuple-element.66), channel_id=1, source_target_pairs={{0,1},{1,0},{2,3},{3,2},{4,5},{5,4},{6,7},{7,6},{8,9},{9,8},{10,11... | collective-permute-start | bytes 414728 | tf_op jit(solution)/shard_map/ppermute | solution.py:40
  36.2 5.5 %collective-permute-start.13 = (bf16[180,256]{1,0:T(8,128)(2,1)S(1)}, bf16[180,256]{1,0:T(8,128)(2,1)S(1)}, u32[]{:S(2)}, u32[]{:S(2)}) collective-permute-start(bf16[180,256]{1,0:T(8,128)(2,1)S(1)} %get-tuple-element.60), channel_id=1, source_target_pairs={{0,1},{1,0},{2,3},{3,2},{4,5},{5,4},{6,7},{7,6},{8,9},{9,8},{10,11... | collective-permute-start | bytes 276488 | tf_op jit(solution)/shard_map/ppermute | solution.py:40
  36.7 5.9 %collective-permute-start.11 = (bf16[180,256]{1,0:T(8,128)(2,1)S(1)}, bf16[180,256]{1,0:T(8,128)(2,1)S(1)}, u32[]{:S(2)}, u32[]{:S(2)}) collective-permute-start(bf16[180,256]{1,0:T(8,128)(2,1)S(1)} %get-tuple-element.57), channel_id=1, source_target_pairs={{0,2},{1,3},{2,0},{3,1},{4,6},{5,7},{6,4},{7,5},{8,10},{9,11},{10,... | collective-permute-start | bytes 276488 | tf_op jit(solution)/shard_map/ppermute | solution.py:40
  36.7 7.2 %collective-permute-start.12 = (bf16[180,256]{1,0:T(8,128)(2,1)S(1)}, bf16[180,256]{1,0:T(8,128)(2,1)S(1)}, u32[]{:S(2)}, u32[]{:S(2)}) collective-permute-start(bf16[180,256]{1,0:T(8,128)(2,1)S(1)} %get-tuple-element.58), channel_id=1, source_target_pairs={{0,3},{1,2},{2,1},{3,0},{4,7},{5,6},{6,5},{7,4},{8,11},{9,10},{10,... | collective-permute-start | bytes 276488 | tf_op jit(solution)/shard_map/ppermute | solution.py:40

commit v7 on v6

--- a/solution.py
+++ b/solution.py
@@ -103,7 +103,7 @@
             tall[row * wide + whole : (row + 1) * wide, :] = jnp.zeros((wide - whole, channels), jnp.bfloat16)
             tall[row * wide : row * wide + part, :] = source[half * rows + row]
 
-    group = 48
+    group = 32
     groups = rows * wide // group
 
     def span(step):
@@ -123,29 +123,35 @@
             value = back_ref[step % 2, some, :] * twice_gelu_slope(pre_ref[step % 2, some, :] * root + bias)
             slope_ref[some, span(step)] = value.astype(jnp.bfloat16)
 
-    def gather(first, last):
+    def gather(first, last, part):
         at = slice(first * block, last * block)
-        term = dot_nt(win_ref[:, at], slope_ref[:, at])
-        total_ref[...] = term if first == 0 else total_ref[...] + term
+        some = slice(part * channels // 2, (part + 1) * channels // 2)
+        term = dot_nt(win_ref[some, at], slope_ref[:, at])
+        total_ref[some] = term if first == 0 else total_ref[some] + term
 
     stack(tall_conv, conv_ref)
     project_pre(0)
     stack(tall_grad, grad_ref)
     project_back(0)
     gathered = 0
-    thirds = [groups * n // 3 for n in range(4)]
+    ends = [groups * n // 4 for n in range(5)]
     for step in range(steps):
+        ready = step - gathered == 2
         if step + 1 < steps:
             project_pre(step + 1)
-        slope(step, thirds[0], thirds[1])
-        if step - gathered == 2:
-            gather(gathered, step)
+        slope(step, ends[0], ends[1])
+        if ready:
+            gather(gathered, step, 0)
+        slope(step, ends[1], ends[2])
+        if ready:
+            gather(gathered, step, 1)
             gathered = step
-        slope(step, thirds[1], thirds[2])
+        slope(step, ends[2], ends[3])
         if step + 1 < steps:
             project_back(step + 1)
-        slope(step, thirds[2], thirds[3])
-    gather(gathered, steps)
+        slope(step, ends[3], ends[4])
+    for part_at in range(2):
+        gather(gathered, steps, part_at)
     for out, (k, start, size) in zip(outs, sent):
         target = partner(me, k, count, 1)
         for begin, width in chunks:

time: 45.1 us -> 45.7 us (1.013)
  Pallas kernels: 15.6 us -> 16.2 us
  transfers between devices with their start and end apart: 19 -> 19, of which waited for: 7 -> 7; matrix products, arithmetic and copies ran while one was open for 0% -> 0% of each run, Pallas kernels for 25% -> 26%
where the time goes in v7:
time: 45.7 us; the launch traced here: 45.5 us
  starting transfers between devices  17 us (37%)
  Pallas kernels  16.2 us (35%)
  waiting for transfers between devices  9.23 us (20%)
  local copies, waits for them, and re-layouts  2.77 us (6%)
    ppermute x15, starting transfers between devices, exchange(): return lax.ppermute(block, 'azimuth', pairs)  11.8 us
    ppermute x15, waiting for transfers between devices, exchange(): return lax.ppermute(block, 'azimuth', pairs)  7.7 us
    pallas_call x2, Pallas kernels, mlp(): pl.pallas_call(functools.partial(mlp_kernel, count, half, sent, chunks),...  5.9 us
    ppermute x4, starting transfers between devices, halo(): blocks.append(lax.ppermute(block, ('polar', 'azimuth'), pairs))  5.2 us
    pallas_call x3, Pallas kernels, add_chunk(): pl.pallas_call(functools.partial(add_kernel, count, chunk, [k for k, _ in...  2.92 us
    unnamed x18, local copies, waits for them, and re-layouts  2.77 us
    pallas_call x2, Pallas kernels, finish(): pl.pallas_call(functools.partial(finish_kernel, count, len(halos)), in_sp...  2.55 us
    pallas_call x2, Pallas kernels, own_terms(): pl.pallas_call(functools.partial(own_kernel, start), in_specs=[pl.BlockSp...  1.7 us
  transfers between devices with their start and end apart: 19, of which 7 were waited for; matrix products, arithmetic and copies ran while one was open for 0% of the time, Pallas kernels for 26%

profile of v7, /device:TPU:1, one launch (start us, length us, event | category | flops | bytes accessed | tf_op | source)
XLA Modules:
  0.0 45.5 jit_solution(9985696412374466685)
XLA Ops:
  0.0 0.0 copy-start.1
  0.0 1.4 %copy.19.grad_ref = bf16[4,180,640]{2,1,0:T(8,128)(2,1)S(1)} copy(bf16[4,180,640]{2,0,1:T(4,128)(2,1)} %param.11) | data formatting | bytes 1843200 | tf_op args[1]
  1.5 1.3 %copy.15.conv_ref = bf16[4,180,640]{2,1,0:T(8,128)(2,1)S(1)} copy(bf16[4,180,640]{2,0,1:T(4,128)(2,1)} %param.10) | data formatting | bytes 1843200 | tf_op args[0]
  2.8 0.0 copy-done.1
  2.8 0.0 copy-done.6
  2.8 0.0 copy-done
  2.8 2.9 %mlp.2 = (bf16[160,384]{1,0:T(8,128)(2,1)S(1)}, bf16[160,384]{1,0:T(8,128)(2,1)S(1)}, bf16[160,384]{1,0:T(8,128)(2,1)S(1)}, bf16[160,384]{1,0:T(8,128)(2,1)S(1)}) custom-call(bf16[4,180,640]{2,1,0:T(8,128)(2,1)S(1)} %copy.15.conv_ref, bf16[4,180,640]{2,1,0:T(8,128)(2,1)S(1)} %copy.19.grad_ref, bf16[640,1280]{1,0:T(8,128)(2,1)S(1)} %copy-done, ...), custom_call_target="tpu_custom_call" | custom-call | tf_op jit(solution)/shard_map/mlp/pallas_call | solution.py:171
  5.7 2.1 %collective-permute-start.3 = (bf16[160,384]{1,0:T(8,128)(2,1)S(1)}, bf16[160,384]{1,0:T(8,128)(2,1)S(1)}, u32[]{:S(2)}, u32[]{:S(2)}) collective-permute-start(bf16[160,384]{1,0:T(8,128)(2,1)S(1)} %get-tuple-element.42), channel_id=1, source_target_pairs={{0,2},{1,3},{2,0},{3,1},{4,6},{5,7},{6,4},{7,5},{8,10},{9,11},{10,... | collective-permute-start | bytes 368648 | tf_op jit(solution)/shard_map/ppermute | solution.py:40
  7.9 0.6 %collective-permute-start.4 = (bf16[160,384]{1,0:T(8,128)(2,1)S(1)}, bf16[160,384]{1,0:T(8,128)(2,1)S(1)}, u32[]{:S(2)}, u32[]{:S(2)}) collective-permute-start(bf16[160,384]{1,0:T(8,128)(2,1)S(1)} %get-tuple-element.43), channel_id=1, source_target_pairs={{0,3},{1,2},{2,1},{3,0},{4,7},{5,6},{6,5},{7,4},{8,11},{9,10},{10,... | collective-permute-start | bytes 368648 | tf_op jit(solution)/shard_map/ppermute | solution.py:40
  8.5 0.3 collective-permute-start.5
  8.8 0.0 copy-start.7
  8.8 2.9 %mlp.3 = (bf16[160,384]{1,0:T(8,128)(2,1)S(1)}, bf16[96,384]{1,0:T(8,128)(2,1)S(1)}, bf16[96,384]{1,0:T(8,128)(2,1)S(1)}, bf16[96,384]{1,0:T(8,128)(2,1)S(1)}, b...) custom-call(bf16[4,180,640]{2,1,0:T(8,128)(2,1)S(1)} %copy.15.conv_ref, ...), custom_call_target="tpu_custom_call" | custom-call | tf_op jit(solution)/shard_map/mlp/pallas_call | solution.py:171
  11.8 1.4 %collective-permute-start.6 = (bf16[96,384]{1,0:T(8,128)(2,1)S(1)}, bf16[96,384]{1,0:T(8,128)(2,1)S(1)}, u32[]{:S(2)}, u32[]{:S(2)}) collective-permute-start(bf16[96,384]{1,0:T(8,128)(2,1)S(1)} %get-tuple-element.45), channel_id=1, source_target_pairs={{0,2},{1,3},{2,0},{3,1},{4,6},{5,7},{6,4},{7,5},{8,10},{9,11},{10,... | collective-permute-start | bytes 221192 | tf_op jit(solution)/shard_map/ppermute | solution.py:40
  13.2 0.5 collective-permute-start.7
  13.7 0.0 collective-permute-done.3.refs_0_
  13.7 0.3 collective-permute-start.8
  14.0 0.0 copy-done.2
  14.0 0.0 copy-done.3
  14.0 0.0 copy-done.4
  14.0 0.0 copy-done.5
  14.0 0.0 copy-done.7
  14.0 0.7 %prepare.1 = (bf16[10,32,768]{2,1,0:T(8,128)(2,1)S(1)}, s32[10,32]{1,0:T(8,128)S(1)}, bf16[4,320,640]{2,1,0:T(8,128)(2,1)S(1)}, bf16[768,640]{1,0:T(8,128)(2,1)S...) custom-call(f32[9,640]{1,0:T(8,128)S(1)} %copy-done.5, bf16[9,16,640]{2,1,0:T(8,128)(2,1)S(1)} %copy-done.4, ...), custom_call_target="tpu_custom_call" | custom-call | tf_op jit(solution)/shard_map/prepare/pallas_call | solution.py:530
  14.7 0.0 collective-permute-done.4.refs_1_
  14.7 0.0 collective-permute-done.5.refs_3_
  14.8 0.7 %analysis_early.1.refs_5_.rest_0_ = f32[2,160,640]{2,1,0:T(8,128)S(1)} custom-call(bf16[160,384]{1,0:T(8,128)(2,1)S(1)} %collective-permute-done.3.refs_0_, bf16[160,384]{1,0:T(8,128)(2,1)S(1)} %collective-permute-done.4.refs_1_, bf16[160,384]{1,0:T(8,128)(2,1)S(1)} %get-tuple-element.36.rest_0_.refs_2_, ...), custom_call_target="tpu_custom_call" | custom-call | tf_op jit(solution)/shard_map/analysis_early/pallas_call | solution.py:220
  15.4 0.1 collective-permute-done.6.refs_0_
  15.5 2.5 %collective-permute-done.7.refs_1_ = bf16[96,384]{1,0:T(8,128)(2,1)S(1)} collective-permute-done((bf16[96,384]{1,0:T(8,128)(2,1)S(1)}, bf16[96,384]{1,0:T(8,128)(2,1)S(1)}, u32[]{:S(2)}, u32[]{:S(2)}) %collective-permute-start.7) | collective-permute-done | bytes 73760 | tf_op jit(solution)/shard_map/ppermute | solution.py:40
  18.0 0.0 collective-permute-done.8.refs_3_
  18.0 0.6 %analysis.2 = (f32[2,96,640]{2,1,0:T(8,128)S(1)}, bf16[3,96,640]{2,1,0:T(8,128)(2,1)S(1)}, bf16[3,96,640]{2,1,0:T(8,128)(2,1)S(1)}) custom-call(bf16[96,384]{1,0:T(8,128)(2,1)S(1)} %collective-permute-done.6.refs_0_, bf16[96,384]{1,0:T(8,128)(2,1)S(1)} %collective-permute-done.7.refs_1_, bf16[160,384]{1,0:T(8,128)(2,1)S(1)} %get-tuple-element.39.refs_2_, ...), custom_call_target="tpu_custom_call" | custom-call | tf_op jit(solution)/shard_map/analysis/pallas_call | solution.py:261
  18.6 1.4 %collective-permute-start.14 = (bf16[3,96,640]{2,1,0:T(8,128)(2,1)S(1)}, bf16[3,96,640]{2,1,0:T(8,128)(2,1)S(1)}, u32[]{:S(2)}, u32[]{:S(2)}) collective-permute-start(bf16[3,96,640]{2,1,0:T(8,128)(2,1)S(1)} %get-tuple-element.61), channel_id=1, source_target_pairs={{0,4},{1,5},{2,6},{3,7},{4,0},{5,1},{6,2},{7,3},{8,12},{9,13},{10,... | collective-permute-start | bytes 1105928 | tf_op jit(solution)/shard_map/ppermute | solution.py:552
  20.0 0.8 %collective-permute-start.15 = (bf16[3,96,640]{2,1,0:T(8,128)(2,1)S(1)}, bf16[3,96,640]{2,1,0:T(8,128)(2,1)S(1)}, u32[]{:S(2)}, u32[]{:S(2)}) collective-permute-start(bf16[3,96,640]{2,1,0:T(8,128)(2,1)S(1)} %get-tuple-element.62), channel_id=1, source_target_pairs={{0,1},{1,0},{2,3},{3,2},{4,8},{5,9},{6,10},{7,11},{8,4},{9,5},{10,... | collective-permute-start | bytes 1105928 | tf_op jit(solution)/shard_map/ppermute | solution.py:552
  20.8 0.3 collective-permute-start
  21.1 1.3 %collective-permute-start.1 = (bf16[64,384]{1,0:T(8,128)(2,1)S(1)}, bf16[64,384]{1,0:T(8,128)(2,1)S(1)}, u32[]{:S(2)}, u32[]{:S(2)}) collective-permute-start(bf16[64,384]{1,0:T(8,128)(2,1)S(1)} %get-tuple-element.38), channel_id=1, source_target_pairs={{0,3},{1,2},{2,1},{3,0},{4,7},{5,6},{6,5},{7,4},{8,11},{9,10},{10,... | collective-permute-start | bytes 147464 | tf_op jit(solution)/shard_map/ppermute | solution.py:40
  22.4 0.2 collective-permute-start.2
  22.6 1.0 %own_terms.2.refs_6_.part_ref = f32[4,96,640]{2,1,0:T(8,128)S(1)} custom-call(f32[2,96,640]{2,1,0:T(8,128)S(1)} %get-tuple-element.48.own_ref, f32[96,32]{1,0:T(8,128)S(1)} %get-tuple-element.49.weight_ref.refs_1_, s32[10,32]{1,0:T(8,128)S(1)} %get-tuple-element.50.target_ref.refs_3_.refs_2_, ...), custom_call_target="tpu_custom_call" | custom-call | tf_op jit(solution)/shard_map/own_terms/pallas_call | solution.py:317
  23.6 0.5 %collective-permute-done.refs_0_ = bf16[64,384]{1,0:T(8,128)(2,1)S(1)} collective-permute-done((bf16[64,384]{1,0:T(8,128)(2,1)S(1)}, bf16[64,384]{1,0:T(8,128)(2,1)S(1)}, u32[]{:S(2)}, u32[]{:S(2)}) %collective-permute-start) | collective-permute-done | bytes 49184 | tf_op jit(solution)/shard_map/ppermute | solution.py:40
  24.1 1.4 %collective-permute-done.1.refs_1_ = bf16[64,384]{1,0:T(8,128)(2,1)S(1)} collective-permute-done((bf16[64,384]{1,0:T(8,128)(2,1)S(1)}, bf16[64,384]{1,0:T(8,128)(2,1)S(1)}, u32[]{:S(2)}, u32[]{:S(2)}) %collective-permute-start.1) | collective-permute-done | bytes 49184 | tf_op jit(solution)/shard_map/ppermute | solution.py:40
  25.6 0.0 collective-permute-done.2.refs_3_
  25.6 0.6 %analysis.3 = (f32[2,64,640]{2,1,0:T(8,128)S(1)}, bf16[3,64,640]{2,1,0:T(8,128)(2,1)S(1)}, bf16[3,64,640]{2,1,0:T(8,128)(2,1)S(1)}) custom-call(bf16[64,384]{1,0:T(8,128)(2,1)S(1)} %collective-permute-done.refs_0_, bf16[64,384]{1,0:T(8,128)(2,1)S(1)} %collective-permute-done.1.refs_1_, bf16[160,384]{1,0:T(8,128)(2,1)S(1)} %get-tuple-element.39.refs_2_, ...), custom_call_target="tpu_custom_call" | custom-call | tf_op jit(solution)/shard_map/analysis/pallas_call | solution.py:261
  26.2 2.9 %collective-permute-start.9 = (bf16[3,64,640]{2,1,0:T(8,128)(2,1)S(1)}, bf16[3,64,640]{2,1,0:T(8,128)(2,1)S(1)}, u32[]{:S(2)}, u32[]{:S(2)}) collective-permute-start(bf16[3,64,640]{2,1,0:T(8,128)(2,1)S(1)} %get-tuple-element.54), channel_id=1, source_target_pairs={{0,4},{1,5},{2,6},{3,7},{4,0},{5,1},{6,2},{7,3},{8,12},{9,13},{10,... | collective-permute-start | bytes 737288 | tf_op jit(solution)/shard_map/ppermute | solution.py:552
  29.1 0.2 collective-permute-start.10
  29.2 0.7 %own_terms.3.part_ref.rest_0_ = f32[4,64,640]{2,1,0:T(8,128)S(1)} custom-call(f32[2,64,640]{2,1,0:T(8,128)S(1)} %get-tuple-element.52.own_ref, f32[64,32]{1,0:T(8,128)S(1)} %get-tuple-element.53.weight_ref.refs_2_, s32[10,32]{1,0:T(8,128)S(1)} %get-tuple-element.50.target_ref.refs_3_.refs_2_, ...), custom_call_target="tpu_custom_call" | custom-call | tf_op jit(solution)/shard_map/own_terms/pallas_call | solution.py:317
  29.9 0.0 collective-permute-done.14.first_ref
  29.9 0.5 %side_terms.1.part_ref = f32[4,96,640]{2,1,0:T(8,128)S(1)} custom-call(f32[4,96,640]{2,1,0:T(8,128)S(1)} %own_terms.2.refs_6_.part_ref, bf16[3,96,640]{2,1,0:T(8,128)(2,1)S(1)} %collective-permute-done.14.first_ref, f32[96,32]{1,0:T(8,128)S(1)} %get-tuple-element.49.weight_ref.refs_1_, s32[10,32]{1,0:T(8,128)S(1)} %get-tuple-element.50.target_ref.refs_3_.refs_2_, ...), custom_call_target="tpu_custom_call" | custom-call | tf_op jit(solution)/shard_map/side_terms/pallas_call | solution.py:359
  30.5 0.0 collective-permute-done.15.refs_0_
  30.5 1.5 %finish.3 = (bf16[180,384]{1,0:T(8,128)(2,1)S(1)}, bf16[180,384]{1,0:T(8,128)(2,1)S(1)}, bf16[180,384]{1,0:T(8,128)(2,1)S(1)}, bf16[180,384]{1,0:T(8,128)(2,1)S(1)}) custom-call(f32[4,96,640]{2,1,0:T(8,128)S(1)} %side_terms.1.part_ref, bf16[3,96,640]{2,1,0:T(8,128)(2,1)S(1)} %collective-permute-done.15.refs_0_, ...), custom_call_target="tpu_custom_call" | custom-call | tf_op jit(solution)/shard_map/finish/pallas_call | solution.py:393
  31.9 0.9 %collective-permute-start.16 = (bf16[180,384]{1,0:T(8,128)(2,1)S(1)}, bf16[180,384]{1,0:T(8,128)(2,1)S(1)}, u32[]{:S(2)}, u32[]{:S(2)}) collective-permute-start(bf16[180,384]{1,0:T(8,128)(2,1)S(1)} %get-tuple-element.63), channel_id=1, source_target_pairs={{0,2},{1,3},{2,0},{3,1},{4,6},{5,7},{6,4},{7,5},{8,10},{9,11},{10,... | collective-permute-start | bytes 414728 | tf_op jit(solution)/shard_map/ppermute | solution.py:40
  32.8 1.1 %collective-permute-start.17 = (bf16[180,384]{1,0:T(8,128)(2,1)S(1)}, bf16[180,384]{1,0:T(8,128)(2,1)S(1)}, u32[]{:S(2)}, u32[]{:S(2)}) collective-permute-start(bf16[180,384]{1,0:T(8,128)(2,1)S(1)} %get-tuple-element.64), channel_id=1, source_target_pairs={{0,3},{1,2},{2,1},{3,0},{4,7},{5,6},{6,5},{7,4},{8,11},{9,10},{10,... | collective-permute-start | bytes 414728 | tf_op jit(solution)/shard_map/ppermute | solution.py:40
  34.0 0.0 collective-permute-start.18
  34.0 1.5 %collective-permute-done.9.refs_0_ = bf16[3,64,640]{2,1,0:T(8,128)(2,1)S(1)} collective-permute-done((bf16[3,64,640]{2,1,0:T(8,128)(2,1)S(1)}, bf16[3,64,640]{2,1,0:T(8,128)(2,1)S(1)}, u32[]{:S(2)}, u32[]{:S(2)}) %collective-permute-start.9) | collective-permute-done | bytes 245792 | tf_op jit(solution)/shard_map/ppermute | solution.py:552
  35.5 0.0 collective-permute-done.10.refs_1_
  35.5 1.1 %finish.2 = (bf16[180,256]{1,0:T(8,128)(2,1)S(1)}, bf16[180,256]{1,0:T(8,128)(2,1)S(1)}, bf16[180,256]{1,0:T(8,128)(2,1)S(1)}, bf16[180,256]{1,0:T(8,128)(2,1)S(1)}) custom-call(f32[4,64,640]{2,1,0:T(8,128)S(1)} %own_terms.3.part_ref.rest_0_, bf16[3,64,640]{2,1,0:T(8,128)(2,1)S(1)} %collective-permute-done.9.refs_0_, ...), custom_call_target="tpu_custom_call" | custom-call | tf_op jit(solution)/shard_map/finish/pallas_call | solution.py:393
  36.6 0.5 %collective-permute-start.13 = (bf16[180,256]{1,0:T(8,128)(2,1)S(1)}, bf16[180,256]{1,0:T(8,128)(2,1)S(1)}, u32[]{:S(2)}, u32[]{:S(2)}) collective-permute-start(bf16[180,256]{1,0:T(8,128)(2,1)S(1)} %get-tuple-element.60), channel_id=1, source_target_pairs={{0,1},{1,0},{2,3},{3,2},{4,5},{5,4},{6,7},{7,6},{8,9},{9,8},{10,11... | collective-permute-start | bytes 276488 | tf_op jit(solution)/shard_map/ppermute | solution.py:40
  37.1 0.0 collective-permute-start.11
  37.2 0.0 collective-permute-done.16.refs_0_
  37.2 2.1 %collective-permute-start.12 = (bf16[180,256]{1,0:T(8,128)(2,1)S(1)}, bf16[180,256]{1,0:T(8,128)(2,1)S(1)}, u32[]{:S(2)}, u32[]{:S(2)}) collective-permute-start(bf16[180,256]{1,0:T(8,128)(2,1)S(1)} %get-tuple-element.58), channel_id=1, source_target_pairs={{0,3},{1,2},{2,1},{3,0},{4,7},{5,6},{6,5},{7,4},{8,11},{9,10},{10,... | collective-permute-start | bytes 276488 | tf_op jit(solution)/shard_map/ppermute | solution.py:40
  39.2 2.0 %collective-permute-done.17.refs_1_ = bf16[180,384]{1,0:T(8,128)(2,1)S(1)} collective-permute-done((bf16[180,384]{1,0:T(8,128)(2,1)S(1)}, bf16[180,384]{1,0:T(8,128)(2,1)S(1)}, u32[]{:S(2)}, u32[]{:S(2)}) %collective-permute-start.17) | collective-permute-done | bytes 138272 | tf_op jit(solution)/shard_map/ppermute | solution.py:40
  41.2 0.0 collective-permute-done.18.refs_3_
  41.2 1.2 %add_chunk.3.refs_2_ = bf16[180,4,640]{2,1,0:T(4,128)(2,1)} custom-call(bf16[4,180,640]{2,1,0:T(8,128)(2,1)S(1)} %copy.19.grad_ref, bf16[180,384]{1,0:T(8,128)(2,1)S(1)} %collective-permute-done.16.refs_0_, bf16[180,384]{1,0:T(8,128)(2,1)S(1)} %collective-permute-done.17.refs_1_, bf16[180,384]{1,0:T(8,128)(2,1)S(1)} %get-tuple-element.65.refs_2_, ...), custom_call_target="tpu_custom_call" | custom-call | tf_op jit(solution)/shard_map/add_chunk/pallas_call | solution.py:454
  42.4 0.0 collective-permute-done.13.refs_1_
  42.4 0.9 %add_chunk.4.refs_2_ = bf16[180,4,640]{2,1,0:T(4,128)(2,1)} custom-call(bf16[4,180,640]{2,1,0:T(8,128)(2,1)S(1)} %copy.19.grad_ref, bf16[180,256]{1,0:T(8,128)(2,1)S(1)} %get-tuple-element.59.refs_0_, bf16[180,256]{1,0:T(8,128)(2,1)S(1)} %collective-permute-done.13.refs_1_, bf16[180,4,640]{2,1,0:T(4,128)(2,1)} %add_chunk.3.refs_2_), custom_call_target="tpu_custom_call", output_to_operand_aliasing={{}: (3, {})} | custom-call | tf_op jit(solution)/shard_map/add_chunk/pallas_call | solution.py:454
  43.3 0.0 collective-permute-done.11.refs_0_
  43.3 1.2 %collective-permute-done.12.refs_1_ = bf16[180,256]{1,0:T(8,128)(2,1)S(1)} collective-permute-done((bf16[180,256]{1,0:T(8,128)(2,1)S(1)}, bf16[180,256]{1,0:T(8,128)(2,1)S(1)}, u32[]{:S(2)}, u32[]{:S(2)}) %collective-permute-start.12) | collective-permute-done | bytes 92192 | tf_op jit(solution)/shard_map/ppermute | solution.py:40
  44.5 0.9 %add_chunk.5 = bf16[180,4,640]{2,1,0:T(4,128)(2,1)} custom-call(bf16[4,180,640]{2,1,0:T(8,128)(2,1)S(1)} %copy.19.grad_ref, bf16[180,256]{1,0:T(8,128)(2,1)S(1)} %collective-permute-done.11.refs_0_, bf16[180,256]{1,0:T(8,128)(2,1)S(1)} %collective-permute-done.12.refs_1_, bf16[180,4,640]{2,1,0:T(4,128)(2,1)} %add_chunk.4.refs_2_), custom_call_target="tpu_custom_call", output_to_operand_aliasing={{}: (3, {})} | custom-call | tf_op jit(solution)/shard_map/add_chunk/pallas_call | solution.py:454
  (6 shorter events, 0.0 us)
Async XLA Ops:
  0.0 2.8 %copy-start.1 = (bf16[1280,640]{1,0:T(8,128)(2,1)S(1)}, bf16[1280,640]{1,0:T(8,128)(2,1)}, u32[]{:S(2)}) copy-start(bf16[1280,640]{1,0:T(8,128)(2,1)} %wout_ref.3) | copy-start | bytes 4915204
  0.0 2.8 %copy-start.6 = (f32[1280]{0:T(1024)S(1)}, f32[1280]{0:T(1024)}, u32[]{:S(2)}) copy-start(f32[1280]{0:T(1024)} %bias_ref.3) | copy-start | bytes 15364
  0.0 2.8 %copy-start = (bf16[640,1280]{1,0:T(8,128)(2,1)S(1)}, bf16[640,1280]{1,0:T(8,128)(2,1)}, u32[]{:S(2)}) copy-start(bf16[640,1280]{1,0:T(8,128)(2,1)} %win_ref.3) | copy-start | bytes 4915204
  5.7 7.9 %collective-permute-start.3 = (bf16[160,384]{1,0:T(8,128)(2,1)S(1)}, bf16[160,384]{1,0:T(8,128)(2,1)S(1)}, u32[]{:S(2)}, u32[]{:S(2)}) collective-permute-start(bf16[160,384]{1,0:T(8,128)(2,1)S(1)} %get-tuple-element.42), channel_id=1, source_target_pairs={{0,2},{1,3},{2,0},{3,1},{4,6},{5,7},{6,4},{7,5},{8,10},{9,11},{10,... | collective-permute-start | bytes 368648 | tf_op jit(solution)/shard_map/ppermute | solution.py:40
  7.9 6.9 %collective-permute-start.4 = (bf16[160,384]{1,0:T(8,128)(2,1)S(1)}, bf16[160,384]{1,0:T(8,128)(2,1)S(1)}, u32[]{:S(2)}, u32[]{:S(2)}) collective-permute-start(bf16[160,384]{1,0:T(8,128)(2,1)S(1)} %get-tuple-element.43), channel_id=1, source_target_pairs={{0,3},{1,2},{2,1},{3,0},{4,7},{5,6},{6,5},{7,4},{8,11},{9,10},{10,... | collective-permute-start | bytes 368648 | tf_op jit(solution)/shard_map/ppermute | solution.py:40
  8.5 6.3 %collective-permute-start.5 = (bf16[160,384]{1,0:T(8,128)(2,1)S(1)}, bf16[160,384]{1,0:T(8,128)(2,1)S(1)}, u32[]{:S(2)}, u32[]{:S(2)}) collective-permute-start(bf16[160,384]{1,0:T(8,128)(2,1)S(1)} %get-tuple-element.44), channel_id=1, source_target_pairs={{0,1},{1,0},{2,3},{3,2},{4,5},{5,4},{6,7},{7,6},{8,9},{9,8},{10,11... | collective-permute-start | bytes 368648 | tf_op jit(solution)/shard_map/ppermute | solution.py:40
  8.8 5.2 %copy-start.2 = (bf16[4,320,640]{2,1,0:T(8,128)(2,1)S(1)}, bf16[4,320,640]{2,1,0:T(8,128)(2,1)}, u32[]{:S(2)}) copy-start(bf16[4,320,640]{2,1,0:T(8,128)(2,1)} %constant.4.clone.forth_ref) | copy-start | bytes 4915204
  8.8 5.2 %copy-start.3 = (bf16[768,640]{1,0:T(8,128)(2,1)S(1)}, bf16[768,640]{1,0:T(8,128)(2,1)}, u32[]{:S(2)}) copy-start(bf16[768,640]{1,0:T(8,128)(2,1)} %constant.5.clone.back_ref) | copy-start | bytes 2949124
  8.8 5.2 %copy-start.4 = (bf16[9,16,640]{2,1,0:T(8,128)(2,1)S(1)}, bf16[9,16,640]{2,1,0:T(8,128)(2,1)}, u32[]{:S(2)}) copy-start(bf16[9,16,640]{2,1,0:T(8,128)(2,1)} %filt_ref.1) | copy-start | bytes 552964
  8.8 5.2 %copy-start.5 = (f32[9,640]{1,0:T(8,128)S(1)}, f32[9,640]{1,0:T(8,128)}, u32[]{:S(2)}) copy-start(f32[9,640]{1,0:T(8,128)} %weight_ref.1) | copy-start | bytes 69124
  8.8 5.2 %copy-start.7 = (s32[16,9]{1,0:T(8,128)S(1)}, s32[16,9]{1,0:T(8,128)}, u32[]{:S(2)}) copy-start(s32[16,9]{1,0:T(8,128)} %offset_ref.1) | copy-start | bytes 1732
  11.8 3.8 %collective-permute-start.6 = (bf16[96,384]{1,0:T(8,128)(2,1)S(1)}, bf16[96,384]{1,0:T(8,128)(2,1)S(1)}, u32[]{:S(2)}, u32[]{:S(2)}) collective-permute-start(bf16[96,384]{1,0:T(8,128)(2,1)S(1)} %get-tuple-element.45), channel_id=1, source_target_pairs={{0,2},{1,3},{2,0},{3,1},{4,6},{5,7},{6,4},{7,5},{8,10},{9,11},{10,... | collective-permute-start | bytes 221192 | tf_op jit(solution)/shard_map/ppermute | solution.py:40
  13.2 4.8 %collective-permute-start.7 = (bf16[96,384]{1,0:T(8,128)(2,1)S(1)}, bf16[96,384]{1,0:T(8,128)(2,1)S(1)}, u32[]{:S(2)}, u32[]{:S(2)}) collective-permute-start(bf16[96,384]{1,0:T(8,128)(2,1)S(1)} %get-tuple-element.46), channel_id=1, source_target_pairs={{0,3},{1,2},{2,1},{3,0},{4,7},{5,6},{6,5},{7,4},{8,11},{9,10},{10,... | collective-permute-start | bytes 221192 | tf_op jit(solution)/shard_map/ppermute | solution.py:40
  13.7 4.3 %collective-permute-start.8 = (bf16[96,384]{1,0:T(8,128)(2,1)S(1)}, bf16[96,384]{1,0:T(8,128)(2,1)S(1)}, u32[]{:S(2)}, u32[]{:S(2)}) collective-permute-start(bf16[96,384]{1,0:T(8,128)(2,1)S(1)} %get-tuple-element.47), channel_id=1, source_target_pairs={{0,1},{1,0},{2,3},{3,2},{4,5},{5,4},{6,7},{7,6},{8,9},{9,8},{10,11... | collective-permute-start | bytes 221192 | tf_op jit(solution)/shard_map/ppermute | solution.py:40
  18.6 11.3 %collective-permute-start.14 = (bf16[3,96,640]{2,1,0:T(8,128)(2,1)S(1)}, bf16[3,96,640]{2,1,0:T(8,128)(2,1)S(1)}, u32[]{:S(2)}, u32[]{:S(2)}) collective-permute-start(bf16[3,96,640]{2,1,0:T(8,128)(2,1)S(1)} %get-tuple-element.61), channel_id=1, source_target_pairs={{0,4},{1,5},{2,6},{3,7},{4,0},{5,1},{6,2},{7,3},{8,12},{9,13},{10,... | collective-permute-start | bytes 1105928 | tf_op jit(solution)/shard_map/ppermute | solution.py:552
  20.0 10.5 %collective-permute-start.15 = (bf16[3,96,640]{2,1,0:T(8,128)(2,1)S(1)}, bf16[3,96,640]{2,1,0:T(8,128)(2,1)S(1)}, u32[]{:S(2)}, u32[]{:S(2)}) collective-permute-start(bf16[3,96,640]{2,1,0:T(8,128)(2,1)S(1)} %get-tuple-element.62), channel_id=1, source_target_pairs={{0,1},{1,0},{2,3},{3,2},{4,8},{5,9},{6,10},{7,11},{8,4},{9,5},{10,... | collective-permute-start | bytes 1105928 | tf_op jit(solution)/shard_map/ppermute | solution.py:552
  20.8 3.4 %collective-permute-start = (bf16[64,384]{1,0:T(8,128)(2,1)S(1)}, bf16[64,384]{1,0:T(8,128)(2,1)S(1)}, u32[]{:S(2)}, u32[]{:S(2)}) collective-permute-start(bf16[64,384]{1,0:T(8,128)(2,1)S(1)} %get-tuple-element.37), channel_id=1, source_target_pairs={{0,2},{1,3},{2,0},{3,1},{4,6},{5,7},{6,4},{7,5},{8,10},{9,11},{10,... | collective-permute-start | bytes 147464 | tf_op jit(solution)/shard_map/ppermute | solution.py:40
  21.1 4.5 %collective-permute-start.1 = (bf16[64,384]{1,0:T(8,128)(2,1)S(1)}, bf16[64,384]{1,0:T(8,128)(2,1)S(1)}, u32[]{:S(2)}, u32[]{:S(2)}) collective-permute-start(bf16[64,384]{1,0:T(8,128)(2,1)S(1)} %get-tuple-element.38), channel_id=1, source_target_pairs={{0,3},{1,2},{2,1},{3,0},{4,7},{5,6},{6,5},{7,4},{8,11},{9,10},{10,... | collective-permute-start | bytes 147464 | tf_op jit(solution)/shard_map/ppermute | solution.py:40
  22.4 3.2 %collective-permute-start.2 = (bf16[64,384]{1,0:T(8,128)(2,1)S(1)}, bf16[64,384]{1,0:T(8,128)(2,1)S(1)}, u32[]{:S(2)}, u32[]{:S(2)}) collective-permute-start(bf16[64,384]{1,0:T(8,128)(2,1)S(1)} %get-tuple-element.40), channel_id=1, source_target_pairs={{0,1},{1,0},{2,3},{3,2},{4,5},{5,4},{6,7},{7,6},{8,9},{9,8},{10,11... | collective-permute-start | bytes 147464 | tf_op jit(solution)/shard_map/ppermute | solution.py:40
  26.2 9.3 %collective-permute-start.9 = (bf16[3,64,640]{2,1,0:T(8,128)(2,1)S(1)}, bf16[3,64,640]{2,1,0:T(8,128)(2,1)S(1)}, u32[]{:S(2)}, u32[]{:S(2)}) collective-permute-start(bf16[3,64,640]{2,1,0:T(8,128)(2,1)S(1)} %get-tuple-element.54), channel_id=1, source_target_pairs={{0,4},{1,5},{2,6},{3,7},{4,0},{5,1},{6,2},{7,3},{8,12},{9,13},{10,... | collective-permute-start | bytes 737288 | tf_op jit(solution)/shard_map/ppermute | solution.py:552
  29.1 6.4 %collective-permute-start.10 = (bf16[3,64,640]{2,1,0:T(8,128)(2,1)S(1)}, bf16[3,64,640]{2,1,0:T(8,128)(2,1)S(1)}, u32[]{:S(2)}, u32[]{:S(2)}) collective-permute-start(bf16[3,64,640]{2,1,0:T(8,128)(2,1)S(1)} %get-tuple-element.55), channel_id=1, source_target_pairs={{0,1},{1,0},{2,3},{3,2},{4,8},{5,9},{6,10},{7,11},{8,4},{9,5},{10,... | collective-permute-start | bytes 737288 | tf_op jit(solution)/shard_map/ppermute | solution.py:552
  31.9 5.2 %collective-permute-start.16 = (bf16[180,384]{1,0:T(8,128)(2,1)S(1)}, bf16[180,384]{1,0:T(8,128)(2,1)S(1)}, u32[]{:S(2)}, u32[]{:S(2)}) collective-permute-start(bf16[180,384]{1,0:T(8,128)(2,1)S(1)} %get-tuple-element.63), channel_id=1, source_target_pairs={{0,2},{1,3},{2,0},{3,1},{4,6},{5,7},{6,4},{7,5},{8,10},{9,11},{10,... | collective-permute-start | bytes 414728 | tf_op jit(solution)/shard_map/ppermute | solution.py:40
  32.8 8.4 %collective-permute-start.17 = (bf16[180,384]{1,0:T(8,128)(2,1)S(1)}, bf16[180,384]{1,0:T(8,128)(2,1)S(1)}, u32[]{:S(2)}, u32[]{:S(2)}) collective-permute-start(bf16[180,384]{1,0:T(8,128)(2,1)S(1)} %get-tuple-element.64), channel_id=1, source_target_pairs={{0,3},{1,2},{2,1},{3,0},{4,7},{5,6},{6,5},{7,4},{8,11},{9,10},{10,... | collective-permute-start | bytes 414728 | tf_op jit(solution)/shard_map/ppermute | solution.py:40
  34.0 7.3 %collective-permute-start.18 = (bf16[180,384]{1,0:T(8,128)(2,1)S(1)}, bf16[180,384]{1,0:T(8,128)(2,1)S(1)}, u32[]{:S(2)}, u32[]{:S(2)}) collective-permute-start(bf16[180,384]{1,0:T(8,128)(2,1)S(1)} %get-tuple-element.66), channel_id=1, source_target_pairs={{0,1},{1,0},{2,3},{3,2},{4,5},{5,4},{6,7},{7,6},{8,9},{9,8},{10,11... | collective-permute-start | bytes 414728 | tf_op jit(solution)/shard_map/ppermute | solution.py:40
  36.6 5.8 %collective-permute-start.13 = (bf16[180,256]{1,0:T(8,128)(2,1)S(1)}, bf16[180,256]{1,0:T(8,128)(2,1)S(1)}, u32[]{:S(2)}, u32[]{:S(2)}) collective-permute-start(bf16[180,256]{1,0:T(8,128)(2,1)S(1)} %get-tuple-element.60), channel_id=1, source_target_pairs={{0,1},{1,0},{2,3},{3,2},{4,5},{5,4},{6,7},{7,6},{8,9},{9,8},{10,11... | collective-permute-start | bytes 276488 | tf_op jit(solution)/shard_map/ppermute | solution.py:40
  37.1 6.2 %collective-permute-start.11 = (bf16[180,256]{1,0:T(8,128)(2,1)S(1)}, bf16[180,256]{1,0:T(8,128)(2,1)S(1)}, u32[]{:S(2)}, u32[]{:S(2)}) collective-permute-start(bf16[180,256]{1,0:T(8,128)(2,1)S(1)} %get-tuple-element.57), channel_id=1, source_target_pairs={{0,2},{1,3},{2,0},{3,1},{4,6},{5,7},{6,4},{7,5},{8,10},{9,11},{10,... | collective-permute-start | bytes 276488 | tf_op jit(solution)/shard_map/ppermute | solution.py:40
  37.2 7.4 %collective-permute-start.12 = (bf16[180,256]{1,0:T(8,128)(2,1)S(1)}, bf16[180,256]{1,0:T(8,128)(2,1)S(1)}, u32[]{:S(2)}, u32[]{:S(2)}) collective-permute-start(bf16[180,256]{1,0:T(8,128)(2,1)S(1)} %get-tuple-element.58), channel_id=1, source_target_pairs={{0,3},{1,2},{2,1},{3,0},{4,7},{5,6},{6,5},{7,4},{8,11},{9,10},{10,... | collective-permute-start | bytes 276488 | tf_op jit(solution)/shard_map/ppermute | solution.py:40

commit v8 on v6

--- a/solution.py
+++ b/solution.py
@@ -103,7 +103,7 @@
             tall[row * wide + whole : (row + 1) * wide, :] = jnp.zeros((wide - whole, channels), jnp.bfloat16)
             tall[row * wide : row * wide + part, :] = source[half * rows + row]
 
-    group = 48
+    group = 96
     groups = rows * wide // group
 
     def span(step):
@@ -133,7 +133,7 @@
     stack(tall_grad, grad_ref)
     project_back(0)
     gathered = 0
-    thirds = [groups * n // 3 for n in range(4)]
+    thirds = [groups * n // 4 for n in (0, 1, 3, 4)]
     for step in range(steps):
         if step + 1 < steps:
             project_pre(step + 1)

time: 45.1 us -> 45.1 us (level)
  no operation moved by 1% of the time
where the time goes in v8:
time: 45.1 us; the launch traced here: 45 us
  starting transfers between devices  16.8 us (37%)
  Pallas kernels  15.6 us (35%)
  waiting for transfers between devices  9.45 us (21%)
  local copies, waits for them, and re-layouts  2.77 us (6%)
    ppermute x15, starting transfers between devices, exchange(): return lax.ppermute(block, 'azimuth', pairs)  11.6 us
    ppermute x15, waiting for transfers between devices, exchange(): return lax.ppermute(block, 'azimuth', pairs)  7.73 us
    pallas_call x2, Pallas kernels, mlp(): pl.pallas_call(functools.partial(mlp_kernel, count, half, sent, chunks),...  5.53 us
    ppermute x4, starting transfers between devices, halo(): blocks.append(lax.ppermute(block, ('polar', 'azimuth'), pairs))  5.17 us
    pallas_call x3, Pallas kernels, add_chunk(): pl.pallas_call(functools.partial(add_kernel, count, chunk, [k for k, _ in...  2.92 us
    unnamed x18, local copies, waits for them, and re-layouts  2.77 us
    pallas_call x2, Pallas kernels, finish(): pl.pallas_call(functools.partial(finish_kernel, count, len(halos)), in_sp...  2.35 us
    ppermute x4, waiting for transfers between devices, halo(): blocks.append(lax.ppermute(block, ('polar', 'azimuth'), pairs))  1.72 us
  transfers between devices with their start and end apart: 19, of which 7 were waited for; matrix products, arithmetic and copies ran while one was open for 0% of the time, Pallas kernels for 25%

profile of v8, /device:TPU:1, one launch (start us, length us, event | category | flops | bytes accessed | tf_op | source)
XLA Modules:
  0.0 45.0 jit_solution(13659221021750985816)
XLA Ops:
  0.0 0.0 copy-start.1
  0.0 1.4 %copy.19.grad_ref = bf16[4,180,640]{2,1,0:T(8,128)(2,1)S(1)} copy(bf16[4,180,640]{2,0,1:T(4,128)(2,1)} %param.11) | data formatting | bytes 1843200 | tf_op args[1]
  1.5 1.3 %copy.15.conv_ref = bf16[4,180,640]{2,1,0:T(8,128)(2,1)S(1)} copy(bf16[4,180,640]{2,0,1:T(4,128)(2,1)} %param.10) | data formatting | bytes 1843200 | tf_op args[0]
  2.8 0.0 copy-done.1
  2.8 0.0 copy-done.6
  2.8 0.0 copy-done
  2.8 2.8 %mlp.2 = (bf16[160,384]{1,0:T(8,128)(2,1)S(1)}, bf16[160,384]{1,0:T(8,128)(2,1)S(1)}, bf16[160,384]{1,0:T(8,128)(2,1)S(1)}, bf16[160,384]{1,0:T(8,128)(2,1)S(1)}) custom-call(bf16[4,180,640]{2,1,0:T(8,128)(2,1)S(1)} %copy.15.conv_ref, bf16[4,180,640]{2,1,0:T(8,128)(2,1)S(1)} %copy.19.grad_ref, bf16[640,1280]{1,0:T(8,128)(2,1)S(1)} %copy-done, ...), custom_call_target="tpu_custom_call" | custom-call | tf_op jit(solution)/shard_map/mlp/pallas_call | solution.py:165
  5.6 2.1 %collective-permute-start.3 = (bf16[160,384]{1,0:T(8,128)(2,1)S(1)}, bf16[160,384]{1,0:T(8,128)(2,1)S(1)}, u32[]{:S(2)}, u32[]{:S(2)}) collective-permute-start(bf16[160,384]{1,0:T(8,128)(2,1)S(1)} %get-tuple-element.42), channel_id=1, source_target_pairs={{0,2},{1,3},{2,0},{3,1},{4,6},{5,7},{6,4},{7,5},{8,10},{9,11},{10,... | collective-permute-start | bytes 368648 | tf_op jit(solution)/shard_map/ppermute | solution.py:40
  7.7 0.6 %collective-permute-start.4 = (bf16[160,384]{1,0:T(8,128)(2,1)S(1)}, bf16[160,384]{1,0:T(8,128)(2,1)S(1)}, u32[]{:S(2)}, u32[]{:S(2)}) collective-permute-start(bf16[160,384]{1,0:T(8,128)(2,1)S(1)} %get-tuple-element.43), channel_id=1, source_target_pairs={{0,3},{1,2},{2,1},{3,0},{4,7},{5,6},{6,5},{7,4},{8,11},{9,10},{10,... | collective-permute-start | bytes 368648 | tf_op jit(solution)/shard_map/ppermute | solution.py:40
  8.3 0.3 collective-permute-start.5
  8.6 0.0 copy-start.7
  8.6 2.8 %mlp.3 = (bf16[160,384]{1,0:T(8,128)(2,1)S(1)}, bf16[96,384]{1,0:T(8,128)(2,1)S(1)}, bf16[96,384]{1,0:T(8,128)(2,1)S(1)}, bf16[96,384]{1,0:T(8,128)(2,1)S(1)}, b...) custom-call(bf16[4,180,640]{2,1,0:T(8,128)(2,1)S(1)} %copy.15.conv_ref, ...), custom_call_target="tpu_custom_call" | custom-call | tf_op jit(solution)/shard_map/mlp/pallas_call | solution.py:165
  11.4 1.4 %collective-permute-start.6 = (bf16[96,384]{1,0:T(8,128)(2,1)S(1)}, bf16[96,384]{1,0:T(8,128)(2,1)S(1)}, u32[]{:S(2)}, u32[]{:S(2)}) collective-permute-start(bf16[96,384]{1,0:T(8,128)(2,1)S(1)} %get-tuple-element.45), channel_id=1, source_target_pairs={{0,2},{1,3},{2,0},{3,1},{4,6},{5,7},{6,4},{7,5},{8,10},{9,11},{10,... | collective-permute-start | bytes 221192 | tf_op jit(solution)/shard_map/ppermute | solution.py:40
  12.9 0.4 collective-permute-start.7
  13.3 0.0 collective-permute-done.3.refs_0_
  13.3 0.3 collective-permute-start.8
  13.6 0.0 copy-done.2
  13.6 0.0 copy-done.3
  13.6 0.0 copy-done.4
  13.6 0.0 copy-done.5
  13.6 0.0 copy-done.7
  13.6 0.7 %prepare.1 = (bf16[10,32,768]{2,1,0:T(8,128)(2,1)S(1)}, s32[10,32]{1,0:T(8,128)S(1)}, bf16[4,320,640]{2,1,0:T(8,128)(2,1)S(1)}, bf16[768,640]{1,0:T(8,128)(2,1)S...) custom-call(f32[9,640]{1,0:T(8,128)S(1)} %copy-done.5, bf16[9,16,640]{2,1,0:T(8,128)(2,1)S(1)} %copy-done.4, ...), custom_call_target="tpu_custom_call" | custom-call | tf_op jit(solution)/shard_map/prepare/pallas_call | solution.py:524
  14.4 0.0 collective-permute-done.4.refs_1_
  14.4 0.0 collective-permute-done.5.refs_3_
  14.4 0.7 %analysis_early.1.refs_5_.rest_0_ = f32[2,160,640]{2,1,0:T(8,128)S(1)} custom-call(bf16[160,384]{1,0:T(8,128)(2,1)S(1)} %collective-permute-done.3.refs_0_, bf16[160,384]{1,0:T(8,128)(2,1)S(1)} %collective-permute-done.4.refs_1_, bf16[160,384]{1,0:T(8,128)(2,1)S(1)} %get-tuple-element.36.rest_0_.refs_2_, ...), custom_call_target="tpu_custom_call" | custom-call | tf_op jit(solution)/shard_map/analysis_early/pallas_call | solution.py:214
  15.1 0.1 collective-permute-done.6.refs_0_
  15.2 2.5 %collective-permute-done.7.refs_1_ = bf16[96,384]{1,0:T(8,128)(2,1)S(1)} collective-permute-done((bf16[96,384]{1,0:T(8,128)(2,1)S(1)}, bf16[96,384]{1,0:T(8,128)(2,1)S(1)}, u32[]{:S(2)}, u32[]{:S(2)}) %collective-permute-start.7) | collective-permute-done | bytes 73760 | tf_op jit(solution)/shard_map/ppermute | solution.py:40
  17.7 0.0 collective-permute-done.8.refs_3_
  17.7 0.6 %analysis.2 = (f32[2,96,640]{2,1,0:T(8,128)S(1)}, bf16[3,96,640]{2,1,0:T(8,128)(2,1)S(1)}, bf16[3,96,640]{2,1,0:T(8,128)(2,1)S(1)}) custom-call(bf16[96,384]{1,0:T(8,128)(2,1)S(1)} %collective-permute-done.6.refs_0_, bf16[96,384]{1,0:T(8,128)(2,1)S(1)} %collective-permute-done.7.refs_1_, bf16[160,384]{1,0:T(8,128)(2,1)S(1)} %get-tuple-element.39.refs_2_, ...), custom_call_target="tpu_custom_call" | custom-call | tf_op jit(solution)/shard_map/analysis/pallas_call | solution.py:255
  18.3 1.4 %collective-permute-start.14 = (bf16[3,96,640]{2,1,0:T(8,128)(2,1)S(1)}, bf16[3,96,640]{2,1,0:T(8,128)(2,1)S(1)}, u32[]{:S(2)}, u32[]{:S(2)}) collective-permute-start(bf16[3,96,640]{2,1,0:T(8,128)(2,1)S(1)} %get-tuple-element.61), channel_id=1, source_target_pairs={{0,4},{1,5},{2,6},{3,7},{4,0},{5,1},{6,2},{7,3},{8,12},{9,13},{10,... | collective-permute-start | bytes 1105928 | tf_op jit(solution)/shard_map/ppermute | solution.py:546
  19.7 0.7 %collective-permute-start.15 = (bf16[3,96,640]{2,1,0:T(8,128)(2,1)S(1)}, bf16[3,96,640]{2,1,0:T(8,128)(2,1)S(1)}, u32[]{:S(2)}, u32[]{:S(2)}) collective-permute-start(bf16[3,96,640]{2,1,0:T(8,128)(2,1)S(1)} %get-tuple-element.62), channel_id=1, source_target_pairs={{0,1},{1,0},{2,3},{3,2},{4,8},{5,9},{6,10},{7,11},{8,4},{9,5},{10,... | collective-permute-start | bytes 1105928 | tf_op jit(solution)/shard_map/ppermute | solution.py:546
  20.4 0.3 collective-permute-start
  20.7 1.3 %collective-permute-start.1 = (bf16[64,384]{1,0:T(8,128)(2,1)S(1)}, bf16[64,384]{1,0:T(8,128)(2,1)S(1)}, u32[]{:S(2)}, u32[]{:S(2)}) collective-permute-start(bf16[64,384]{1,0:T(8,128)(2,1)S(1)} %get-tuple-element.38), channel_id=1, source_target_pairs={{0,3},{1,2},{2,1},{3,0},{4,7},{5,6},{6,5},{7,4},{8,11},{9,10},{10,... | collective-permute-start | bytes 147464 | tf_op jit(solution)/shard_map/ppermute | solution.py:40
  22.0 0.2 collective-permute-start.2
  22.3 1.0 %own_terms.2.refs_6_.part_ref = f32[4,96,640]{2,1,0:T(8,128)S(1)} custom-call(f32[2,96,640]{2,1,0:T(8,128)S(1)} %get-tuple-element.48.own_ref, f32[96,32]{1,0:T(8,128)S(1)} %get-tuple-element.49.weight_ref.refs_1_, s32[10,32]{1,0:T(8,128)S(1)} %get-tuple-element.50.target_ref.refs_3_.refs_2_, ...), custom_call_target="tpu_custom_call" | custom-call | tf_op jit(solution)/shard_map/own_terms/pallas_call | solution.py:311
  23.3 0.5 %collective-permute-done.refs_0_ = bf16[64,384]{1,0:T(8,128)(2,1)S(1)} collective-permute-done((bf16[64,384]{1,0:T(8,128)(2,1)S(1)}, bf16[64,384]{1,0:T(8,128)(2,1)S(1)}, u32[]{:S(2)}, u32[]{:S(2)}) %collective-permute-start) | collective-permute-done | bytes 49184 | tf_op jit(solution)/shard_map/ppermute | solution.py:40
  23.8 1.4 %collective-permute-done.1.refs_1_ = bf16[64,384]{1,0:T(8,128)(2,1)S(1)} collective-permute-done((bf16[64,384]{1,0:T(8,128)(2,1)S(1)}, bf16[64,384]{1,0:T(8,128)(2,1)S(1)}, u32[]{:S(2)}, u32[]{:S(2)}) %collective-permute-start.1) | collective-permute-done | bytes 49184 | tf_op jit(solution)/shard_map/ppermute | solution.py:40
  25.2 0.0 collective-permute-done.2.refs_3_
  25.2 0.6 %analysis.3 = (f32[2,64,640]{2,1,0:T(8,128)S(1)}, bf16[3,64,640]{2,1,0:T(8,128)(2,1)S(1)}, bf16[3,64,640]{2,1,0:T(8,128)(2,1)S(1)}) custom-call(bf16[64,384]{1,0:T(8,128)(2,1)S(1)} %collective-permute-done.refs_0_, bf16[64,384]{1,0:T(8,128)(2,1)S(1)} %collective-permute-done.1.refs_1_, bf16[160,384]{1,0:T(8,128)(2,1)S(1)} %get-tuple-element.39.refs_2_, ...), custom_call_target="tpu_custom_call" | custom-call | tf_op jit(solution)/shard_map/analysis/pallas_call | solution.py:255
  25.8 2.9 %collective-permute-start.9 = (bf16[3,64,640]{2,1,0:T(8,128)(2,1)S(1)}, bf16[3,64,640]{2,1,0:T(8,128)(2,1)S(1)}, u32[]{:S(2)}, u32[]{:S(2)}) collective-permute-start(bf16[3,64,640]{2,1,0:T(8,128)(2,1)S(1)} %get-tuple-element.54), channel_id=1, source_target_pairs={{0,4},{1,5},{2,6},{3,7},{4,0},{5,1},{6,2},{7,3},{8,12},{9,13},{10,... | collective-permute-start | bytes 737288 | tf_op jit(solution)/shard_map/ppermute | solution.py:546
  28.7 0.2 collective-permute-start.10
  28.9 0.7 %own_terms.3.part_ref.rest_0_ = f32[4,64,640]{2,1,0:T(8,128)S(1)} custom-call(f32[2,64,640]{2,1,0:T(8,128)S(1)} %get-tuple-element.52.own_ref, f32[64,32]{1,0:T(8,128)S(1)} %get-tuple-element.53.weight_ref.refs_2_, s32[10,32]{1,0:T(8,128)S(1)} %get-tuple-element.50.target_ref.refs_3_.refs_2_, ...), custom_call_target="tpu_custom_call" | custom-call | tf_op jit(solution)/shard_map/own_terms/pallas_call | solution.py:311
  29.6 0.0 collective-permute-done.14.first_ref
  29.6 0.5 %side_terms.1.part_ref = f32[4,96,640]{2,1,0:T(8,128)S(1)} custom-call(f32[4,96,640]{2,1,0:T(8,128)S(1)} %own_terms.2.refs_6_.part_ref, bf16[3,96,640]{2,1,0:T(8,128)(2,1)S(1)} %collective-permute-done.14.first_ref, f32[96,32]{1,0:T(8,128)S(1)} %get-tuple-element.49.weight_ref.refs_1_, s32[10,32]{1,0:T(8,128)S(1)} %get-tuple-element.50.target_ref.refs_3_.refs_2_, ...), custom_call_target="tpu_custom_call" | custom-call | tf_op jit(solution)/shard_map/side_terms/pallas_call | solution.py:353
  30.1 0.0 collective-permute-done.15.refs_0_
  30.1 1.3 %finish.3 = (bf16[180,384]{1,0:T(8,128)(2,1)S(1)}, bf16[180,384]{1,0:T(8,128)(2,1)S(1)}, bf16[180,384]{1,0:T(8,128)(2,1)S(1)}, bf16[180,384]{1,0:T(8,128)(2,1)S(1)}) custom-call(f32[4,96,640]{2,1,0:T(8,128)S(1)} %side_terms.1.part_ref, bf16[3,96,640]{2,1,0:T(8,128)(2,1)S(1)} %collective-permute-done.15.refs_0_, ...), custom_call_target="tpu_custom_call" | custom-call | tf_op jit(solution)/shard_map/finish/pallas_call | solution.py:387
  31.4 0.9 %collective-permute-start.16 = (bf16[180,384]{1,0:T(8,128)(2,1)S(1)}, bf16[180,384]{1,0:T(8,128)(2,1)S(1)}, u32[]{:S(2)}, u32[]{:S(2)}) collective-permute-start(bf16[180,384]{1,0:T(8,128)(2,1)S(1)} %get-tuple-element.63), channel_id=1, source_target_pairs={{0,2},{1,3},{2,0},{3,1},{4,6},{5,7},{6,4},{7,5},{8,10},{9,11},{10,... | collective-permute-start | bytes 414728 | tf_op jit(solution)/shard_map/ppermute | solution.py:40
  32.3 1.2 %collective-permute-start.17 = (bf16[180,384]{1,0:T(8,128)(2,1)S(1)}, bf16[180,384]{1,0:T(8,128)(2,1)S(1)}, u32[]{:S(2)}, u32[]{:S(2)}) collective-permute-start(bf16[180,384]{1,0:T(8,128)(2,1)S(1)} %get-tuple-element.64), channel_id=1, source_target_pairs={{0,3},{1,2},{2,1},{3,0},{4,7},{5,6},{6,5},{7,4},{8,11},{9,10},{10,... | collective-permute-start | bytes 414728 | tf_op jit(solution)/shard_map/ppermute | solution.py:40
  33.4 0.0 collective-permute-start.18
  33.4 1.7 %collective-permute-done.9.refs_0_ = bf16[3,64,640]{2,1,0:T(8,128)(2,1)S(1)} collective-permute-done((bf16[3,64,640]{2,1,0:T(8,128)(2,1)S(1)}, bf16[3,64,640]{2,1,0:T(8,128)(2,1)S(1)}, u32[]{:S(2)}, u32[]{:S(2)}) %collective-permute-start.9) | collective-permute-done | bytes 245792 | tf_op jit(solution)/shard_map/ppermute | solution.py:546
  35.1 0.0 collective-permute-done.10.refs_1_
  35.2 1.1 %finish.2 = (bf16[180,256]{1,0:T(8,128)(2,1)S(1)}, bf16[180,256]{1,0:T(8,128)(2,1)S(1)}, bf16[180,256]{1,0:T(8,128)(2,1)S(1)}, bf16[180,256]{1,0:T(8,128)(2,1)S(1)}) custom-call(f32[4,64,640]{2,1,0:T(8,128)S(1)} %own_terms.3.part_ref.rest_0_, bf16[3,64,640]{2,1,0:T(8,128)(2,1)S(1)} %collective-permute-done.9.refs_0_, ...), custom_call_target="tpu_custom_call" | custom-call | tf_op jit(solution)/shard_map/finish/pallas_call | solution.py:387
  36.2 0.5 %collective-permute-start.13 = (bf16[180,256]{1,0:T(8,128)(2,1)S(1)}, bf16[180,256]{1,0:T(8,128)(2,1)S(1)}, u32[]{:S(2)}, u32[]{:S(2)}) collective-permute-start(bf16[180,256]{1,0:T(8,128)(2,1)S(1)} %get-tuple-element.60), channel_id=1, source_target_pairs={{0,1},{1,0},{2,3},{3,2},{4,5},{5,4},{6,7},{7,6},{8,9},{9,8},{10,11... | collective-permute-start | bytes 276488 | tf_op jit(solution)/shard_map/ppermute | solution.py:40
  36.8 0.0 collective-permute-start.11
  36.8 0.0 collective-permute-done.16.refs_0_
  36.8 1.9 %collective-permute-start.12 = (bf16[180,256]{1,0:T(8,128)(2,1)S(1)}, bf16[180,256]{1,0:T(8,128)(2,1)S(1)}, u32[]{:S(2)}, u32[]{:S(2)}) collective-permute-start(bf16[180,256]{1,0:T(8,128)(2,1)S(1)} %get-tuple-element.58), channel_id=1, source_target_pairs={{0,3},{1,2},{2,1},{3,0},{4,7},{5,6},{6,5},{7,4},{8,11},{9,10},{10,... | collective-permute-start | bytes 276488 | tf_op jit(solution)/shard_map/ppermute | solution.py:40
  38.7 1.9 %collective-permute-done.17.refs_1_ = bf16[180,384]{1,0:T(8,128)(2,1)S(1)} collective-permute-done((bf16[180,384]{1,0:T(8,128)(2,1)S(1)}, bf16[180,384]{1,0:T(8,128)(2,1)S(1)}, u32[]{:S(2)}, u32[]{:S(2)}) %collective-permute-start.17) | collective-permute-done | bytes 138272 | tf_op jit(solution)/shard_map/ppermute | solution.py:40
  40.6 0.0 collective-permute-done.18.refs_3_
  40.6 1.2 %add_chunk.3.refs_2_ = bf16[180,4,640]{2,1,0:T(4,128)(2,1)} custom-call(bf16[4,180,640]{2,1,0:T(8,128)(2,1)S(1)} %copy.19.grad_ref, bf16[180,384]{1,0:T(8,128)(2,1)S(1)} %collective-permute-done.16.refs_0_, bf16[180,384]{1,0:T(8,128)(2,1)S(1)} %collective-permute-done.17.refs_1_, bf16[180,384]{1,0:T(8,128)(2,1)S(1)} %get-tuple-element.65.refs_2_, ...), custom_call_target="tpu_custom_call" | custom-call | tf_op jit(solution)/shard_map/add_chunk/pallas_call | solution.py:448
  41.8 0.0 collective-permute-done.13.refs_1_
  41.8 0.9 %add_chunk.4.refs_2_ = bf16[180,4,640]{2,1,0:T(4,128)(2,1)} custom-call(bf16[4,180,640]{2,1,0:T(8,128)(2,1)S(1)} %copy.19.grad_ref, bf16[180,256]{1,0:T(8,128)(2,1)S(1)} %get-tuple-element.59.refs_0_, bf16[180,256]{1,0:T(8,128)(2,1)S(1)} %collective-permute-done.13.refs_1_, bf16[180,4,640]{2,1,0:T(4,128)(2,1)} %add_chunk.3.refs_2_), custom_call_target="tpu_custom_call", output_to_operand_aliasing={{}: (3, {})} | custom-call | tf_op jit(solution)/shard_map/add_chunk/pallas_call | solution.py:448
  42.7 0.0 collective-permute-done.11.refs_0_
  42.7 1.3 %collective-permute-done.12.refs_1_ = bf16[180,256]{1,0:T(8,128)(2,1)S(1)} collective-permute-done((bf16[180,256]{1,0:T(8,128)(2,1)S(1)}, bf16[180,256]{1,0:T(8,128)(2,1)S(1)}, u32[]{:S(2)}, u32[]{:S(2)}) %collective-permute-start.12) | collective-permute-done | bytes 92192 | tf_op jit(solution)/shard_map/ppermute | solution.py:40
  44.0 0.9 %add_chunk.5 = bf16[180,4,640]{2,1,0:T(4,128)(2,1)} custom-call(bf16[4,180,640]{2,1,0:T(8,128)(2,1)S(1)} %copy.19.grad_ref, bf16[180,256]{1,0:T(8,128)(2,1)S(1)} %collective-permute-done.11.refs_0_, bf16[180,256]{1,0:T(8,128)(2,1)S(1)} %collective-permute-done.12.refs_1_, bf16[180,4,640]{2,1,0:T(4,128)(2,1)} %add_chunk.4.refs_2_), custom_call_target="tpu_custom_call", output_to_operand_aliasing={{}: (3, {})} | custom-call | tf_op jit(solution)/shard_map/add_chunk/pallas_call | solution.py:448
  (6 shorter events, 0.0 us)
Async XLA Ops:
  0.0 2.8 %copy-start.1 = (bf16[1280,640]{1,0:T(8,128)(2,1)S(1)}, bf16[1280,640]{1,0:T(8,128)(2,1)}, u32[]{:S(2)}) copy-start(bf16[1280,640]{1,0:T(8,128)(2,1)} %wout_ref.3) | copy-start | bytes 4915204
  0.0 2.8 %copy-start.6 = (f32[1280]{0:T(1024)S(1)}, f32[1280]{0:T(1024)}, u32[]{:S(2)}) copy-start(f32[1280]{0:T(1024)} %bias_ref.3) | copy-start | bytes 15364
  0.0 2.8 %copy-start = (bf16[640,1280]{1,0:T(8,128)(2,1)S(1)}, bf16[640,1280]{1,0:T(8,128)(2,1)}, u32[]{:S(2)}) copy-start(bf16[640,1280]{1,0:T(8,128)(2,1)} %win_ref.3) | copy-start | bytes 4915204
  5.6 7.7 %collective-permute-start.3 = (bf16[160,384]{1,0:T(8,128)(2,1)S(1)}, bf16[160,384]{1,0:T(8,128)(2,1)S(1)}, u32[]{:S(2)}, u32[]{:S(2)}) collective-permute-start(bf16[160,384]{1,0:T(8,128)(2,1)S(1)} %get-tuple-element.42), channel_id=1, source_target_pairs={{0,2},{1,3},{2,0},{3,1},{4,6},{5,7},{6,4},{7,5},{8,10},{9,11},{10,... | collective-permute-start | bytes 368648 | tf_op jit(solution)/shard_map/ppermute | solution.py:40
  7.7 6.7 %collective-permute-start.4 = (bf16[160,384]{1,0:T(8,128)(2,1)S(1)}, bf16[160,384]{1,0:T(8,128)(2,1)S(1)}, u32[]{:S(2)}, u32[]{:S(2)}) collective-permute-start(bf16[160,384]{1,0:T(8,128)(2,1)S(1)} %get-tuple-element.43), channel_id=1, source_target_pairs={{0,3},{1,2},{2,1},{3,0},{4,7},{5,6},{6,5},{7,4},{8,11},{9,10},{10,... | collective-permute-start | bytes 368648 | tf_op jit(solution)/shard_map/ppermute | solution.py:40
  8.3 6.1 %collective-permute-start.5 = (bf16[160,384]{1,0:T(8,128)(2,1)S(1)}, bf16[160,384]{1,0:T(8,128)(2,1)S(1)}, u32[]{:S(2)}, u32[]{:S(2)}) collective-permute-start(bf16[160,384]{1,0:T(8,128)(2,1)S(1)} %get-tuple-element.44), channel_id=1, source_target_pairs={{0,1},{1,0},{2,3},{3,2},{4,5},{5,4},{6,7},{7,6},{8,9},{9,8},{10,11... | collective-permute-start | bytes 368648 | tf_op jit(solution)/shard_map/ppermute | solution.py:40
  8.6 5.0 %copy-start.2 = (bf16[4,320,640]{2,1,0:T(8,128)(2,1)S(1)}, bf16[4,320,640]{2,1,0:T(8,128)(2,1)}, u32[]{:S(2)}) copy-start(bf16[4,320,640]{2,1,0:T(8,128)(2,1)} %constant.4.clone.forth_ref) | copy-start | bytes 4915204
  8.6 5.0 %copy-start.3 = (bf16[768,640]{1,0:T(8,128)(2,1)S(1)}, bf16[768,640]{1,0:T(8,128)(2,1)}, u32[]{:S(2)}) copy-start(bf16[768,640]{1,0:T(8,128)(2,1)} %constant.5.clone.back_ref) | copy-start | bytes 2949124
  8.6 5.0 %copy-start.4 = (bf16[9,16,640]{2,1,0:T(8,128)(2,1)S(1)}, bf16[9,16,640]{2,1,0:T(8,128)(2,1)}, u32[]{:S(2)}) copy-start(bf16[9,16,640]{2,1,0:T(8,128)(2,1)} %filt_ref.1) | copy-start | bytes 552964
  8.6 5.0 %copy-start.5 = (f32[9,640]{1,0:T(8,128)S(1)}, f32[9,640]{1,0:T(8,128)}, u32[]{:S(2)}) copy-start(f32[9,640]{1,0:T(8,128)} %weight_ref.1) | copy-start | bytes 69124
  8.6 5.0 %copy-start.7 = (s32[16,9]{1,0:T(8,128)S(1)}, s32[16,9]{1,0:T(8,128)}, u32[]{:S(2)}) copy-start(s32[16,9]{1,0:T(8,128)} %offset_ref.1) | copy-start | bytes 1732
  11.4 3.8 %collective-permute-start.6 = (bf16[96,384]{1,0:T(8,128)(2,1)S(1)}, bf16[96,384]{1,0:T(8,128)(2,1)S(1)}, u32[]{:S(2)}, u32[]{:S(2)}) collective-permute-start(bf16[96,384]{1,0:T(8,128)(2,1)S(1)} %get-tuple-element.45), channel_id=1, source_target_pairs={{0,2},{1,3},{2,0},{3,1},{4,6},{5,7},{6,4},{7,5},{8,10},{9,11},{10,... | collective-permute-start | bytes 221192 | tf_op jit(solution)/shard_map/ppermute | solution.py:40
  12.9 4.8 %collective-permute-start.7 = (bf16[96,384]{1,0:T(8,128)(2,1)S(1)}, bf16[96,384]{1,0:T(8,128)(2,1)S(1)}, u32[]{:S(2)}, u32[]{:S(2)}) collective-permute-start(bf16[96,384]{1,0:T(8,128)(2,1)S(1)} %get-tuple-element.46), channel_id=1, source_target_pairs={{0,3},{1,2},{2,1},{3,0},{4,7},{5,6},{6,5},{7,4},{8,11},{9,10},{10,... | collective-permute-start | bytes 221192 | tf_op jit(solution)/shard_map/ppermute | solution.py:40
  13.3 4.4 %collective-permute-start.8 = (bf16[96,384]{1,0:T(8,128)(2,1)S(1)}, bf16[96,384]{1,0:T(8,128)(2,1)S(1)}, u32[]{:S(2)}, u32[]{:S(2)}) collective-permute-start(bf16[96,384]{1,0:T(8,128)(2,1)S(1)} %get-tuple-element.47), channel_id=1, source_target_pairs={{0,1},{1,0},{2,3},{3,2},{4,5},{5,4},{6,7},{7,6},{8,9},{9,8},{10,11... | collective-permute-start | bytes 221192 | tf_op jit(solution)/shard_map/ppermute | solution.py:40
  18.3 11.3 %collective-permute-start.14 = (bf16[3,96,640]{2,1,0:T(8,128)(2,1)S(1)}, bf16[3,96,640]{2,1,0:T(8,128)(2,1)S(1)}, u32[]{:S(2)}, u32[]{:S(2)}) collective-permute-start(bf16[3,96,640]{2,1,0:T(8,128)(2,1)S(1)} %get-tuple-element.61), channel_id=1, source_target_pairs={{0,4},{1,5},{2,6},{3,7},{4,0},{5,1},{6,2},{7,3},{8,12},{9,13},{10,... | collective-permute-start | bytes 1105928 | tf_op jit(solution)/shard_map/ppermute | solution.py:546
  19.7 10.4 %collective-permute-start.15 = (bf16[3,96,640]{2,1,0:T(8,128)(2,1)S(1)}, bf16[3,96,640]{2,1,0:T(8,128)(2,1)S(1)}, u32[]{:S(2)}, u32[]{:S(2)}) collective-permute-start(bf16[3,96,640]{2,1,0:T(8,128)(2,1)S(1)} %get-tuple-element.62), channel_id=1, source_target_pairs={{0,1},{1,0},{2,3},{3,2},{4,8},{5,9},{6,10},{7,11},{8,4},{9,5},{10,... | collective-permute-start | bytes 1105928 | tf_op jit(solution)/shard_map/ppermute | solution.py:546
  20.4 3.4 %collective-permute-start = (bf16[64,384]{1,0:T(8,128)(2,1)S(1)}, bf16[64,384]{1,0:T(8,128)(2,1)S(1)}, u32[]{:S(2)}, u32[]{:S(2)}) collective-permute-start(bf16[64,384]{1,0:T(8,128)(2,1)S(1)} %get-tuple-element.37), channel_id=1, source_target_pairs={{0,2},{1,3},{2,0},{3,1},{4,6},{5,7},{6,4},{7,5},{8,10},{9,11},{10,... | collective-permute-start | bytes 147464 | tf_op jit(solution)/shard_map/ppermute | solution.py:40
  20.7 4.5 %collective-permute-start.1 = (bf16[64,384]{1,0:T(8,128)(2,1)S(1)}, bf16[64,384]{1,0:T(8,128)(2,1)S(1)}, u32[]{:S(2)}, u32[]{:S(2)}) collective-permute-start(bf16[64,384]{1,0:T(8,128)(2,1)S(1)} %get-tuple-element.38), channel_id=1, source_target_pairs={{0,3},{1,2},{2,1},{3,0},{4,7},{5,6},{6,5},{7,4},{8,11},{9,10},{10,... | collective-permute-start | bytes 147464 | tf_op jit(solution)/shard_map/ppermute | solution.py:40
  22.0 3.2 %collective-permute-start.2 = (bf16[64,384]{1,0:T(8,128)(2,1)S(1)}, bf16[64,384]{1,0:T(8,128)(2,1)S(1)}, u32[]{:S(2)}, u32[]{:S(2)}) collective-permute-start(bf16[64,384]{1,0:T(8,128)(2,1)S(1)} %get-tuple-element.40), channel_id=1, source_target_pairs={{0,1},{1,0},{2,3},{3,2},{4,5},{5,4},{6,7},{7,6},{8,9},{9,8},{10,11... | collective-permute-start | bytes 147464 | tf_op jit(solution)/shard_map/ppermute | solution.py:40
  25.8 9.3 %collective-permute-start.9 = (bf16[3,64,640]{2,1,0:T(8,128)(2,1)S(1)}, bf16[3,64,640]{2,1,0:T(8,128)(2,1)S(1)}, u32[]{:S(2)}, u32[]{:S(2)}) collective-permute-start(bf16[3,64,640]{2,1,0:T(8,128)(2,1)S(1)} %get-tuple-element.54), channel_id=1, source_target_pairs={{0,4},{1,5},{2,6},{3,7},{4,0},{5,1},{6,2},{7,3},{8,12},{9,13},{10,... | collective-permute-start | bytes 737288 | tf_op jit(solution)/shard_map/ppermute | solution.py:546
  28.7 6.5 %collective-permute-start.10 = (bf16[3,64,640]{2,1,0:T(8,128)(2,1)S(1)}, bf16[3,64,640]{2,1,0:T(8,128)(2,1)S(1)}, u32[]{:S(2)}, u32[]{:S(2)}) collective-permute-start(bf16[3,64,640]{2,1,0:T(8,128)(2,1)S(1)} %get-tuple-element.55), channel_id=1, source_target_pairs={{0,1},{1,0},{2,3},{3,2},{4,8},{5,9},{6,10},{7,11},{8,4},{9,5},{10,... | collective-permute-start | bytes 737288 | tf_op jit(solution)/shard_map/ppermute | solution.py:546
  31.4 5.4 %collective-permute-start.16 = (bf16[180,384]{1,0:T(8,128)(2,1)S(1)}, bf16[180,384]{1,0:T(8,128)(2,1)S(1)}, u32[]{:S(2)}, u32[]{:S(2)}) collective-permute-start(bf16[180,384]{1,0:T(8,128)(2,1)S(1)} %get-tuple-element.63), channel_id=1, source_target_pairs={{0,2},{1,3},{2,0},{3,1},{4,6},{5,7},{6,4},{7,5},{8,10},{9,11},{10,... | collective-permute-start | bytes 414728 | tf_op jit(solution)/shard_map/ppermute | solution.py:40
  32.3 8.3 %collective-permute-start.17 = (bf16[180,384]{1,0:T(8,128)(2,1)S(1)}, bf16[180,384]{1,0:T(8,128)(2,1)S(1)}, u32[]{:S(2)}, u32[]{:S(2)}) collective-permute-start(bf16[180,384]{1,0:T(8,128)(2,1)S(1)} %get-tuple-element.64), channel_id=1, source_target_pairs={{0,3},{1,2},{2,1},{3,0},{4,7},{5,6},{6,5},{7,4},{8,11},{9,10},{10,... | collective-permute-start | bytes 414728 | tf_op jit(solution)/shard_map/ppermute | solution.py:40
  33.4 7.1 %collective-permute-start.18 = (bf16[180,384]{1,0:T(8,128)(2,1)S(1)}, bf16[180,384]{1,0:T(8,128)(2,1)S(1)}, u32[]{:S(2)}, u32[]{:S(2)}) collective-permute-start(bf16[180,384]{1,0:T(8,128)(2,1)S(1)} %get-tuple-element.66), channel_id=1, source_target_pairs={{0,1},{1,0},{2,3},{3,2},{4,5},{5,4},{6,7},{7,6},{8,9},{9,8},{10,11... | collective-permute-start | bytes 414728 | tf_op jit(solution)/shard_map/ppermute | solution.py:40
  36.2 5.5 %collective-permute-start.13 = (bf16[180,256]{1,0:T(8,128)(2,1)S(1)}, bf16[180,256]{1,0:T(8,128)(2,1)S(1)}, u32[]{:S(2)}, u32[]{:S(2)}) collective-permute-start(bf16[180,256]{1,0:T(8,128)(2,1)S(1)} %get-tuple-element.60), channel_id=1, source_target_pairs={{0,1},{1,0},{2,3},{3,2},{4,5},{5,4},{6,7},{7,6},{8,9},{9,8},{10,11... | collective-permute-start | bytes 276488 | tf_op jit(solution)/shard_map/ppermute | solution.py:40
  36.8 5.9 %collective-permute-start.11 = (bf16[180,256]{1,0:T(8,128)(2,1)S(1)}, bf16[180,256]{1,0:T(8,128)(2,1)S(1)}, u32[]{:S(2)}, u32[]{:S(2)}) collective-permute-start(bf16[180,256]{1,0:T(8,128)(2,1)S(1)} %get-tuple-element.57), channel_id=1, source_target_pairs={{0,2},{1,3},{2,0},{3,1},{4,6},{5,7},{6,4},{7,5},{8,10},{9,11},{10,... | collective-permute-start | bytes 276488 | tf_op jit(solution)/shard_map/ppermute | solution.py:40
  36.8 7.2 %collective-permute-start.12 = (bf16[180,256]{1,0:T(8,128)(2,1)S(1)}, bf16[180,256]{1,0:T(8,128)(2,1)S(1)}, u32[]{:S(2)}, u32[]{:S(2)}) collective-permute-start(bf16[180,256]{1,0:T(8,128)(2,1)S(1)} %get-tuple-element.58), channel_id=1, source_target_pairs={{0,3},{1,2},{2,1},{3,0},{4,7},{5,6},{6,5},{7,4},{8,11},{9,10},{10,... | collective-permute-start | bytes 276488 | tf_op jit(solution)/shard_map/ppermute | solution.py:40

commit v9 on v8

--- a/solution.py
+++ b/solution.py
@@ -409,17 +409,27 @@
         for at, tile in enumerate(tiles[mine]):
             lanes = range(tile * LANES, (tile + 1) * LANES)
             first = count * start + tile * LANES
-            for row in range(rows):
-                parts = []
-                for s in owners(tile, size):
-                    low, high = max(lanes[0], s * size) - s * size, min(lanes[-1] + 1, (s + 1) * size) - s * size
-                    parts.append(pieces[order[s]][:, row * size + low : row * size + high])
-                conv = jnp.concatenate(parts, axis=1).astype(jnp.float32)
-                total = grad_ref[row, :, first : first + LANES].astype(jnp.float32) + conv
-                tall_ref[at, pl.ds(row, part, stride=rows), :] = total
-            done_ref[at] = tall_ref[at].reshape(part, rows, LANES).astype(jnp.bfloat16)
-            copies.append(pltpu.make_async_copy(done_ref.at[at], out_ref.at[:, :, pl.ds(first, LANES)], sems.at[at]))
-            copies[-1].start()
+            cut = round_up(part, 32) // 2
+            for side, (low, high) in enumerate(((0, cut), (cut, part))):
+                for row in range(rows):
+                    parts = []
+                    for s in owners(tile, size):
+                        left, right = max(lanes[0], s * size), min(lanes[-1] + 1, (s + 1) * size)
+                        base = (row - s) * size
+                        parts.append(pieces[order[s]][low:high, base + left : base + right])
+                    conv = jnp.concatenate(parts, axis=1).astype(jnp.float32)
+                    total = grad_ref[row, low:high, first : first + LANES].astype(jnp.float32) + conv
+                    tall_ref[at, pl.ds(low * rows + row, high - low, stride=rows), :] = total
+                block = tall_ref[at, low * rows : high * rows, :].reshape(high - low, rows, LANES)
+                done_ref[at, low:high] = block.astype(jnp.bfloat16)
+                copies.append(
+                    pltpu.make_async_copy(
+                        done_ref.at[at, low:high],
+                        out_ref.at[low:high, :, pl.ds(first, LANES)],
+                        sems.at[2 * at + side],
+                    )
+                )
+                copies[-1].start()
         for copy in copies:
             copy.wait()
 
@@ -453,7 +463,7 @@
         scratch_shapes=[
             pltpu.VMEM((number, rows * part, LANES), jnp.float32),
             pltpu.VMEM((number, part, rows, LANES), jnp.bfloat16),
-            pltpu.SemaphoreType.DMA((number,)),
+            pltpu.SemaphoreType.DMA((2 * number,)),
         ],
         input_output_aliases={1 + len(pieces): 0} if before else {},
         compiler_params=pltpu.CompilerParams(vmem_limit_bytes=12 * 2**20),

time: 45.1 us -> 45.1 us (level)
  no operation moved by 1% of the time
where the time goes in v9:
time: 45.1 us; the launch traced here: 44.9 us
  starting transfers between devices  16.8 us (37%)
  Pallas kernels  15.5 us (34%)
  waiting for transfers between devices  9.51 us (21%)
  local copies, waits for them, and re-layouts  2.77 us (6%)
    ppermute x15, starting transfers between devices, exchange(): return lax.ppermute(block, 'azimuth', pairs)  11.6 us
    ppermute x15, waiting for transfers between devices, exchange(): return lax.ppermute(block, 'azimuth', pairs)  7.79 us
    pallas_call x2, Pallas kernels, mlp(): pl.pallas_call(functools.partial(mlp_kernel, count, half, sent, chunks),...  5.53 us
    ppermute x4, starting transfers between devices, halo(): blocks.append(lax.ppermute(block, ('polar', 'azimuth'), pairs))  5.17 us
    pallas_call x3, Pallas kernels, add_chunk(): pl.pallas_call(functools.partial(add_kernel, count, chunk, [k for k, _ in...  2.82 us
    unnamed x18, local copies, waits for them, and re-layouts  2.77 us
    pallas_call x2, Pallas kernels, finish(): pl.pallas_call(functools.partial(finish_kernel, count, len(halos)), in_sp...  2.35 us
    ppermute x4, waiting for transfers between devices, halo(): blocks.append(lax.ppermute(block, ('polar', 'azimuth'), pairs))  1.72 us
  transfers between devices with their start and end apart: 19, of which 7 were waited for; matrix products, arithmetic and copies ran while one was open for 0% of the time, Pallas kernels for 25%

profile of v9, /device:TPU:1, one launch (start us, length us, event | category | flops | bytes accessed | tf_op | source)
XLA Modules:
  0.0 44.9 jit_solution(11752778991868317368)
XLA Ops:
  0.0 0.0 copy-start.1
  0.0 1.4 %copy.19.grad_ref = bf16[4,180,640]{2,1,0:T(8,128)(2,1)S(1)} copy(bf16[4,180,640]{2,0,1:T(4,128)(2,1)} %param.11) | data formatting | bytes 1843200 | tf_op args[1]
  1.5 1.3 %copy.15.conv_ref = bf16[4,180,640]{2,1,0:T(8,128)(2,1)S(1)} copy(bf16[4,180,640]{2,0,1:T(4,128)(2,1)} %param.10) | data formatting | bytes 1843200 | tf_op args[0]
  2.8 0.0 copy-done.1
  2.8 0.0 copy-done.6
  2.8 0.0 copy-done
  2.8 2.8 %mlp.2 = (bf16[160,384]{1,0:T(8,128)(2,1)S(1)}, bf16[160,384]{1,0:T(8,128)(2,1)S(1)}, bf16[160,384]{1,0:T(8,128)(2,1)S(1)}, bf16[160,384]{1,0:T(8,128)(2,1)S(1)}) custom-call(bf16[4,180,640]{2,1,0:T(8,128)(2,1)S(1)} %copy.15.conv_ref, bf16[4,180,640]{2,1,0:T(8,128)(2,1)S(1)} %copy.19.grad_ref, bf16[640,1280]{1,0:T(8,128)(2,1)S(1)} %copy-done, ...), custom_call_target="tpu_custom_call" | custom-call | tf_op jit(solution)/shard_map/mlp/pallas_call | solution.py:165
  5.6 2.1 %collective-permute-start.3 = (bf16[160,384]{1,0:T(8,128)(2,1)S(1)}, bf16[160,384]{1,0:T(8,128)(2,1)S(1)}, u32[]{:S(2)}, u32[]{:S(2)}) collective-permute-start(bf16[160,384]{1,0:T(8,128)(2,1)S(1)} %get-tuple-element.42), channel_id=1, source_target_pairs={{0,2},{1,3},{2,0},{3,1},{4,6},{5,7},{6,4},{7,5},{8,10},{9,11},{10,... | collective-permute-start | bytes 368648 | tf_op jit(solution)/shard_map/ppermute | solution.py:40
  7.7 0.6 %collective-permute-start.4 = (bf16[160,384]{1,0:T(8,128)(2,1)S(1)}, bf16[160,384]{1,0:T(8,128)(2,1)S(1)}, u32[]{:S(2)}, u32[]{:S(2)}) collective-permute-start(bf16[160,384]{1,0:T(8,128)(2,1)S(1)} %get-tuple-element.43), channel_id=1, source_target_pairs={{0,3},{1,2},{2,1},{3,0},{4,7},{5,6},{6,5},{7,4},{8,11},{9,10},{10,... | collective-permute-start | bytes 368648 | tf_op jit(solution)/shard_map/ppermute | solution.py:40
  8.3 0.3 collective-permute-start.5
  8.6 0.0 copy-start.7
  8.6 2.8 %mlp.3 = (bf16[160,384]{1,0:T(8,128)(2,1)S(1)}, bf16[96,384]{1,0:T(8,128)(2,1)S(1)}, bf16[96,384]{1,0:T(8,128)(2,1)S(1)}, bf16[96,384]{1,0:T(8,128)(2,1)S(1)}, b...) custom-call(bf16[4,180,640]{2,1,0:T(8,128)(2,1)S(1)} %copy.15.conv_ref, ...), custom_call_target="tpu_custom_call" | custom-call | tf_op jit(solution)/shard_map/mlp/pallas_call | solution.py:165
  11.4 1.4 %collective-permute-start.6 = (bf16[96,384]{1,0:T(8,128)(2,1)S(1)}, bf16[96,384]{1,0:T(8,128)(2,1)S(1)}, u32[]{:S(2)}, u32[]{:S(2)}) collective-permute-start(bf16[96,384]{1,0:T(8,128)(2,1)S(1)} %get-tuple-element.45), channel_id=1, source_target_pairs={{0,2},{1,3},{2,0},{3,1},{4,6},{5,7},{6,4},{7,5},{8,10},{9,11},{10,... | collective-permute-start | bytes 221192 | tf_op jit(solution)/shard_map/ppermute | solution.py:40
  12.9 0.4 collective-permute-start.7
  13.3 0.0 collective-permute-done.3.refs_0_
  13.3 0.3 collective-permute-start.8
  13.6 0.0 copy-done.2
  13.6 0.0 copy-done.3
  13.6 0.0 copy-done.4
  13.6 0.0 copy-done.5
  13.6 0.0 copy-done.7
  13.6 0.7 %prepare.1 = (bf16[10,32,768]{2,1,0:T(8,128)(2,1)S(1)}, s32[10,32]{1,0:T(8,128)S(1)}, bf16[4,320,640]{2,1,0:T(8,128)(2,1)S(1)}, bf16[768,640]{1,0:T(8,128)(2,1)S...) custom-call(f32[9,640]{1,0:T(8,128)S(1)} %copy-done.5, bf16[9,16,640]{2,1,0:T(8,128)(2,1)S(1)} %copy-done.4, ...), custom_call_target="tpu_custom_call" | custom-call | tf_op jit(solution)/shard_map/prepare/pallas_call | solution.py:534
  14.4 0.0 collective-permute-done.4.refs_1_
  14.4 0.0 collective-permute-done.5.refs_3_
  14.4 0.7 %analysis_early.1.refs_5_.rest_0_ = f32[2,160,640]{2,1,0:T(8,128)S(1)} custom-call(bf16[160,384]{1,0:T(8,128)(2,1)S(1)} %collective-permute-done.3.refs_0_, bf16[160,384]{1,0:T(8,128)(2,1)S(1)} %collective-permute-done.4.refs_1_, bf16[160,384]{1,0:T(8,128)(2,1)S(1)} %get-tuple-element.36.rest_0_.refs_2_, ...), custom_call_target="tpu_custom_call" | custom-call | tf_op jit(solution)/shard_map/analysis_early/pallas_call | solution.py:214
  15.1 0.1 collective-permute-done.6.refs_0_
  15.2 2.5 %collective-permute-done.7.refs_1_ = bf16[96,384]{1,0:T(8,128)(2,1)S(1)} collective-permute-done((bf16[96,384]{1,0:T(8,128)(2,1)S(1)}, bf16[96,384]{1,0:T(8,128)(2,1)S(1)}, u32[]{:S(2)}, u32[]{:S(2)}) %collective-permute-start.7) | collective-permute-done | bytes 73760 | tf_op jit(solution)/shard_map/ppermute | solution.py:40
  17.7 0.0 collective-permute-done.8.refs_3_
  17.7 0.6 %analysis.2 = (f32[2,96,640]{2,1,0:T(8,128)S(1)}, bf16[3,96,640]{2,1,0:T(8,128)(2,1)S(1)}, bf16[3,96,640]{2,1,0:T(8,128)(2,1)S(1)}) custom-call(bf16[96,384]{1,0:T(8,128)(2,1)S(1)} %collective-permute-done.6.refs_0_, bf16[96,384]{1,0:T(8,128)(2,1)S(1)} %collective-permute-done.7.refs_1_, bf16[160,384]{1,0:T(8,128)(2,1)S(1)} %get-tuple-element.39.refs_2_, ...), custom_call_target="tpu_custom_call" | custom-call | tf_op jit(solution)/shard_map/analysis/pallas_call | solution.py:255
  18.3 1.4 %collective-permute-start.14 = (bf16[3,96,640]{2,1,0:T(8,128)(2,1)S(1)}, bf16[3,96,640]{2,1,0:T(8,128)(2,1)S(1)}, u32[]{:S(2)}, u32[]{:S(2)}) collective-permute-start(bf16[3,96,640]{2,1,0:T(8,128)(2,1)S(1)} %get-tuple-element.61), channel_id=1, source_target_pairs={{0,4},{1,5},{2,6},{3,7},{4,0},{5,1},{6,2},{7,3},{8,12},{9,13},{10,... | collective-permute-start | bytes 1105928 | tf_op jit(solution)/shard_map/ppermute | solution.py:556
  19.7 0.7 %collective-permute-start.15 = (bf16[3,96,640]{2,1,0:T(8,128)(2,1)S(1)}, bf16[3,96,640]{2,1,0:T(8,128)(2,1)S(1)}, u32[]{:S(2)}, u32[]{:S(2)}) collective-permute-start(bf16[3,96,640]{2,1,0:T(8,128)(2,1)S(1)} %get-tuple-element.62), channel_id=1, source_target_pairs={{0,1},{1,0},{2,3},{3,2},{4,8},{5,9},{6,10},{7,11},{8,4},{9,5},{10,... | collective-permute-start | bytes 1105928 | tf_op jit(solution)/shard_map/ppermute | solution.py:556
  20.4 0.3 collective-permute-start
  20.7 1.3 %collective-permute-start.1 = (bf16[64,384]{1,0:T(8,128)(2,1)S(1)}, bf16[64,384]{1,0:T(8,128)(2,1)S(1)}, u32[]{:S(2)}, u32[]{:S(2)}) collective-permute-start(bf16[64,384]{1,0:T(8,128)(2,1)S(1)} %get-tuple-element.38), channel_id=1, source_target_pairs={{0,3},{1,2},{2,1},{3,0},{4,7},{5,6},{6,5},{7,4},{8,11},{9,10},{10,... | collective-permute-start | bytes 147464 | tf_op jit(solution)/shard_map/ppermute | solution.py:40
  22.0 0.2 collective-permute-start.2
  22.3 1.0 %own_terms.2.refs_6_.part_ref = f32[4,96,640]{2,1,0:T(8,128)S(1)} custom-call(f32[2,96,640]{2,1,0:T(8,128)S(1)} %get-tuple-element.48.own_ref, f32[96,32]{1,0:T(8,128)S(1)} %get-tuple-element.49.weight_ref.refs_1_, s32[10,32]{1,0:T(8,128)S(1)} %get-tuple-element.50.target_ref.refs_3_.refs_2_, ...), custom_call_target="tpu_custom_call" | custom-call | tf_op jit(solution)/shard_map/own_terms/pallas_call | solution.py:311
  23.3 0.5 %collective-permute-done.refs_0_ = bf16[64,384]{1,0:T(8,128)(2,1)S(1)} collective-permute-done((bf16[64,384]{1,0:T(8,128)(2,1)S(1)}, bf16[64,384]{1,0:T(8,128)(2,1)S(1)}, u32[]{:S(2)}, u32[]{:S(2)}) %collective-permute-start) | collective-permute-done | bytes 49184 | tf_op jit(solution)/shard_map/ppermute | solution.py:40
  23.8 1.4 %collective-permute-done.1.refs_1_ = bf16[64,384]{1,0:T(8,128)(2,1)S(1)} collective-permute-done((bf16[64,384]{1,0:T(8,128)(2,1)S(1)}, bf16[64,384]{1,0:T(8,128)(2,1)S(1)}, u32[]{:S(2)}, u32[]{:S(2)}) %collective-permute-start.1) | collective-permute-done | bytes 49184 | tf_op jit(solution)/shard_map/ppermute | solution.py:40
  25.2 0.0 collective-permute-done.2.refs_3_
  25.2 0.6 %analysis.3 = (f32[2,64,640]{2,1,0:T(8,128)S(1)}, bf16[3,64,640]{2,1,0:T(8,128)(2,1)S(1)}, bf16[3,64,640]{2,1,0:T(8,128)(2,1)S(1)}) custom-call(bf16[64,384]{1,0:T(8,128)(2,1)S(1)} %collective-permute-done.refs_0_, bf16[64,384]{1,0:T(8,128)(2,1)S(1)} %collective-permute-done.1.refs_1_, bf16[160,384]{1,0:T(8,128)(2,1)S(1)} %get-tuple-element.39.refs_2_, ...), custom_call_target="tpu_custom_call" | custom-call | tf_op jit(solution)/shard_map/analysis/pallas_call | solution.py:255
  25.8 2.9 %collective-permute-start.9 = (bf16[3,64,640]{2,1,0:T(8,128)(2,1)S(1)}, bf16[3,64,640]{2,1,0:T(8,128)(2,1)S(1)}, u32[]{:S(2)}, u32[]{:S(2)}) collective-permute-start(bf16[3,64,640]{2,1,0:T(8,128)(2,1)S(1)} %get-tuple-element.54), channel_id=1, source_target_pairs={{0,4},{1,5},{2,6},{3,7},{4,0},{5,1},{6,2},{7,3},{8,12},{9,13},{10,... | collective-permute-start | bytes 737288 | tf_op jit(solution)/shard_map/ppermute | solution.py:556
  28.7 0.2 collective-permute-start.10
  28.9 0.7 %own_terms.3.part_ref.rest_0_ = f32[4,64,640]{2,1,0:T(8,128)S(1)} custom-call(f32[2,64,640]{2,1,0:T(8,128)S(1)} %get-tuple-element.52.own_ref, f32[64,32]{1,0:T(8,128)S(1)} %get-tuple-element.53.weight_ref.refs_2_, s32[10,32]{1,0:T(8,128)S(1)} %get-tuple-element.50.target_ref.refs_3_.refs_2_, ...), custom_call_target="tpu_custom_call" | custom-call | tf_op jit(solution)/shard_map/own_terms/pallas_call | solution.py:311
  29.6 0.0 collective-permute-done.14.first_ref
  29.6 0.5 %side_terms.1.part_ref = f32[4,96,640]{2,1,0:T(8,128)S(1)} custom-call(f32[4,96,640]{2,1,0:T(8,128)S(1)} %own_terms.2.refs_6_.part_ref, bf16[3,96,640]{2,1,0:T(8,128)(2,1)S(1)} %collective-permute-done.14.first_ref, f32[96,32]{1,0:T(8,128)S(1)} %get-tuple-element.49.weight_ref.refs_1_, s32[10,32]{1,0:T(8,128)S(1)} %get-tuple-element.50.target_ref.refs_3_.refs_2_, ...), custom_call_target="tpu_custom_call" | custom-call | tf_op jit(solution)/shard_map/side_terms/pallas_call | solution.py:353
  30.1 0.0 collective-permute-done.15.refs_0_
  30.1 1.3 %finish.3 = (bf16[180,384]{1,0:T(8,128)(2,1)S(1)}, bf16[180,384]{1,0:T(8,128)(2,1)S(1)}, bf16[180,384]{1,0:T(8,128)(2,1)S(1)}, bf16[180,384]{1,0:T(8,128)(2,1)S(1)}) custom-call(f32[4,96,640]{2,1,0:T(8,128)S(1)} %side_terms.1.part_ref, bf16[3,96,640]{2,1,0:T(8,128)(2,1)S(1)} %collective-permute-done.15.refs_0_, ...), custom_call_target="tpu_custom_call" | custom-call | tf_op jit(solution)/shard_map/finish/pallas_call | solution.py:387
  31.4 0.9 %collective-permute-start.16 = (bf16[180,384]{1,0:T(8,128)(2,1)S(1)}, bf16[180,384]{1,0:T(8,128)(2,1)S(1)}, u32[]{:S(2)}, u32[]{:S(2)}) collective-permute-start(bf16[180,384]{1,0:T(8,128)(2,1)S(1)} %get-tuple-element.63), channel_id=1, source_target_pairs={{0,2},{1,3},{2,0},{3,1},{4,6},{5,7},{6,4},{7,5},{8,10},{9,11},{10,... | collective-permute-start | bytes 414728 | tf_op jit(solution)/shard_map/ppermute | solution.py:40
  32.3 1.2 %collective-permute-start.17 = (bf16[180,384]{1,0:T(8,128)(2,1)S(1)}, bf16[180,384]{1,0:T(8,128)(2,1)S(1)}, u32[]{:S(2)}, u32[]{:S(2)}) collective-permute-start(bf16[180,384]{1,0:T(8,128)(2,1)S(1)} %get-tuple-element.64), channel_id=1, source_target_pairs={{0,3},{1,2},{2,1},{3,0},{4,7},{5,6},{6,5},{7,4},{8,11},{9,10},{10,... | collective-permute-start | bytes 414728 | tf_op jit(solution)/shard_map/ppermute | solution.py:40
  33.4 0.0 collective-permute-start.18
  33.4 1.7 %collective-permute-done.9.refs_0_ = bf16[3,64,640]{2,1,0:T(8,128)(2,1)S(1)} collective-permute-done((bf16[3,64,640]{2,1,0:T(8,128)(2,1)S(1)}, bf16[3,64,640]{2,1,0:T(8,128)(2,1)S(1)}, u32[]{:S(2)}, u32[]{:S(2)}) %collective-permute-start.9) | collective-permute-done | bytes 245792 | tf_op jit(solution)/shard_map/ppermute | solution.py:556
  35.1 0.0 collective-permute-done.10.refs_1_
  35.2 1.1 %finish.2 = (bf16[180,256]{1,0:T(8,128)(2,1)S(1)}, bf16[180,256]{1,0:T(8,128)(2,1)S(1)}, bf16[180,256]{1,0:T(8,128)(2,1)S(1)}, bf16[180,256]{1,0:T(8,128)(2,1)S(1)}) custom-call(f32[4,64,640]{2,1,0:T(8,128)S(1)} %own_terms.3.part_ref.rest_0_, bf16[3,64,640]{2,1,0:T(8,128)(2,1)S(1)} %collective-permute-done.9.refs_0_, ...), custom_call_target="tpu_custom_call" | custom-call | tf_op jit(solution)/shard_map/finish/pallas_call | solution.py:387
  36.2 0.5 %collective-permute-start.13 = (bf16[180,256]{1,0:T(8,128)(2,1)S(1)}, bf16[180,256]{1,0:T(8,128)(2,1)S(1)}, u32[]{:S(2)}, u32[]{:S(2)}) collective-permute-start(bf16[180,256]{1,0:T(8,128)(2,1)S(1)} %get-tuple-element.60), channel_id=1, source_target_pairs={{0,1},{1,0},{2,3},{3,2},{4,5},{5,4},{6,7},{7,6},{8,9},{9,8},{10,11... | collective-permute-start | bytes 276488 | tf_op jit(solution)/shard_map/ppermute | solution.py:40
  36.8 0.0 collective-permute-start.11
  36.8 0.0 collective-permute-done.16.refs_0_
  36.8 1.9 %collective-permute-start.12 = (bf16[180,256]{1,0:T(8,128)(2,1)S(1)}, bf16[180,256]{1,0:T(8,128)(2,1)S(1)}, u32[]{:S(2)}, u32[]{:S(2)}) collective-permute-start(bf16[180,256]{1,0:T(8,128)(2,1)S(1)} %get-tuple-element.58), channel_id=1, source_target_pairs={{0,3},{1,2},{2,1},{3,0},{4,7},{5,6},{6,5},{7,4},{8,11},{9,10},{10,... | collective-permute-start | bytes 276488 | tf_op jit(solution)/shard_map/ppermute | solution.py:40
  38.7 1.9 %collective-permute-done.17.refs_1_ = bf16[180,384]{1,0:T(8,128)(2,1)S(1)} collective-permute-done((bf16[180,384]{1,0:T(8,128)(2,1)S(1)}, bf16[180,384]{1,0:T(8,128)(2,1)S(1)}, u32[]{:S(2)}, u32[]{:S(2)}) %collective-permute-start.17) | collective-permute-done | bytes 138272 | tf_op jit(solution)/shard_map/ppermute | solution.py:40
  40.6 0.0 collective-permute-done.18.refs_3_
  40.6 1.1 %add_chunk.3.refs_2_ = bf16[180,4,640]{2,1,0:T(4,128)(2,1)} custom-call(bf16[4,180,640]{2,1,0:T(8,128)(2,1)S(1)} %copy.19.grad_ref, bf16[180,384]{1,0:T(8,128)(2,1)S(1)} %collective-permute-done.16.refs_0_, bf16[180,384]{1,0:T(8,128)(2,1)S(1)} %collective-permute-done.17.refs_1_, bf16[180,384]{1,0:T(8,128)(2,1)S(1)} %get-tuple-element.65.refs_2_, ...), custom_call_target="tpu_custom_call" | custom-call | tf_op jit(solution)/shard_map/add_chunk/pallas_call | solution.py:458
  41.7 0.0 collective-permute-done.13.refs_1_
  41.7 0.8 %add_chunk.4.refs_2_ = bf16[180,4,640]{2,1,0:T(4,128)(2,1)} custom-call(bf16[4,180,640]{2,1,0:T(8,128)(2,1)S(1)} %copy.19.grad_ref, bf16[180,256]{1,0:T(8,128)(2,1)S(1)} %get-tuple-element.59.refs_0_, bf16[180,256]{1,0:T(8,128)(2,1)S(1)} %collective-permute-done.13.refs_1_, bf16[180,4,640]{2,1,0:T(4,128)(2,1)} %add_chunk.3.refs_2_), custom_call_target="tpu_custom_call", output_to_operand_aliasing={{}: (3, {})} | custom-call | tf_op jit(solution)/shard_map/add_chunk/pallas_call | solution.py:458
  42.6 0.0 collective-permute-done.11.refs_0_
  42.6 1.3 %collective-permute-done.12.refs_1_ = bf16[180,256]{1,0:T(8,128)(2,1)S(1)} collective-permute-done((bf16[180,256]{1,0:T(8,128)(2,1)S(1)}, bf16[180,256]{1,0:T(8,128)(2,1)S(1)}, u32[]{:S(2)}, u32[]{:S(2)}) %collective-permute-start.12) | collective-permute-done | bytes 92192 | tf_op jit(solution)/shard_map/ppermute | solution.py:40
  44.0 0.8 %add_chunk.5 = bf16[180,4,640]{2,1,0:T(4,128)(2,1)} custom-call(bf16[4,180,640]{2,1,0:T(8,128)(2,1)S(1)} %copy.19.grad_ref, bf16[180,256]{1,0:T(8,128)(2,1)S(1)} %collective-permute-done.11.refs_0_, bf16[180,256]{1,0:T(8,128)(2,1)S(1)} %collective-permute-done.12.refs_1_, bf16[180,4,640]{2,1,0:T(4,128)(2,1)} %add_chunk.4.refs_2_), custom_call_target="tpu_custom_call", output_to_operand_aliasing={{}: (3, {})} | custom-call | tf_op jit(solution)/shard_map/add_chunk/pallas_call | solution.py:458
  (6 shorter events, 0.0 us)
Async XLA Ops:
  0.0 2.8 %copy-start.1 = (bf16[1280,640]{1,0:T(8,128)(2,1)S(1)}, bf16[1280,640]{1,0:T(8,128)(2,1)}, u32[]{:S(2)}) copy-start(bf16[1280,640]{1,0:T(8,128)(2,1)} %wout_ref.3) | copy-start | bytes 4915204
  0.0 2.8 %copy-start.6 = (f32[1280]{0:T(1024)S(1)}, f32[1280]{0:T(1024)}, u32[]{:S(2)}) copy-start(f32[1280]{0:T(1024)} %bias_ref.3) | copy-start | bytes 15364
  0.0 2.8 %copy-start = (bf16[640,1280]{1,0:T(8,128)(2,1)S(1)}, bf16[640,1280]{1,0:T(8,128)(2,1)}, u32[]{:S(2)}) copy-start(bf16[640,1280]{1,0:T(8,128)(2,1)} %win_ref.3) | copy-start | bytes 4915204
  5.6 7.7 %collective-permute-start.3 = (bf16[160,384]{1,0:T(8,128)(2,1)S(1)}, bf16[160,384]{1,0:T(8,128)(2,1)S(1)}, u32[]{:S(2)}, u32[]{:S(2)}) collective-permute-start(bf16[160,384]{1,0:T(8,128)(2,1)S(1)} %get-tuple-element.42), channel_id=1, source_target_pairs={{0,2},{1,3},{2,0},{3,1},{4,6},{5,7},{6,4},{7,5},{8,10},{9,11},{10,... | collective-permute-start | bytes 368648 | tf_op jit(solution)/shard_map/ppermute | solution.py:40
  7.7 6.7 %collective-permute-start.4 = (bf16[160,384]{1,0:T(8,128)(2,1)S(1)}, bf16[160,384]{1,0:T(8,128)(2,1)S(1)}, u32[]{:S(2)}, u32[]{:S(2)}) collective-permute-start(bf16[160,384]{1,0:T(8,128)(2,1)S(1)} %get-tuple-element.43), channel_id=1, source_target_pairs={{0,3},{1,2},{2,1},{3,0},{4,7},{5,6},{6,5},{7,4},{8,11},{9,10},{10,... | collective-permute-start | bytes 368648 | tf_op jit(solution)/shard_map/ppermute | solution.py:40
  8.3 6.1 %collective-permute-start.5 = (bf16[160,384]{1,0:T(8,128)(2,1)S(1)}, bf16[160,384]{1,0:T(8,128)(2,1)S(1)}, u32[]{:S(2)}, u32[]{:S(2)}) collective-permute-start(bf16[160,384]{1,0:T(8,128)(2,1)S(1)} %get-tuple-element.44), channel_id=1, source_target_pairs={{0,1},{1,0},{2,3},{3,2},{4,5},{5,4},{6,7},{7,6},{8,9},{9,8},{10,11... | collective-permute-start | bytes 368648 | tf_op jit(solution)/shard_map/ppermute | solution.py:40
  8.6 5.0 %copy-start.2 = (bf16[4,320,640]{2,1,0:T(8,128)(2,1)S(1)}, bf16[4,320,640]{2,1,0:T(8,128)(2,1)}, u32[]{:S(2)}) copy-start(bf16[4,320,640]{2,1,0:T(8,128)(2,1)} %constant.4.clone.forth_ref) | copy-start | bytes 4915204
  8.6 5.0 %copy-start.3 = (bf16[768,640]{1,0:T(8,128)(2,1)S(1)}, bf16[768,640]{1,0:T(8,128)(2,1)}, u32[]{:S(2)}) copy-start(bf16[768,640]{1,0:T(8,128)(2,1)} %constant.5.clone.back_ref) | copy-start | bytes 2949124
  8.6 5.0 %copy-start.4 = (bf16[9,16,640]{2,1,0:T(8,128)(2,1)S(1)}, bf16[9,16,640]{2,1,0:T(8,128)(2,1)}, u32[]{:S(2)}) copy-start(bf16[9,16,640]{2,1,0:T(8,128)(2,1)} %filt_ref.1) | copy-start | bytes 552964
  8.6 5.0 %copy-start.5 = (f32[9,640]{1,0:T(8,128)S(1)}, f32[9,640]{1,0:T(8,128)}, u32[]{:S(2)}) copy-start(f32[9,640]{1,0:T(8,128)} %weight_ref.1) | copy-start | bytes 69124
  8.6 5.0 %copy-start.7 = (s32[16,9]{1,0:T(8,128)S(1)}, s32[16,9]{1,0:T(8,128)}, u32[]{:S(2)}) copy-start(s32[16,9]{1,0:T(8,128)} %offset_ref.1) | copy-start | bytes 1732
  11.4 3.8 %collective-permute-start.6 = (bf16[96,384]{1,0:T(8,128)(2,1)S(1)}, bf16[96,384]{1,0:T(8,128)(2,1)S(1)}, u32[]{:S(2)}, u32[]{:S(2)}) collective-permute-start(bf16[96,384]{1,0:T(8,128)(2,1)S(1)} %get-tuple-element.45), channel_id=1, source_target_pairs={{0,2},{1,3},{2,0},{3,1},{4,6},{5,7},{6,4},{7,5},{8,10},{9,11},{10,... | collective-permute-start | bytes 221192 | tf_op jit(solution)/shard_map/ppermute | solution.py:40
  12.9 4.8 %collective-permute-start.7 = (bf16[96,384]{1,0:T(8,128)(2,1)S(1)}, bf16[96,384]{1,0:T(8,128)(2,1)S(1)}, u32[]{:S(2)}, u32[]{:S(2)}) collective-permute-start(bf16[96,384]{1,0:T(8,128)(2,1)S(1)} %get-tuple-element.46), channel_id=1, source_target_pairs={{0,3},{1,2},{2,1},{3,0},{4,7},{5,6},{6,5},{7,4},{8,11},{9,10},{10,... | collective-permute-start | bytes 221192 | tf_op jit(solution)/shard_map/ppermute | solution.py:40
  13.3 4.4 %collective-permute-start.8 = (bf16[96,384]{1,0:T(8,128)(2,1)S(1)}, bf16[96,384]{1,0:T(8,128)(2,1)S(1)}, u32[]{:S(2)}, u32[]{:S(2)}) collective-permute-start(bf16[96,384]{1,0:T(8,128)(2,1)S(1)} %get-tuple-element.47), channel_id=1, source_target_pairs={{0,1},{1,0},{2,3},{3,2},{4,5},{5,4},{6,7},{7,6},{8,9},{9,8},{10,11... | collective-permute-start | bytes 221192 | tf_op jit(solution)/shard_map/ppermute | solution.py:40
  18.3 11.3 %collective-permute-start.14 = (bf16[3,96,640]{2,1,0:T(8,128)(2,1)S(1)}, bf16[3,96,640]{2,1,0:T(8,128)(2,1)S(1)}, u32[]{:S(2)}, u32[]{:S(2)}) collective-permute-start(bf16[3,96,640]{2,1,0:T(8,128)(2,1)S(1)} %get-tuple-element.61), channel_id=1, source_target_pairs={{0,4},{1,5},{2,6},{3,7},{4,0},{5,1},{6,2},{7,3},{8,12},{9,13},{10,... | collective-permute-start | bytes 1105928 | tf_op jit(solution)/shard_map/ppermute | solution.py:556
  19.7 10.4 %collective-permute-start.15 = (bf16[3,96,640]{2,1,0:T(8,128)(2,1)S(1)}, bf16[3,96,640]{2,1,0:T(8,128)(2,1)S(1)}, u32[]{:S(2)}, u32[]{:S(2)}) collective-permute-start(bf16[3,96,640]{2,1,0:T(8,128)(2,1)S(1)} %get-tuple-element.62), channel_id=1, source_target_pairs={{0,1},{1,0},{2,3},{3,2},{4,8},{5,9},{6,10},{7,11},{8,4},{9,5},{10,... | collective-permute-start | bytes 1105928 | tf_op jit(solution)/shard_map/ppermute | solution.py:556
  20.4 3.4 %collective-permute-start = (bf16[64,384]{1,0:T(8,128)(2,1)S(1)}, bf16[64,384]{1,0:T(8,128)(2,1)S(1)}, u32[]{:S(2)}, u32[]{:S(2)}) collective-permute-start(bf16[64,384]{1,0:T(8,128)(2,1)S(1)} %get-tuple-element.37), channel_id=1, source_target_pairs={{0,2},{1,3},{2,0},{3,1},{4,6},{5,7},{6,4},{7,5},{8,10},{9,11},{10,... | collective-permute-start | bytes 147464 | tf_op jit(solution)/shard_map/ppermute | solution.py:40
  20.7 4.5 %collective-permute-start.1 = (bf16[64,384]{1,0:T(8,128)(2,1)S(1)}, bf16[64,384]{1,0:T(8,128)(2,1)S(1)}, u32[]{:S(2)}, u32[]{:S(2)}) collective-permute-start(bf16[64,384]{1,0:T(8,128)(2,1)S(1)} %get-tuple-element.38), channel_id=1, source_target_pairs={{0,3},{1,2},{2,1},{3,0},{4,7},{5,6},{6,5},{7,4},{8,11},{9,10},{10,... | collective-permute-start | bytes 147464 | tf_op jit(solution)/shard_map/ppermute | solution.py:40
  22.0 3.2 %collective-permute-start.2 = (bf16[64,384]{1,0:T(8,128)(2,1)S(1)}, bf16[64,384]{1,0:T(8,128)(2,1)S(1)}, u32[]{:S(2)}, u32[]{:S(2)}) collective-permute-start(bf16[64,384]{1,0:T(8,128)(2,1)S(1)} %get-tuple-element.40), channel_id=1, source_target_pairs={{0,1},{1,0},{2,3},{3,2},{4,5},{5,4},{6,7},{7,6},{8,9},{9,8},{10,11... | collective-permute-start | bytes 147464 | tf_op jit(solution)/shard_map/ppermute | solution.py:40
  25.8 9.3 %collective-permute-start.9 = (bf16[3,64,640]{2,1,0:T(8,128)(2,1)S(1)}, bf16[3,64,640]{2,1,0:T(8,128)(2,1)S(1)}, u32[]{:S(2)}, u32[]{:S(2)}) collective-permute-start(bf16[3,64,640]{2,1,0:T(8,128)(2,1)S(1)} %get-tuple-element.54), channel_id=1, source_target_pairs={{0,4},{1,5},{2,6},{3,7},{4,0},{5,1},{6,2},{7,3},{8,12},{9,13},{10,... | collective-permute-start | bytes 737288 | tf_op jit(solution)/shard_map/ppermute | solution.py:556
  28.7 6.5 %collective-permute-start.10 = (bf16[3,64,640]{2,1,0:T(8,128)(2,1)S(1)}, bf16[3,64,640]{2,1,0:T(8,128)(2,1)S(1)}, u32[]{:S(2)}, u32[]{:S(2)}) collective-permute-start(bf16[3,64,640]{2,1,0:T(8,128)(2,1)S(1)} %get-tuple-element.55), channel_id=1, source_target_pairs={{0,1},{1,0},{2,3},{3,2},{4,8},{5,9},{6,10},{7,11},{8,4},{9,5},{10,... | collective-permute-start | bytes 737288 | tf_op jit(solution)/shard_map/ppermute | solution.py:556
  31.4 5.4 %collective-permute-start.16 = (bf16[180,384]{1,0:T(8,128)(2,1)S(1)}, bf16[180,384]{1,0:T(8,128)(2,1)S(1)}, u32[]{:S(2)}, u32[]{:S(2)}) collective-permute-start(bf16[180,384]{1,0:T(8,128)(2,1)S(1)} %get-tuple-element.63), channel_id=1, source_target_pairs={{0,2},{1,3},{2,0},{3,1},{4,6},{5,7},{6,4},{7,5},{8,10},{9,11},{10,... | collective-permute-start | bytes 414728 | tf_op jit(solution)/shard_map/ppermute | solution.py:40
  32.3 8.3 %collective-permute-start.17 = (bf16[180,384]{1,0:T(8,128)(2,1)S(1)}, bf16[180,384]{1,0:T(8,128)(2,1)S(1)}, u32[]{:S(2)}, u32[]{:S(2)}) collective-permute-start(bf16[180,384]{1,0:T(8,128)(2,1)S(1)} %get-tuple-element.64), channel_id=1, source_target_pairs={{0,3},{1,2},{2,1},{3,0},{4,7},{5,6},{6,5},{7,4},{8,11},{9,10},{10,... | collective-permute-start | bytes 414728 | tf_op jit(solution)/shard_map/ppermute | solution.py:40
  33.4 7.1 %collective-permute-start.18 = (bf16[180,384]{1,0:T(8,128)(2,1)S(1)}, bf16[180,384]{1,0:T(8,128)(2,1)S(1)}, u32[]{:S(2)}, u32[]{:S(2)}) collective-permute-start(bf16[180,384]{1,0:T(8,128)(2,1)S(1)} %get-tuple-element.66), channel_id=1, source_target_pairs={{0,1},{1,0},{2,3},{3,2},{4,5},{5,4},{6,7},{7,6},{8,9},{9,8},{10,11... | collective-permute-start | bytes 414728 | tf_op jit(solution)/shard_map/ppermute | solution.py:40
  36.2 5.5 %collective-permute-start.13 = (bf16[180,256]{1,0:T(8,128)(2,1)S(1)}, bf16[180,256]{1,0:T(8,128)(2,1)S(1)}, u32[]{:S(2)}, u32[]{:S(2)}) collective-permute-start(bf16[180,256]{1,0:T(8,128)(2,1)S(1)} %get-tuple-element.60), channel_id=1, source_target_pairs={{0,1},{1,0},{2,3},{3,2},{4,5},{5,4},{6,7},{7,6},{8,9},{9,8},{10,11... | collective-permute-start | bytes 276488 | tf_op jit(solution)/shard_map/ppermute | solution.py:40
  36.8 5.8 %collective-permute-start.11 = (bf16[180,256]{1,0:T(8,128)(2,1)S(1)}, bf16[180,256]{1,0:T(8,128)(2,1)S(1)}, u32[]{:S(2)}, u32[]{:S(2)}) collective-permute-start(bf16[180,256]{1,0:T(8,128)(2,1)S(1)} %get-tuple-element.57), channel_id=1, source_target_pairs={{0,2},{1,3},{2,0},{3,1},{4,6},{5,7},{6,4},{7,5},{8,10},{9,11},{10,... | collective-permute-start | bytes 276488 | tf_op jit(solution)/shard_map/ppermute | solution.py:40
  36.8 7.2 %collective-permute-start.12 = (bf16[180,256]{1,0:T(8,128)(2,1)S(1)}, bf16[180,256]{1,0:T(8,128)(2,1)S(1)}, u32[]{:S(2)}, u32[]{:S(2)}) collective-permute-start(bf16[180,256]{1,0:T(8,128)(2,1)S(1)} %get-tuple-element.58), channel_id=1, source_target_pairs={{0,3},{1,2},{2,1},{3,0},{4,7},{5,6},{6,5},{7,4},{8,11},{9,10},{10,... | collective-permute-start | bytes 276488 | tf_op jit(solution)/shard_map/ppermute | solution.py:40

commit v10 on v9

--- a/solution.py
+++ b/solution.py
@@ -265,9 +265,12 @@
 
 
 def add_row(accs, spectrum, weight, target_row, filter_row, targets):
+    masked = jnp.concatenate([jnp.where(target_row == t, weight, 0.0) for t in targets], axis=0)
+    add_gains(accs, spectrum, dot_nn(masked.astype(jnp.bfloat16), filter_row), targets)
+
+
+def add_gains(accs, spectrum, gains, targets):
     size = spectrum.shape[0]
-    masked = jnp.concatenate([jnp.where(target_row == t, weight, 0.0) for t in targets], axis=0)
-    gains = dot_nn(masked.astype(jnp.bfloat16), filter_row)
     whole = (gains.shape[1] // 2) // LANES * LANES - LANES
     spec_re = spectrum[:, :whole]
     spec_im = spectrum[:, whole : 2 * whole]
@@ -320,18 +323,24 @@
 
 
 def add_halo(accs, sides, rows, weight_ref, target_ref, filter_ref):
-    for side, base in sides:
-        for h in range(REACH):
-            at = base + h + REACH
-            targets = [t for t in range(rows) if abs(base + h - t) <= REACH]
-            add_row(
-                accs,
-                side[h].astype(jnp.float32),
-                weight_ref[...],
-                target_ref[at : at + 1, :],
-                filter_ref[at],
-                targets,
-            )
+    rows_at = [(side, h, base + h) for side, base in sides for h in range(REACH)]
+    size, depth = weight_ref.shape
+    number = len(rows_at)
+    weight = jnp.concatenate([weight_ref[...]] * number, axis=1)
+    wanted = jnp.concatenate([target_ref[row + REACH : row + REACH + 1, :] for _, _, row in rows_at], axis=1)
+    lane = lax.broadcasted_iota(jnp.int32, wanted.shape, 1)
+    left, reached = [], []
+    for i, (_, _, row) in enumerate(rows_at):
+        reached.append([t for t in range(rows) if abs(row - t) <= REACH])
+        mine = jnp.where((lane >= i * depth) & (lane < (i + 1) * depth), wanted, -1)
+        left += [jnp.where(mine == t, weight, 0.0).astype(jnp.bfloat16) for t in reached[i]]
+    filters = jnp.concatenate([filter_ref[row + REACH] for _, _, row in rows_at], axis=0)
+    gains = dot_nn(jnp.concatenate(left, axis=0), filters)
+    first = 0
+    for (side, h, _), targets in zip(rows_at, reached):
+        last = first + len(targets) * size
+        add_gains(accs, side[h].astype(jnp.float32), gains[first:last], targets)
+        first = last
 
 
 def side_kernel(part_ref, first_ref, weight_ref, target_ref, filter_ref, *rest):

time: 45.1 us -> 45.4 us (level)
  Pallas kernels: 15.5 us -> 16 us
  transfers between devices with their start and end apart: 19 -> 19, of which waited for: 7 -> 7; matrix products, arithmetic and copies ran while one was open for 0% -> 0% of each run, Pallas kernels for 25% -> 26%
where the time goes in v10:
time: 45.4 us; the launch traced here: 45.3 us
  starting transfers between devices  17 us (37%)
  Pallas kernels  16 us (35%)
  waiting for transfers between devices  9.15 us (20%)
  local copies, waits for them, and re-layouts  2.77 us (6%)
    ppermute x15, starting transfers between devices, exchange(): return lax.ppermute(block, 'azimuth', pairs)  11.8 us
    ppermute x15, waiting for transfers between devices, exchange(): return lax.ppermute(block, 'azimuth', pairs)  7.79 us
    pallas_call x2, Pallas kernels, mlp(): pl.pallas_call(functools.partial(mlp_kernel, count, half, sent, chunks),...  5.53 us
    ppermute x4, starting transfers between devices, halo(): blocks.append(lax.ppermute(block, ('polar', 'azimuth'), pairs))  5.17 us
    pallas_call x3, Pallas kernels, add_chunk(): pl.pallas_call(functools.partial(add_kernel, count, chunk, [k for k, _ in...  2.82 us
    unnamed x18, local copies, waits for them, and re-layouts  2.77 us
    pallas_call x2, Pallas kernels, finish(): pl.pallas_call(functools.partial(finish_kernel, count, len(halos)), in_sp...  2.74 us
    pallas_call x2, Pallas kernels, own_terms(): pl.pallas_call(functools.partial(own_kernel, start), in_specs=[pl.BlockSp...  1.71 us
  transfers between devices with their start and end apart: 19, of which 7 were waited for; matrix products, arithmetic and copies ran while one was open for 0% of the time, Pallas kernels for 26%

profile of v10, /device:TPU:1, one launch (start us, length us, event | category | flops | bytes accessed | tf_op | source)
XLA Modules:
  0.0 45.3 jit_solution(17024652106905614421)
XLA Ops:
  0.0 0.0 copy-start.1
  0.0 1.4 %copy.19.grad_ref = bf16[4,180,640]{2,1,0:T(8,128)(2,1)S(1)} copy(bf16[4,180,640]{2,0,1:T(4,128)(2,1)} %param.11) | data formatting | bytes 1843200 | tf_op args[1]
  1.5 1.3 %copy.15.conv_ref = bf16[4,180,640]{2,1,0:T(8,128)(2,1)S(1)} copy(bf16[4,180,640]{2,0,1:T(4,128)(2,1)} %param.10) | data formatting | bytes 1843200 | tf_op args[0]
  2.8 0.0 copy-done.1
  2.8 0.0 copy-done.6
  2.8 0.0 copy-done
  2.8 2.8 %mlp.2 = (bf16[160,384]{1,0:T(8,128)(2,1)S(1)}, bf16[160,384]{1,0:T(8,128)(2,1)S(1)}, bf16[160,384]{1,0:T(8,128)(2,1)S(1)}, bf16[160,384]{1,0:T(8,128)(2,1)S(1)}) custom-call(bf16[4,180,640]{2,1,0:T(8,128)(2,1)S(1)} %copy.15.conv_ref, bf16[4,180,640]{2,1,0:T(8,128)(2,1)S(1)} %copy.19.grad_ref, bf16[640,1280]{1,0:T(8,128)(2,1)S(1)} %copy-done, ...), custom_call_target="tpu_custom_call" | custom-call | tf_op jit(solution)/shard_map/mlp/pallas_call | solution.py:165
  5.6 2.1 %collective-permute-start.3 = (bf16[160,384]{1,0:T(8,128)(2,1)S(1)}, bf16[160,384]{1,0:T(8,128)(2,1)S(1)}, u32[]{:S(2)}, u32[]{:S(2)}) collective-permute-start(bf16[160,384]{1,0:T(8,128)(2,1)S(1)} %get-tuple-element.42), channel_id=1, source_target_pairs={{0,2},{1,3},{2,0},{3,1},{4,6},{5,7},{6,4},{7,5},{8,10},{9,11},{10,... | collective-permute-start | bytes 368648 | tf_op jit(solution)/shard_map/ppermute | solution.py:40
  7.7 0.6 %collective-permute-start.4 = (bf16[160,384]{1,0:T(8,128)(2,1)S(1)}, bf16[160,384]{1,0:T(8,128)(2,1)S(1)}, u32[]{:S(2)}, u32[]{:S(2)}) collective-permute-start(bf16[160,384]{1,0:T(8,128)(2,1)S(1)} %get-tuple-element.43), channel_id=1, source_target_pairs={{0,3},{1,2},{2,1},{3,0},{4,7},{5,6},{6,5},{7,4},{8,11},{9,10},{10,... | collective-permute-start | bytes 368648 | tf_op jit(solution)/shard_map/ppermute | solution.py:40
  8.3 0.3 collective-permute-start.5
  8.6 0.0 copy-start.7
  8.6 2.8 %mlp.3 = (bf16[160,384]{1,0:T(8,128)(2,1)S(1)}, bf16[96,384]{1,0:T(8,128)(2,1)S(1)}, bf16[96,384]{1,0:T(8,128)(2,1)S(1)}, bf16[96,384]{1,0:T(8,128)(2,1)S(1)}, b...) custom-call(bf16[4,180,640]{2,1,0:T(8,128)(2,1)S(1)} %copy.15.conv_ref, ...), custom_call_target="tpu_custom_call" | custom-call | tf_op jit(solution)/shard_map/mlp/pallas_call | solution.py:165
  11.4 1.4 %collective-permute-start.6 = (bf16[96,384]{1,0:T(8,128)(2,1)S(1)}, bf16[96,384]{1,0:T(8,128)(2,1)S(1)}, u32[]{:S(2)}, u32[]{:S(2)}) collective-permute-start(bf16[96,384]{1,0:T(8,128)(2,1)S(1)} %get-tuple-element.45), channel_id=1, source_target_pairs={{0,2},{1,3},{2,0},{3,1},{4,6},{5,7},{6,4},{7,5},{8,10},{9,11},{10,... | collective-permute-start | bytes 221192 | tf_op jit(solution)/shard_map/ppermute | solution.py:40
  12.9 0.4 collective-permute-start.7
  13.3 0.0 collective-permute-done.3.refs_0_
  13.3 0.3 collective-permute-start.8
  13.6 0.0 copy-done.2
  13.6 0.0 copy-done.3
  13.6 0.0 copy-done.4
  13.6 0.0 copy-done.5
  13.6 0.0 copy-done.7
  13.6 0.7 %prepare.1 = (bf16[10,32,768]{2,1,0:T(8,128)(2,1)S(1)}, s32[10,32]{1,0:T(8,128)S(1)}, bf16[4,320,640]{2,1,0:T(8,128)(2,1)S(1)}, bf16[768,640]{1,0:T(8,128)(2,1)S...) custom-call(f32[9,640]{1,0:T(8,128)S(1)} %copy-done.5, bf16[9,16,640]{2,1,0:T(8,128)(2,1)S(1)} %copy-done.4, ...), custom_call_target="tpu_custom_call" | custom-call | tf_op jit(solution)/shard_map/prepare/pallas_call | solution.py:543
  14.4 0.0 collective-permute-done.4.refs_1_
  14.4 0.0 collective-permute-done.5.refs_3_
  14.4 0.7 %analysis_early.1.refs_5_.rest_0_ = f32[2,160,640]{2,1,0:T(8,128)S(1)} custom-call(bf16[160,384]{1,0:T(8,128)(2,1)S(1)} %collective-permute-done.3.refs_0_, bf16[160,384]{1,0:T(8,128)(2,1)S(1)} %collective-permute-done.4.refs_1_, bf16[160,384]{1,0:T(8,128)(2,1)S(1)} %get-tuple-element.36.rest_0_.refs_2_, ...), custom_call_target="tpu_custom_call" | custom-call | tf_op jit(solution)/shard_map/analysis_early/pallas_call | solution.py:214
  15.1 0.1 collective-permute-done.6.refs_0_
  15.2 2.5 %collective-permute-done.7.refs_1_ = bf16[96,384]{1,0:T(8,128)(2,1)S(1)} collective-permute-done((bf16[96,384]{1,0:T(8,128)(2,1)S(1)}, bf16[96,384]{1,0:T(8,128)(2,1)S(1)}, u32[]{:S(2)}, u32[]{:S(2)}) %collective-permute-start.7) | collective-permute-done | bytes 73760 | tf_op jit(solution)/shard_map/ppermute | solution.py:40
  17.7 0.0 collective-permute-done.8.refs_3_
  17.7 0.6 %analysis.2 = (f32[2,96,640]{2,1,0:T(8,128)S(1)}, bf16[3,96,640]{2,1,0:T(8,128)(2,1)S(1)}, bf16[3,96,640]{2,1,0:T(8,128)(2,1)S(1)}) custom-call(bf16[96,384]{1,0:T(8,128)(2,1)S(1)} %collective-permute-done.6.refs_0_, bf16[96,384]{1,0:T(8,128)(2,1)S(1)} %collective-permute-done.7.refs_1_, bf16[160,384]{1,0:T(8,128)(2,1)S(1)} %get-tuple-element.39.refs_2_, ...), custom_call_target="tpu_custom_call" | custom-call | tf_op jit(solution)/shard_map/analysis/pallas_call | solution.py:255
  18.3 1.4 %collective-permute-start.14 = (bf16[3,96,640]{2,1,0:T(8,128)(2,1)S(1)}, bf16[3,96,640]{2,1,0:T(8,128)(2,1)S(1)}, u32[]{:S(2)}, u32[]{:S(2)}) collective-permute-start(bf16[3,96,640]{2,1,0:T(8,128)(2,1)S(1)} %get-tuple-element.61), channel_id=1, source_target_pairs={{0,4},{1,5},{2,6},{3,7},{4,0},{5,1},{6,2},{7,3},{8,12},{9,13},{10,... | collective-permute-start | bytes 1105928 | tf_op jit(solution)/shard_map/ppermute | solution.py:565
  19.7 0.7 %collective-permute-start.15 = (bf16[3,96,640]{2,1,0:T(8,128)(2,1)S(1)}, bf16[3,96,640]{2,1,0:T(8,128)(2,1)S(1)}, u32[]{:S(2)}, u32[]{:S(2)}) collective-permute-start(bf16[3,96,640]{2,1,0:T(8,128)(2,1)S(1)} %get-tuple-element.62), channel_id=1, source_target_pairs={{0,1},{1,0},{2,3},{3,2},{4,8},{5,9},{6,10},{7,11},{8,4},{9,5},{10,... | collective-permute-start | bytes 1105928 | tf_op jit(solution)/shard_map/ppermute | solution.py:565
  20.4 0.3 collective-permute-start
  20.7 1.3 %collective-permute-start.1 = (bf16[64,384]{1,0:T(8,128)(2,1)S(1)}, bf16[64,384]{1,0:T(8,128)(2,1)S(1)}, u32[]{:S(2)}, u32[]{:S(2)}) collective-permute-start(bf16[64,384]{1,0:T(8,128)(2,1)S(1)} %get-tuple-element.38), channel_id=1, source_target_pairs={{0,3},{1,2},{2,1},{3,0},{4,7},{5,6},{6,5},{7,4},{8,11},{9,10},{10,... | collective-permute-start | bytes 147464 | tf_op jit(solution)/shard_map/ppermute | solution.py:40
  22.0 0.2 collective-permute-start.2
  22.3 1.0 %own_terms.2.refs_6_.part_ref = f32[4,96,640]{2,1,0:T(8,128)S(1)} custom-call(f32[2,96,640]{2,1,0:T(8,128)S(1)} %get-tuple-element.48.own_ref, f32[96,32]{1,0:T(8,128)S(1)} %get-tuple-element.49.weight_ref.refs_1_, s32[10,32]{1,0:T(8,128)S(1)} %get-tuple-element.50.target_ref.refs_3_.refs_2_, ...), custom_call_target="tpu_custom_call" | custom-call | tf_op jit(solution)/shard_map/own_terms/pallas_call | solution.py:314
  23.3 0.5 %collective-permute-done.refs_0_ = bf16[64,384]{1,0:T(8,128)(2,1)S(1)} collective-permute-done((bf16[64,384]{1,0:T(8,128)(2,1)S(1)}, bf16[64,384]{1,0:T(8,128)(2,1)S(1)}, u32[]{:S(2)}, u32[]{:S(2)}) %collective-permute-start) | collective-permute-done | bytes 49184 | tf_op jit(solution)/shard_map/ppermute | solution.py:40
  23.8 1.4 %collective-permute-done.1.refs_1_ = bf16[64,384]{1,0:T(8,128)(2,1)S(1)} collective-permute-done((bf16[64,384]{1,0:T(8,128)(2,1)S(1)}, bf16[64,384]{1,0:T(8,128)(2,1)S(1)}, u32[]{:S(2)}, u32[]{:S(2)}) %collective-permute-start.1) | collective-permute-done | bytes 49184 | tf_op jit(solution)/shard_map/ppermute | solution.py:40
  25.2 0.0 collective-permute-done.2.refs_3_
  25.2 0.6 %analysis.3 = (f32[2,64,640]{2,1,0:T(8,128)S(1)}, bf16[3,64,640]{2,1,0:T(8,128)(2,1)S(1)}, bf16[3,64,640]{2,1,0:T(8,128)(2,1)S(1)}) custom-call(bf16[64,384]{1,0:T(8,128)(2,1)S(1)} %collective-permute-done.refs_0_, bf16[64,384]{1,0:T(8,128)(2,1)S(1)} %collective-permute-done.1.refs_1_, bf16[160,384]{1,0:T(8,128)(2,1)S(1)} %get-tuple-element.39.refs_2_, ...), custom_call_target="tpu_custom_call" | custom-call | tf_op jit(solution)/shard_map/analysis/pallas_call | solution.py:255
  25.8 2.9 %collective-permute-start.9 = (bf16[3,64,640]{2,1,0:T(8,128)(2,1)S(1)}, bf16[3,64,640]{2,1,0:T(8,128)(2,1)S(1)}, u32[]{:S(2)}, u32[]{:S(2)}) collective-permute-start(bf16[3,64,640]{2,1,0:T(8,128)(2,1)S(1)} %get-tuple-element.54), channel_id=1, source_target_pairs={{0,4},{1,5},{2,6},{3,7},{4,0},{5,1},{6,2},{7,3},{8,12},{9,13},{10,... | collective-permute-start | bytes 737288 | tf_op jit(solution)/shard_map/ppermute | solution.py:565
  28.7 0.2 collective-permute-start.10
  28.9 0.7 %own_terms.3.part_ref.rest_0_ = f32[4,64,640]{2,1,0:T(8,128)S(1)} custom-call(f32[2,64,640]{2,1,0:T(8,128)S(1)} %get-tuple-element.52.own_ref, f32[64,32]{1,0:T(8,128)S(1)} %get-tuple-element.53.weight_ref.refs_2_, s32[10,32]{1,0:T(8,128)S(1)} %get-tuple-element.50.target_ref.refs_3_.refs_2_, ...), custom_call_target="tpu_custom_call" | custom-call | tf_op jit(solution)/shard_map/own_terms/pallas_call | solution.py:314
  29.6 0.0 collective-permute-done.14.first_ref
  29.6 0.6 %side_terms.1.part_ref = f32[4,96,640]{2,1,0:T(8,128)S(1)} custom-call(f32[4,96,640]{2,1,0:T(8,128)S(1)} %own_terms.2.refs_6_.part_ref, bf16[3,96,640]{2,1,0:T(8,128)(2,1)S(1)} %collective-permute-done.14.first_ref, f32[96,32]{1,0:T(8,128)S(1)} %get-tuple-element.49.weight_ref.refs_1_, s32[10,32]{1,0:T(8,128)S(1)} %get-tuple-element.50.target_ref.refs_3_.refs_2_, ...), custom_call_target="tpu_custom_call" | custom-call | tf_op jit(solution)/shard_map/side_terms/pallas_call | solution.py:362
  30.2 0.0 collective-permute-done.15.refs_0_
  30.2 1.5 %finish.3 = (bf16[180,384]{1,0:T(8,128)(2,1)S(1)}, bf16[180,384]{1,0:T(8,128)(2,1)S(1)}, bf16[180,384]{1,0:T(8,128)(2,1)S(1)}, bf16[180,384]{1,0:T(8,128)(2,1)S(1)}) custom-call(f32[4,96,640]{2,1,0:T(8,128)S(1)} %side_terms.1.part_ref, bf16[3,96,640]{2,1,0:T(8,128)(2,1)S(1)} %collective-permute-done.15.refs_0_, ...), custom_call_target="tpu_custom_call" | custom-call | tf_op jit(solution)/shard_map/finish/pallas_call | solution.py:396
  31.7 0.9 %collective-permute-start.16 = (bf16[180,384]{1,0:T(8,128)(2,1)S(1)}, bf16[180,384]{1,0:T(8,128)(2,1)S(1)}, u32[]{:S(2)}, u32[]{:S(2)}) collective-permute-start(bf16[180,384]{1,0:T(8,128)(2,1)S(1)} %get-tuple-element.63), channel_id=1, source_target_pairs={{0,2},{1,3},{2,0},{3,1},{4,6},{5,7},{6,4},{7,5},{8,10},{9,11},{10,... | collective-permute-start | bytes 414728 | tf_op jit(solution)/shard_map/ppermute | solution.py:40
  32.6 1.2 %collective-permute-start.17 = (bf16[180,384]{1,0:T(8,128)(2,1)S(1)}, bf16[180,384]{1,0:T(8,128)(2,1)S(1)}, u32[]{:S(2)}, u32[]{:S(2)}) collective-permute-start(bf16[180,384]{1,0:T(8,128)(2,1)S(1)} %get-tuple-element.64), channel_id=1, source_target_pairs={{0,3},{1,2},{2,1},{3,0},{4,7},{5,6},{6,5},{7,4},{8,11},{9,10},{10,... | collective-permute-start | bytes 414728 | tf_op jit(solution)/shard_map/ppermute | solution.py:40
  33.8 0.0 collective-permute-start.18
  33.8 1.4 %collective-permute-done.9.refs_0_ = bf16[3,64,640]{2,1,0:T(8,128)(2,1)S(1)} collective-permute-done((bf16[3,64,640]{2,1,0:T(8,128)(2,1)S(1)}, bf16[3,64,640]{2,1,0:T(8,128)(2,1)S(1)}, u32[]{:S(2)}, u32[]{:S(2)}) %collective-permute-start.9) | collective-permute-done | bytes 245792 | tf_op jit(solution)/shard_map/ppermute | solution.py:565
  35.1 0.0 collective-permute-done.10.refs_1_
  35.2 1.2 %finish.2 = (bf16[180,256]{1,0:T(8,128)(2,1)S(1)}, bf16[180,256]{1,0:T(8,128)(2,1)S(1)}, bf16[180,256]{1,0:T(8,128)(2,1)S(1)}, bf16[180,256]{1,0:T(8,128)(2,1)S(1)}) custom-call(f32[4,64,640]{2,1,0:T(8,128)S(1)} %own_terms.3.part_ref.rest_0_, bf16[3,64,640]{2,1,0:T(8,128)(2,1)S(1)} %collective-permute-done.9.refs_0_, ...), custom_call_target="tpu_custom_call" | custom-call | tf_op jit(solution)/shard_map/finish/pallas_call | solution.py:396
  36.4 0.5 %collective-permute-start.13 = (bf16[180,256]{1,0:T(8,128)(2,1)S(1)}, bf16[180,256]{1,0:T(8,128)(2,1)S(1)}, u32[]{:S(2)}, u32[]{:S(2)}) collective-permute-start(bf16[180,256]{1,0:T(8,128)(2,1)S(1)} %get-tuple-element.60), channel_id=1, source_target_pairs={{0,1},{1,0},{2,3},{3,2},{4,5},{5,4},{6,7},{7,6},{8,9},{9,8},{10,11... | collective-permute-start | bytes 276488 | tf_op jit(solution)/shard_map/ppermute | solution.py:40
  36.9 0.0 collective-permute-start.11
  36.9 0.0 collective-permute-done.16.refs_0_
  36.9 2.1 %collective-permute-start.12 = (bf16[180,256]{1,0:T(8,128)(2,1)S(1)}, bf16[180,256]{1,0:T(8,128)(2,1)S(1)}, u32[]{:S(2)}, u32[]{:S(2)}) collective-permute-start(bf16[180,256]{1,0:T(8,128)(2,1)S(1)} %get-tuple-element.58), channel_id=1, source_target_pairs={{0,3},{1,2},{2,1},{3,0},{4,7},{5,6},{6,5},{7,4},{8,11},{9,10},{10,... | collective-permute-start | bytes 276488 | tf_op jit(solution)/shard_map/ppermute | solution.py:40
  39.0 2.0 %collective-permute-done.17.refs_1_ = bf16[180,384]{1,0:T(8,128)(2,1)S(1)} collective-permute-done((bf16[180,384]{1,0:T(8,128)(2,1)S(1)}, bf16[180,384]{1,0:T(8,128)(2,1)S(1)}, u32[]{:S(2)}, u32[]{:S(2)}) %collective-permute-start.17) | collective-permute-done | bytes 138272 | tf_op jit(solution)/shard_map/ppermute | solution.py:40
  41.1 0.0 collective-permute-done.18.refs_3_
  41.1 1.1 %add_chunk.3.refs_2_ = bf16[180,4,640]{2,1,0:T(4,128)(2,1)} custom-call(bf16[4,180,640]{2,1,0:T(8,128)(2,1)S(1)} %copy.19.grad_ref, bf16[180,384]{1,0:T(8,128)(2,1)S(1)} %collective-permute-done.16.refs_0_, bf16[180,384]{1,0:T(8,128)(2,1)S(1)} %collective-permute-done.17.refs_1_, bf16[180,384]{1,0:T(8,128)(2,1)S(1)} %get-tuple-element.65.refs_2_, ...), custom_call_target="tpu_custom_call" | custom-call | tf_op jit(solution)/shard_map/add_chunk/pallas_call | solution.py:467
  42.2 0.0 collective-permute-done.13.refs_1_
  42.2 0.8 %add_chunk.4.refs_2_ = bf16[180,4,640]{2,1,0:T(4,128)(2,1)} custom-call(bf16[4,180,640]{2,1,0:T(8,128)(2,1)S(1)} %copy.19.grad_ref, bf16[180,256]{1,0:T(8,128)(2,1)S(1)} %get-tuple-element.59.refs_0_, bf16[180,256]{1,0:T(8,128)(2,1)S(1)} %collective-permute-done.13.refs_1_, bf16[180,4,640]{2,1,0:T(4,128)(2,1)} %add_chunk.3.refs_2_), custom_call_target="tpu_custom_call", output_to_operand_aliasing={{}: (3, {})} | custom-call | tf_op jit(solution)/shard_map/add_chunk/pallas_call | solution.py:467
  43.1 0.0 collective-permute-done.11.refs_0_
  43.1 1.2 %collective-permute-done.12.refs_1_ = bf16[180,256]{1,0:T(8,128)(2,1)S(1)} collective-permute-done((bf16[180,256]{1,0:T(8,128)(2,1)S(1)}, bf16[180,256]{1,0:T(8,128)(2,1)S(1)}, u32[]{:S(2)}, u32[]{:S(2)}) %collective-permute-start.12) | collective-permute-done | bytes 92192 | tf_op jit(solution)/shard_map/ppermute | solution.py:40
  44.3 0.8 %add_chunk.5 = bf16[180,4,640]{2,1,0:T(4,128)(2,1)} custom-call(bf16[4,180,640]{2,1,0:T(8,128)(2,1)S(1)} %copy.19.grad_ref, bf16[180,256]{1,0:T(8,128)(2,1)S(1)} %collective-permute-done.11.refs_0_, bf16[180,256]{1,0:T(8,128)(2,1)S(1)} %collective-permute-done.12.refs_1_, bf16[180,4,640]{2,1,0:T(4,128)(2,1)} %add_chunk.4.refs_2_), custom_call_target="tpu_custom_call", output_to_operand_aliasing={{}: (3, {})} | custom-call | tf_op jit(solution)/shard_map/add_chunk/pallas_call | solution.py:467
  (6 shorter events, 0.0 us)
Async XLA Ops:
  0.0 2.8 %copy-start.1 = (bf16[1280,640]{1,0:T(8,128)(2,1)S(1)}, bf16[1280,640]{1,0:T(8,128)(2,1)}, u32[]{:S(2)}) copy-start(bf16[1280,640]{1,0:T(8,128)(2,1)} %wout_ref.3) | copy-start | bytes 4915204
  0.0 2.8 %copy-start.6 = (f32[1280]{0:T(1024)S(1)}, f32[1280]{0:T(1024)}, u32[]{:S(2)}) copy-start(f32[1280]{0:T(1024)} %bias_ref.3) | copy-start | bytes 15364
  0.0 2.8 %copy-start = (bf16[640,1280]{1,0:T(8,128)(2,1)S(1)}, bf16[640,1280]{1,0:T(8,128)(2,1)}, u32[]{:S(2)}) copy-start(bf16[640,1280]{1,0:T(8,128)(2,1)} %win_ref.3) | copy-start | bytes 4915204
  5.6 7.7 %collective-permute-start.3 = (bf16[160,384]{1,0:T(8,128)(2,1)S(1)}, bf16[160,384]{1,0:T(8,128)(2,1)S(1)}, u32[]{:S(2)}, u32[]{:S(2)}) collective-permute-start(bf16[160,384]{1,0:T(8,128)(2,1)S(1)} %get-tuple-element.42), channel_id=1, source_target_pairs={{0,2},{1,3},{2,0},{3,1},{4,6},{5,7},{6,4},{7,5},{8,10},{9,11},{10,... | collective-permute-start | bytes 368648 | tf_op jit(solution)/shard_map/ppermute | solution.py:40
  7.7 6.7 %collective-permute-start.4 = (bf16[160,384]{1,0:T(8,128)(2,1)S(1)}, bf16[160,384]{1,0:T(8,128)(2,1)S(1)}, u32[]{:S(2)}, u32[]{:S(2)}) collective-permute-start(bf16[160,384]{1,0:T(8,128)(2,1)S(1)} %get-tuple-element.43), channel_id=1, source_target_pairs={{0,3},{1,2},{2,1},{3,0},{4,7},{5,6},{6,5},{7,4},{8,11},{9,10},{10,... | collective-permute-start | bytes 368648 | tf_op jit(solution)/shard_map/ppermute | solution.py:40
  8.3 6.1 %collective-permute-start.5 = (bf16[160,384]{1,0:T(8,128)(2,1)S(1)}, bf16[160,384]{1,0:T(8,128)(2,1)S(1)}, u32[]{:S(2)}, u32[]{:S(2)}) collective-permute-start(bf16[160,384]{1,0:T(8,128)(2,1)S(1)} %get-tuple-element.44), channel_id=1, source_target_pairs={{0,1},{1,0},{2,3},{3,2},{4,5},{5,4},{6,7},{7,6},{8,9},{9,8},{10,11... | collective-permute-start | bytes 368648 | tf_op jit(solution)/shard_map/ppermute | solution.py:40
  8.6 5.0 %copy-start.2 = (bf16[4,320,640]{2,1,0:T(8,128)(2,1)S(1)}, bf16[4,320,640]{2,1,0:T(8,128)(2,1)}, u32[]{:S(2)}) copy-start(bf16[4,320,640]{2,1,0:T(8,128)(2,1)} %constant.4.clone.forth_ref) | copy-start | bytes 4915204
  8.6 5.0 %copy-start.3 = (bf16[768,640]{1,0:T(8,128)(2,1)S(1)}, bf16[768,640]{1,0:T(8,128)(2,1)}, u32[]{:S(2)}) copy-start(bf16[768,640]{1,0:T(8,128)(2,1)} %constant.5.clone.back_ref) | copy-start | bytes 2949124
  8.6 5.0 %copy-start.4 = (bf16[9,16,640]{2,1,0:T(8,128)(2,1)S(1)}, bf16[9,16,640]{2,1,0:T(8,128)(2,1)}, u32[]{:S(2)}) copy-start(bf16[9,16,640]{2,1,0:T(8,128)(2,1)} %filt_ref.1) | copy-start | bytes 552964
  8.6 5.0 %copy-start.5 = (f32[9,640]{1,0:T(8,128)S(1)}, f32[9,640]{1,0:T(8,128)}, u32[]{:S(2)}) copy-start(f32[9,640]{1,0:T(8,128)} %weight_ref.1) | copy-start | bytes 69124
  8.6 5.0 %copy-start.7 = (s32[16,9]{1,0:T(8,128)S(1)}, s32[16,9]{1,0:T(8,128)}, u32[]{:S(2)}) copy-start(s32[16,9]{1,0:T(8,128)} %offset_ref.1) | copy-start | bytes 1732
  11.4 3.8 %collective-permute-start.6 = (bf16[96,384]{1,0:T(8,128)(2,1)S(1)}, bf16[96,384]{1,0:T(8,128)(2,1)S(1)}, u32[]{:S(2)}, u32[]{:S(2)}) collective-permute-start(bf16[96,384]{1,0:T(8,128)(2,1)S(1)} %get-tuple-element.45), channel_id=1, source_target_pairs={{0,2},{1,3},{2,0},{3,1},{4,6},{5,7},{6,4},{7,5},{8,10},{9,11},{10,... | collective-permute-start | bytes 221192 | tf_op jit(solution)/shard_map/ppermute | solution.py:40
  12.9 4.8 %collective-permute-start.7 = (bf16[96,384]{1,0:T(8,128)(2,1)S(1)}, bf16[96,384]{1,0:T(8,128)(2,1)S(1)}, u32[]{:S(2)}, u32[]{:S(2)}) collective-permute-start(bf16[96,384]{1,0:T(8,128)(2,1)S(1)} %get-tuple-element.46), channel_id=1, source_target_pairs={{0,3},{1,2},{2,1},{3,0},{4,7},{5,6},{6,5},{7,4},{8,11},{9,10},{10,... | collective-permute-start | bytes 221192 | tf_op jit(solution)/shard_map/ppermute | solution.py:40
  13.3 4.4 %collective-permute-start.8 = (bf16[96,384]{1,0:T(8,128)(2,1)S(1)}, bf16[96,384]{1,0:T(8,128)(2,1)S(1)}, u32[]{:S(2)}, u32[]{:S(2)}) collective-permute-start(bf16[96,384]{1,0:T(8,128)(2,1)S(1)} %get-tuple-element.47), channel_id=1, source_target_pairs={{0,1},{1,0},{2,3},{3,2},{4,5},{5,4},{6,7},{7,6},{8,9},{9,8},{10,11... | collective-permute-start | bytes 221192 | tf_op jit(solution)/shard_map/ppermute | solution.py:40
  18.3 11.3 %collective-permute-start.14 = (bf16[3,96,640]{2,1,0:T(8,128)(2,1)S(1)}, bf16[3,96,640]{2,1,0:T(8,128)(2,1)S(1)}, u32[]{:S(2)}, u32[]{:S(2)}) collective-permute-start(bf16[3,96,640]{2,1,0:T(8,128)(2,1)S(1)} %get-tuple-element.61), channel_id=1, source_target_pairs={{0,4},{1,5},{2,6},{3,7},{4,0},{5,1},{6,2},{7,3},{8,12},{9,13},{10,... | collective-permute-start | bytes 1105928 | tf_op jit(solution)/shard_map/ppermute | solution.py:565
  19.7 10.5 %collective-permute-start.15 = (bf16[3,96,640]{2,1,0:T(8,128)(2,1)S(1)}, bf16[3,96,640]{2,1,0:T(8,128)(2,1)S(1)}, u32[]{:S(2)}, u32[]{:S(2)}) collective-permute-start(bf16[3,96,640]{2,1,0:T(8,128)(2,1)S(1)} %get-tuple-element.62), channel_id=1, source_target_pairs={{0,1},{1,0},{2,3},{3,2},{4,8},{5,9},{6,10},{7,11},{8,4},{9,5},{10,... | collective-permute-start | bytes 1105928 | tf_op jit(solution)/shard_map/ppermute | solution.py:565
  20.4 3.4 %collective-permute-start = (bf16[64,384]{1,0:T(8,128)(2,1)S(1)}, bf16[64,384]{1,0:T(8,128)(2,1)S(1)}, u32[]{:S(2)}, u32[]{:S(2)}) collective-permute-start(bf16[64,384]{1,0:T(8,128)(2,1)S(1)} %get-tuple-element.37), channel_id=1, source_target_pairs={{0,2},{1,3},{2,0},{3,1},{4,6},{5,7},{6,4},{7,5},{8,10},{9,11},{10,... | collective-permute-start | bytes 147464 | tf_op jit(solution)/shard_map/ppermute | solution.py:40
  20.7 4.5 %collective-permute-start.1 = (bf16[64,384]{1,0:T(8,128)(2,1)S(1)}, bf16[64,384]{1,0:T(8,128)(2,1)S(1)}, u32[]{:S(2)}, u32[]{:S(2)}) collective-permute-start(bf16[64,384]{1,0:T(8,128)(2,1)S(1)} %get-tuple-element.38), channel_id=1, source_target_pairs={{0,3},{1,2},{2,1},{3,0},{4,7},{5,6},{6,5},{7,4},{8,11},{9,10},{10,... | collective-permute-start | bytes 147464 | tf_op jit(solution)/shard_map/ppermute | solution.py:40
  22.0 3.2 %collective-permute-start.2 = (bf16[64,384]{1,0:T(8,128)(2,1)S(1)}, bf16[64,384]{1,0:T(8,128)(2,1)S(1)}, u32[]{:S(2)}, u32[]{:S(2)}) collective-permute-start(bf16[64,384]{1,0:T(8,128)(2,1)S(1)} %get-tuple-element.40), channel_id=1, source_target_pairs={{0,1},{1,0},{2,3},{3,2},{4,5},{5,4},{6,7},{7,6},{8,9},{9,8},{10,11... | collective-permute-start | bytes 147464 | tf_op jit(solution)/shard_map/ppermute | solution.py:40
  25.8 9.3 %collective-permute-start.9 = (bf16[3,64,640]{2,1,0:T(8,128)(2,1)S(1)}, bf16[3,64,640]{2,1,0:T(8,128)(2,1)S(1)}, u32[]{:S(2)}, u32[]{:S(2)}) collective-permute-start(bf16[3,64,640]{2,1,0:T(8,128)(2,1)S(1)} %get-tuple-element.54), channel_id=1, source_target_pairs={{0,4},{1,5},{2,6},{3,7},{4,0},{5,1},{6,2},{7,3},{8,12},{9,13},{10,... | collective-permute-start | bytes 737288 | tf_op jit(solution)/shard_map/ppermute | solution.py:565
  28.7 6.5 %collective-permute-start.10 = (bf16[3,64,640]{2,1,0:T(8,128)(2,1)S(1)}, bf16[3,64,640]{2,1,0:T(8,128)(2,1)S(1)}, u32[]{:S(2)}, u32[]{:S(2)}) collective-permute-start(bf16[3,64,640]{2,1,0:T(8,128)(2,1)S(1)} %get-tuple-element.55), channel_id=1, source_target_pairs={{0,1},{1,0},{2,3},{3,2},{4,8},{5,9},{6,10},{7,11},{8,4},{9,5},{10,... | collective-permute-start | bytes 737288 | tf_op jit(solution)/shard_map/ppermute | solution.py:565
  31.7 5.2 %collective-permute-start.16 = (bf16[180,384]{1,0:T(8,128)(2,1)S(1)}, bf16[180,384]{1,0:T(8,128)(2,1)S(1)}, u32[]{:S(2)}, u32[]{:S(2)}) collective-permute-start(bf16[180,384]{1,0:T(8,128)(2,1)S(1)} %get-tuple-element.63), channel_id=1, source_target_pairs={{0,2},{1,3},{2,0},{3,1},{4,6},{5,7},{6,4},{7,5},{8,10},{9,11},{10,... | collective-permute-start | bytes 414728 | tf_op jit(solution)/shard_map/ppermute | solution.py:40
  32.6 8.4 %collective-permute-start.17 = (bf16[180,384]{1,0:T(8,128)(2,1)S(1)}, bf16[180,384]{1,0:T(8,128)(2,1)S(1)}, u32[]{:S(2)}, u32[]{:S(2)}) collective-permute-start(bf16[180,384]{1,0:T(8,128)(2,1)S(1)} %get-tuple-element.64), channel_id=1, source_target_pairs={{0,3},{1,2},{2,1},{3,0},{4,7},{5,6},{6,5},{7,4},{8,11},{9,10},{10,... | collective-permute-start | bytes 414728 | tf_op jit(solution)/shard_map/ppermute | solution.py:40
  33.8 7.3 %collective-permute-start.18 = (bf16[180,384]{1,0:T(8,128)(2,1)S(1)}, bf16[180,384]{1,0:T(8,128)(2,1)S(1)}, u32[]{:S(2)}, u32[]{:S(2)}) collective-permute-start(bf16[180,384]{1,0:T(8,128)(2,1)S(1)} %get-tuple-element.66), channel_id=1, source_target_pairs={{0,1},{1,0},{2,3},{3,2},{4,5},{5,4},{6,7},{7,6},{8,9},{9,8},{10,11... | collective-permute-start | bytes 414728 | tf_op jit(solution)/shard_map/ppermute | solution.py:40
  36.4 5.9 %collective-permute-start.13 = (bf16[180,256]{1,0:T(8,128)(2,1)S(1)}, bf16[180,256]{1,0:T(8,128)(2,1)S(1)}, u32[]{:S(2)}, u32[]{:S(2)}) collective-permute-start(bf16[180,256]{1,0:T(8,128)(2,1)S(1)} %get-tuple-element.60), channel_id=1, source_target_pairs={{0,1},{1,0},{2,3},{3,2},{4,5},{5,4},{6,7},{7,6},{8,9},{9,8},{10,11... | collective-permute-start | bytes 276488 | tf_op jit(solution)/shard_map/ppermute | solution.py:40
  36.9 6.2 %collective-permute-start.11 = (bf16[180,256]{1,0:T(8,128)(2,1)S(1)}, bf16[180,256]{1,0:T(8,128)(2,1)S(1)}, u32[]{:S(2)}, u32[]{:S(2)}) collective-permute-start(bf16[180,256]{1,0:T(8,128)(2,1)S(1)} %get-tuple-element.57), channel_id=1, source_target_pairs={{0,2},{1,3},{2,0},{3,1},{4,6},{5,7},{6,4},{7,5},{8,10},{9,11},{10,... | collective-permute-start | bytes 276488 | tf_op jit(solution)/shard_map/ppermute | solution.py:40
  36.9 7.4 %collective-permute-start.12 = (bf16[180,256]{1,0:T(8,128)(2,1)S(1)}, bf16[180,256]{1,0:T(8,128)(2,1)S(1)}, u32[]{:S(2)}, u32[]{:S(2)}) collective-permute-start(bf16[180,256]{1,0:T(8,128)(2,1)S(1)} %get-tuple-element.58), channel_id=1, source_target_pairs={{0,3},{1,2},{2,1},{3,0},{4,7},{5,6},{6,5},{7,4},{8,11},{9,10},{10,... | collective-permute-start | bytes 276488 | tf_op jit(solution)/shard_map/ppermute | solution.py:40

commit v11 on v9

--- a/solution.py
+++ b/solution.py
@@ -589,7 +589,7 @@
     for q in range(len(chunks)):
         halos = spectra[q]
         if q == 0:
-            others = [terms[other] for other in terms if other > q]
+            others = []
             terms[q] = side_terms(terms[q], halos[0], weights[q], target, filters, others)
             halos = halos[1:]
         grids = finish(terms[q], halos, weights[q], target, filters, back, count, part)

time: 45.1 us -> 44.9 us (level); the launches traced: 44.9 us -> 44.3 us
  waiting for transfers between devices: 9.51 us -> 8.88 us
    ppermute x15, waiting for transfers between devices: 7.79 us -> 7.25 us  [exchange(): return lax.ppermute(block, 'azimuth', pairs)]
where the time goes in v11:
time: 44.9 us; the launch traced here: 44.3 us
  starting transfers between devices  16.7 us (37%)
  Pallas kernels  15.5 us (35%)
  waiting for transfers between devices  8.88 us (20%)
  local copies, waits for them, and re-layouts  2.77 us (6%)
    ppermute x15, starting transfers between devices, exchange(): return lax.ppermute(block, 'azimuth', pairs)  11.6 us
    ppermute x15, waiting for transfers between devices, exchange(): return lax.ppermute(block, 'azimuth', pairs)  7.25 us
    pallas_call x2, Pallas kernels, mlp(): pl.pallas_call(functools.partial(mlp_kernel, count, half, sent, chunks),...  5.53 us
    ppermute x4, starting transfers between devices, halo(): blocks.append(lax.ppermute(block, ('polar', 'azimuth'), pairs))  5.17 us
    pallas_call x3, Pallas kernels, add_chunk(): pl.pallas_call(functools.partial(add_kernel, count, chunk, [k for k, _ in...  2.83 us
    unnamed x18, local copies, waits for them, and re-layouts  2.77 us
    pallas_call x2, Pallas kernels, finish(): pl.pallas_call(functools.partial(finish_kernel, count, len(halos)), in_sp...  2.35 us
    pallas_call x2, Pallas kernels, own_terms(): pl.pallas_call(functools.partial(own_kernel, start), in_specs=[pl.BlockSp...  1.72 us
  transfers between devices with their start and end apart: 19, of which 7 were waited for; matrix products, arithmetic and copies ran while one was open for 0% of the time, Pallas kernels for 25%

profile of v11, /device:TPU:1, one launch (start us, length us, event | category | flops | bytes accessed | tf_op | source)
XLA Modules:
  0.0 44.3 jit_solution(11972615536688242687)
XLA Ops:
  0.0 0.0 copy-start.1
  0.0 1.4 %copy.19.grad_ref = bf16[4,180,640]{2,1,0:T(8,128)(2,1)S(1)} copy(bf16[4,180,640]{2,0,1:T(4,128)(2,1)} %param.11) | data formatting | bytes 1843200 | tf_op args[1]
  1.5 1.3 %copy.15.conv_ref = bf16[4,180,640]{2,1,0:T(8,128)(2,1)S(1)} copy(bf16[4,180,640]{2,0,1:T(4,128)(2,1)} %param.10) | data formatting | bytes 1843200 | tf_op args[0]
  2.8 0.0 copy-done.1
  2.8 0.0 copy-done.6
  2.8 0.0 copy-done
  2.8 2.8 %mlp.2 = (bf16[160,384]{1,0:T(8,128)(2,1)S(1)}, bf16[160,384]{1,0:T(8,128)(2,1)S(1)}, bf16[160,384]{1,0:T(8,128)(2,1)S(1)}, bf16[160,384]{1,0:T(8,128)(2,1)S(1)}) custom-call(bf16[4,180,640]{2,1,0:T(8,128)(2,1)S(1)} %copy.15.conv_ref, bf16[4,180,640]{2,1,0:T(8,128)(2,1)S(1)} %copy.19.grad_ref, bf16[640,1280]{1,0:T(8,128)(2,1)S(1)} %copy-done, ...), custom_call_target="tpu_custom_call" | custom-call | tf_op jit(solution)/shard_map/mlp/pallas_call | solution.py:165
  5.6 2.1 %collective-permute-start.3 = (bf16[160,384]{1,0:T(8,128)(2,1)S(1)}, bf16[160,384]{1,0:T(8,128)(2,1)S(1)}, u32[]{:S(2)}, u32[]{:S(2)}) collective-permute-start(bf16[160,384]{1,0:T(8,128)(2,1)S(1)} %get-tuple-element.42), channel_id=1, source_target_pairs={{0,2},{1,3},{2,0},{3,1},{4,6},{5,7},{6,4},{7,5},{8,10},{9,11},{10,... | collective-permute-start | bytes 368648 | tf_op jit(solution)/shard_map/ppermute | solution.py:40
  7.7 0.6 %collective-permute-start.4 = (bf16[160,384]{1,0:T(8,128)(2,1)S(1)}, bf16[160,384]{1,0:T(8,128)(2,1)S(1)}, u32[]{:S(2)}, u32[]{:S(2)}) collective-permute-start(bf16[160,384]{1,0:T(8,128)(2,1)S(1)} %get-tuple-element.43), channel_id=1, source_target_pairs={{0,3},{1,2},{2,1},{3,0},{4,7},{5,6},{6,5},{7,4},{8,11},{9,10},{10,... | collective-permute-start | bytes 368648 | tf_op jit(solution)/shard_map/ppermute | solution.py:40
  8.3 0.3 collective-permute-start.5
  8.6 0.0 copy-start.7
  8.6 2.8 %mlp.3 = (bf16[160,384]{1,0:T(8,128)(2,1)S(1)}, bf16[96,384]{1,0:T(8,128)(2,1)S(1)}, bf16[96,384]{1,0:T(8,128)(2,1)S(1)}, bf16[96,384]{1,0:T(8,128)(2,1)S(1)}, b...) custom-call(bf16[4,180,640]{2,1,0:T(8,128)(2,1)S(1)} %copy.15.conv_ref, ...), custom_call_target="tpu_custom_call" | custom-call | tf_op jit(solution)/shard_map/mlp/pallas_call | solution.py:165
  11.4 1.4 %collective-permute-start.6 = (bf16[96,384]{1,0:T(8,128)(2,1)S(1)}, bf16[96,384]{1,0:T(8,128)(2,1)S(1)}, u32[]{:S(2)}, u32[]{:S(2)}) collective-permute-start(bf16[96,384]{1,0:T(8,128)(2,1)S(1)} %get-tuple-element.45), channel_id=1, source_target_pairs={{0,2},{1,3},{2,0},{3,1},{4,6},{5,7},{6,4},{7,5},{8,10},{9,11},{10,... | collective-permute-start | bytes 221192 | tf_op jit(solution)/shard_map/ppermute | solution.py:40
  12.9 0.4 collective-permute-start.7
  13.3 0.0 collective-permute-done.3.refs_0_
  13.3 0.3 collective-permute-start.8
  13.6 0.0 copy-done.2
  13.6 0.0 copy-done.3
  13.6 0.0 copy-done.4
  13.6 0.0 copy-done.5
  13.6 0.0 copy-done.7
  13.6 0.7 %prepare.1 = (bf16[10,32,768]{2,1,0:T(8,128)(2,1)S(1)}, s32[10,32]{1,0:T(8,128)S(1)}, bf16[4,320,640]{2,1,0:T(8,128)(2,1)S(1)}, bf16[768,640]{1,0:T(8,128)(2,1)S...) custom-call(f32[9,640]{1,0:T(8,128)S(1)} %copy-done.5, bf16[9,16,640]{2,1,0:T(8,128)(2,1)S(1)} %copy-done.4, ...), custom_call_target="tpu_custom_call" | custom-call | tf_op jit(solution)/shard_map/prepare/pallas_call | solution.py:534
  14.4 0.0 collective-permute-done.4.refs_1_
  14.4 0.0 collective-permute-done.5.refs_3_
  14.4 0.7 %analysis_early.1.refs_5_.rest_0_ = f32[2,160,640]{2,1,0:T(8,128)S(1)} custom-call(bf16[160,384]{1,0:T(8,128)(2,1)S(1)} %collective-permute-done.3.refs_0_, bf16[160,384]{1,0:T(8,128)(2,1)S(1)} %collective-permute-done.4.refs_1_, bf16[160,384]{1,0:T(8,128)(2,1)S(1)} %get-tuple-element.36.rest_0_.refs_2_, ...), custom_call_target="tpu_custom_call" | custom-call | tf_op jit(solution)/shard_map/analysis_early/pallas_call | solution.py:214
  15.1 0.1 collective-permute-done.6.refs_0_
  15.2 2.5 %collective-permute-done.7.refs_1_ = bf16[96,384]{1,0:T(8,128)(2,1)S(1)} collective-permute-done((bf16[96,384]{1,0:T(8,128)(2,1)S(1)}, bf16[96,384]{1,0:T(8,128)(2,1)S(1)}, u32[]{:S(2)}, u32[]{:S(2)}) %collective-permute-start.7) | collective-permute-done | bytes 73760 | tf_op jit(solution)/shard_map/ppermute | solution.py:40
  17.7 0.0 collective-permute-done.8.refs_3_
  17.7 0.6 %analysis.2 = (f32[2,96,640]{2,1,0:T(8,128)S(1)}, bf16[3,96,640]{2,1,0:T(8,128)(2,1)S(1)}, bf16[3,96,640]{2,1,0:T(8,128)(2,1)S(1)}) custom-call(bf16[96,384]{1,0:T(8,128)(2,1)S(1)} %collective-permute-done.6.refs_0_, bf16[96,384]{1,0:T(8,128)(2,1)S(1)} %collective-permute-done.7.refs_1_, bf16[160,384]{1,0:T(8,128)(2,1)S(1)} %get-tuple-element.39.refs_2_, ...), custom_call_target="tpu_custom_call" | custom-call | tf_op jit(solution)/shard_map/analysis/pallas_call | solution.py:255
  18.3 1.4 %collective-permute-start.14 = (bf16[3,96,640]{2,1,0:T(8,128)(2,1)S(1)}, bf16[3,96,640]{2,1,0:T(8,128)(2,1)S(1)}, u32[]{:S(2)}, u32[]{:S(2)}) collective-permute-start(bf16[3,96,640]{2,1,0:T(8,128)(2,1)S(1)} %get-tuple-element.61), channel_id=1, source_target_pairs={{0,4},{1,5},{2,6},{3,7},{4,0},{5,1},{6,2},{7,3},{8,12},{9,13},{10,... | collective-permute-start | bytes 1105928 | tf_op jit(solution)/shard_map/ppermute | solution.py:556
  19.7 0.7 %collective-permute-start.15 = (bf16[3,96,640]{2,1,0:T(8,128)(2,1)S(1)}, bf16[3,96,640]{2,1,0:T(8,128)(2,1)S(1)}, u32[]{:S(2)}, u32[]{:S(2)}) collective-permute-start(bf16[3,96,640]{2,1,0:T(8,128)(2,1)S(1)} %get-tuple-element.62), channel_id=1, source_target_pairs={{0,1},{1,0},{2,3},{3,2},{4,8},{5,9},{6,10},{7,11},{8,4},{9,5},{10,... | collective-permute-start | bytes 1105928 | tf_op jit(solution)/shard_map/ppermute | solution.py:556
  20.4 0.3 collective-permute-start
  20.7 1.3 %collective-permute-start.1 = (bf16[64,384]{1,0:T(8,128)(2,1)S(1)}, bf16[64,384]{1,0:T(8,128)(2,1)S(1)}, u32[]{:S(2)}, u32[]{:S(2)}) collective-permute-start(bf16[64,384]{1,0:T(8,128)(2,1)S(1)} %get-tuple-element.38), channel_id=1, source_target_pairs={{0,3},{1,2},{2,1},{3,0},{4,7},{5,6},{6,5},{7,4},{8,11},{9,10},{10,... | collective-permute-start | bytes 147464 | tf_op jit(solution)/shard_map/ppermute | solution.py:40
  22.0 0.2 collective-permute-start.2
  22.3 1.0 %own_terms.2.refs_6_.part_ref = f32[4,96,640]{2,1,0:T(8,128)S(1)} custom-call(f32[2,96,640]{2,1,0:T(8,128)S(1)} %get-tuple-element.48.own_ref, f32[96,32]{1,0:T(8,128)S(1)} %get-tuple-element.49.weight_ref.refs_1_, s32[10,32]{1,0:T(8,128)S(1)} %get-tuple-element.50.target_ref.refs_3_.refs_2_, ...), custom_call_target="tpu_custom_call" | custom-call | tf_op jit(solution)/shard_map/own_terms/pallas_call | solution.py:311
  23.3 0.5 %collective-permute-done.refs_0_ = bf16[64,384]{1,0:T(8,128)(2,1)S(1)} collective-permute-done((bf16[64,384]{1,0:T(8,128)(2,1)S(1)}, bf16[64,384]{1,0:T(8,128)(2,1)S(1)}, u32[]{:S(2)}, u32[]{:S(2)}) %collective-permute-start) | collective-permute-done | bytes 49184 | tf_op jit(solution)/shard_map/ppermute | solution.py:40
  23.8 1.4 %collective-permute-done.1.refs_1_ = bf16[64,384]{1,0:T(8,128)(2,1)S(1)} collective-permute-done((bf16[64,384]{1,0:T(8,128)(2,1)S(1)}, bf16[64,384]{1,0:T(8,128)(2,1)S(1)}, u32[]{:S(2)}, u32[]{:S(2)}) %collective-permute-start.1) | collective-permute-done | bytes 49184 | tf_op jit(solution)/shard_map/ppermute | solution.py:40
  25.2 0.0 collective-permute-done.2.refs_3_
  25.2 0.6 %analysis.3 = (f32[2,64,640]{2,1,0:T(8,128)S(1)}, bf16[3,64,640]{2,1,0:T(8,128)(2,1)S(1)}, bf16[3,64,640]{2,1,0:T(8,128)(2,1)S(1)}) custom-call(bf16[64,384]{1,0:T(8,128)(2,1)S(1)} %collective-permute-done.refs_0_, bf16[64,384]{1,0:T(8,128)(2,1)S(1)} %collective-permute-done.1.refs_1_, bf16[160,384]{1,0:T(8,128)(2,1)S(1)} %get-tuple-element.39.refs_2_, ...), custom_call_target="tpu_custom_call" | custom-call | tf_op jit(solution)/shard_map/analysis/pallas_call | solution.py:255
  25.8 2.9 %collective-permute-start.9 = (bf16[3,64,640]{2,1,0:T(8,128)(2,1)S(1)}, bf16[3,64,640]{2,1,0:T(8,128)(2,1)S(1)}, u32[]{:S(2)}, u32[]{:S(2)}) collective-permute-start(bf16[3,64,640]{2,1,0:T(8,128)(2,1)S(1)} %get-tuple-element.54), channel_id=1, source_target_pairs={{0,4},{1,5},{2,6},{3,7},{4,0},{5,1},{6,2},{7,3},{8,12},{9,13},{10,... | collective-permute-start | bytes 737288 | tf_op jit(solution)/shard_map/ppermute | solution.py:556
  28.7 0.2 collective-permute-start.10
  28.9 0.0 collective-permute-done.14.first_ref
  28.9 0.5 %side_terms.1.part_ref = f32[4,96,640]{2,1,0:T(8,128)S(1)} custom-call(f32[4,96,640]{2,1,0:T(8,128)S(1)} %own_terms.2.refs_6_.part_ref, bf16[3,96,640]{2,1,0:T(8,128)(2,1)S(1)} %collective-permute-done.14.first_ref, f32[96,32]{1,0:T(8,128)S(1)} %get-tuple-element.49.weight_ref.refs_1_, s32[10,32]{1,0:T(8,128)S(1)} %get-tuple-element.50.target_ref.refs_3_.refs_2_, ...), custom_call_target="tpu_custom_call" | custom-call | tf_op jit(solution)/shard_map/side_terms/pallas_call | solution.py:353
  29.4 0.0 collective-permute-done.15.refs_0_
  29.4 1.2 %finish.3 = (bf16[180,384]{1,0:T(8,128)(2,1)S(1)}, bf16[180,384]{1,0:T(8,128)(2,1)S(1)}, bf16[180,384]{1,0:T(8,128)(2,1)S(1)}, bf16[180,384]{1,0:T(8,128)(2,1)S(1)}) custom-call(f32[4,96,640]{2,1,0:T(8,128)S(1)} %side_terms.1.part_ref, bf16[3,96,640]{2,1,0:T(8,128)(2,1)S(1)} %collective-permute-done.15.refs_0_, ...), custom_call_target="tpu_custom_call" | custom-call | tf_op jit(solution)/shard_map/finish/pallas_call | solution.py:387
  30.6 0.9 %collective-permute-start.16 = (bf16[180,384]{1,0:T(8,128)(2,1)S(1)}, bf16[180,384]{1,0:T(8,128)(2,1)S(1)}, u32[]{:S(2)}, u32[]{:S(2)}) collective-permute-start(bf16[180,384]{1,0:T(8,128)(2,1)S(1)} %get-tuple-element.63), channel_id=1, source_target_pairs={{0,2},{1,3},{2,0},{3,1},{4,6},{5,7},{6,4},{7,5},{8,10},{9,11},{10,... | collective-permute-start | bytes 414728 | tf_op jit(solution)/shard_map/ppermute | solution.py:40
  31.5 1.3 %collective-permute-start.17 = (bf16[180,384]{1,0:T(8,128)(2,1)S(1)}, bf16[180,384]{1,0:T(8,128)(2,1)S(1)}, u32[]{:S(2)}, u32[]{:S(2)}) collective-permute-start(bf16[180,384]{1,0:T(8,128)(2,1)S(1)} %get-tuple-element.64), channel_id=1, source_target_pairs={{0,3},{1,2},{2,1},{3,0},{4,7},{5,6},{6,5},{7,4},{8,11},{9,10},{10,... | collective-permute-start | bytes 414728 | tf_op jit(solution)/shard_map/ppermute | solution.py:40
  32.8 0.0 collective-permute-start.18
  32.8 0.7 %own_terms.3.part_ref = f32[4,64,640]{2,1,0:T(8,128)S(1)} custom-call(f32[2,64,640]{2,1,0:T(8,128)S(1)} %get-tuple-element.52.own_ref, f32[64,32]{1,0:T(8,128)S(1)} %get-tuple-element.53.weight_ref.refs_2_, s32[10,32]{1,0:T(8,128)S(1)} %get-tuple-element.50.target_ref.refs_3_.refs_2_, bf16[10,32,768]{2,1,0:T(8,128)(2,1)S(1)} %get-tuple-element.51.filter_ref.refs_4_.refs_3_, ...), custom_call_target="tpu_custom_call" | custom-call | tf_op jit(solution)/shard_map/own_terms/pallas_call | solution.py:311
  33.5 1.6 %collective-permute-done.9.refs_0_ = bf16[3,64,640]{2,1,0:T(8,128)(2,1)S(1)} collective-permute-done((bf16[3,64,640]{2,1,0:T(8,128)(2,1)S(1)}, bf16[3,64,640]{2,1,0:T(8,128)(2,1)S(1)}, u32[]{:S(2)}, u32[]{:S(2)}) %collective-permute-start.9) | collective-permute-done | bytes 245792 | tf_op jit(solution)/shard_map/ppermute | solution.py:556
  35.1 0.0 collective-permute-done.10.refs_1_
  35.2 1.1 %finish.2 = (bf16[180,256]{1,0:T(8,128)(2,1)S(1)}, bf16[180,256]{1,0:T(8,128)(2,1)S(1)}, bf16[180,256]{1,0:T(8,128)(2,1)S(1)}, bf16[180,256]{1,0:T(8,128)(2,1)S(1)}) custom-call(f32[4,64,640]{2,1,0:T(8,128)S(1)} %own_terms.3.part_ref, bf16[3,64,640]{2,1,0:T(8,128)(2,1)S(1)} %collective-permute-done.9.refs_0_, ...), custom_call_target="tpu_custom_call" | custom-call | tf_op jit(solution)/shard_map/finish/pallas_call | solution.py:387
  36.3 0.5 %collective-permute-start.13 = (bf16[180,256]{1,0:T(8,128)(2,1)S(1)}, bf16[180,256]{1,0:T(8,128)(2,1)S(1)}, u32[]{:S(2)}, u32[]{:S(2)}) collective-permute-start(bf16[180,256]{1,0:T(8,128)(2,1)S(1)} %get-tuple-element.60), channel_id=1, source_target_pairs={{0,1},{1,0},{2,3},{3,2},{4,5},{5,4},{6,7},{7,6},{8,9},{9,8},{10,11... | collective-permute-start | bytes 276488 | tf_op jit(solution)/shard_map/ppermute | solution.py:40
  36.8 0.0 collective-permute-start.11
  36.8 0.0 collective-permute-done.16.refs_0_
  36.8 1.7 %collective-permute-start.12 = (bf16[180,256]{1,0:T(8,128)(2,1)S(1)}, bf16[180,256]{1,0:T(8,128)(2,1)S(1)}, u32[]{:S(2)}, u32[]{:S(2)}) collective-permute-start(bf16[180,256]{1,0:T(8,128)(2,1)S(1)} %get-tuple-element.58), channel_id=1, source_target_pairs={{0,3},{1,2},{2,1},{3,0},{4,7},{5,6},{6,5},{7,4},{8,11},{9,10},{10,... | collective-permute-start | bytes 276488 | tf_op jit(solution)/shard_map/ppermute | solution.py:40
  38.5 0.6 %collective-permute-done.17.refs_1_ = bf16[180,384]{1,0:T(8,128)(2,1)S(1)} collective-permute-done((bf16[180,384]{1,0:T(8,128)(2,1)S(1)}, bf16[180,384]{1,0:T(8,128)(2,1)S(1)}, u32[]{:S(2)}, u32[]{:S(2)}) %collective-permute-start.17) | collective-permute-done | bytes 138272 | tf_op jit(solution)/shard_map/ppermute | solution.py:40
  39.2 0.0 collective-permute-done.18.refs_3_
  39.2 1.2 %add_chunk.3.refs_2_ = bf16[180,4,640]{2,1,0:T(4,128)(2,1)} custom-call(bf16[4,180,640]{2,1,0:T(8,128)(2,1)S(1)} %copy.19.grad_ref, bf16[180,384]{1,0:T(8,128)(2,1)S(1)} %collective-permute-done.16.refs_0_, bf16[180,384]{1,0:T(8,128)(2,1)S(1)} %collective-permute-done.17.refs_1_, bf16[180,384]{1,0:T(8,128)(2,1)S(1)} %get-tuple-element.65.refs_2_, ...), custom_call_target="tpu_custom_call" | custom-call | tf_op jit(solution)/shard_map/add_chunk/pallas_call | solution.py:458
  40.3 0.0 collective-permute-done.13.refs_1_
  40.3 0.8 %add_chunk.4.refs_2_ = bf16[180,4,640]{2,1,0:T(4,128)(2,1)} custom-call(bf16[4,180,640]{2,1,0:T(8,128)(2,1)S(1)} %copy.19.grad_ref, bf16[180,256]{1,0:T(8,128)(2,1)S(1)} %get-tuple-element.59.refs_0_, bf16[180,256]{1,0:T(8,128)(2,1)S(1)} %collective-permute-done.13.refs_1_, bf16[180,4,640]{2,1,0:T(4,128)(2,1)} %add_chunk.3.refs_2_), custom_call_target="tpu_custom_call", output_to_operand_aliasing={{}: (3, {})} | custom-call | tf_op jit(solution)/shard_map/add_chunk/pallas_call | solution.py:458
  41.2 0.0 collective-permute-done.11.refs_0_
  41.2 2.1 %collective-permute-done.12.refs_1_ = bf16[180,256]{1,0:T(8,128)(2,1)S(1)} collective-permute-done((bf16[180,256]{1,0:T(8,128)(2,1)S(1)}, bf16[180,256]{1,0:T(8,128)(2,1)S(1)}, u32[]{:S(2)}, u32[]{:S(2)}) %collective-permute-start.12) | collective-permute-done | bytes 92192 | tf_op jit(solution)/shard_map/ppermute | solution.py:40
  43.3 0.8 %add_chunk.5 = bf16[180,4,640]{2,1,0:T(4,128)(2,1)} custom-call(bf16[4,180,640]{2,1,0:T(8,128)(2,1)S(1)} %copy.19.grad_ref, bf16[180,256]{1,0:T(8,128)(2,1)S(1)} %collective-permute-done.11.refs_0_, bf16[180,256]{1,0:T(8,128)(2,1)S(1)} %collective-permute-done.12.refs_1_, bf16[180,4,640]{2,1,0:T(4,128)(2,1)} %add_chunk.4.refs_2_), custom_call_target="tpu_custom_call", output_to_operand_aliasing={{}: (3, {})} | custom-call | tf_op jit(solution)/shard_map/add_chunk/pallas_call | solution.py:458
  (6 shorter events, 0.0 us)
Async XLA Ops:
  0.0 2.8 %copy-start.1 = (bf16[1280,640]{1,0:T(8,128)(2,1)S(1)}, bf16[1280,640]{1,0:T(8,128)(2,1)}, u32[]{:S(2)}) copy-start(bf16[1280,640]{1,0:T(8,128)(2,1)} %wout_ref.3) | copy-start | bytes 4915204
  0.0 2.8 %copy-start.6 = (f32[1280]{0:T(1024)S(1)}, f32[1280]{0:T(1024)}, u32[]{:S(2)}) copy-start(f32[1280]{0:T(1024)} %bias_ref.3) | copy-start | bytes 15364
  0.0 2.8 %copy-start = (bf16[640,1280]{1,0:T(8,128)(2,1)S(1)}, bf16[640,1280]{1,0:T(8,128)(2,1)}, u32[]{:S(2)}) copy-start(bf16[640,1280]{1,0:T(8,128)(2,1)} %win_ref.3) | copy-start | bytes 4915204
  5.6 7.7 %collective-permute-start.3 = (bf16[160,384]{1,0:T(8,128)(2,1)S(1)}, bf16[160,384]{1,0:T(8,128)(2,1)S(1)}, u32[]{:S(2)}, u32[]{:S(2)}) collective-permute-start(bf16[160,384]{1,0:T(8,128)(2,1)S(1)} %get-tuple-element.42), channel_id=1, source_target_pairs={{0,2},{1,3},{2,0},{3,1},{4,6},{5,7},{6,4},{7,5},{8,10},{9,11},{10,... | collective-permute-start | bytes 368648 | tf_op jit(solution)/shard_map/ppermute | solution.py:40
  7.7 6.7 %collective-permute-start.4 = (bf16[160,384]{1,0:T(8,128)(2,1)S(1)}, bf16[160,384]{1,0:T(8,128)(2,1)S(1)}, u32[]{:S(2)}, u32[]{:S(2)}) collective-permute-start(bf16[160,384]{1,0:T(8,128)(2,1)S(1)} %get-tuple-element.43), channel_id=1, source_target_pairs={{0,3},{1,2},{2,1},{3,0},{4,7},{5,6},{6,5},{7,4},{8,11},{9,10},{10,... | collective-permute-start | bytes 368648 | tf_op jit(solution)/shard_map/ppermute | solution.py:40
  8.3 6.1 %collective-permute-start.5 = (bf16[160,384]{1,0:T(8,128)(2,1)S(1)}, bf16[160,384]{1,0:T(8,128)(2,1)S(1)}, u32[]{:S(2)}, u32[]{:S(2)}) collective-permute-start(bf16[160,384]{1,0:T(8,128)(2,1)S(1)} %get-tuple-element.44), channel_id=1, source_target_pairs={{0,1},{1,0},{2,3},{3,2},{4,5},{5,4},{6,7},{7,6},{8,9},{9,8},{10,11... | collective-permute-start | bytes 368648 | tf_op jit(solution)/shard_map/ppermute | solution.py:40
  8.6 5.0 %copy-start.2 = (bf16[4,320,640]{2,1,0:T(8,128)(2,1)S(1)}, bf16[4,320,640]{2,1,0:T(8,128)(2,1)}, u32[]{:S(2)}) copy-start(bf16[4,320,640]{2,1,0:T(8,128)(2,1)} %constant.4.clone.forth_ref) | copy-start | bytes 4915204
  8.6 5.0 %copy-start.3 = (bf16[768,640]{1,0:T(8,128)(2,1)S(1)}, bf16[768,640]{1,0:T(8,128)(2,1)}, u32[]{:S(2)}) copy-start(bf16[768,640]{1,0:T(8,128)(2,1)} %constant.5.clone.back_ref) | copy-start | bytes 2949124
  8.6 5.0 %copy-start.4 = (bf16[9,16,640]{2,1,0:T(8,128)(2,1)S(1)}, bf16[9,16,640]{2,1,0:T(8,128)(2,1)}, u32[]{:S(2)}) copy-start(bf16[9,16,640]{2,1,0:T(8,128)(2,1)} %filt_ref.1) | copy-start | bytes 552964
  8.6 5.0 %copy-start.5 = (f32[9,640]{1,0:T(8,128)S(1)}, f32[9,640]{1,0:T(8,128)}, u32[]{:S(2)}) copy-start(f32[9,640]{1,0:T(8,128)} %weight_ref.1) | copy-start | bytes 69124
  8.6 5.0 %copy-start.7 = (s32[16,9]{1,0:T(8,128)S(1)}, s32[16,9]{1,0:T(8,128)}, u32[]{:S(2)}) copy-start(s32[16,9]{1,0:T(8,128)} %offset_ref.1) | copy-start | bytes 1732
  11.4 3.8 %collective-permute-start.6 = (bf16[96,384]{1,0:T(8,128)(2,1)S(1)}, bf16[96,384]{1,0:T(8,128)(2,1)S(1)}, u32[]{:S(2)}, u32[]{:S(2)}) collective-permute-start(bf16[96,384]{1,0:T(8,128)(2,1)S(1)} %get-tuple-element.45), channel_id=1, source_target_pairs={{0,2},{1,3},{2,0},{3,1},{4,6},{5,7},{6,4},{7,5},{8,10},{9,11},{10,... | collective-permute-start | bytes 221192 | tf_op jit(solution)/shard_map/ppermute | solution.py:40
  12.9 4.8 %collective-permute-start.7 = (bf16[96,384]{1,0:T(8,128)(2,1)S(1)}, bf16[96,384]{1,0:T(8,128)(2,1)S(1)}, u32[]{:S(2)}, u32[]{:S(2)}) collective-permute-start(bf16[96,384]{1,0:T(8,128)(2,1)S(1)} %get-tuple-element.46), channel_id=1, source_target_pairs={{0,3},{1,2},{2,1},{3,0},{4,7},{5,6},{6,5},{7,4},{8,11},{9,10},{10,... | collective-permute-start | bytes 221192 | tf_op jit(solution)/shard_map/ppermute | solution.py:40
  13.3 4.4 %collective-permute-start.8 = (bf16[96,384]{1,0:T(8,128)(2,1)S(1)}, bf16[96,384]{1,0:T(8,128)(2,1)S(1)}, u32[]{:S(2)}, u32[]{:S(2)}) collective-permute-start(bf16[96,384]{1,0:T(8,128)(2,1)S(1)} %get-tuple-element.47), channel_id=1, source_target_pairs={{0,1},{1,0},{2,3},{3,2},{4,5},{5,4},{6,7},{7,6},{8,9},{9,8},{10,11... | collective-permute-start | bytes 221192 | tf_op jit(solution)/shard_map/ppermute | solution.py:40
  18.3 10.6 %collective-permute-start.14 = (bf16[3,96,640]{2,1,0:T(8,128)(2,1)S(1)}, bf16[3,96,640]{2,1,0:T(8,128)(2,1)S(1)}, u32[]{:S(2)}, u32[]{:S(2)}) collective-permute-start(bf16[3,96,640]{2,1,0:T(8,128)(2,1)S(1)} %get-tuple-element.61), channel_id=1, source_target_pairs={{0,4},{1,5},{2,6},{3,7},{4,0},{5,1},{6,2},{7,3},{8,12},{9,13},{10,... | collective-permute-start | bytes 1105928 | tf_op jit(solution)/shard_map/ppermute | solution.py:556
  19.7 9.7 %collective-permute-start.15 = (bf16[3,96,640]{2,1,0:T(8,128)(2,1)S(1)}, bf16[3,96,640]{2,1,0:T(8,128)(2,1)S(1)}, u32[]{:S(2)}, u32[]{:S(2)}) collective-permute-start(bf16[3,96,640]{2,1,0:T(8,128)(2,1)S(1)} %get-tuple-element.62), channel_id=1, source_target_pairs={{0,1},{1,0},{2,3},{3,2},{4,8},{5,9},{6,10},{7,11},{8,4},{9,5},{10,... | collective-permute-start | bytes 1105928 | tf_op jit(solution)/shard_map/ppermute | solution.py:556
  20.4 3.4 %collective-permute-start = (bf16[64,384]{1,0:T(8,128)(2,1)S(1)}, bf16[64,384]{1,0:T(8,128)(2,1)S(1)}, u32[]{:S(2)}, u32[]{:S(2)}) collective-permute-start(bf16[64,384]{1,0:T(8,128)(2,1)S(1)} %get-tuple-element.37), channel_id=1, source_target_pairs={{0,2},{1,3},{2,0},{3,1},{4,6},{5,7},{6,4},{7,5},{8,10},{9,11},{10,... | collective-permute-start | bytes 147464 | tf_op jit(solution)/shard_map/ppermute | solution.py:40
  20.7 4.5 %collective-permute-start.1 = (bf16[64,384]{1,0:T(8,128)(2,1)S(1)}, bf16[64,384]{1,0:T(8,128)(2,1)S(1)}, u32[]{:S(2)}, u32[]{:S(2)}) collective-permute-start(bf16[64,384]{1,0:T(8,128)(2,1)S(1)} %get-tuple-element.38), channel_id=1, source_target_pairs={{0,3},{1,2},{2,1},{3,0},{4,7},{5,6},{6,5},{7,4},{8,11},{9,10},{10,... | collective-permute-start | bytes 147464 | tf_op jit(solution)/shard_map/ppermute | solution.py:40
  22.0 3.2 %collective-permute-start.2 = (bf16[64,384]{1,0:T(8,128)(2,1)S(1)}, bf16[64,384]{1,0:T(8,128)(2,1)S(1)}, u32[]{:S(2)}, u32[]{:S(2)}) collective-permute-start(bf16[64,384]{1,0:T(8,128)(2,1)S(1)} %get-tuple-element.40), channel_id=1, source_target_pairs={{0,1},{1,0},{2,3},{3,2},{4,5},{5,4},{6,7},{7,6},{8,9},{9,8},{10,11... | collective-permute-start | bytes 147464 | tf_op jit(solution)/shard_map/ppermute | solution.py:40
  25.8 9.3 %collective-permute-start.9 = (bf16[3,64,640]{2,1,0:T(8,128)(2,1)S(1)}, bf16[3,64,640]{2,1,0:T(8,128)(2,1)S(1)}, u32[]{:S(2)}, u32[]{:S(2)}) collective-permute-start(bf16[3,64,640]{2,1,0:T(8,128)(2,1)S(1)} %get-tuple-element.54), channel_id=1, source_target_pairs={{0,4},{1,5},{2,6},{3,7},{4,0},{5,1},{6,2},{7,3},{8,12},{9,13},{10,... | collective-permute-start | bytes 737288 | tf_op jit(solution)/shard_map/ppermute | solution.py:556
  28.7 6.5 %collective-permute-start.10 = (bf16[3,64,640]{2,1,0:T(8,128)(2,1)S(1)}, bf16[3,64,640]{2,1,0:T(8,128)(2,1)S(1)}, u32[]{:S(2)}, u32[]{:S(2)}) collective-permute-start(bf16[3,64,640]{2,1,0:T(8,128)(2,1)S(1)} %get-tuple-element.55), channel_id=1, source_target_pairs={{0,1},{1,0},{2,3},{3,2},{4,8},{5,9},{6,10},{7,11},{8,4},{9,5},{10,... | collective-permute-start | bytes 737288 | tf_op jit(solution)/shard_map/ppermute | solution.py:556
  30.6 6.2 %collective-permute-start.16 = (bf16[180,384]{1,0:T(8,128)(2,1)S(1)}, bf16[180,384]{1,0:T(8,128)(2,1)S(1)}, u32[]{:S(2)}, u32[]{:S(2)}) collective-permute-start(bf16[180,384]{1,0:T(8,128)(2,1)S(1)} %get-tuple-element.63), channel_id=1, source_target_pairs={{0,2},{1,3},{2,0},{3,1},{4,6},{5,7},{6,4},{7,5},{8,10},{9,11},{10,... | collective-permute-start | bytes 414728 | tf_op jit(solution)/shard_map/ppermute | solution.py:40
  31.5 7.6 %collective-permute-start.17 = (bf16[180,384]{1,0:T(8,128)(2,1)S(1)}, bf16[180,384]{1,0:T(8,128)(2,1)S(1)}, u32[]{:S(2)}, u32[]{:S(2)}) collective-permute-start(bf16[180,384]{1,0:T(8,128)(2,1)S(1)} %get-tuple-element.64), channel_id=1, source_target_pairs={{0,3},{1,2},{2,1},{3,0},{4,7},{5,6},{6,5},{7,4},{8,11},{9,10},{10,... | collective-permute-start | bytes 414728 | tf_op jit(solution)/shard_map/ppermute | solution.py:40
  32.8 6.3 %collective-permute-start.18 = (bf16[180,384]{1,0:T(8,128)(2,1)S(1)}, bf16[180,384]{1,0:T(8,128)(2,1)S(1)}, u32[]{:S(2)}, u32[]{:S(2)}) collective-permute-start(bf16[180,384]{1,0:T(8,128)(2,1)S(1)} %get-tuple-element.66), channel_id=1, source_target_pairs={{0,1},{1,0},{2,3},{3,2},{4,5},{5,4},{6,7},{7,6},{8,9},{9,8},{10,11... | collective-permute-start | bytes 414728 | tf_op jit(solution)/shard_map/ppermute | solution.py:40
  36.3 4.1 %collective-permute-start.13 = (bf16[180,256]{1,0:T(8,128)(2,1)S(1)}, bf16[180,256]{1,0:T(8,128)(2,1)S(1)}, u32[]{:S(2)}, u32[]{:S(2)}) collective-permute-start(bf16[180,256]{1,0:T(8,128)(2,1)S(1)} %get-tuple-element.60), channel_id=1, source_target_pairs={{0,1},{1,0},{2,3},{3,2},{4,5},{5,4},{6,7},{7,6},{8,9},{9,8},{10,11... | collective-permute-start | bytes 276488 | tf_op jit(solution)/shard_map/ppermute | solution.py:40
  36.8 4.4 %collective-permute-start.11 = (bf16[180,256]{1,0:T(8,128)(2,1)S(1)}, bf16[180,256]{1,0:T(8,128)(2,1)S(1)}, u32[]{:S(2)}, u32[]{:S(2)}) collective-permute-start(bf16[180,256]{1,0:T(8,128)(2,1)S(1)} %get-tuple-element.57), channel_id=1, source_target_pairs={{0,2},{1,3},{2,0},{3,1},{4,6},{5,7},{6,4},{7,5},{8,10},{9,11},{10,... | collective-permute-start | bytes 276488 | tf_op jit(solution)/shard_map/ppermute | solution.py:40
  36.8 6.5 %collective-permute-start.12 = (bf16[180,256]{1,0:T(8,128)(2,1)S(1)}, bf16[180,256]{1,0:T(8,128)(2,1)S(1)}, u32[]{:S(2)}, u32[]{:S(2)}) collective-permute-start(bf16[180,256]{1,0:T(8,128)(2,1)S(1)} %get-tuple-element.58), channel_id=1, source_target_pairs={{0,3},{1,2},{2,1},{3,0},{4,7},{5,6},{6,5},{7,4},{8,11},{9,10},{10,... | collective-permute-start | bytes 276488 | tf_op jit(solution)/shard_map/ppermute | solution.py:40
